TPU v7x, 32 devices: a whole 2x2x4 slice. The times are simulated.
32 devices in a mesh: ctx: 16 (over z, y, x), tp: 2 (over core).
Axes of the slice: x: 2, y: 2, z: 4, core: 2. Of those that a mesh axis runs over, the one named last changes fastest.
Arguments:
- layer_cotangent: bfloat16 [4096, 5376], P('ctx', 'tp'), may hold values from -6 to 6
- out_weight: bfloat16 [2048, 5376], P(None, 'tp'), may hold values from -0.078125 to 0.078125
- queries: bfloat16 [4096, 2048], P('ctx', 'tp'), may hold values from -38 to 38
- keys: bfloat16 [4096, 1024], P('ctx', 'tp'), may hold values from -13 to 13
- values: bfloat16 [4096, 1024], P('ctx', 'tp'), may hold values from -6 to 6
Outputs:
- query_grads: bfloat16 [4096, 2048], P('ctx', 'tp')
- key_gradients: bfloat16 [4096, 1024], P('ctx', 'tp')
- value_gradients: bfloat16 [4096, 1024], P('ctx', 'tp')
All inputs are finite; a program needn't handle non-finite values.
Results may differ from a plain program's by a relative error of at most 0.03.
Values may be sent and summed in bfloat16 or wider, within the bound.
No kernel may reach another device: no remote copies, remote signals or barrier semaphores. Data moves between devices by JAX's collectives and lax.ppermute only.
A program may use at most 128 MiB of HBM per device.

v0:
```python
import jax
import jax.numpy as jnp
from jax import lax
from jax.sharding import PartitionSpec as P

HEAD_SIZE = 128
WINDOW_LENGTH = 1024


score_scale = 168.0 ** (-0.5)


def shifted(value, axis, steps):
    count = lax.axis_size(axis)
    leading, last = (max(0, -steps), min(count, count - steps))
    return lax.ppermute(value, axis, [(source, source + steps) for source in range(leading, last)])


def local(layer_cotangent, out_weight, queries, keys, values):
    tokens_here = queries.shape[0]
    query_heads = queries.shape[1] // HEAD_SIZE
    kv_heads = keys.shape[1] // HEAD_SIZE
    query_group = query_heads // kv_heads
    blocks_back = WINDOW_LENGTH // tokens_here
    head_rows = query_heads * HEAD_SIZE
    grads_turned = lax.psum_scatter(
        lax.dot_general(
            out_weight,
            layer_cotangent,
            (((1,), (1,)), ((), ())),
            preferred_element_type=jnp.float32,
        ).astype(jnp.bfloat16),
        "tp",
        scatter_dimension=0,
        tiled=True,
    )
    earlier = []
    for offset in range(blocks_back):
        earlier.append(shifted((keys, values), "ctx", offset + 1))
    key_whole = jnp.concatenate(
        [earlier[blocks_back - 1 - number][0] for number in range(blocks_back)] + [keys], axis=0
    )
    value_whole = jnp.concatenate(
        [earlier[blocks_back - 1 - number][1] for number in range(blocks_back)] + [values], axis=0
    )
    key_whole = key_whole.reshape(WINDOW_LENGTH + tokens_here, kv_heads, HEAD_SIZE)
    value_whole = value_whole.reshape(WINDOW_LENGTH + tokens_here, kv_heads, HEAD_SIZE)
    query_quad = queries.reshape(tokens_here, kv_heads, query_group, HEAD_SIZE)
    grads_four = grads_turned.reshape(kv_heads, query_group, HEAD_SIZE, tokens_here)
    base_pos = lax.axis_index("ctx") * tokens_here - WINDOW_LENGTH
    block = min(tokens_here, 512)
    key_total = jnp.zeros((WINDOW_LENGTH + tokens_here, kv_heads, HEAD_SIZE), jnp.float32)
    value_total = jnp.zeros((WINDOW_LENGTH + tokens_here, kv_heads, HEAD_SIZE), jnp.float32)
    row_ids = jnp.arange(block, dtype=jnp.int32)[:, None]
    col_ids = jnp.arange(block + WINDOW_LENGTH, dtype=jnp.int32)[None, :]
    reach = col_ids - row_ids
    visible = (reach >= 1) & (reach <= WINDOW_LENGTH) & (base_pos + 0 + col_ids >= 0)
    scores = (
        jnp.einsum("qhgd,khd->hgqk", query_quad, key_whole, preferred_element_type=jnp.float32)
        * score_scale
    )
    scores = jnp.where(visible, scores, -jnp.inf)
    top = jnp.max(scores, axis=-1, keepdims=True)
    expo = jnp.exp(scores - top)
    probs = expo / jnp.sum(expo, axis=-1, keepdims=True)
    probs_low = probs.astype(jnp.bfloat16)
    dprobs = jnp.einsum(
        "hgdq,khd->hgqk", grads_four, value_whole, preferred_element_type=jnp.float32
    )
    delta = jnp.sum(probs * dprobs, axis=-1, keepdims=True)
    dscores = (probs * (dprobs - delta) * score_scale).astype(jnp.bfloat16)
    query_part = jnp.einsum(
        "hgqk,khd->qhgd", dscores, key_whole, preferred_element_type=jnp.float32
    )
    query_pieces = query_part.astype(jnp.bfloat16).reshape(block, head_rows)
    key_part = jnp.einsum("hgqk,qhgd->khd", dscores, query_quad, preferred_element_type=jnp.float32)
    value_part = jnp.einsum(
        "hgqk,hgdq->khd", probs_low, grads_four, preferred_element_type=jnp.float32
    )
    key_total = key_total.at[0 : block + WINDOW_LENGTH].add(key_part)
    value_total = value_total.at[0 : block + WINDOW_LENGTH].add(value_part)
    flat_width = kv_heads * HEAD_SIZE
    key_sum = key_total[WINDOW_LENGTH:].reshape(tokens_here, flat_width)
    value_sum = value_total[WINDOW_LENGTH:].reshape(tokens_here, flat_width)
    key_parts = []
    value_parts = []
    for offset in range(1, blocks_back + 1):
        lower = WINDOW_LENGTH - offset * tokens_here
        key_parts.append(
            key_total[lower : lower + tokens_here]
            .reshape(tokens_here, flat_width)
            .astype(jnp.bfloat16)
        )
        value_parts.append(
            value_total[lower : lower + tokens_here]
            .reshape(tokens_here, flat_width)
            .astype(jnp.bfloat16)
        )
    for offset in range(1, blocks_back + 1):
        arrived = shifted((key_parts[offset - 1], value_parts[offset - 1]), "ctx", -offset)
        key_sum = key_sum + arrived[0].astype(jnp.float32)
        value_sum = value_sum + arrived[1].astype(jnp.float32)
    return (query_pieces, key_sum.astype(jnp.bfloat16), value_sum.astype(jnp.bfloat16))


def solution(mesh):
    in_specs = (P("ctx", "tp"), P(None, "tp"), P("ctx", "tp"), P("ctx", "tp"), P("ctx", "tp"))
    out_specs = (P("ctx", "tp"), P("ctx", "tp"), P("ctx", "tp"))
    return jax.shard_map(local, mesh=mesh, in_specs=in_specs, out_specs=out_specs, check_vma=False)
```

profile of v0, /device:TPU:24, one launch (start us, length us, event | category | flops | bytes accessed | tf_op | source)
XLA Modules:
  0.0 168.4 jit_solution(1896557641684807198)
XLA Ops:
  7.2 1.2 copy.28
  8.4 1.4 collective-permute-start
  9.9 4.4 %collective-permute-start.1 = (bf16[256,512]{0,1:T(8,128)(2,1)S(1)}, bf16[256,512]{0,1:T(8,128)(2,1)}, u32[]{:S(2)}, u32[]{:S(2)}) collective-permute-start(bf16[256,512]{0,1:T(8,128)(2,1)S(1)} %copy.28), channel_id=1, source_target_pairs={{0,6},{2,8},{4,10},{6,12},{8,14},{10,16},{12,18},{14,20},{16,22},{... | collective-permute-start | bytes 786440 | tf_op jit(solution)/shard_map/ppermute | solution.py:16
  14.2 1.9 %collective-permute-start.2 = (bf16[256,512]{0,1:T(8,128)(2,1)S(1)}, bf16[256,512]{0,1:T(8,128)(2,1)}, u32[]{:S(2)}, u32[]{:S(2)}) collective-permute-start(bf16[256,512]{0,1:T(8,128)(2,1)S(1)} %copy.28), channel_id=1, source_target_pairs={{0,4},{2,6},{4,8},{6,10},{8,12},{10,14},{12,16},{14,18},{16,20},{1... | collective-permute-start | bytes 786440 | tf_op jit(solution)/shard_map/ppermute | solution.py:16
  16.2 1.9 %collective-permute-start.3 = (bf16[256,512]{0,1:T(8,128)(2,1)S(1)}, bf16[256,512]{0,1:T(8,128)(2,1)S(1)}, u32[]{:S(2)}, u32[]{:S(2)}) collective-permute-start(bf16[256,512]{0,1:T(8,128)(2,1)S(1)} %copy.28), channel_id=1, source_target_pairs={{0,2},{2,4},{4,6},{6,8},{8,10},{10,12},{12,14},{14,16},{16,18},{18... | collective-permute-start | bytes 786440 | tf_op jit(solution)/shard_map/ppermute | solution.py:16
  18.1 8.3 %convolution_convert_fusion = bf16[2048,256]{1,0:T(8,128)(2,1)} fusion(bf16[2048,2688]{1,0:T(8,128)(2,1)} %param.14, bf16[256,2688]{1,0:T(8,128)(2,1)S(1)} %copy-done), kind=kOutput, calls=%fused_computation.18 | convolution fusion | flops 2819096576 | bytes 13434880 | tf_op jit(solution)/shard_map/dot_general | solution.py:27
  26.6 1.3 collective-permute-start.4
  28.4 1.9 %collective-permute-start.5 = (bf16[256,512]{0,1:T(8,128)(2,1)S(1)}, bf16[256,512]{0,1:T(8,128)(2,1)S(1)}, u32[]{:S(2)}, u32[]{:S(2)}) collective-permute-start(bf16[256,512]{0,1:T(8,128)(2,1)S(1)} %copy.35), channel_id=1, source_target_pairs={{0,6},{2,8},{4,10},{6,12},{8,14},{10,16},{12,18},{14,20},{16,22},{... | collective-permute-start | bytes 786440 | tf_op jit(solution)/shard_map/ppermute | solution.py:16
  31.3 1.9 %collective-permute-start.6 = (bf16[256,512]{0,1:T(8,128)(2,1)S(1)}, bf16[256,512]{0,1:T(8,128)(2,1)S(1)}, u32[]{:S(2)}, u32[]{:S(2)}) collective-permute-start(bf16[256,512]{0,1:T(8,128)(2,1)S(1)} %copy.35), channel_id=1, source_target_pairs={{0,4},{2,6},{4,8},{6,10},{8,12},{10,14},{12,16},{14,18},{16,20},{1... | collective-permute-start | bytes 786440 | tf_op jit(solution)/shard_map/ppermute | solution.py:16
  34.2 2.1 %collective-permute-start.7 = (bf16[256,512]{0,1:T(8,128)(2,1)S(1)}, bf16[256,512]{0,1:T(8,128)(2,1)S(1)}, u32[]{:S(2)}, u32[]{:S(2)}) collective-permute-start(bf16[256,512]{0,1:T(8,128)(2,1)S(1)} %copy.35), channel_id=1, source_target_pairs={{0,2},{2,4},{4,6},{6,8},{8,10},{10,12},{12,14},{14,16},{16,18},{18... | collective-permute-start | bytes 786440 | tf_op jit(solution)/shard_map/ppermute | solution.py:16
  38.5 1.9 %constant_dynamic-update-slice_fusion.9 = bf16[1280,512]{0,1:T(8,128)(2,1)} fusion(bf16[256,512]{0,1:T(8,128)(2,1)} %collective-permute-done.4), kind=kLoop, calls=%fused_computation.36 | loop fusion | bytes 524288
  40.4 3.6 %collective-permute-done.5 = bf16[256,512]{0,1:T(8,128)(2,1)S(1)} collective-permute-done((bf16[256,512]{0,1:T(8,128)(2,1)S(1)}, bf16[256,512]{0,1:T(8,128)(2,1)S(1)}, u32[]{:S(2)}, u32[]{:S(2)}) %collective-permute-start.5) | collective-permute-done | bytes 262176 | tf_op jit(solution)/shard_map/ppermute | solution.py:16
  44.8 3.7 %collective-permute-done.6 = bf16[256,512]{0,1:T(8,128)(2,1)S(1)} collective-permute-done((bf16[256,512]{0,1:T(8,128)(2,1)S(1)}, bf16[256,512]{0,1:T(8,128)(2,1)S(1)}, u32[]{:S(2)}, u32[]{:S(2)}) %collective-permute-start.6) | collective-permute-done | bytes 262176 | tf_op jit(solution)/shard_map/ppermute | solution.py:16
  49.2 10.6 %collective-permute-done.7 = bf16[256,512]{0,1:T(8,128)(2,1)S(1)} collective-permute-done((bf16[256,512]{0,1:T(8,128)(2,1)S(1)}, bf16[256,512]{0,1:T(8,128)(2,1)S(1)}, u32[]{:S(2)}, u32[]{:S(2)}) %collective-permute-start.7) | collective-permute-done | bytes 262176 | tf_op jit(solution)/shard_map/ppermute | solution.py:16
  61.2 8.9 %fusion.40 = (f32[4,2,256]{2,1,0:T(2,128)S(1)}, f32[4,2,256,1280]{2,3,1,0:T(8,128)}) fusion(pred[256,1280]{0,1:T(8,128)(4,1)S(1)} %fusion.26, bf16[1280,4,128,1]{0,2,3,1:T(8,128)(2,1)} %bitcast.78, bf16[256,4,2,128]{0,3,2,1:T(8,128)(2,1)S(1)} %bitcast.74), kind=kOutput, calls=%fused_computation.47 | convolution fusion | flops 681575680 | bytes 12656640 | tf_op jit(solution)/shard_map/sub | solution.py:64
  70.1 8.5 %fusion.44 = (bf16[1280,4,128]{0,2,1:T(8,128)(2,1)}, f32[1280,4,128]{0,2,1:T(8,128)}) fusion(bf16[4,2,128,256]{3,2,1,0:T(8,128)(2,1)} %bitcast.72, f32[4,2,256]{2,1,0:T(2,128)S(1)} %get-tuple-element.57, pred[256,1280]{0,1:T(8,128)(4,1)S(1)} %fusion.26, bf16[1280,4,128,1]{0,2,3,1:T(8,128)(2,1)} %bitcast.79, bf16[256,4,2,128]{0,3,2,1:T(8,128)(2,1)S(1)} %bitcast.75), kind=kOutput, calls=%fused_computation.49 | convolution fusion | flops 1355943168 | bytes 6627328 | tf_op jit(solution)/shard_map/hgqk,hgdq->khd/dot_general | solution.py:77
  78.6 1.3 fusion.38
  80.8 1.9 %collective-permute-start.12 = (bf16[256,512]{1,0:T(8,128)(2,1)}, bf16[256,512]{1,0:T(8,128)(2,1)}, u32[]{:S(2)}, u32[]{:S(2)}) collective-permute-start(bf16[256,512]{1,0:T(8,128)(2,1)} %copy.53), channel_id=1, source_target_pairs={{2,0},{4,2},{6,4},{8,6},{10,8},{12,10},{14,12},{16,14},{18,16},{20... | collective-permute-start | bytes 786440 | tf_op jit(solution)/shard_map/ppermute | solution.py:16
  83.5 1.9 %collective-permute-start.13 = (bf16[256,512]{1,0:T(8,128)(2,1)}, bf16[256,512]{1,0:T(8,128)(2,1)}, u32[]{:S(2)}, u32[]{:S(2)}) collective-permute-start(bf16[256,512]{1,0:T(8,128)(2,1)} %copy.55), channel_id=1, source_target_pairs={{4,0},{6,2},{8,4},{10,6},{12,8},{14,10},{16,12},{18,14},{20,16},{2... | collective-permute-start | bytes 786440 | tf_op jit(solution)/shard_map/ppermute | solution.py:16
  86.3 3.8 %collective-permute-start.14 = (bf16[256,512]{1,0:T(8,128)(2,1)}, bf16[256,512]{1,0:T(8,128)(2,1)}, u32[]{:S(2)}, u32[]{:S(2)}) collective-permute-start(bf16[256,512]{1,0:T(8,128)(2,1)} %copy.56), channel_id=1, source_target_pairs={{6,0},{8,2},{10,4},{12,6},{14,8},{16,10},{18,12},{20,14},{22,16},{... | collective-permute-start | bytes 786440 | tf_op jit(solution)/shard_map/ppermute | solution.py:16
  90.9 3.0 %collective-permute-start.15 = (bf16[256,512]{1,0:T(8,128)(2,1)}, bf16[256,512]{1,0:T(8,128)(2,1)}, u32[]{:S(2)}, u32[]{:S(2)}) collective-permute-start(bf16[256,512]{1,0:T(8,128)(2,1)} %copy.57), channel_id=1, source_target_pairs={{8,0},{10,2},{12,4},{14,6},{16,8},{18,10},{20,12},{22,14},{24,16},... | collective-permute-start | bytes 786440 | tf_op jit(solution)/shard_map/ppermute | solution.py:16
  95.3 6.7 %fusion.45 = f32[4,2,256,1280]{2,3,1,0:T(8,128)} fusion(bf16[4,2,128,256]{3,2,1,0:T(8,128)(2,1)S(1)} %bitcast.73, bf16[1280,4,128,1]{0,2,3,1:T(8,128)(2,1)} %bitcast.32), kind=kOutput, calls=%fused_computation.50 | convolution fusion | flops 671088640 | bytes 12320768 | tf_op jit(solution)/shard_map/hgdq,khd->hgqk/dot_general | solution.py:67
  102.0 16.9 %fusion.41 = (bf16[1280,4,128]{0,2,1:T(8,128)(2,1)}, f32[1280,4,128]{0,2,1:T(8,128)}) fusion(bf16[256,4,2,128]{0,3,2,1:T(8,128)(2,1)S(1)} %bitcast.76, f32[4,2,256,1280]{2,3,1,0:T(8,128)} %fusion.45, f32[4,2,256,1280]{2,3,1,0:T(8,128)} %get-tuple-element.58, f32[4,2,256]{2,1,0:T(2,128)S(1)} %get-tuple-element.57), kind=kOutput, calls=%fused_computation.48 | convolution fusion | flops 690097408 | bytes 25436160 | tf_op jit(solution)/shard_map/hgqk,qhgd->khd/dot_general | solution.py:76
  118.9 1.3 fusion.39
  121.1 2.3 %collective-permute-start.10 = (bf16[256,512]{1,0:T(8,128)(2,1)}, bf16[256,512]{1,0:T(8,128)(2,1)S(1)}, u32[]{:S(2)}, u32[]{:S(2)}) collective-permute-start(bf16[256,512]{1,0:T(8,128)(2,1)} %copy.50), channel_id=1, source_target_pairs={{6,0},{8,2},{10,4},{12,6},{14,8},{16,10},{18,12},{20,14},{22,16},{... | collective-permute-start | bytes 786440 | tf_op jit(solution)/shard_map/ppermute | solution.py:16
  127.3 15.2 %fusion.27 = bf16[4,128,2,256]{3,1,2,0:T(8,128)(2,1)S(1)} fusion(bf16[1280,4,128,1]{0,2,3,1:T(8,128)(2,1)} %bitcast.80, f32[4,2,256,1280]{2,3,1,0:T(8,128)} %fusion.45, f32[4,2,256,1280]{2,3,1,0:T(8,128)} %get-tuple-element.58, f32[4,2,256]{2,1,0:T(2,128)S(1)} %get-tuple-element.57), kind=kOutput, calls=%fused_computation.24 | convolution fusion | flops 689704192 | bytes 22814720 | tf_op jit(solution)/shard_map/hgqk,khd->qhgd/dot_general | solution.py:72
  143.5 1.3 collective-permute-start.11
  144.8 4.0 %collective-permute-start.8 = (bf16[256,512]{1,0:T(8,128)(2,1)}, bf16[256,512]{1,0:T(8,128)(2,1)S(1)}, u32[]{:S(2)}, u32[]{:S(2)}) collective-permute-start(bf16[256,512]{1,0:T(8,128)(2,1)} %copy.47), channel_id=1, source_target_pairs={{2,0},{4,2},{6,4},{8,6},{10,8},{12,10},{14,12},{16,14},{18,16},{20... | collective-permute-start | bytes 786440 | tf_op jit(solution)/shard_map/ppermute | solution.py:16
  148.8 1.9 %collective-permute-start.9 = (bf16[256,512]{1,0:T(8,128)(2,1)}, bf16[256,512]{1,0:T(8,128)(2,1)S(1)}, u32[]{:S(2)}, u32[]{:S(2)}) collective-permute-start(bf16[256,512]{1,0:T(8,128)(2,1)} %copy.49), channel_id=1, source_target_pairs={{4,0},{6,2},{8,4},{10,6},{12,8},{14,10},{16,12},{18,14},{20,16},{2... | collective-permute-start | bytes 786440 | tf_op jit(solution)/shard_map/ppermute | solution.py:16
  150.7 2.1 %add_convert_fusion = bf16[256,512]{1,0:T(8,128)(2,1)} fusion(bf16[256,512]{1,0:T(8,128)(2,1)} %collective-permute-done.15, bf16[256,512]{1,0:T(8,128)(2,1)} %collective-permute-done.14, bf16[256,512]{1,0:T(8,128)(2,1)} %collective-permute-done.13, f32[256,512]{1,0:T(8,128)S(1)} %copy.54, bf16[256,512]{1,0:T(8,128)(2,1)} %collective-permute-done.12), kind=kLoop, calls=%fused_computation.25 | loop fusion | flops 1179648 | bytes 1835008 | tf_op jit(solution)/shard_map/convert_element_type | solution.py:103
  152.8 4.1 %collective-permute-done.8 = bf16[256,512]{1,0:T(8,128)(2,1)S(1)} collective-permute-done((bf16[256,512]{1,0:T(8,128)(2,1)}, bf16[256,512]{1,0:T(8,128)(2,1)S(1)}, u32[]{:S(2)}, u32[]{:S(2)}) %collective-permute-start.8) | collective-permute-done | bytes 262176 | tf_op jit(solution)/shard_map/ppermute | solution.py:16
  156.9 3.8 %collective-permute-done.9 = bf16[256,512]{1,0:T(8,128)(2,1)S(1)} collective-permute-done((bf16[256,512]{1,0:T(8,128)(2,1)}, bf16[256,512]{1,0:T(8,128)(2,1)S(1)}, u32[]{:S(2)}, u32[]{:S(2)}) %collective-permute-start.9) | collective-permute-done | bytes 262176 | tf_op jit(solution)/shard_map/ppermute | solution.py:16
  (51 shorter events, 19.0 us)
Async XLA Ops:
  7.2 10.9 %copy-start = (bf16[256,2688]{1,0:T(8,128)(2,1)S(1)}, bf16[256,2688]{1,0:T(8,128)(2,1)}, u32[]{:S(2)}) copy-start(bf16[256,2688]{1,0:T(8,128)(2,1)} %param.13) | copy-start | bytes 4128772
  7.2 62.9 %reduce-scatter.2.cloned.1.call-start = ((), (), s32[]{:S(2)}) async-start(), calls=%async_computation.1 | async-start | bytes 1572864 | tf_op jit(solution)/shard_map/reduce_scatter | solution.py:26
  8.4 18.0 %copy-start.3 = (bf16[256,512]{1,0:T(8,128)(2,1)S(1)}, bf16[256,512]{1,0:T(8,128)(2,1)}, u32[]{:S(2)}) copy-start(bf16[256,512]{1,0:T(8,128)(2,1)} %param.17) | copy-start | bytes 786436
  8.4 19.7 %copy-start.2 = (bf16[256,1024]{1,0:T(8,128)(2,1)S(1)}, bf16[256,1024]{1,0:T(8,128)(2,1)}, u32[]{:S(2)}) copy-start(bf16[256,1024]{1,0:T(8,128)(2,1)} %param.15) | copy-start | bytes 1572868
  8.4 19.9 %collective-permute-start = (bf16[256,512]{0,1:T(8,128)(2,1)S(1)}, bf16[256,512]{0,1:T(8,128)(2,1)}, u32[]{:S(2)}, u32[]{:S(2)}) collective-permute-start(bf16[256,512]{0,1:T(8,128)(2,1)S(1)} %copy.28), channel_id=1, source_target_pairs={{0,8},{2,10},{4,12},{6,14},{8,16},{10,18},{12,20},{14,22},{16,24},... | collective-permute-start | bytes 786440 | tf_op jit(solution)/shard_map/ppermute | solution.py:16
  9.9 21.4 %collective-permute-start.1 = (bf16[256,512]{0,1:T(8,128)(2,1)S(1)}, bf16[256,512]{0,1:T(8,128)(2,1)}, u32[]{:S(2)}, u32[]{:S(2)}) collective-permute-start(bf16[256,512]{0,1:T(8,128)(2,1)S(1)} %copy.28), channel_id=1, source_target_pairs={{0,6},{2,8},{4,10},{6,12},{8,14},{10,16},{12,18},{14,20},{16,22},{... | collective-permute-start | bytes 786440 | tf_op jit(solution)/shard_map/ppermute | solution.py:16
  14.2 20.0 %collective-permute-start.2 = (bf16[256,512]{0,1:T(8,128)(2,1)S(1)}, bf16[256,512]{0,1:T(8,128)(2,1)}, u32[]{:S(2)}, u32[]{:S(2)}) collective-permute-start(bf16[256,512]{0,1:T(8,128)(2,1)S(1)} %copy.28), channel_id=1, source_target_pairs={{0,4},{2,6},{4,8},{6,10},{8,12},{10,14},{12,16},{14,18},{16,20},{1... | collective-permute-start | bytes 786440 | tf_op jit(solution)/shard_map/ppermute | solution.py:16
  16.2 22.2 %collective-permute-start.3 = (bf16[256,512]{0,1:T(8,128)(2,1)S(1)}, bf16[256,512]{0,1:T(8,128)(2,1)S(1)}, u32[]{:S(2)}, u32[]{:S(2)}) collective-permute-start(bf16[256,512]{0,1:T(8,128)(2,1)S(1)} %copy.28), channel_id=1, source_target_pairs={{0,2},{2,4},{4,6},{6,8},{8,10},{10,12},{12,14},{14,16},{16,18},{18... | collective-permute-start | bytes 786440 | tf_op jit(solution)/shard_map/ppermute | solution.py:16
  26.6 11.9 %collective-permute-start.4 = (bf16[256,512]{0,1:T(8,128)(2,1)S(1)}, bf16[256,512]{0,1:T(8,128)(2,1)}, u32[]{:S(2)}, u32[]{:S(2)}) collective-permute-start(bf16[256,512]{0,1:T(8,128)(2,1)S(1)} %copy.35), channel_id=1, source_target_pairs={{0,8},{2,10},{4,12},{6,14},{8,16},{10,18},{12,20},{14,22},{16,24},... | collective-permute-start | bytes 786440 | tf_op jit(solution)/shard_map/ppermute | solution.py:16
  28.4 15.7 %collective-permute-start.5 = (bf16[256,512]{0,1:T(8,128)(2,1)S(1)}, bf16[256,512]{0,1:T(8,128)(2,1)S(1)}, u32[]{:S(2)}, u32[]{:S(2)}) collective-permute-start(bf16[256,512]{0,1:T(8,128)(2,1)S(1)} %copy.35), channel_id=1, source_target_pairs={{0,6},{2,8},{4,10},{6,12},{8,14},{10,16},{12,18},{14,20},{16,22},{... | collective-permute-start | bytes 786440 | tf_op jit(solution)/shard_map/ppermute | solution.py:16
  31.3 17.1 %collective-permute-start.6 = (bf16[256,512]{0,1:T(8,128)(2,1)S(1)}, bf16[256,512]{0,1:T(8,128)(2,1)S(1)}, u32[]{:S(2)}, u32[]{:S(2)}) collective-permute-start(bf16[256,512]{0,1:T(8,128)(2,1)S(1)} %copy.35), channel_id=1, source_target_pairs={{0,4},{2,6},{4,8},{6,10},{8,12},{10,14},{12,16},{14,18},{16,20},{1... | collective-permute-start | bytes 786440 | tf_op jit(solution)/shard_map/ppermute | solution.py:16
  34.2 25.5 %collective-permute-start.7 = (bf16[256,512]{0,1:T(8,128)(2,1)S(1)}, bf16[256,512]{0,1:T(8,128)(2,1)S(1)}, u32[]{:S(2)}, u32[]{:S(2)}) collective-permute-start(bf16[256,512]{0,1:T(8,128)(2,1)S(1)} %copy.35), channel_id=1, source_target_pairs={{0,2},{2,4},{4,6},{6,8},{8,10},{10,12},{12,14},{14,16},{16,18},{18... | collective-permute-start | bytes 786440 | tf_op jit(solution)/shard_map/ppermute | solution.py:16
  38.5 22.8 %copy-start.4 = (bf16[1280,512]{0,1:T(8,128)(2,1)}, bf16[1280,512]{0,1:T(8,128)(2,1)S(1)}, u32[]{:S(2)}) copy-start(bf16[1280,512]{0,1:T(8,128)(2,1)S(1)} %constant_dynamic-update-slice_fusion) | copy-start | bytes 3932164
  78.6 16.7 %copy-start.1 = (bf16[1024,256]{1,0:T(8,128)(2,1)S(1)}, bf16[1024,256]{1,0:T(8,128)(2,1)}, u32[]{:S(2)}) copy-start(bf16[1024,256]{1,0:T(8,128)(2,1)} %reduce-scatter.2.cloned.1.call-done) | copy-start | bytes 1572868
  80.8 62.7 %collective-permute-start.12 = (bf16[256,512]{1,0:T(8,128)(2,1)}, bf16[256,512]{1,0:T(8,128)(2,1)}, u32[]{:S(2)}, u32[]{:S(2)}) collective-permute-start(bf16[256,512]{1,0:T(8,128)(2,1)} %copy.53), channel_id=1, source_target_pairs={{2,0},{4,2},{6,4},{8,6},{10,8},{12,10},{14,12},{16,14},{18,16},{20... | collective-permute-start | bytes 786440 | tf_op jit(solution)/shard_map/ppermute | solution.py:16
  83.5 61.2 %collective-permute-start.13 = (bf16[256,512]{1,0:T(8,128)(2,1)}, bf16[256,512]{1,0:T(8,128)(2,1)}, u32[]{:S(2)}, u32[]{:S(2)}) collective-permute-start(bf16[256,512]{1,0:T(8,128)(2,1)} %copy.55), channel_id=1, source_target_pairs={{4,0},{6,2},{8,4},{10,6},{12,8},{14,10},{16,12},{18,14},{20,16},{2... | collective-permute-start | bytes 786440 | tf_op jit(solution)/shard_map/ppermute | solution.py:16
  86.3 62.5 %collective-permute-start.14 = (bf16[256,512]{1,0:T(8,128)(2,1)}, bf16[256,512]{1,0:T(8,128)(2,1)}, u32[]{:S(2)}, u32[]{:S(2)}) collective-permute-start(bf16[256,512]{1,0:T(8,128)(2,1)} %copy.56), channel_id=1, source_target_pairs={{6,0},{8,2},{10,4},{12,6},{14,8},{16,10},{18,12},{20,14},{22,16},{... | collective-permute-start | bytes 786440 | tf_op jit(solution)/shard_map/ppermute | solution.py:16
  90.9 59.8 %collective-permute-start.15 = (bf16[256,512]{1,0:T(8,128)(2,1)}, bf16[256,512]{1,0:T(8,128)(2,1)}, u32[]{:S(2)}, u32[]{:S(2)}) collective-permute-start(bf16[256,512]{1,0:T(8,128)(2,1)} %copy.57), channel_id=1, source_target_pairs={{8,0},{10,2},{12,4},{14,6},{16,8},{18,10},{20,12},{22,14},{24,16},... | collective-permute-start | bytes 786440 | tf_op jit(solution)/shard_map/ppermute | solution.py:16
  121.1 31.7 %collective-permute-start.10 = (bf16[256,512]{1,0:T(8,128)(2,1)}, bf16[256,512]{1,0:T(8,128)(2,1)S(1)}, u32[]{:S(2)}, u32[]{:S(2)}) collective-permute-start(bf16[256,512]{1,0:T(8,128)(2,1)} %copy.50), channel_id=1, source_target_pairs={{6,0},{8,2},{10,4},{12,6},{14,8},{16,10},{18,12},{20,14},{22,16},{... | collective-permute-start | bytes 786440 | tf_op jit(solution)/shard_map/ppermute | solution.py:16
  143.5 9.3 %collective-permute-start.11 = (bf16[256,512]{1,0:T(8,128)(2,1)}, bf16[256,512]{1,0:T(8,128)(2,1)S(1)}, u32[]{:S(2)}, u32[]{:S(2)}) collective-permute-start(bf16[256,512]{1,0:T(8,128)(2,1)} %copy.51), channel_id=1, source_target_pairs={{8,0},{10,2},{12,4},{14,6},{16,8},{18,10},{20,12},{22,14},{24,16},... | collective-permute-start | bytes 786440 | tf_op jit(solution)/shard_map/ppermute | solution.py:16
  144.8 12.1 %collective-permute-start.8 = (bf16[256,512]{1,0:T(8,128)(2,1)}, bf16[256,512]{1,0:T(8,128)(2,1)S(1)}, u32[]{:S(2)}, u32[]{:S(2)}) collective-permute-start(bf16[256,512]{1,0:T(8,128)(2,1)} %copy.47), channel_id=1, source_target_pairs={{2,0},{4,2},{6,4},{8,6},{10,8},{12,10},{14,12},{16,14},{18,16},{20... | collective-permute-start | bytes 786440 | tf_op jit(solution)/shard_map/ppermute | solution.py:16
  148.8 11.9 %collective-permute-start.9 = (bf16[256,512]{1,0:T(8,128)(2,1)}, bf16[256,512]{1,0:T(8,128)(2,1)S(1)}, u32[]{:S(2)}, u32[]{:S(2)}) collective-permute-start(bf16[256,512]{1,0:T(8,128)(2,1)} %copy.49), channel_id=1, source_target_pairs={{4,0},{6,2},{8,4},{10,6},{12,8},{14,10},{16,12},{18,14},{20,16},{2... | collective-permute-start | bytes 786440 | tf_op jit(solution)/shard_map/ppermute | solution.py:16
Sparse Core Ops, SparseCore 0:
  26.6 11.9 reduce-scatter.1
where the time goes:
time: 171 us; the launch traced here: 168 us
  matrix products  64.4 us (38%)
  starting transfers between devices  37.1 us (22%)
  waiting for transfers between devices  26.9 us (16%)
  local copies, waits for them, and re-layouts  22.4 us (13%)
  between operations  14.4 us (8%)
  other arithmetic  3.19 us (2%)
    ppermute x16, starting transfers between devices, shifted(): lax.ppermute(value, axis, [(source, source + steps) for source in range(l...  37 us
    ppermute x16, waiting for transfers between devices, shifted(): lax.ppermute(value, axis, [(source, source + steps) for source in range(l...  26.9 us
    dot_general x1, matrix products, local(): jnp.einsum('hgqk,qhgd->khd', dscores, query_quad, preferred_element_type=...  16.9 us
    dot_general x1, matrix products, local(): jnp.einsum('hgqk,khd->qhgd', dscores, key_whole, preferred_element_type=j...  15.2 us
    unnamed x21, local copies, waits for them, and re-layouts  9.4 us
    sub x1, matrix products, local(): expo = jnp.exp(scores - top)  8.86 us
    dot_general x1, matrix products, local(): jnp.einsum('hgqk,hgdq->khd', probs_low, grads_four, preferred_element_typ...  8.45 us
    dot_general x1, matrix products, local(): lax.dot_general(out_weight, layer_cotangent, (((1,), (1,)), ((), ())), pr...  8.31 us
  transfers between devices with their start and end apart: 17, of which 6 were waited for; matrix products, arithmetic and copies ran while one was open for 46% of the time, Pallas kernels for 0%

commit v1 on v0

v1 whole, which is shorter than its diff:
```python
import functools

import jax
import jax.numpy as jnp
from jax import lax
from jax.experimental import pallas as pl
from jax.experimental.pallas import tpu as pltpu
from jax.sharding import PartitionSpec as P

HEAD_SIZE = 128
WINDOW_LENGTH = 1024
LOG2_E = 1.4426950408889634

score_scale = 168.0 ** (-0.5)

VMEM = pl.BlockSpec(memory_space=pltpu.VMEM)
SMEM = pl.BlockSpec(memory_space=pltpu.SMEM)
NT = (((1,), (1,)), ((), ()))
NN = (((1,), (0,)), ((), ()))


def shifted(value, axis, steps):
    count = lax.axis_size(axis)
    leading, last = (max(0, -steps), min(count, count - steps))
    return lax.ppermute(value, axis, [(source, source + steps) for source in range(leading, last)])


def swapped(value, axis, bits):
    count = lax.axis_size(axis)
    return lax.ppermute(value, axis, [(source, source ^ bits) for source in range(count)])


def call(body, outs, scratch=(), flops=0, count=0, exps=0):
    def run(*args):
        moved = sum(a.size * a.dtype.itemsize for a in args)
        moved += sum(o.size * o.dtype.itemsize for o in outs)
        return pl.pallas_call(
            body,
            out_shape=tuple(outs),
            in_specs=[SMEM] + [VMEM] * (len(args) - 1),
            out_specs=tuple(VMEM for _ in outs),
            scratch_shapes=list(scratch),
            compiler_params=pltpu.CompilerParams(vmem_limit_bytes=48 * 1024 * 1024),
            cost_estimate=pl.CostEstimate(flops=flops, bytes_accessed=moved, transcendentals=exps),
        )(*args)

    return run


def lanes(index, width):
    return pl.ds(pl.multiple_of(index * width, width), width)


def pack_inputs(group, ids, keys, values, queries):
    tokens = keys.shape[0]
    kv_width, query_width = keys.shape[1] // group, queries.shape[1] // group

    def body(ids_ref, k_ref, v_ref, q_ref, *out_refs):
        for r in range(group):
            member = ids_ref[0] ^ r
            out_refs[r][:, :kv_width] = k_ref[:, lanes(member, kv_width)]
            out_refs[r][:, kv_width : 2 * kv_width] = v_ref[:, lanes(member, kv_width)]
            out_refs[r][:, 2 * kv_width :] = q_ref[:, lanes(member, query_width)]

    outs = [jax.ShapeDtypeStruct((tokens, 2 * kv_width + query_width), jnp.bfloat16)] * group
    return call(body, outs)(ids, keys, values, queries)


def order_inputs(group, ids, pieces, kv_width):
    tokens, width = pieces[0].shape

    def body(ids_ref, *refs):
        kv_ref, q_ref = refs[group:]
        for r in range(group):
            member = ids_ref[0] ^ r
            kv_ref[member] = refs[r][:, : 2 * kv_width]
            q_ref[member] = refs[r][:, 2 * kv_width :]

    outs = [
        jax.ShapeDtypeStruct((group, tokens, 2 * kv_width), jnp.bfloat16),
        jax.ShapeDtypeStruct((group, tokens, width - 2 * kv_width), jnp.bfloat16),
    ]
    return call(body, outs)(ids, *pieces)


def head_product(start, rows, out_weight, layer_cotangent):
    tokens, depth = layer_cotangent.shape
    tile = min(rows, 256)
    steps = rows // tile

    def body(start_ref, w_ref, c_ref, o_ref):
        o_ref[...] = lax.dot_general(
            w_ref[...], c_ref[...], NT, preferred_element_type=jnp.float32
        ).astype(jnp.bfloat16)

    return pl.pallas_call(
        body,
        out_shape=jax.ShapeDtypeStruct((rows, tokens), jnp.bfloat16),
        grid_spec=pltpu.PrefetchScalarGridSpec(
            num_scalar_prefetch=1,
            grid=(steps,),
            in_specs=[
                pl.BlockSpec((tile, depth), lambda i, s: (s[0] * steps + i, 0)),
                pl.BlockSpec((tokens, depth), lambda i, s: (0, 0)),
            ],
            out_specs=pl.BlockSpec((tile, tokens), lambda i, s: (i, 0)),
        ),
        compiler_params=pltpu.CompilerParams(vmem_limit_bytes=48 * 1024 * 1024),
        cost_estimate=pl.CostEstimate(
            flops=2 * rows * tokens * depth,
            bytes_accessed=2 * (rows * depth + tokens * depth + rows * tokens),
            transcendentals=0,
        ),
    )(start, out_weight, layer_cotangent)


def pack_grads(group, ids, terms):
    rows, tokens = terms[0].shape
    rows //= group

    def body(ids_ref, *refs):
        for r in range(group):
            there = lanes(ids_ref[0] ^ r, rows)
            total = refs[0][there, :]
            if len(terms) > 1:
                total = total.astype(jnp.float32)
                for term in refs[1 : len(terms)]:
                    total = total + term[there, :].astype(jnp.float32)
            refs[len(terms) + r][...] = total.astype(jnp.bfloat16)

    outs = [jax.ShapeDtypeStruct((rows, tokens), jnp.bfloat16)] * group
    return call(body, outs)(ids, *terms)


def attention(group, heads, per_head, ids, kv_own, kv_earlier, queries, grads):
    back = len(kv_earlier) * group
    tokens = kv_own.shape[1]
    span = back + 1
    total = back + group
    wide = per_head * tokens
    kv_width = heads * HEAD_SIZE
    factor = score_scale * LOG2_E

    def body(ids_ref, *refs):
        own_ref = refs[0]
        earlier_refs = refs[1 : 1 + len(kv_earlier)]
        q_ref = refs[1 + len(kv_earlier)]
        grad_refs = refs[2 + len(kv_earlier) : 2 + len(kv_earlier) + group]
        refs = refs[2 + len(kv_earlier) + group :]
        dq_refs, dkv_own, dkv_earlier = refs[:group], refs[group], refs[group + 1 : group + 1 + len(kv_earlier)]
        k_all, kt_all, v_all, g_all, q_all, dq_all, dk_all, dv_all, s_all, dp_all = refs[
            group + 1 + len(kv_earlier) :
        ]
        place, first = ids_ref[0], ids_ref[1]
        key_id = lax.broadcasted_iota(jnp.int32, (tokens, wide), 0)
        query_id = lax.broadcasted_iota(jnp.int32, (tokens, wide), 1) & (tokens - 1)

        for head in range(heads):
            at_k = slice(head * HEAD_SIZE, (head + 1) * HEAD_SIZE)
            at_v = slice(kv_width + head * HEAD_SIZE, kv_width + (head + 1) * HEAD_SIZE)
            for number in range(total):
                if number < back:
                    source = earlier_refs[number // group].at[number % group]
                else:
                    source = own_ref.at[number - back]
                k_all[number] = source[:, at_k]
                kt_all[number] = source[:, at_k].T
                v_all[number] = source[:, at_v]
            for r in range(group):
                for j in range(per_head):
                    lower = (head * per_head + j) * HEAD_SIZE
                    g_all[place ^ r, :, j * tokens : (j + 1) * tokens] = grad_refs[r][
                        lower : lower + HEAD_SIZE, :
                    ]
                    q_all[r, j * tokens : (j + 1) * tokens, :] = q_ref[r, :, lower : lower + HEAD_SIZE]
            dk_all[...] = jnp.zeros_like(dk_all)
            dv_all[...] = jnp.zeros_like(dv_all)

            @pl.loop(0, group)
            def _(b):
                q = q_all[b]
                g = g_all[b]
                top = None
                for c in range(span):
                    s = lax.dot_general(k_all[b + c], q, NT, preferred_element_type=jnp.float32) * factor
                    if c == 0:
                        s = jnp.where(key_id > query_id, s, -jnp.inf)
                    if c < back:
                        s = s + jnp.where(first + b + c >= back, 0.0, -jnp.inf)
                    else:
                        s = jnp.where(key_id <= query_id, s, -jnp.inf)
                    s_all[c] = s
                    here = jnp.max(s, axis=0, keepdims=True)
                    top = here if top is None else jnp.maximum(top, here)
                norm = jnp.zeros((1, wide), jnp.float32)
                delta = jnp.zeros((1, wide), jnp.float32)
                for c in range(span):
                    e = jnp.exp2(s_all[c] - top)
                    dp = lax.dot_general(v_all[b + c], g, NN, preferred_element_type=jnp.float32)
                    norm = norm + jnp.sum(e, axis=0, keepdims=True)
                    delta = delta + jnp.sum(e * dp, axis=0, keepdims=True)
                    s_all[c] = e
                    dp_all[c] = dp
                inverse = 1.0 / norm
                delta = delta * inverse
                dqt = jnp.zeros((HEAD_SIZE, wide), jnp.float32)
                for c in range(span):
                    p = s_all[c] * inverse
                    ds = (p * (dp_all[c] - delta) * score_scale).astype(jnp.bfloat16)
                    p = p.astype(jnp.bfloat16)
                    dv_all[b + c] += lax.dot_general(p, g, NT, preferred_element_type=jnp.float32)
                    dk_all[b + c] += lax.dot_general(ds, q, NN, preferred_element_type=jnp.float32)
                    dqt = dqt + lax.dot_general(kt_all[b + c], ds, NN, preferred_element_type=jnp.float32)
                for j in range(per_head):
                    lower = (head * per_head + j) * HEAD_SIZE
                    dq_all[b, :, lower : lower + HEAD_SIZE] = (
                        dqt[:, j * tokens : (j + 1) * tokens].T.astype(jnp.bfloat16)
                    )

            for number in range(back):
                target = dkv_earlier[number // group].at[number % group]
                target[:, at_k] = dk_all[number].astype(jnp.bfloat16)
                target[:, at_v] = dv_all[number].astype(jnp.bfloat16)
            dkv_own[:, :, at_k] = dk_all[back:]
            dkv_own[:, :, at_v] = dv_all[back:]
        for r in range(group):
            dq_refs[r][...] = dq_all[place ^ r]

    width = heads * per_head * HEAD_SIZE
    outs = [jax.ShapeDtypeStruct((tokens, width), jnp.bfloat16)] * group
    outs += [jax.ShapeDtypeStruct((group, tokens, 2 * kv_width), jnp.float32)]
    outs += [jax.ShapeDtypeStruct((group, tokens, 2 * kv_width), jnp.bfloat16)] * len(kv_earlier)
    scratch = [
        pltpu.VMEM((total, tokens, HEAD_SIZE), jnp.bfloat16),
        pltpu.VMEM((total, HEAD_SIZE, tokens), jnp.bfloat16),
        pltpu.VMEM((total, tokens, HEAD_SIZE), jnp.bfloat16),
        pltpu.VMEM((group, HEAD_SIZE, wide), jnp.bfloat16),
        pltpu.VMEM((group, wide, HEAD_SIZE), jnp.bfloat16),
        pltpu.VMEM((group, tokens, width), jnp.bfloat16),
        pltpu.VMEM((total, tokens, HEAD_SIZE), jnp.float32),
        pltpu.VMEM((total, tokens, HEAD_SIZE), jnp.float32),
        pltpu.VMEM((span, tokens, wide), jnp.float32),
        pltpu.VMEM((span, tokens, wide), jnp.float32),
    ]
    entries = group * heads * wide * span * tokens
    results = call(body, outs, scratch, flops=10 * entries * HEAD_SIZE, exps=entries)(
        ids, kv_own, *kv_earlier, queries, *grads
    )
    return results[:group], results[group], results[group + 1 :]


def pack_kv_grads(group, ids, own, arrived):
    shape = own.shape[1:]

    def body(ids_ref, *refs):
        for r in range(group):
            member = ids_ref[0] ^ r
            total = refs[0][member]
            for term in refs[1 : 1 + len(arrived)]:
                total = total + term[member].astype(jnp.float32)
            refs[1 + len(arrived) + r][...] = total.astype(jnp.bfloat16)

    outs = [jax.ShapeDtypeStruct(shape, jnp.bfloat16)] * group
    return call(body, outs)(ids, own, *arrived)


def unpack(group, ids, pieces, widths):
    tokens = pieces[0].shape[0]

    def body(ids_ref, *refs):
        for r in range(group):
            lower = 0
            for number, width in enumerate(widths):
                refs[group + number][:, lanes(ids_ref[0] ^ r, width)] = refs[r][:, lower : lower + width]
                lower += width

    outs = [jax.ShapeDtypeStruct((tokens, group * width), jnp.bfloat16) for width in widths]
    return call(body, outs)(ids, *pieces)


def local(layer_cotangent, out_weight, queries, keys, values):
    tokens = queries.shape[0]
    kv_heads = keys.shape[1] // HEAD_SIZE
    per_head = queries.shape[1] // keys.shape[1]
    count, tp_count = lax.axis_size("ctx"), lax.axis_size("tp")
    group = 1
    while (
        kv_heads % (2 * group) == 0
        and count % (2 * group) == 0
        and WINDOW_LENGTH % (2 * group * tokens) == 0
    ):
        group *= 2
    heads = kv_heads // group
    kv_width = heads * HEAD_SIZE
    back_groups = WINDOW_LENGTH // (group * tokens)
    index = lax.axis_index("ctx")
    place = index % group
    ids = jnp.stack([place, index - place]).astype(jnp.int32)
    rows = out_weight.shape[0] // tp_count

    sent = pack_inputs(group, ids, keys, values, queries)
    pieces = [sent[0]] + [swapped(sent[r], "ctx", r) for r in range(1, group)]
    if tp_count == 2:
        mine = lax.axis_index("tp").reshape(1)
        other = head_product(1 - mine, rows, out_weight, layer_cotangent)
        terms = [swapped(other, "tp", 1)]
        terms = [head_product(mine, rows, out_weight, layer_cotangent)] + terms
    else:
        product = head_product(jnp.zeros(1, jnp.int32), rows * tp_count, out_weight, layer_cotangent)
        terms = [lax.psum_scatter(product, "tp", scatter_dimension=0, tiled=True)]
    kv_own, query_all = order_inputs(group, ids, pieces, kv_width)
    kv_earlier = [shifted(kv_own, "ctx", group * step) for step in range(back_groups, 0, -1)]
    sent = pack_grads(group, ids, terms)
    grads = [sent[0]] + [swapped(sent[r], "ctx", r) for r in range(1, group)]
    dq, dkv_own, dkv_earlier = attention(
        group, heads, per_head, ids, kv_own, kv_earlier, query_all, grads
    )
    arrived = [
        shifted(dkv_earlier[number], "ctx", -group * (back_groups - number))
        for number in range(back_groups)
    ]
    dq = [dq[0]] + [swapped(dq[r], "ctx", r) for r in range(1, group)]
    sent = pack_kv_grads(group, ids, dkv_own, arrived)
    dkv = [sent[0]] + [swapped(sent[r], "ctx", r) for r in range(1, group)]
    (query_grads,) = unpack(group, ids, dq, [dq[0].shape[1]])
    key_gradients, value_gradients = unpack(group, ids, dkv, [kv_width, kv_width])
    return (query_grads, key_gradients, value_gradients)


def solution(mesh):
    in_specs = (P("ctx", "tp"), P(None, "tp"), P("ctx", "tp"), P("ctx", "tp"), P("ctx", "tp"))
    out_specs = (P("ctx", "tp"), P("ctx", "tp"), P("ctx", "tp"))
    return jax.shard_map(local, mesh=mesh, in_specs=in_specs, out_specs=out_specs, check_vma=False)
```

time: 171 us -> 73.6 us (0.43)
  the two profiles are of different devices: /device:TPU:24 before, /device:TPU:0 now
where the time goes in v1:
time: 73.6 us; the launch traced here: 73.2 us
  Pallas kernels  26.4 us (36%)
  waiting for transfers between devices  21.2 us (29%)
  starting transfers between devices  20.4 us (28%)
  local copies, waits for them, and re-layouts  4.28 us (6%)
  between operations  0.76 us (1%)
    pallas_call x7, Pallas kernels, run(): pl.pallas_call(body, out_shape=tuple(outs), in_specs=[SMEM] + [VMEM] * (l...  17.2 us
    ppermute x13, starting transfers between devices, swapped(): lax.ppermute(value, axis, [(source, source ^ bits) for source in range(co...  15.6 us
    ppermute x13, waiting for transfers between devices, swapped(): lax.ppermute(value, axis, [(source, source ^ bits) for source in range(co...  13.3 us
    pallas_call x2, Pallas kernels, head_product(): pl.pallas_call(body, out_shape=jax.ShapeDtypeStruct((rows, tokens), jnp.b...  9.21 us
    ppermute x2, waiting for transfers between devices, shifted(): lax.ppermute(value, axis, [(source, source + steps) for source in range(l...  7.98 us
    ppermute x2, starting transfers between devices, shifted(): lax.ppermute(value, axis, [(source, source + steps) for source in range(l...  4.81 us
    unnamed x10, local copies, waits for them, and re-layouts  4.28 us
  transfers between devices with their start and end apart: 15, of which 7 were waited for; matrix products, arithmetic and copies ran while one was open for 0% of the time, Pallas kernels for 17%

profile of v1, /device:TPU:0, one launch (start us, length us, event | category | flops | bytes accessed | tf_op | source)
XLA Modules:
  0.0 73.2 jit_solution(3929289710939151959)
XLA Ops:
  0.7 1.0 %copy-done.2 = bf16[256,1024]{1,0:T(8,128)(2,1)S(1)} copy-done((bf16[256,1024]{1,0:T(8,128)(2,1)S(1)}, bf16[256,1024]{1,0:T(8,128)(2,1)}, u32[]{:S(2)}) %copy-start.2) | copy-done | bytes 524312
  1.8 0.9 %copy-done.3 = bf16[256,512]{1,0:T(8,128)(2,1)S(1)} copy-done((bf16[256,512]{1,0:T(8,128)(2,1)S(1)}, bf16[256,512]{1,0:T(8,128)(2,1)}, u32[]{:S(2)}) %copy-start.3) | copy-done | bytes 262168
  2.7 0.9 %copy-done.4 = bf16[256,512]{1,0:T(8,128)(2,1)S(1)} copy-done((bf16[256,512]{1,0:T(8,128)(2,1)S(1)}, bf16[256,512]{1,0:T(8,128)(2,1)}, u32[]{:S(2)}) %copy-start.4) | copy-done | bytes 262168
  3.7 0.7 shard_map.76
  4.4 3.0 %collective-permute-start = (bf16[256,512]{1,0:T(8,128)(2,1)S(1)}, bf16[256,512]{1,0:T(8,128)(2,1)S(1)}, u32[]{:S(2)}, u32[]{:S(2)}) collective-permute-start(bf16[256,512]{1,0:T(8,128)(2,1)S(1)} %get-tuple-element.26), channel_id=1, source_target_pairs={{0,2},{2,0},{4,6},{6,4},{8,10},{10,8},{12,14},{14,12},{16,18},{18,... | collective-permute-start | bytes 786440 | tf_op jit(solution)/shard_map/ppermute | solution.py:30
  7.4 1.5 %collective-permute-start.1 = (bf16[256,512]{1,0:T(8,128)(2,1)S(1)}, bf16[256,512]{1,0:T(8,128)(2,1)S(1)}, u32[]{:S(2)}, u32[]{:S(2)}) collective-permute-start(bf16[256,512]{1,0:T(8,128)(2,1)S(1)} %get-tuple-element.27), channel_id=1, source_target_pairs={{0,4},{2,6},{4,0},{6,2},{8,12},{10,14},{12,8},{14,10},{16,20},{18,... | collective-permute-start | bytes 786440 | tf_op jit(solution)/shard_map/ppermute | solution.py:30
  8.9 1.3 %copy-done = bf16[256,2688]{1,0:T(8,128)(2,1)S(1)} copy-done((bf16[256,2688]{1,0:T(8,128)(2,1)S(1)}, bf16[256,2688]{1,0:T(8,128)(2,1)}, u32[]{:S(2)}) %copy-start) | copy-done | bytes 1376280
  10.3 4.6 %shard_map.79 = bf16[1024,256]{1,0:T(8,128)(2,1)S(1)} custom-call(s32[1]{0:T(128)S(6)} %sub.7.start_ref, bf16[2048,2688]{1,0:T(8,128)(2,1)} %w_ref.3, bf16[256,2688]{1,0:T(8,128)(2,1)S(1)} %copy-done), custom_call_target="tpu_custom_call" | custom-call | flops 1409286144 | bytes 7405568 | tf_op jit(solution)/shard_map/pallas_call | solution.py:96
  15.0 5.8 %collective-permute-done.1.refs_2_ = bf16[256,512]{1,0:T(8,128)(2,1)S(1)} collective-permute-done((bf16[256,512]{1,0:T(8,128)(2,1)S(1)}, bf16[256,512]{1,0:T(8,128)(2,1)S(1)}, u32[]{:S(2)}, u32[]{:S(2)}) %collective-permute-start.1) | collective-permute-done | bytes 262176 | tf_op jit(solution)/shard_map/ppermute | solution.py:30
  20.8 0.6 shard_map.77
  21.4 3.5 %collective-permute-start.3 = (bf16[4,256,256]{2,1,0:T(8,128)(2,1)S(1)}, bf16[4,256,256]{2,1,0:T(8,128)(2,1)S(1)}, u32[]{:S(2)}, u32[]{:S(2)}) collective-permute-start(bf16[4,256,256]{2,1,0:T(8,128)(2,1)S(1)} %get-tuple-element.29.refs_0_), channel_id=1, source_target_pairs={{0,8},{2,10},{4,12},{6,14},{8,16},{10,18},{12,20},{14,22},{16,24},... | collective-permute-start | bytes 1572872 | tf_op jit(solution)/shard_map/ppermute | solution.py:25
  24.9 4.6 %shard_map.78.refs_0_ = bf16[1024,256]{1,0:T(8,128)(2,1)S(1)} custom-call(s32[1]{0:T(128)} %bitcast.2.start_ref, bf16[2048,2688]{1,0:T(8,128)(2,1)} %w_ref.3, bf16[256,2688]{1,0:T(8,128)(2,1)S(1)} %copy-done.1), custom_call_target="tpu_custom_call" | custom-call | flops 1409286144 | bytes 7405568 | tf_op jit(solution)/shard_map/pallas_call | solution.py:96
  29.5 0.7 shard_map.80
  30.2 1.3 %collective-permute-start.5 = (bf16[256,256]{1,0:T(8,128)(2,1)S(1)}, bf16[256,256]{1,0:T(8,128)(2,1)S(1)}, u32[]{:S(2)}, u32[]{:S(2)}) collective-permute-start(bf16[256,256]{1,0:T(8,128)(2,1)S(1)} %get-tuple-element.32), channel_id=1, source_target_pairs={{0,2},{2,0},{4,6},{6,4},{8,10},{10,8},{12,14},{14,12},{16,18},{18,... | collective-permute-start | bytes 393224 | tf_op jit(solution)/shard_map/ppermute | solution.py:30
  31.5 0.8 %collective-permute-start.6 = (bf16[256,256]{1,0:T(8,128)(2,1)S(1)}, bf16[256,256]{1,0:T(8,128)(2,1)S(1)}, u32[]{:S(2)}, u32[]{:S(2)}) collective-permute-start(bf16[256,256]{1,0:T(8,128)(2,1)S(1)} %get-tuple-element.33), channel_id=1, source_target_pairs={{0,4},{2,6},{4,0},{6,2},{8,12},{10,14},{12,8},{14,10},{16,20},{18,... | collective-permute-start | bytes 393224 | tf_op jit(solution)/shard_map/ppermute | solution.py:30
  32.3 1.4 %collective-permute-start.7 = (bf16[256,256]{1,0:T(8,128)(2,1)S(1)}, bf16[256,256]{1,0:T(8,128)(2,1)S(1)}, u32[]{:S(2)}, u32[]{:S(2)}) collective-permute-start(bf16[256,256]{1,0:T(8,128)(2,1)S(1)} %get-tuple-element.34), channel_id=1, source_target_pairs={{0,6},{2,4},{4,2},{6,0},{8,14},{10,12},{12,10},{14,8},{16,22},{18,... | collective-permute-start | bytes 393224 | tf_op jit(solution)/shard_map/ppermute | solution.py:30
  33.7 2.7 %collective-permute-done.5.refs_4_ = bf16[256,256]{1,0:T(8,128)(2,1)S(1)} collective-permute-done((bf16[256,256]{1,0:T(8,128)(2,1)S(1)}, bf16[256,256]{1,0:T(8,128)(2,1)S(1)}, u32[]{:S(2)}, u32[]{:S(2)}) %collective-permute-start.5) | collective-permute-done | bytes 131104 | tf_op jit(solution)/shard_map/ppermute | solution.py:30
  36.7 1.5 %collective-permute-done.7.refs_6_ = bf16[256,256]{1,0:T(8,128)(2,1)S(1)} collective-permute-done((bf16[256,256]{1,0:T(8,128)(2,1)S(1)}, bf16[256,256]{1,0:T(8,128)(2,1)S(1)}, u32[]{:S(2)}, u32[]{:S(2)}) %collective-permute-start.7) | collective-permute-done | bytes 131104 | tf_op jit(solution)/shard_map/ppermute | solution.py:30
  38.2 11.8 %shard_map.81 = (bf16[256,256]{1,0:T(8,128)(2,1)S(1)}, bf16[256,256]{1,0:T(8,128)(2,1)S(1)}, bf16[256,256]{1,0:T(8,128)(2,1)S(1)}, bf16[256,256]{1,0:T(8,128)(2,...) custom-call(s32[2]{0:T(128)S(1)} %pad_add_fusion.ids_ref, ...), custom_call_target="tpu_custom_call" | custom-call | flops 3355443200 | bytes 4194312 | tf_op jit(solution)/shard_map/pallas_call | solution.py:37
  50.0 1.3 %collective-permute-start.11 = (bf16[4,256,256]{2,1,0:T(8,128)(2,1)S(1)}, bf16[4,256,256]{2,1,0:T(8,128)(2,1)S(1)}, u32[]{:S(2)}, u32[]{:S(2)}) collective-permute-start(bf16[4,256,256]{2,1,0:T(8,128)(2,1)S(1)} %get-tuple-element.40), channel_id=1, source_target_pairs={{8,0},{10,2},{12,4},{14,6},{16,8},{18,10},{20,12},{22,14},{24,16},... | collective-permute-start | bytes 1572872 | tf_op jit(solution)/shard_map/ppermute | solution.py:25
  51.3 1.6 %collective-permute-start.8 = (bf16[256,256]{1,0:T(8,128)(2,1)S(1)}, bf16[256,256]{1,0:T(8,128)(2,1)S(1)}, u32[]{:S(2)}, u32[]{:S(2)}) collective-permute-start(bf16[256,256]{1,0:T(8,128)(2,1)S(1)} %get-tuple-element.36), channel_id=1, source_target_pairs={{0,2},{2,0},{4,6},{6,4},{8,10},{10,8},{12,14},{14,12},{16,18},{18,... | collective-permute-start | bytes 393224 | tf_op jit(solution)/shard_map/ppermute | solution.py:30
  52.8 0.7 collective-permute-start.9
  53.5 1.3 %collective-permute-start.10 = (bf16[256,256]{1,0:T(8,128)(2,1)S(1)}, bf16[256,256]{1,0:T(8,128)(2,1)S(1)}, u32[]{:S(2)}, u32[]{:S(2)}) collective-permute-start(bf16[256,256]{1,0:T(8,128)(2,1)S(1)} %get-tuple-element.38), channel_id=1, source_target_pairs={{0,6},{2,4},{4,2},{6,0},{8,14},{10,12},{12,10},{14,8},{16,22},{18,... | collective-permute-start | bytes 393224 | tf_op jit(solution)/shard_map/ppermute | solution.py:30
  54.8 8.0 %collective-permute-done.11.refs_1_ = bf16[4,256,256]{2,1,0:T(8,128)(2,1)S(1)} collective-permute-done((bf16[4,256,256]{2,1,0:T(8,128)(2,1)S(1)}, bf16[4,256,256]{2,1,0:T(8,128)(2,1)S(1)}, u32[]{:S(2)}, u32[]{:S(2)}) %collective-permute-start.11) | collective-permute-done | bytes 524320 | tf_op jit(solution)/shard_map/ppermute | solution.py:25
  62.8 0.6 shard_map.83
  63.4 0.8 %collective-permute-start.12 = (bf16[256,256]{1,0:T(8,128)(2,1)S(1)}, bf16[256,256]{1,0:T(8,128)(2,1)S(1)}, u32[]{:S(2)}, u32[]{:S(2)}) collective-permute-start(bf16[256,256]{1,0:T(8,128)(2,1)S(1)} %get-tuple-element.42), channel_id=1, source_target_pairs={{0,2},{2,0},{4,6},{6,4},{8,10},{10,8},{12,14},{14,12},{16,18},{18,... | collective-permute-start | bytes 393224 | tf_op jit(solution)/shard_map/ppermute | solution.py:30
  64.2 1.7 %collective-permute-start.13 = (bf16[256,256]{1,0:T(8,128)(2,1)S(1)}, bf16[256,256]{1,0:T(8,128)(2,1)S(1)}, u32[]{:S(2)}, u32[]{:S(2)}) collective-permute-start(bf16[256,256]{1,0:T(8,128)(2,1)S(1)} %get-tuple-element.43), channel_id=1, source_target_pairs={{0,4},{2,6},{4,0},{6,2},{8,12},{10,14},{12,8},{14,10},{16,20},{18,... | collective-permute-start | bytes 393224 | tf_op jit(solution)/shard_map/ppermute | solution.py:30
  65.9 1.4 %collective-permute-start.14 = (bf16[256,256]{1,0:T(8,128)(2,1)S(1)}, bf16[256,256]{1,0:T(8,128)(2,1)S(1)}, u32[]{:S(2)}, u32[]{:S(2)}) collective-permute-start(bf16[256,256]{1,0:T(8,128)(2,1)S(1)} %get-tuple-element.44), channel_id=1, source_target_pairs={{0,6},{2,4},{4,2},{6,0},{8,14},{10,12},{12,10},{14,8},{16,22},{18,... | collective-permute-start | bytes 393224 | tf_op jit(solution)/shard_map/ppermute | solution.py:30
  67.3 1.4 %shard_map.82 = bf16[256,1024]{1,0:T(8,128)(2,1)} custom-call(s32[2]{0:T(128)S(1)} %pad_add_fusion.ids_ref, bf16[256,256]{1,0:T(8,128)(2,1)S(1)} %get-tuple-element.35.refs_0_, bf16[256,256]{1,0:T(8,128)(2,1)S(1)} %collective-permute-done.8.refs_1_, bf16[256,256]{1,0:T(8,128)(2,1)S(1)} %collective-permute-done.9.refs_2_, ...), custom_call_target="tpu_custom_call" | custom-call | bytes 1048584 | tf_op jit(solution)/shard_map/pallas_call | solution.py:37
  68.7 0.5 collective-permute-done.13.refs_2_
  69.2 2.6 %collective-permute-done.14.refs_3_ = bf16[256,256]{1,0:T(8,128)(2,1)S(1)} collective-permute-done((bf16[256,256]{1,0:T(8,128)(2,1)S(1)}, bf16[256,256]{1,0:T(8,128)(2,1)S(1)}, u32[]{:S(2)}, u32[]{:S(2)}) %collective-permute-start.14) | collective-permute-done | bytes 131104 | tf_op jit(solution)/shard_map/ppermute | solution.py:30
  71.8 1.4 %shard_map.84 = (bf16[256,512]{1,0:T(8,128)(2,1)}, bf16[256,512]{1,0:T(8,128)(2,1)}) custom-call(s32[2]{0:T(128)S(1)} %pad_add_fusion.ids_ref, bf16[256,256]{1,0:T(8,128)(2,1)S(1)} %get-tuple-element.41.refs_0_, bf16[256,256]{1,0:T(8,128)(2,1)S(1)} %collective-permute-done.12.refs_1_, bf16[256,256]{1,0:T(8,128)(2,1)S(1)} %collective-permute-done.13.refs_2_, ...), custom_call_target="tpu_custom_call" | custom-call | bytes 1048584 | tf_op jit(solution)/shard_map/pallas_call | solution.py:37
  (18 shorter events, 0.4 us)
Async XLA Ops:
  0.7 1.0 %copy-start.2 = (bf16[256,1024]{1,0:T(8,128)(2,1)S(1)}, bf16[256,1024]{1,0:T(8,128)(2,1)}, u32[]{:S(2)}) copy-start(bf16[256,1024]{1,0:T(8,128)(2,1)} %q_ref.1) | copy-start | bytes 1572868
  1.8 0.9 %copy-start.3 = (bf16[256,512]{1,0:T(8,128)(2,1)S(1)}, bf16[256,512]{1,0:T(8,128)(2,1)}, u32[]{:S(2)}) copy-start(bf16[256,512]{1,0:T(8,128)(2,1)} %k_ref.1) | copy-start | bytes 786436
  2.7 0.9 %copy-start.4 = (bf16[256,512]{1,0:T(8,128)(2,1)S(1)}, bf16[256,512]{1,0:T(8,128)(2,1)}, u32[]{:S(2)}) copy-start(bf16[256,512]{1,0:T(8,128)(2,1)} %v_ref.1) | copy-start | bytes 786436
  4.4 10.6 %collective-permute-start = (bf16[256,512]{1,0:T(8,128)(2,1)S(1)}, bf16[256,512]{1,0:T(8,128)(2,1)S(1)}, u32[]{:S(2)}, u32[]{:S(2)}) collective-permute-start(bf16[256,512]{1,0:T(8,128)(2,1)S(1)} %get-tuple-element.26), channel_id=1, source_target_pairs={{0,2},{2,0},{4,6},{6,4},{8,10},{10,8},{12,14},{14,12},{16,18},{18,... | collective-permute-start | bytes 786440 | tf_op jit(solution)/shard_map/ppermute | solution.py:30
  7.4 13.4 %collective-permute-start.1 = (bf16[256,512]{1,0:T(8,128)(2,1)S(1)}, bf16[256,512]{1,0:T(8,128)(2,1)S(1)}, u32[]{:S(2)}, u32[]{:S(2)}) collective-permute-start(bf16[256,512]{1,0:T(8,128)(2,1)S(1)} %get-tuple-element.27), channel_id=1, source_target_pairs={{0,4},{2,6},{4,0},{6,2},{8,12},{10,14},{12,8},{14,10},{16,20},{18,... | collective-permute-start | bytes 786440 | tf_op jit(solution)/shard_map/ppermute | solution.py:30
  8.9 11.9 %collective-permute-start.2 = (bf16[256,512]{1,0:T(8,128)(2,1)S(1)}, bf16[256,512]{1,0:T(8,128)(2,1)S(1)}, u32[]{:S(2)}, u32[]{:S(2)}) collective-permute-start(bf16[256,512]{1,0:T(8,128)(2,1)S(1)} %get-tuple-element.28), channel_id=1, source_target_pairs={{0,6},{2,4},{4,2},{6,0},{8,14},{10,12},{12,10},{14,8},{16,22},{18,... | collective-permute-start | bytes 786440 | tf_op jit(solution)/shard_map/ppermute | solution.py:30
  8.9 1.3 %copy-start = (bf16[256,2688]{1,0:T(8,128)(2,1)S(1)}, bf16[256,2688]{1,0:T(8,128)(2,1)}, u32[]{:S(2)}) copy-start(bf16[256,2688]{1,0:T(8,128)(2,1)} %c_ref.3) | copy-start | bytes 4128772
  10.3 14.7 %copy-start.1 = (bf16[256,2688]{1,0:T(8,128)(2,1)S(1)}, bf16[256,2688]{1,0:T(8,128)(2,1)}, u32[]{:S(2)}) copy-start(bf16[256,2688]{1,0:T(8,128)(2,1)} %c_ref.3) | copy-start | bytes 4128772
  14.9 14.6 %collective-permute-start.4 = (bf16[1024,256]{1,0:T(8,128)(2,1)S(1)}, bf16[1024,256]{1,0:T(8,128)(2,1)S(1)}, u32[]{:S(2)}, u32[]{:S(2)}) collective-permute-start(bf16[1024,256]{1,0:T(8,128)(2,1)S(1)} %shard_map.79), channel_id=1, source_target_pairs={{0,1},{1,0},{2,3},{3,2},{4,5},{5,4},{6,7},{7,6},{8,9},{9,8},{10,11... | collective-permute-start | bytes 1572872 | tf_op jit(solution)/shard_map/ppermute | solution.py:30
  21.4 16.8 %collective-permute-start.3 = (bf16[4,256,256]{2,1,0:T(8,128)(2,1)S(1)}, bf16[4,256,256]{2,1,0:T(8,128)(2,1)S(1)}, u32[]{:S(2)}, u32[]{:S(2)}) collective-permute-start(bf16[4,256,256]{2,1,0:T(8,128)(2,1)S(1)} %get-tuple-element.29.refs_0_), channel_id=1, source_target_pairs={{0,8},{2,10},{4,12},{6,14},{8,16},{10,18},{12,20},{14,22},{16,24},... | collective-permute-start | bytes 1572872 | tf_op jit(solution)/shard_map/ppermute | solution.py:25
  30.2 6.3 %collective-permute-start.5 = (bf16[256,256]{1,0:T(8,128)(2,1)S(1)}, bf16[256,256]{1,0:T(8,128)(2,1)S(1)}, u32[]{:S(2)}, u32[]{:S(2)}) collective-permute-start(bf16[256,256]{1,0:T(8,128)(2,1)S(1)} %get-tuple-element.32), channel_id=1, source_target_pairs={{0,2},{2,0},{4,6},{6,4},{8,10},{10,8},{12,14},{14,12},{16,18},{18,... | collective-permute-start | bytes 393224 | tf_op jit(solution)/shard_map/ppermute | solution.py:30
  31.5 5.2 %collective-permute-start.6 = (bf16[256,256]{1,0:T(8,128)(2,1)S(1)}, bf16[256,256]{1,0:T(8,128)(2,1)S(1)}, u32[]{:S(2)}, u32[]{:S(2)}) collective-permute-start(bf16[256,256]{1,0:T(8,128)(2,1)S(1)} %get-tuple-element.33), channel_id=1, source_target_pairs={{0,4},{2,6},{4,0},{6,2},{8,12},{10,14},{12,8},{14,10},{16,20},{18,... | collective-permute-start | bytes 393224 | tf_op jit(solution)/shard_map/ppermute | solution.py:30
  32.3 5.9 %collective-permute-start.7 = (bf16[256,256]{1,0:T(8,128)(2,1)S(1)}, bf16[256,256]{1,0:T(8,128)(2,1)S(1)}, u32[]{:S(2)}, u32[]{:S(2)}) collective-permute-start(bf16[256,256]{1,0:T(8,128)(2,1)S(1)} %get-tuple-element.34), channel_id=1, source_target_pairs={{0,6},{2,4},{4,2},{6,0},{8,14},{10,12},{12,10},{14,8},{16,22},{18,... | collective-permute-start | bytes 393224 | tf_op jit(solution)/shard_map/ppermute | solution.py:30
  50.0 12.8 %collective-permute-start.11 = (bf16[4,256,256]{2,1,0:T(8,128)(2,1)S(1)}, bf16[4,256,256]{2,1,0:T(8,128)(2,1)S(1)}, u32[]{:S(2)}, u32[]{:S(2)}) collective-permute-start(bf16[4,256,256]{2,1,0:T(8,128)(2,1)S(1)} %get-tuple-element.40), channel_id=1, source_target_pairs={{8,0},{10,2},{12,4},{14,6},{16,8},{18,10},{20,12},{22,14},{24,16},... | collective-permute-start | bytes 1572872 | tf_op jit(solution)/shard_map/ppermute | solution.py:25
  51.3 14.6 %collective-permute-start.8 = (bf16[256,256]{1,0:T(8,128)(2,1)S(1)}, bf16[256,256]{1,0:T(8,128)(2,1)S(1)}, u32[]{:S(2)}, u32[]{:S(2)}) collective-permute-start(bf16[256,256]{1,0:T(8,128)(2,1)S(1)} %get-tuple-element.36), channel_id=1, source_target_pairs={{0,2},{2,0},{4,6},{6,4},{8,10},{10,8},{12,14},{14,12},{16,18},{18,... | collective-permute-start | bytes 393224 | tf_op jit(solution)/shard_map/ppermute | solution.py:30
  52.8 14.5 %collective-permute-start.9 = (bf16[256,256]{1,0:T(8,128)(2,1)S(1)}, bf16[256,256]{1,0:T(8,128)(2,1)S(1)}, u32[]{:S(2)}, u32[]{:S(2)}) collective-permute-start(bf16[256,256]{1,0:T(8,128)(2,1)S(1)} %get-tuple-element.37), channel_id=1, source_target_pairs={{0,4},{2,6},{4,0},{6,2},{8,12},{10,14},{12,8},{14,10},{16,20},{18,... | collective-permute-start | bytes 393224 | tf_op jit(solution)/shard_map/ppermute | solution.py:30
  53.5 13.8 %collective-permute-start.10 = (bf16[256,256]{1,0:T(8,128)(2,1)S(1)}, bf16[256,256]{1,0:T(8,128)(2,1)S(1)}, u32[]{:S(2)}, u32[]{:S(2)}) collective-permute-start(bf16[256,256]{1,0:T(8,128)(2,1)S(1)} %get-tuple-element.38), channel_id=1, source_target_pairs={{0,6},{2,4},{4,2},{6,0},{8,14},{10,12},{12,10},{14,8},{16,22},{18,... | collective-permute-start | bytes 393224 | tf_op jit(solution)/shard_map/ppermute | solution.py:30
  63.4 5.3 %collective-permute-start.12 = (bf16[256,256]{1,0:T(8,128)(2,1)S(1)}, bf16[256,256]{1,0:T(8,128)(2,1)S(1)}, u32[]{:S(2)}, u32[]{:S(2)}) collective-permute-start(bf16[256,256]{1,0:T(8,128)(2,1)S(1)} %get-tuple-element.42), channel_id=1, source_target_pairs={{0,2},{2,0},{4,6},{6,4},{8,10},{10,8},{12,14},{14,12},{16,18},{18,... | collective-permute-start | bytes 393224 | tf_op jit(solution)/shard_map/ppermute | solution.py:30
  64.2 5.0 %collective-permute-start.13 = (bf16[256,256]{1,0:T(8,128)(2,1)S(1)}, bf16[256,256]{1,0:T(8,128)(2,1)S(1)}, u32[]{:S(2)}, u32[]{:S(2)}) collective-permute-start(bf16[256,256]{1,0:T(8,128)(2,1)S(1)} %get-tuple-element.43), channel_id=1, source_target_pairs={{0,4},{2,6},{4,0},{6,2},{8,12},{10,14},{12,8},{14,10},{16,20},{18,... | collective-permute-start | bytes 393224 | tf_op jit(solution)/shard_map/ppermute | solution.py:30
  65.9 5.9 %collective-permute-start.14 = (bf16[256,256]{1,0:T(8,128)(2,1)S(1)}, bf16[256,256]{1,0:T(8,128)(2,1)S(1)}, u32[]{:S(2)}, u32[]{:S(2)}) collective-permute-start(bf16[256,256]{1,0:T(8,128)(2,1)S(1)} %get-tuple-element.44), channel_id=1, source_target_pairs={{0,6},{2,4},{4,2},{6,0},{8,14},{10,12},{12,10},{14,8},{16,22},{18,... | collective-permute-start | bytes 393224 | tf_op jit(solution)/shard_map/ppermute | solution.py:30

commit v2 on v1

v2 whole, which is shorter than its diff:
```python
import functools

import jax
import jax.numpy as jnp
from jax import lax
from jax.experimental import pallas as pl
from jax.experimental.pallas import tpu as pltpu
from jax.sharding import PartitionSpec as P

HEAD_SIZE = 128
WINDOW_LENGTH = 1024
LOG2_E = 1.4426950408889634

score_scale = 168.0 ** (-0.5)

VMEM = pl.BlockSpec(memory_space=pltpu.VMEM)
SMEM = pl.BlockSpec(memory_space=pltpu.SMEM)
NT = (((1,), (1,)), ((), ()))
NN = (((1,), (0,)), ((), ()))


def shifted(value, axis, steps):
    count = lax.axis_size(axis)
    leading, last = (max(0, -steps), min(count, count - steps))
    return lax.ppermute(value, axis, [(source, source + steps) for source in range(leading, last)])


def swapped(value, axis, bits):
    count = lax.axis_size(axis)
    return lax.ppermute(value, axis, [(source, source ^ bits) for source in range(count)])


def traded(value, axis, group):
    if group == 1:
        return value
    count = lax.axis_size(axis)
    groups = [list(range(first, first + group)) for first in range(0, count, group)]
    return lax.all_to_all(value, axis, 0, 0, axis_index_groups=groups, tiled=True)


def call(body, outs, scratch=(), flops=0, count=0, exps=0):
    def run(*args):
        moved = sum(a.size * a.dtype.itemsize for a in args)
        moved += sum(o.size * o.dtype.itemsize for o in outs)
        return pl.pallas_call(
            body,
            out_shape=tuple(outs),
            in_specs=[SMEM if a.dtype == jnp.int32 else VMEM for a in args],
            out_specs=tuple(VMEM for _ in outs),
            scratch_shapes=list(scratch),
            compiler_params=pltpu.CompilerParams(vmem_limit_bytes=48 * 1024 * 1024),
            cost_estimate=pl.CostEstimate(flops=flops, bytes_accessed=moved, transcendentals=exps),
        )(*args)

    return run


def split_heads(group, arrays):
    tokens = arrays[0].shape[0]
    widths = [array.shape[1] // group for array in arrays]

    def body(*refs):
        out_ref, sems = refs[-2:]
        copies = []
        for member in range(group):
            lower = 0
            for number, width in enumerate(widths):
                copies.append(
                    pltpu.make_async_copy(
                        refs[number].at[:, member * width : (member + 1) * width],
                        out_ref.at[member, :, lower : lower + width],
                        sems.at[len(copies)],
                    )
                )
                lower += width
        for copy in copies:
            copy.start()
        for copy in copies:
            copy.wait()

    moved = 2 * sum(array.size * array.dtype.itemsize for array in arrays)
    return pl.pallas_call(
        body,
        out_shape=jax.ShapeDtypeStruct((group, tokens, sum(widths)), jnp.bfloat16),
        in_specs=[pl.BlockSpec(memory_space=pltpu.HBM)] * len(arrays),
        out_specs=VMEM,
        scratch_shapes=[pltpu.SemaphoreType.DMA((group * len(arrays),))],
        cost_estimate=pl.CostEstimate(flops=0, bytes_accessed=moved, transcendentals=0),
    )(*arrays)


def head_product(start, rows, out_weight, layer_cotangent):
    tokens, depth = layer_cotangent.shape
    chunk = next((depth // parts for parts in range(3, depth) if depth % (parts * 128) == 0), depth)
    steps = depth // chunk

    def body(start_ref, w_ref, c_ref, o_ref, total):
        step = pl.program_id(0)
        term = lax.dot_general(w_ref[...], c_ref[...], NT, preferred_element_type=jnp.float32)

        if steps == 1:
            o_ref[...] = term.astype(jnp.bfloat16)
            return

        @pl.when(step == 0)
        def _():
            total[...] = term

        @pl.when((step > 0) & (step < steps - 1))
        def _():
            total[...] += term

        @pl.when(step == steps - 1)
        def _():
            o_ref[...] = (total[...] + term).astype(jnp.bfloat16)

    return pl.pallas_call(
        body,
        out_shape=jax.ShapeDtypeStruct((rows, tokens), jnp.bfloat16),
        grid_spec=pltpu.PrefetchScalarGridSpec(
            num_scalar_prefetch=1,
            grid=(steps,),
            in_specs=[
                pl.BlockSpec((rows, chunk), lambda i, s: (s[0], i)),
                pl.BlockSpec((tokens, chunk), lambda i, s: (0, i)),
            ],
            out_specs=pl.BlockSpec((rows, tokens), lambda i, s: (0, 0)),
            scratch_shapes=[pltpu.VMEM((rows, tokens), jnp.float32)],
        ),
        compiler_params=pltpu.CompilerParams(vmem_limit_bytes=48 * 1024 * 1024),
        cost_estimate=pl.CostEstimate(
            flops=2 * rows * tokens * depth,
            bytes_accessed=2 * (rows * depth + tokens * depth + rows * tokens),
            transcendentals=0,
        ),
    )(start, out_weight, layer_cotangent)


def add_grads(terms):
    def body(*refs):
        total = refs[0][...].astype(jnp.float32)
        for term in refs[1:-1]:
            total = total + term[...].astype(jnp.float32)
        refs[-1][...] = total.astype(jnp.bfloat16)

    return call(body, [jax.ShapeDtypeStruct(terms[0].shape, jnp.bfloat16)])(*terms)[0]


def attention(group, heads, per_head, ids, kv_own, kv_earlier, queries, grads):
    back = len(kv_earlier) * group
    tokens = kv_own.shape[1]
    span = back + 1
    total = back + group
    wide = per_head * tokens
    kv_width = heads * HEAD_SIZE
    factor = score_scale * LOG2_E

    def body(ids_ref, *refs):
        own_ref = refs[0]
        earlier_refs = refs[1 : 1 + len(kv_earlier)]
        q_ref = refs[1 + len(kv_earlier)]
        grad_ref = refs[2 + len(kv_earlier)]
        refs = refs[3 + len(kv_earlier) :]
        dq_ref, dkv_own, dkv_earlier = refs[0], refs[1], refs[2 : 2 + len(kv_earlier)]
        k_all, kt_all, v_all, g_all, q_all, dk_all, dv_all, s_all, dp_all = refs[2 + len(kv_earlier) :]
        first = ids_ref[0]
        key_id = lax.broadcasted_iota(jnp.int32, (tokens, wide), 0)
        query_id = lax.broadcasted_iota(jnp.int32, (tokens, wide), 1) & (tokens - 1)

        for head in range(heads):
            at_k = slice(head * HEAD_SIZE, (head + 1) * HEAD_SIZE)
            at_v = slice(kv_width + head * HEAD_SIZE, kv_width + (head + 1) * HEAD_SIZE)
            for number in range(total):
                if number < back:
                    source = earlier_refs[number // group].at[number % group]
                else:
                    source = own_ref.at[number - back]
                k_all[number] = source[:, at_k]
                kt_all[number] = source[:, at_k].T
                v_all[number] = source[:, at_v]
            for r in range(group):
                for j in range(per_head):
                    lower = (head * per_head + j) * HEAD_SIZE
                    g_all[r, :, j * tokens : (j + 1) * tokens] = grad_ref[r, lower : lower + HEAD_SIZE, :]
                    q_all[r, j * tokens : (j + 1) * tokens, :] = q_ref[r, :, lower : lower + HEAD_SIZE]
            dk_all[...] = jnp.zeros_like(dk_all)
            dv_all[...] = jnp.zeros_like(dv_all)

            @pl.loop(0, group)
            def _(b):
                q = q_all[b]
                g = g_all[b]
                top = None
                for c in range(span):
                    s = lax.dot_general(k_all[b + c], q, NT, preferred_element_type=jnp.float32) * factor
                    if c == 0:
                        s = jnp.where(key_id > query_id, s, -jnp.inf)
                    if c < back:
                        s = s + jnp.where(first + b + c >= back, 0.0, -jnp.inf)
                    else:
                        s = jnp.where(key_id <= query_id, s, -jnp.inf)
                    s_all[c] = s
                    here = jnp.max(s, axis=0, keepdims=True)
                    top = here if top is None else jnp.maximum(top, here)
                norm = jnp.zeros((1, wide), jnp.float32)
                delta = jnp.zeros((1, wide), jnp.float32)
                for c in range(span):
                    e = jnp.exp2(s_all[c] - top)
                    dp = lax.dot_general(v_all[b + c], g, NN, preferred_element_type=jnp.float32)
                    norm = norm + jnp.sum(e, axis=0, keepdims=True)
                    delta = delta + jnp.sum(e * dp, axis=0, keepdims=True)
                    s_all[c] = e
                    dp_all[c] = dp
                inverse = 1.0 / norm
                delta = delta * inverse
                dqt = jnp.zeros((HEAD_SIZE, wide), jnp.float32)
                for c in range(span):
                    p = s_all[c] * inverse
                    ds = (p * (dp_all[c] - delta) * score_scale).astype(jnp.bfloat16)
                    p = p.astype(jnp.bfloat16)
                    dv_all[b + c] += lax.dot_general(p, g, NT, preferred_element_type=jnp.float32)
                    dk_all[b + c] += lax.dot_general(ds, q, NN, preferred_element_type=jnp.float32)
                    dqt = dqt + lax.dot_general(kt_all[b + c], ds, NN, preferred_element_type=jnp.float32)
                for j in range(per_head):
                    lower = (head * per_head + j) * HEAD_SIZE
                    dq_ref[b, :, lower : lower + HEAD_SIZE] = (
                        dqt[:, j * tokens : (j + 1) * tokens].T.astype(jnp.bfloat16)
                    )

            for number in range(back):
                target = dkv_earlier[number // group].at[number % group]
                target[:, at_k] = dk_all[number].astype(jnp.bfloat16)
                target[:, at_v] = dv_all[number].astype(jnp.bfloat16)
            dkv_own[:, :, at_k] = dk_all[back:]
            dkv_own[:, :, at_v] = dv_all[back:]

    width = heads * per_head * HEAD_SIZE
    outs = [jax.ShapeDtypeStruct((group, tokens, width), jnp.bfloat16)]
    outs += [jax.ShapeDtypeStruct((group, tokens, 2 * kv_width), jnp.float32)]
    outs += [jax.ShapeDtypeStruct((group, tokens, 2 * kv_width), jnp.bfloat16)] * len(kv_earlier)
    scratch = [
        pltpu.VMEM((total, tokens, HEAD_SIZE), jnp.bfloat16),
        pltpu.VMEM((total, HEAD_SIZE, tokens), jnp.bfloat16),
        pltpu.VMEM((total, tokens, HEAD_SIZE), jnp.bfloat16),
        pltpu.VMEM((group, HEAD_SIZE, wide), jnp.bfloat16),
        pltpu.VMEM((group, wide, HEAD_SIZE), jnp.bfloat16),
        pltpu.VMEM((total, tokens, HEAD_SIZE), jnp.float32),
        pltpu.VMEM((total, tokens, HEAD_SIZE), jnp.float32),
        pltpu.VMEM((span, tokens, wide), jnp.float32),
        pltpu.VMEM((span, tokens, wide), jnp.float32),
    ]
    entries = group * heads * wide * span * tokens
    results = call(body, outs, scratch, flops=10 * entries * HEAD_SIZE, exps=entries)(
        ids, kv_own, *kv_earlier, queries, grads
    )
    return results[0], results[1], results[2:]


def join_heads(group, pieces, widths):
    tokens = pieces.shape[1]

    def body(in_ref, *out_refs):
        for member in range(group):
            lower = 0
            for out_ref, width in zip(out_refs, widths):
                out_ref[:, member * width : (member + 1) * width] = in_ref[member, :, lower : lower + width]
                lower += width

    outs = [jax.ShapeDtypeStruct((tokens, group * width), jnp.bfloat16) for width in widths]
    return call(body, outs)(pieces)


def local(layer_cotangent, out_weight, queries, keys, values):
    tokens = queries.shape[0]
    kv_heads = keys.shape[1] // HEAD_SIZE
    per_head = queries.shape[1] // keys.shape[1]
    count, tp_count = lax.axis_size("ctx"), lax.axis_size("tp")
    group = 1
    while (
        kv_heads % (2 * group) == 0
        and count % (2 * group) == 0
        and WINDOW_LENGTH % (2 * group * tokens) == 0
    ):
        group *= 2
    heads = kv_heads // group
    kv_width = heads * HEAD_SIZE
    back_groups = WINDOW_LENGTH // (group * tokens)
    index = lax.axis_index("ctx")
    ids = (index - index % group).astype(jnp.int32).reshape(1)
    rows = out_weight.shape[0] // tp_count

    kv_own = traded(split_heads(group, [keys, values]), "ctx", group)
    query_all = traded(split_heads(group, [queries]), "ctx", group)
    if tp_count == 2:
        mine = lax.axis_index("tp").astype(jnp.int32).reshape(1)
        other = head_product(1 - mine, rows, out_weight, layer_cotangent)
        terms = [swapped(other, "tp", 1)]
        terms = [head_product(mine, rows, out_weight, layer_cotangent)] + terms
        grads = add_grads(terms)
    else:
        product = head_product(jnp.zeros(1, jnp.int32), rows * tp_count, out_weight, layer_cotangent)
        grads = lax.psum_scatter(product, "tp", scatter_dimension=0, tiled=True)
    kv_earlier = [shifted(kv_own, "ctx", group * step) for step in range(back_groups, 0, -1)]
    grads = traded(grads.reshape(group, rows // group, tokens), "ctx", group)
    dq, dkv_own, dkv_earlier = attention(
        group, heads, per_head, ids, kv_own, kv_earlier, query_all, grads
    )
    arrived = [
        shifted(dkv_earlier[number], "ctx", -group * (back_groups - number))
        for number in range(back_groups)
    ]
    dq = traded(dq, "ctx", group)
    dkv = traded(add_grads([dkv_own] + arrived), "ctx", group)
    (query_grads,) = join_heads(group, dq, [dq.shape[2]])
    key_gradients, value_gradients = join_heads(group, dkv, [kv_width, kv_width])
    return (query_grads, key_gradients, value_gradients)


def solution(mesh):
    in_specs = (P("ctx", "tp"), P(None, "tp"), P("ctx", "tp"), P("ctx", "tp"), P("ctx", "tp"))
    out_specs = (P("ctx", "tp"), P("ctx", "tp"), P("ctx", "tp"))
    return jax.shard_map(local, mesh=mesh, in_specs=in_specs, out_specs=out_specs, check_vma=False)
```

time: 73.6 us -> 82 us (1.11)
  starting transfers between devices: 20.4 us -> 26.1 us
  Pallas kernels: 26.4 us -> 30 us
  local copies, waits for them, and re-layouts: 4.28 us -> 1.34 us
  waiting for transfers between devices: 21.2 us -> 23.1 us
    all_to_all x0 -> x5, starting transfers between devices: none -> 20.5 us  [traded(): lax.all_to_all(value, axis, 0, 0, axis_index_groups=groups, tiled=True)]
    ppermute x13 -> x1, starting transfers between devices: 15.6 us -> 0.07 us  [swapped(): lax.ppermute(value, axis, [(source, source ^ bits) for source in range(co...]
    ppermute x13 -> x1, waiting for transfers between devices: 13.3 us -> 0.01 us  [swapped(): lax.ppermute(value, axis, [(source, source ^ bits) for source in range(co...]
    all_to_all x0 -> x5, waiting for transfers between devices: none -> 12.6 us  [traded(): lax.all_to_all(value, axis, 0, 0, axis_index_groups=groups, tiled=True)]
    pallas_call x7, Pallas kernels: 17.2 us -> 20.7 us  [the longest x5 16.7 us: run(): pl.pallas_call(body, out_shape=tuple(outs), in_specs=[SMEM if a.dtype ==...]
    unnamed x10 -> x4, local copies, waits for them, and re-layouts: 4.28 us -> 1.34 us
    ppermute x2, waiting for transfers between devices: 7.98 us -> 10.6 us  [shifted(): lax.ppermute(value, axis, [(source, source + steps) for source in range(l...]
  transfers between devices with their start and end apart: 15 -> 8, of which waited for: 7 -> 4; matrix products, arithmetic and copies ran while one was open for 0% -> 0% of each run, Pallas kernels for 17% -> 17%
where the time goes in v2:
time: 82 us; the launch traced here: 81.4 us
  Pallas kernels  30 us (37%)
  starting transfers between devices  26.1 us (32%)
  waiting for transfers between devices  23.1 us (28%)
  local copies, waits for them, and re-layouts  1.34 us (2%)
    all_to_all x5, starting transfers between devices, traded(): lax.all_to_all(value, axis, 0, 0, axis_index_groups=groups, tiled=True)  20.5 us
    pallas_call x5, Pallas kernels, run(): pl.pallas_call(body, out_shape=tuple(outs), in_specs=[SMEM if a.dtype ==...  16.7 us
    all_to_all x5, waiting for transfers between devices, traded(): lax.all_to_all(value, axis, 0, 0, axis_index_groups=groups, tiled=True)  12.6 us
    ppermute x2, waiting for transfers between devices, shifted(): lax.ppermute(value, axis, [(source, source + steps) for source in range(l...  10.6 us
    pallas_call x2, Pallas kernels, head_product(): pl.pallas_call(body, out_shape=jax.ShapeDtypeStruct((rows, tokens), jnp.b...  9.34 us
    ppermute x2, starting transfers between devices, shifted(): lax.ppermute(value, axis, [(source, source + steps) for source in range(l...  5.55 us
    pallas_call x2, Pallas kernels, split_heads(): pl.pallas_call(body, out_shape=jax.ShapeDtypeStruct((group, tokens, sum(w...  3.98 us
  transfers between devices with their start and end apart: 8, of which 4 were waited for; matrix products, arithmetic and copies ran while one was open for 0% of the time, Pallas kernels for 17%

profile of v2, /device:TPU:0, one launch (start us, length us, event | category | flops | bytes accessed | tf_op | source)
XLA Modules:
  0.0 81.4 jit_solution(9081517698025244006)
XLA Ops:
  0.6 0.0 copy-start.1
  0.6 2.0 %shard_map.76 = bf16[4,256,256]{2,1,0:T(8,128)(2,1)} custom-call(bf16[256,512]{1,0:T(8,128)(2,1)} %refs_0_.2, bf16[256,512]{1,0:T(8,128)(2,1)} %refs_1_.1), custom_call_target="tpu_custom_call" | custom-call | bytes 1048576 | tf_op jit(solution)/shard_map/pallas_call | solution.py:82
  2.7 5.2 %all-to-all-start = ((bf16[4,256,256]{2,1,0:T(8,128)(2,1)}), bf16[4,256,256]{2,1,0:T(8,128)(2,1)S(1)}, u32[]{:S(2)}, u32[]{:S(2)}) async-start(bf16[4,256,256]{2,1,0:T(8,128)(2,1)} %shard_map.76), calls=%async_computation | async-start | bytes 1048576 | tf_op jit(solution)/shard_map/all_to_all | solution.py:38
  7.9 0.0 copy-start
  7.9 1.3 %copy-done = bf16[256,2688]{1,0:T(8,128)(2,1)S(1)} copy-done((bf16[256,2688]{1,0:T(8,128)(2,1)S(1)}, bf16[256,2688]{1,0:T(8,128)(2,1)}, u32[]{:S(2)}) %copy-start) | copy-done | bytes 1376280
  9.2 4.7 %shard_map.79 = bf16[1024,256]{1,0:T(8,128)(2,1)S(1)} custom-call(s32[1]{0:T(128)S(6)} %sub.7.start_ref, bf16[2048,2688]{1,0:T(8,128)(2,1)} %w_ref.3, bf16[256,2688]{1,0:T(8,128)(2,1)S(1)} %copy-done), custom_call_target="tpu_custom_call" | custom-call | flops 1409286144 | bytes 7405568 | tf_op jit(solution)/shard_map/pallas_call | solution.py:117
  13.9 0.1 collective-permute-start.1
  14.0 1.9 %shard_map.77 = bf16[4,256,256]{2,1,0:T(8,128)(2,1)} custom-call(bf16[256,1024]{1,0:T(8,128)(2,1)} %refs_0_.3), custom_call_target="tpu_custom_call" | custom-call | bytes 1048576 | tf_op jit(solution)/shard_map/pallas_call | solution.py:82
  15.9 0.0 all-to-all-done.refs_0_
  15.9 4.2 %all-to-all-start.1 = ((bf16[4,256,256]{2,1,0:T(8,128)(2,1)}), bf16[4,256,256]{2,1,0:T(8,128)(2,1)S(1)}, u32[]{:S(2)}, u32[]{:S(2)}) async-start(bf16[4,256,256]{2,1,0:T(8,128)(2,1)} %shard_map.77), calls=%async_computation.1 | async-start | bytes 1048576 | tf_op jit(solution)/shard_map/all_to_all | solution.py:38
  20.1 4.3 %collective-permute-start = (bf16[4,256,256]{2,1,0:T(8,128)(2,1)S(1)}, bf16[4,256,256]{2,1,0:T(8,128)(2,1)}, u32[]{:S(2)}, u32[]{:S(2)}) collective-permute-start(bf16[4,256,256]{2,1,0:T(8,128)(2,1)S(1)} %all-to-all-done.refs_0_), channel_id=1, source_target_pairs={{0,8},{2,10},{4,12},{6,14},{8,16},{10,18},{12,20},{14,22},{16,24},... | collective-permute-start | bytes 1572872 | tf_op jit(solution)/shard_map/ppermute | solution.py:25
  24.4 0.0 copy-done.1
  24.4 4.7 %shard_map.78.refs_0_ = bf16[1024,256]{1,0:T(8,128)(2,1)S(1)} custom-call(s32[1]{0:T(128)} %bitcast.1.start_ref, bf16[2048,2688]{1,0:T(8,128)(2,1)} %w_ref.3, bf16[256,2688]{1,0:T(8,128)(2,1)S(1)} %copy-done.1), custom_call_target="tpu_custom_call" | custom-call | flops 1409286144 | bytes 7405568 | tf_op jit(solution)/shard_map/pallas_call | solution.py:117
  29.1 0.0 collective-permute-done.1.refs_1_
  29.1 0.9 %shard_map.80 = bf16[1024,256]{1,0:T(8,128)(2,1)} custom-call(bf16[1024,256]{1,0:T(8,128)(2,1)S(1)} %shard_map.78.refs_0_, bf16[1024,256]{1,0:T(8,128)(2,1)S(1)} %collective-permute-done.1.refs_1_), custom_call_target="tpu_custom_call" | custom-call | bytes 1572864 | tf_op jit(solution)/shard_map/pallas_call | solution.py:45
  30.0 0.0 all-to-all-done.1.refs_2_
  30.0 4.2 %all-to-all-start.2 = ((bf16[4,256,256]{2,1,0:T(8,128)(2,1)}), bf16[4,256,256]{2,1,0:T(8,128)(2,1)S(1)}, u32[]{:S(2)}, u32[]{:S(2)}) async-start(bf16[4,256,256]{2,1,0:T(8,128)(2,1)} %bitcast.2), calls=%async_computation.2 | async-start | bytes 1048576 | tf_op jit(solution)/shard_map/all_to_all | solution.py:38
  34.2 0.9 %collective-permute-done.refs_1_ = bf16[4,256,256]{2,1,0:T(8,128)(2,1)} collective-permute-done((bf16[4,256,256]{2,1,0:T(8,128)(2,1)S(1)}, bf16[4,256,256]{2,1,0:T(8,128)(2,1)}, u32[]{:S(2)}, u32[]{:S(2)}) %collective-permute-start) | collective-permute-done | bytes 524320 | tf_op jit(solution)/shard_map/ppermute | solution.py:25
  35.1 6.9 %all-to-all-done.2.refs_3_ = bf16[4,256,256]{2,1,0:T(8,128)(2,1)S(1)} async-done(((bf16[4,256,256]{2,1,0:T(8,128)(2,1)}), bf16[4,256,256]{2,1,0:T(8,128)(2,1)S(1)}, u32[]{:S(2)}, u32[]{:S(2)}) %all-to-all-start.2) | async-done | bytes 524320 | tf_op jit(solution)/shard_map/all_to_all | solution.py:38
  42.0 13.2 %shard_map.81 = (bf16[4,256,256]{2,1,0:T(8,128)(2,1)}, f32[4,256,256]{2,1,0:T(8,128)S(1)}, bf16[4,256,256]{2,1,0:T(8,128)(2,1)}) custom-call(s32[1]{0:T(128)} %bitcast.ids_ref, bf16[4,256,256]{2,1,0:T(8,128)(2,1)S(1)} %all-to-all-done.refs_0_, bf16[4,256,256]{2,1,0:T(8,128)(2,1)} %collective-permute-done.refs_1_, ...), custom_call_target="tpu_custom_call" | custom-call | flops 3355443200 | bytes 4194308 | tf_op jit(solution)/shard_map/pallas_call | solution.py:45
  55.2 1.3 %collective-permute-start.2 = (bf16[4,256,256]{2,1,0:T(8,128)(2,1)}, bf16[4,256,256]{2,1,0:T(8,128)(2,1)S(1)}, u32[]{:S(2)}, u32[]{:S(2)}) collective-permute-start(bf16[4,256,256]{2,1,0:T(8,128)(2,1)} %get-tuple-element.10), channel_id=1, source_target_pairs={{8,0},{10,2},{12,4},{14,6},{16,8},{18,10},{20,12},{22,14},{24,16},... | collective-permute-start | bytes 1572872 | tf_op jit(solution)/shard_map/ppermute | solution.py:25
  56.5 3.5 %all-to-all-start.3 = ((bf16[4,256,256]{2,1,0:T(8,128)(2,1)}), bf16[4,256,256]{2,1,0:T(8,128)(2,1)S(1)}, u32[]{:S(2)}, u32[]{:S(2)}) async-start(bf16[4,256,256]{2,1,0:T(8,128)(2,1)} %get-tuple-element.8), calls=%async_computation.3 | async-start | bytes 1048576 | tf_op jit(solution)/shard_map/all_to_all | solution.py:38
  60.0 9.6 %collective-permute-done.2.refs_1_ = bf16[4,256,256]{2,1,0:T(8,128)(2,1)S(1)} collective-permute-done((bf16[4,256,256]{2,1,0:T(8,128)(2,1)}, bf16[4,256,256]{2,1,0:T(8,128)(2,1)S(1)}, u32[]{:S(2)}, u32[]{:S(2)}) %collective-permute-start.2) | collective-permute-done | bytes 524320 | tf_op jit(solution)/shard_map/ppermute | solution.py:25
  69.6 0.9 %shard_map.83 = bf16[4,256,256]{2,1,0:T(8,128)(2,1)} custom-call(f32[4,256,256]{2,1,0:T(8,128)S(1)} %get-tuple-element.9.refs_0_, bf16[4,256,256]{2,1,0:T(8,128)(2,1)S(1)} %collective-permute-done.2.refs_1_), custom_call_target="tpu_custom_call" | custom-call | bytes 2097152 | tf_op jit(solution)/shard_map/pallas_call | solution.py:45
  70.5 0.0 all-to-all-done.3.in_ref
  70.5 3.5 %all-to-all-start.4 = ((bf16[4,256,256]{2,1,0:T(8,128)(2,1)}), bf16[4,256,256]{2,1,0:T(8,128)(2,1)S(1)}, u32[]{:S(2)}, u32[]{:S(2)}) async-start(bf16[4,256,256]{2,1,0:T(8,128)(2,1)} %shard_map.83), calls=%async_computation.4 | async-start | bytes 1048576 | tf_op jit(solution)/shard_map/all_to_all | solution.py:38
  74.0 0.9 %shard_map.82 = bf16[256,1024]{1,0:T(8,128)(2,1)} custom-call(bf16[4,256,256]{2,1,0:T(8,128)(2,1)S(1)} %all-to-all-done.3.in_ref), custom_call_target="tpu_custom_call" | custom-call | bytes 1048576 | tf_op jit(solution)/shard_map/pallas_call | solution.py:45
  74.8 5.7 %all-to-all-done.4.in_ref = bf16[4,256,256]{2,1,0:T(8,128)(2,1)S(1)} async-done(((bf16[4,256,256]{2,1,0:T(8,128)(2,1)}), bf16[4,256,256]{2,1,0:T(8,128)(2,1)S(1)}, u32[]{:S(2)}, u32[]{:S(2)}) %all-to-all-start.4) | async-done | bytes 524320 | tf_op jit(solution)/shard_map/all_to_all | solution.py:38
  80.5 0.9 %shard_map.84 = (bf16[256,512]{1,0:T(8,128)(2,1)}, bf16[256,512]{1,0:T(8,128)(2,1)}) custom-call(bf16[4,256,256]{2,1,0:T(8,128)(2,1)S(1)} %all-to-all-done.4.in_ref), custom_call_target="tpu_custom_call" | custom-call | bytes 1048576 | tf_op jit(solution)/shard_map/pallas_call | solution.py:45
Async XLA Ops:
  0.6 23.8 %copy-start.1 = (bf16[256,2688]{1,0:T(8,128)(2,1)S(1)}, bf16[256,2688]{1,0:T(8,128)(2,1)}, u32[]{:S(2)}) copy-start(bf16[256,2688]{1,0:T(8,128)(2,1)} %c_ref.3) | copy-start | bytes 4128772
  2.7 13.2 %all-to-all-start = ((bf16[4,256,256]{2,1,0:T(8,128)(2,1)}), bf16[4,256,256]{2,1,0:T(8,128)(2,1)S(1)}, u32[]{:S(2)}, u32[]{:S(2)}) async-start(bf16[4,256,256]{2,1,0:T(8,128)(2,1)} %shard_map.76), calls=%async_computation | async-start | bytes 1048576 | tf_op jit(solution)/shard_map/all_to_all | solution.py:38
  7.9 1.3 %copy-start = (bf16[256,2688]{1,0:T(8,128)(2,1)S(1)}, bf16[256,2688]{1,0:T(8,128)(2,1)}, u32[]{:S(2)}) copy-start(bf16[256,2688]{1,0:T(8,128)(2,1)} %c_ref.3) | copy-start | bytes 4128772
  13.9 15.2 %collective-permute-start.1 = (bf16[1024,256]{1,0:T(8,128)(2,1)S(1)}, bf16[1024,256]{1,0:T(8,128)(2,1)S(1)}, u32[]{:S(2)}, u32[]{:S(2)}) collective-permute-start(bf16[1024,256]{1,0:T(8,128)(2,1)S(1)} %shard_map.79), channel_id=1, source_target_pairs={{0,1},{1,0},{2,3},{3,2},{4,5},{5,4},{6,7},{7,6},{8,9},{9,8},{10,11... | collective-permute-start | bytes 1572872 | tf_op jit(solution)/shard_map/ppermute | solution.py:30
  15.9 14.1 %all-to-all-start.1 = ((bf16[4,256,256]{2,1,0:T(8,128)(2,1)}), bf16[4,256,256]{2,1,0:T(8,128)(2,1)S(1)}, u32[]{:S(2)}, u32[]{:S(2)}) async-start(bf16[4,256,256]{2,1,0:T(8,128)(2,1)} %shard_map.77), calls=%async_computation.1 | async-start | bytes 1048576 | tf_op jit(solution)/shard_map/all_to_all | solution.py:38
  20.1 15.0 %collective-permute-start = (bf16[4,256,256]{2,1,0:T(8,128)(2,1)S(1)}, bf16[4,256,256]{2,1,0:T(8,128)(2,1)}, u32[]{:S(2)}, u32[]{:S(2)}) collective-permute-start(bf16[4,256,256]{2,1,0:T(8,128)(2,1)S(1)} %all-to-all-done.refs_0_), channel_id=1, source_target_pairs={{0,8},{2,10},{4,12},{6,14},{8,16},{10,18},{12,20},{14,22},{16,24},... | collective-permute-start | bytes 1572872 | tf_op jit(solution)/shard_map/ppermute | solution.py:25
  30.0 12.0 %all-to-all-start.2 = ((bf16[4,256,256]{2,1,0:T(8,128)(2,1)}), bf16[4,256,256]{2,1,0:T(8,128)(2,1)S(1)}, u32[]{:S(2)}, u32[]{:S(2)}) async-start(bf16[4,256,256]{2,1,0:T(8,128)(2,1)} %bitcast.2), calls=%async_computation.2 | async-start | bytes 1048576 | tf_op jit(solution)/shard_map/all_to_all | solution.py:38
  55.2 14.4 %collective-permute-start.2 = (bf16[4,256,256]{2,1,0:T(8,128)(2,1)}, bf16[4,256,256]{2,1,0:T(8,128)(2,1)S(1)}, u32[]{:S(2)}, u32[]{:S(2)}) collective-permute-start(bf16[4,256,256]{2,1,0:T(8,128)(2,1)} %get-tuple-element.10), channel_id=1, source_target_pairs={{8,0},{10,2},{12,4},{14,6},{16,8},{18,10},{20,12},{22,14},{24,16},... | collective-permute-start | bytes 1572872 | tf_op jit(solution)/shard_map/ppermute | solution.py:25
  56.5 14.0 %all-to-all-start.3 = ((bf16[4,256,256]{2,1,0:T(8,128)(2,1)}), bf16[4,256,256]{2,1,0:T(8,128)(2,1)S(1)}, u32[]{:S(2)}, u32[]{:S(2)}) async-start(bf16[4,256,256]{2,1,0:T(8,128)(2,1)} %get-tuple-element.8), calls=%async_computation.3 | async-start | bytes 1048576 | tf_op jit(solution)/shard_map/all_to_all | solution.py:38
  70.5 10.0 %all-to-all-start.4 = ((bf16[4,256,256]{2,1,0:T(8,128)(2,1)}), bf16[4,256,256]{2,1,0:T(8,128)(2,1)S(1)}, u32[]{:S(2)}, u32[]{:S(2)}) async-start(bf16[4,256,256]{2,1,0:T(8,128)(2,1)} %shard_map.83), calls=%async_computation.4 | async-start | bytes 1048576 | tf_op jit(solution)/shard_map/all_to_all | solution.py:38

commit v3 on v1

v3 whole, which is shorter than its diff:
```python
import functools

import jax
import jax.numpy as jnp
from jax import lax
from jax.experimental import pallas as pl
from jax.experimental.pallas import tpu as pltpu
from jax.sharding import PartitionSpec as P

HEAD_SIZE = 128
WINDOW_LENGTH = 1024
LOG2_E = 1.4426950408889634

score_scale = 168.0 ** (-0.5)

VMEM = pl.BlockSpec(memory_space=pltpu.VMEM)
HBM = pl.BlockSpec(memory_space=pltpu.HBM)
SMEM = pl.BlockSpec(memory_space=pltpu.SMEM)
NT = (((1,), (1,)), ((), ()))
NN = (((1,), (0,)), ((), ()))


def shifted(value, axis, steps):
    count = lax.axis_size(axis)
    leading, last = (max(0, -steps), min(count, count - steps))
    return lax.ppermute(value, axis, [(source, source + steps) for source in range(leading, last)])


def swapped(value, axis, bits):
    count = lax.axis_size(axis)
    return lax.ppermute(value, axis, [(source, source ^ bits) for source in range(count)])


def call(body, outs, scratch=(), flops=0, exps=0, specs=None, vmem=32):
    def run(*args):
        moved = sum(a.size * a.dtype.itemsize for a in args)
        moved += sum(o.size * o.dtype.itemsize for o in outs)
        return pl.pallas_call(
            body,
            out_shape=tuple(outs),
            in_specs=specs or [SMEM if a.dtype == jnp.int32 else VMEM for a in args],
            out_specs=tuple(VMEM for _ in outs),
            scratch_shapes=list(scratch),
            compiler_params=pltpu.CompilerParams(vmem_limit_bytes=vmem * 1024 * 1024),
            cost_estimate=pl.CostEstimate(flops=flops, bytes_accessed=moved, transcendentals=exps),
        )(*args)

    return run


def lanes(index, width):
    return pl.ds(pl.multiple_of(index * width, width), width)


def fetch_all(refs, held, sems):
    copies = [pltpu.make_async_copy(ref, to, sems.at[i]) for i, (ref, to) in enumerate(zip(refs, held))]
    for copy in copies:
        copy.start()
    for copy in copies:
        copy.wait()


def pack_kv(group, ids, keys, values):
    tokens, width = keys.shape[0], keys.shape[1] // group

    def body(ids_ref, k_in, v_in, *refs):
        k_ref, v_ref, sems = refs[group:]
        fetch_all((k_in, v_in), (k_ref, v_ref), sems)
        for r in range(group):
            member = ids_ref[0] ^ r
            refs[r][:, :width] = k_ref[:, lanes(member, width)]
            refs[r][:, width:] = v_ref[:, lanes(member, width)]

    outs = [jax.ShapeDtypeStruct((tokens, 2 * width), jnp.bfloat16)] * group
    scratch = [pltpu.VMEM(keys.shape, jnp.bfloat16)] * 2 + [pltpu.SemaphoreType.DMA((2,))]
    return call(body, outs, scratch, specs=[SMEM, HBM, HBM], vmem=62)(ids, keys, values)


def pack_queries(group, ids, queries):
    tokens, width = queries.shape[0], queries.shape[1] // group

    def body(ids_ref, q_ref, *out_refs):
        for r in range(group):
            out_refs[r][...] = q_ref[:, lanes(ids_ref[0] ^ r, width)]

    outs = [jax.ShapeDtypeStruct((tokens, width), jnp.bfloat16)] * group
    return call(body, outs)(ids, queries)


def order_pieces(group, ids, pieces):
    def body(ids_ref, *refs):
        for r in range(group):
            refs[group][ids_ref[0] ^ r] = refs[r][...]

    outs = [jax.ShapeDtypeStruct((group,) + pieces[0].shape, jnp.bfloat16)]
    return call(body, outs)(ids, *pieces)[0]


def head_product(start, rows, out_weight, layer_cotangent):
    tokens, depth = layer_cotangent.shape
    cuts = 3 if depth % (3 * 128) == 0 else 1
    chunk = depth // cuts
    strips = 4

    def body(start_ref, w_in, c_in, o_ref, w_ref, c_ref, total, w_sems, c_sems):
        first = start_ref[0] * rows
        copies = []
        for cut in range(cuts):
            columns = slice(cut * chunk, (cut + 1) * chunk)
            here = [pltpu.make_async_copy(c_in.at[:, columns], c_ref.at[:, columns], c_sems.at[cut])]
            for strip in range(strips):
                height = rows // strips
                there = pl.ds(pl.multiple_of(first + strip * height, height), height)
                here.append(
                    pltpu.make_async_copy(
                        w_in.at[there, columns],
                        w_ref.at[strip * height : (strip + 1) * height, columns],
                        w_sems.at[cut, strip],
                    )
                )
            copies.append(here)
        for here in copies:
            for copy in here:
                copy.start()
        for cut in range(cuts):
            columns = slice(cut * chunk, (cut + 1) * chunk)
            for copy in copies[cut]:
                copy.wait()
            term = lax.dot_general(
                w_ref[:, columns], c_ref[:, columns], NT, preferred_element_type=jnp.float32
            )
            if cut > 0:
                term = total[...] + term
            if cut < cuts - 1:
                total[...] = term
            else:
                o_ref[...] = term.astype(jnp.bfloat16)

    outs = [jax.ShapeDtypeStruct((rows, tokens), jnp.bfloat16)]
    scratch = [
        pltpu.VMEM((rows, depth), jnp.bfloat16),
        pltpu.VMEM((tokens, depth), jnp.bfloat16),
        pltpu.VMEM((rows, tokens), jnp.float32),
        pltpu.SemaphoreType.DMA((cuts, strips)),
        pltpu.SemaphoreType.DMA((cuts,)),
    ]
    run = call(body, outs, scratch, flops=2 * rows * tokens * depth, specs=[SMEM, HBM, HBM], vmem=54)
    return run(start, out_weight, layer_cotangent)[0]


def pack_grads(group, ids, terms):
    rows, tokens = terms[0].shape
    rows //= group

    def body(ids_ref, *refs):
        for r in range(group):
            there = lanes(ids_ref[0] ^ r, rows)
            total = refs[0][there, :]
            if len(terms) > 1:
                total = total.astype(jnp.float32)
                for term in refs[1 : len(terms)]:
                    total = total + term[there, :].astype(jnp.float32)
            refs[len(terms) + r][...] = total.astype(jnp.bfloat16)

    outs = [jax.ShapeDtypeStruct((rows, tokens), jnp.bfloat16)] * group
    return call(body, outs)(ids, *terms)


class Shape:
    def __init__(self, group, steps, heads, per_head, tokens):
        self.group, self.steps, self.heads, self.per_head, self.tokens = group, steps, heads, per_head, tokens
        self.back = steps * group
        self.span = self.back + 1
        self.total = self.back + group
        self.wide = per_head * tokens
        self.width = heads * per_head * HEAD_SIZE
        self.kv_width = heads * HEAD_SIZE
        self.entries = group * heads * self.wide * self.span * tokens

    def block(self, own_ref, earlier_refs, number):
        if number < self.back:
            return earlier_refs[number // self.group].at[number % self.group]
        return own_ref.at[number - self.back]


def softmax(z, ids, kv_own, kv_earlier, queries):
    factor = score_scale * LOG2_E

    def body(ids_ref, *refs):
        own_ref, earlier_refs, q_refs = refs[0], refs[1 : 1 + z.steps], refs[1 + z.steps : 1 + z.steps + z.group]
        e_ref, inverse_ref, qt_ref, k_all, s_all = refs[1 + z.steps + z.group :]
        place, first = ids_ref[0], ids_ref[1]
        key_id = lax.broadcasted_iota(jnp.int32, (z.tokens, z.wide), 0)
        query_id = lax.broadcasted_iota(jnp.int32, (z.tokens, z.wide), 1) & (z.tokens - 1)
        for head in range(z.heads):
            at_k = slice(head * HEAD_SIZE, (head + 1) * HEAD_SIZE)
            for number in range(z.total):
                k_all[number] = z.block(own_ref, earlier_refs, number)[:, at_k]
            for r in range(z.group):
                for j in range(z.per_head):
                    lower = (head * z.per_head + j) * HEAD_SIZE
                    qt_ref[head, place ^ r, :, j * z.tokens : (j + 1) * z.tokens] = q_refs[r][
                        :, lower : lower + HEAD_SIZE
                    ].T

            @pl.loop(0, z.group)
            def _(b):
                qt = qt_ref[head, b]
                top = None
                for c in range(z.span):
                    s = lax.dot_general(k_all[b + c], qt, NN, preferred_element_type=jnp.float32)
                    if c == 0:
                        s = jnp.where(key_id > query_id, s, -jnp.inf)
                    if c == z.back:
                        s = jnp.where(key_id <= query_id, s, -jnp.inf)
                    s_all[c] = s
                    here = jnp.max(s, axis=0, keepdims=True)
                    if c < z.back:
                        here = jnp.where(first + b + c >= z.back, here, -jnp.inf)
                    top = here if top is None else jnp.maximum(top, here)
                norm = jnp.zeros((1, z.wide), jnp.float32)
                for c in range(z.span):
                    base = top
                    if c < z.back:
                        base = jnp.where(first + b + c >= z.back, top, jnp.inf)
                    e = jnp.exp2((s_all[c] - base) * factor)
                    norm = norm + jnp.sum(e, axis=0, keepdims=True)
                    e_ref[head, b, c] = e.astype(jnp.bfloat16)
                inverse_ref[head, b] = 1.0 / norm

    outs = [
        jax.ShapeDtypeStruct((z.heads, z.group, z.span, z.tokens, z.wide), jnp.bfloat16),
        jax.ShapeDtypeStruct((z.heads, z.group, 1, z.wide), jnp.float32),
        jax.ShapeDtypeStruct((z.heads, z.group, HEAD_SIZE, z.wide), jnp.bfloat16),
    ]
    scratch = [
        pltpu.VMEM((z.total, z.tokens, HEAD_SIZE), jnp.bfloat16),
        pltpu.VMEM((z.span, z.tokens, z.wide), jnp.float32),
    ]
    return call(body, outs, scratch, flops=2 * z.entries * HEAD_SIZE, exps=z.entries)(
        ids, kv_own, *kv_earlier, *queries
    )


def value_terms(z, ids, e, inverse, grads):
    def body(ids_ref, e_ref, inverse_ref, *refs):
        g_refs, (g_ref, own_ref), earlier_refs = (
            refs[: z.group],
            refs[z.group : z.group + 2],
            refs[z.group + 2 : z.group + 2 + z.steps],
        )
        dv_all = refs[-1]
        place = ids_ref[0]
        for head in range(z.heads):
            at = slice(head * HEAD_SIZE, (head + 1) * HEAD_SIZE)
            for r in range(z.group):
                for j in range(z.per_head):
                    lower = (head * z.per_head + j) * HEAD_SIZE
                    g_ref[head, place ^ r, :, j * z.tokens : (j + 1) * z.tokens] = g_refs[r][
                        lower : lower + HEAD_SIZE, :
                    ]
            dv_all[...] = jnp.zeros_like(dv_all)

            @pl.loop(0, z.group)
            def _(b):
                g = (g_ref[head, b].astype(jnp.float32) * inverse_ref[head, b]).astype(jnp.bfloat16)
                for c in range(z.span):
                    dv_all[b + c] += lax.dot_general(
                        e_ref[head, b, c], g, NT, preferred_element_type=jnp.float32
                    )

            for number in range(z.total):
                part = dv_all[number]
                z.block(own_ref, earlier_refs, number)[:, at] = part.astype(own_ref.dtype if number >= z.back else jnp.bfloat16)

    outs = [
        jax.ShapeDtypeStruct((z.heads, z.group, HEAD_SIZE, z.wide), jnp.bfloat16),
        jax.ShapeDtypeStruct((z.group, z.tokens, z.kv_width), jnp.float32),
    ]
    outs += [jax.ShapeDtypeStruct((z.group, z.tokens, z.kv_width), jnp.bfloat16)] * z.steps
    scratch = [pltpu.VMEM((z.total, z.tokens, HEAD_SIZE), jnp.float32)]
    results = call(body, outs, scratch, flops=2 * z.entries * HEAD_SIZE)(ids, e, inverse, *grads)
    return results[0], results[1], results[2:]


def score_terms(z, ids, e, inverse, qt, g, kv_own, kv_earlier):
    def body(ids_ref, e_ref, inverse_ref, qt_ref, g_ref, own_ref, *refs):
        earlier_refs, dq_refs = refs[: z.steps], refs[z.steps : z.steps + z.group]
        dk_own, dk_earlier = refs[z.steps + z.group], refs[z.steps + z.group + 1 : 2 * z.steps + z.group + 1]
        kt_all, v_all, dq_all, dk_all, dp_all = refs[2 * z.steps + z.group + 1 :]
        place = ids_ref[0]
        for head in range(z.heads):
            at = slice(head * HEAD_SIZE, (head + 1) * HEAD_SIZE)
            at_v = slice(z.kv_width + head * HEAD_SIZE, z.kv_width + (head + 1) * HEAD_SIZE)
            for number in range(z.total):
                source = z.block(own_ref, earlier_refs, number)
                kt_all[number] = source[:, at].T
                v_all[number] = source[:, at_v]
            dk_all[...] = jnp.zeros_like(dk_all)

            @pl.loop(0, z.group)
            def _(b):
                g = g_ref[head, b]
                inverse = inverse_ref[head, b]
                delta = jnp.zeros((1, z.wide), jnp.float32)
                for c in range(z.span):
                    dp = lax.dot_general(v_all[b + c], g, NN, preferred_element_type=jnp.float32)
                    delta = delta + jnp.sum(e_ref[head, b, c].astype(jnp.float32) * dp, axis=0, keepdims=True)
                    dp_all[c] = dp
                delta = delta * inverse
                q = (qt_ref[head, b].astype(jnp.float32) * inverse).astype(jnp.bfloat16)
                dqt = jnp.zeros((HEAD_SIZE, z.wide), jnp.float32)
                for c in range(z.span):
                    ds = (e_ref[head, b, c].astype(jnp.float32) * (dp_all[c] - delta)).astype(jnp.bfloat16)
                    dk_all[b + c] += lax.dot_general(ds, q, NT, preferred_element_type=jnp.float32)
                    dqt = dqt + lax.dot_general(kt_all[b + c], ds, NN, preferred_element_type=jnp.float32)
                dqt = dqt * (inverse * score_scale)
                for j in range(z.per_head):
                    lower = (head * z.per_head + j) * HEAD_SIZE
                    dq_all[b, :, lower : lower + HEAD_SIZE] = (
                        dqt[:, j * z.tokens : (j + 1) * z.tokens].T.astype(jnp.bfloat16)
                    )

            for number in range(z.total):
                part = dk_all[number] * score_scale
                z.block(dk_own, dk_earlier, number)[:, at] = part.astype(dk_own.dtype if number >= z.back else jnp.bfloat16)
        for r in range(z.group):
            dq_refs[r][...] = dq_all[place ^ r]

    outs = [jax.ShapeDtypeStruct((z.tokens, z.width), jnp.bfloat16)] * z.group
    outs += [jax.ShapeDtypeStruct((z.group, z.tokens, z.kv_width), jnp.float32)]
    outs += [jax.ShapeDtypeStruct((z.group, z.tokens, z.kv_width), jnp.bfloat16)] * z.steps
    scratch = [
        pltpu.VMEM((z.total, HEAD_SIZE, z.tokens), jnp.bfloat16),
        pltpu.VMEM((z.total, z.tokens, HEAD_SIZE), jnp.bfloat16),
        pltpu.VMEM((z.group, z.tokens, z.width), jnp.bfloat16),
        pltpu.VMEM((z.total, z.tokens, HEAD_SIZE), jnp.float32),
        pltpu.VMEM((z.span, z.tokens, z.wide), jnp.float32),
    ]
    results = call(body, outs, scratch, flops=6 * z.entries * HEAD_SIZE)(
        ids, e, inverse, qt, g, kv_own, *kv_earlier
    )
    return results[: z.group], results[z.group], results[z.group + 1 :]


def pack_terms(group, ids, own, arrived):
    shape = own.shape[1:]

    def body(ids_ref, *refs):
        for r in range(group):
            member = ids_ref[0] ^ r
            total = refs[0][member]
            for term in refs[1 : 1 + len(arrived)]:
                total = total + term[member].astype(jnp.float32)
            refs[1 + len(arrived) + r][...] = total.astype(jnp.bfloat16)

    outs = [jax.ShapeDtypeStruct(shape, jnp.bfloat16)] * group
    return call(body, outs)(ids, own, *arrived)


def unpack(group, ids, pieces):
    tokens, width = pieces[0].shape

    def body(ids_ref, *refs):
        for r in range(group):
            refs[group][:, lanes(ids_ref[0] ^ r, width)] = refs[r][...]

    return call(body, [jax.ShapeDtypeStruct((tokens, group * width), jnp.bfloat16)])(ids, *pieces)[0]


def local(layer_cotangent, out_weight, queries, keys, values):
    tokens = queries.shape[0]
    kv_heads = keys.shape[1] // HEAD_SIZE
    per_head = queries.shape[1] // keys.shape[1]
    count, tp_count = lax.axis_size("ctx"), lax.axis_size("tp")
    group = 1
    while (
        kv_heads % (2 * group) == 0
        and count % (2 * group) == 0
        and WINDOW_LENGTH % (2 * group * tokens) == 0
    ):
        group *= 2
    heads = kv_heads // group
    kv_width = heads * HEAD_SIZE
    back_groups = WINDOW_LENGTH // (group * tokens)
    index = lax.axis_index("ctx")
    place = index % group
    ids = jnp.stack([place, index - place]).astype(jnp.int32)
    rows = out_weight.shape[0] // tp_count

    def trade(sent):
        return [sent[0]] + [swapped(sent[r], "ctx", r) for r in range(1, group)]

    def returned(own, earlier):
        arrived = [
            shifted(earlier[number], "ctx", -group * (back_groups - number)) for number in range(back_groups)
        ]
        return unpack(group, ids, trade(pack_terms(group, ids, own, arrived)))

    kv_own = order_pieces(group, ids, trade(pack_kv(group, ids, keys, values)))
    kv_earlier = [shifted(kv_own, "ctx", group * step) for step in range(back_groups, 0, -1)]
    query_pieces = trade(pack_queries(group, ids, queries))
    if tp_count == 2:
        mine = lax.axis_index("tp").astype(jnp.int32).reshape(1)
        other = head_product(1 - mine, rows, out_weight, layer_cotangent)
        terms = [swapped(other, "tp", 1)]
        terms = [head_product(mine, rows, out_weight, layer_cotangent)] + terms
    else:
        product = head_product(jnp.zeros(1, jnp.int32), rows * tp_count, out_weight, layer_cotangent)
        terms = [lax.psum_scatter(product, "tp", scatter_dimension=0, tiled=True)]
    grads = trade(pack_grads(group, ids, terms))
    z = Shape(group, back_groups, heads, per_head, tokens)
    e, inverse, qt = softmax(z, ids, kv_own, kv_earlier, query_pieces)
    g, dv_own, dv_earlier = value_terms(z, ids, e, inverse, grads)
    dq, dk_own, dk_earlier = score_terms(z, ids, e, inverse, qt, g, kv_own, kv_earlier)
    value_gradients = returned(dv_own, dv_earlier)
    query_grads = unpack(group, ids, trade(dq))
    key_gradients = returned(dk_own, dk_earlier)
    return (query_grads, key_gradients, value_gradients)


def solution(mesh):
    in_specs = (P("ctx", "tp"), P(None, "tp"), P("ctx", "tp"), P("ctx", "tp"), P("ctx", "tp"))
    out_specs = (P("ctx", "tp"), P("ctx", "tp"), P("ctx", "tp"))
    return jax.shard_map(local, mesh=mesh, in_specs=in_specs, out_specs=out_specs, check_vma=False)
```

time: 73.6 us -> 73 us (level)
  waiting for transfers between devices: 21.2 us -> 4.83 us
  Pallas kernels: 26.4 us -> 35.8 us
  starting transfers between devices: 20.4 us -> 29.6 us
  local copies, waits for them, and re-layouts: 4.28 us -> 1.05 us
    ppermute x13 -> x19, waiting for transfers between devices: 13.3 us -> 2.23 us  [swapped(): lax.ppermute(value, axis, [(source, source ^ bits) for source in range(co...]
    pallas_call x9 -> x14, Pallas kernels: 26.4 us -> 35.8 us  [run(): pl.pallas_call(body, out_shape=tuple(outs), in_specs=specs or [SMEM if a....]
    ppermute x13 -> x19, starting transfers between devices: 15.6 us -> 23.4 us  [swapped(): lax.ppermute(value, axis, [(source, source ^ bits) for source in range(co...]
    ppermute x2 -> x3, waiting for transfers between devices: 7.98 us -> 2.6 us  [shifted(): lax.ppermute(value, axis, [(source, source + steps) for source in range(l...]
    unnamed x10 -> x8, local copies, waits for them, and re-layouts: 4.28 us -> 1.05 us
    ppermute x2 -> x3, starting transfers between devices: 4.81 us -> 6.26 us  [shifted(): lax.ppermute(value, axis, [(source, source + steps) for source in range(l...]
  transfers between devices with their start and end apart: 15 -> 22, of which waited for: 7 -> 5; matrix products, arithmetic and copies ran while one was open for 0% -> 0% of each run, Pallas kernels for 17% -> 40%
where the time goes in v3:
time: 73 us; the launch traced here: 72.7 us
  Pallas kernels  35.8 us (49%)
  starting transfers between devices  29.6 us (41%)
  waiting for transfers between devices  4.83 us (7%)
  local copies, waits for them, and re-layouts  1.05 us (1%)
  between operations  0.82 us (1%)
    pallas_call x14, Pallas kernels, run(): pl.pallas_call(body, out_shape=tuple(outs), in_specs=specs or [SMEM if a....  35.8 us
    ppermute x19, starting transfers between devices, swapped(): lax.ppermute(value, axis, [(source, source ^ bits) for source in range(co...  23.4 us
    ppermute x3, starting transfers between devices, shifted(): lax.ppermute(value, axis, [(source, source + steps) for source in range(l...  6.26 us
    ppermute x3, waiting for transfers between devices, shifted(): lax.ppermute(value, axis, [(source, source + steps) for source in range(l...  2.6 us
    ppermute x19, waiting for transfers between devices, swapped(): lax.ppermute(value, axis, [(source, source ^ bits) for source in range(co...  2.23 us
  transfers between devices with their start and end apart: 22, of which 5 were waited for; matrix products, arithmetic and copies ran while one was open for 0% of the time, Pallas kernels for 40%

profile of v3, /device:TPU:0, one launch (start us, length us, event | category | flops | bytes accessed | tf_op | source)
XLA Modules:
  0.0 72.7 jit_solution(15533512864727877805)
XLA Ops:
  0.6 0.6 pad_add_fusion.ids_ref
  1.3 2.6 %shard_map.76 = (bf16[256,256]{1,0:T(8,128)(2,1)}, bf16[256,256]{1,0:T(8,128)(2,1)}, bf16[256,256]{1,0:T(8,128)(2,1)}, bf16[256,256]{1,0:T(8,128)(2,1)}) custom-call(s32[2]{0:T(128)} %pad_add_fusion.ids_ref, bf16[256,512]{1,0:T(8,128)(2,1)} %k_in.1, bf16[256,512]{1,0:T(8,128)(2,1)} %v_in.1), custom_call_target="tpu_custom_call" | custom-call | bytes 1048584 | tf_op jit(solution)/shard_map/pallas_call | solution.py:38
  3.8 3.0 %collective-permute-start = (bf16[256,256]{1,0:T(8,128)(2,1)}, bf16[256,256]{1,0:T(8,128)(2,1)S(1)}, u32[]{:S(2)}, u32[]{:S(2)}) collective-permute-start(bf16[256,256]{1,0:T(8,128)(2,1)} %get-tuple-element.36), channel_id=1, source_target_pairs={{0,2},{2,0},{4,6},{6,4},{8,10},{10,8},{12,14},{14,12},{16,18},{18,... | collective-permute-start | bytes 393224 | tf_op jit(solution)/shard_map/ppermute | solution.py:31
  6.8 1.5 %collective-permute-start.1 = (bf16[256,256]{1,0:T(8,128)(2,1)}, bf16[256,256]{1,0:T(8,128)(2,1)S(1)}, u32[]{:S(2)}, u32[]{:S(2)}) collective-permute-start(bf16[256,256]{1,0:T(8,128)(2,1)} %get-tuple-element.37), channel_id=1, source_target_pairs={{0,4},{2,6},{4,0},{6,2},{8,12},{10,14},{12,8},{14,10},{16,20},{18,... | collective-permute-start | bytes 393224 | tf_op jit(solution)/shard_map/ppermute | solution.py:31
  8.4 6.0 %shard_map.81 = bf16[1024,256]{1,0:T(8,128)(2,1)} custom-call(s32[1]{0:T(128)S(6)} %sub.7.start_ref, bf16[2048,2688]{1,0:T(8,128)(2,1)} %w_in.3, bf16[256,2688]{1,0:T(8,128)(2,1)} %c_in.3), custom_call_target="tpu_custom_call" | custom-call | flops 1409286144 | bytes 12910596 | tf_op jit(solution)/shard_map/pallas_call | solution.py:38
  15.4 3.7 %collective-permute-start.3 = (bf16[4,256,256]{2,1,0:T(8,128)(2,1)S(1)}, bf16[4,256,256]{2,1,0:T(8,128)(2,1)S(1)}, u32[]{:S(2)}, u32[]{:S(2)}) collective-permute-start(bf16[4,256,256]{2,1,0:T(8,128)(2,1)S(1)} %shard_map.77.refs_0_.own_ref), channel_id=1, source_target_pairs={{0,8},{2,10},{4,12},{6,14},{8,16},{10,18},{12,20},{14,22},{16,24},... | collective-permute-start | bytes 1572872 | tf_op jit(solution)/shard_map/ppermute | solution.py:26
  19.1 0.6 shard_map.78
  19.7 1.6 %collective-permute-start.4 = (bf16[256,256]{1,0:T(8,128)(2,1)S(1)}, bf16[256,256]{1,0:T(8,128)(2,1)S(1)}, u32[]{:S(2)}, u32[]{:S(2)}) collective-permute-start(bf16[256,256]{1,0:T(8,128)(2,1)S(1)} %get-tuple-element.40), channel_id=1, source_target_pairs={{0,2},{2,0},{4,6},{6,4},{8,10},{10,8},{12,14},{14,12},{16,18},{18,... | collective-permute-start | bytes 393224 | tf_op jit(solution)/shard_map/ppermute | solution.py:31
  21.3 1.5 %collective-permute-start.5 = (bf16[256,256]{1,0:T(8,128)(2,1)S(1)}, bf16[256,256]{1,0:T(8,128)(2,1)S(1)}, u32[]{:S(2)}, u32[]{:S(2)}) collective-permute-start(bf16[256,256]{1,0:T(8,128)(2,1)S(1)} %get-tuple-element.41), channel_id=1, source_target_pairs={{0,4},{2,6},{4,0},{6,2},{8,12},{10,14},{12,8},{14,10},{16,20},{18,... | collective-permute-start | bytes 393224 | tf_op jit(solution)/shard_map/ppermute | solution.py:31
  23.3 6.0 %shard_map.80.refs_0_ = bf16[1024,256]{1,0:T(8,128)(2,1)} custom-call(s32[1]{0:T(128)} %bitcast.2.start_ref, bf16[2048,2688]{1,0:T(8,128)(2,1)} %w_in.3, bf16[256,2688]{1,0:T(8,128)(2,1)} %c_in.3), custom_call_target="tpu_custom_call" | custom-call | flops 1409286144 | bytes 12910596 | tf_op jit(solution)/shard_map/pallas_call | solution.py:38
  29.3 1.0 %copy-done = bf16[1024,256]{1,0:T(8,128)(2,1)S(1)} copy-done((bf16[1024,256]{1,0:T(8,128)(2,1)S(1)}, bf16[1024,256]{1,0:T(8,128)(2,1)}, u32[]{:S(2)}) %copy-start) | copy-done | bytes 524312
  30.3 0.7 shard_map.82
  31.0 2.5 %collective-permute-start.10 = (bf16[256,256]{1,0:T(8,128)(2,1)S(1)}, bf16[256,256]{1,0:T(8,128)(2,1)S(1)}, u32[]{:S(2)}, u32[]{:S(2)}) collective-permute-start(bf16[256,256]{1,0:T(8,128)(2,1)S(1)} %get-tuple-element.49), channel_id=1, source_target_pairs={{0,6},{2,4},{4,2},{6,0},{8,14},{10,12},{12,10},{14,8},{16,22},{18,... | collective-permute-start | bytes 393224 | tf_op jit(solution)/shard_map/ppermute | solution.py:31
  34.6 4.5 %shard_map.79 = (bf16[1,4,5,256,512]{4,3,2,1,0:T(8,128)(2,1)S(1)}, f32[1,4,1,512]{3,2,1,0:T(1,128)S(1)}, bf16[1,4,128,512]{3,2,1,0:T(8,128)(2,1)S(1)}) custom-call(s32[2]{0:T(128)S(1)} %copy-done.3, bf16[4,256,256]{2,1,0:T(8,128)(2,1)S(1)} %shard_map.77.refs_0_.own_ref, bf16[4,256,256]{2,1,0:T(8,128)(2,1)S(1)} %collective-permute-done.3.refs_1_.refs_0_, ...), custom_call_target="tpu_custom_call" | custom-call | flops 671088640 | bytes 7348232 | tf_op jit(solution)/shard_map/pallas_call | solution.py:38
  39.7 2.7 %shard_map.83 = (bf16[1,4,128,512]{3,2,1,0:T(8,128)(2,1)S(1)}, f32[4,256,128]{2,1,0:T(8,128)S(1)}, bf16[4,256,128]{2,1,0:T(8,128)(2,1)S(1)}) custom-call(s32[2]{0:T(128)S(1)} %copy-done.3, bf16[1,4,5,256,512]{4,3,2,1,0:T(8,128)(2,1)S(1)} %get-tuple-element.43.e_ref, f32[1,4,1,512]{3,2,1,0:T(1,128)S(1)} %get-tuple-element.44.inverse_ref, ...), custom_call_target="tpu_custom_call" | custom-call | flops 671088640 | bytes 7086088 | tf_op jit(solution)/shard_map/pallas_call | solution.py:38
  42.4 1.3 %collective-permute-start.18 = (bf16[4,256,128]{2,1,0:T(8,128)(2,1)S(1)}, bf16[4,256,128]{2,1,0:T(8,128)(2,1)S(1)}, u32[]{:S(2)}, u32[]{:S(2)}) collective-permute-start(bf16[4,256,128]{2,1,0:T(8,128)(2,1)S(1)} %get-tuple-element.62), channel_id=1, source_target_pairs={{8,0},{10,2},{12,4},{14,6},{16,8},{18,10},{20,12},{22,14},{24,16},... | collective-permute-start | bytes 786440 | tf_op jit(solution)/shard_map/ppermute | solution.py:26
  43.7 7.0 %shard_map.84 = (bf16[256,256]{1,0:T(8,128)(2,1)S(1)}, bf16[256,256]{1,0:T(8,128)(2,1)S(1)}, bf16[256,256]{1,0:T(8,128)(2,1)S(1)}, bf16[256,256]{1,0:T(8,128)(2,...) custom-call(s32[2]{0:T(128)S(1)} %copy-done.3, ...), custom_call_target="tpu_custom_call" | custom-call | flops 2013265920 | bytes 8658952 | tf_op jit(solution)/shard_map/pallas_call | solution.py:38
  50.7 1.3 %collective-permute-start.14 = (bf16[4,256,128]{2,1,0:T(8,128)(2,1)S(1)}, bf16[4,256,128]{2,1,0:T(8,128)(2,1)S(1)}, u32[]{:S(2)}, u32[]{:S(2)}) collective-permute-start(bf16[4,256,128]{2,1,0:T(8,128)(2,1)S(1)} %get-tuple-element.56), channel_id=1, source_target_pairs={{8,0},{10,2},{12,4},{14,6},{16,8},{18,10},{20,12},{22,14},{24,16},... | collective-permute-start | bytes 786440 | tf_op jit(solution)/shard_map/ppermute | solution.py:26
  52.0 1.6 %collective-permute-start.11 = (bf16[256,256]{1,0:T(8,128)(2,1)S(1)}, bf16[256,256]{1,0:T(8,128)(2,1)S(1)}, u32[]{:S(2)}, u32[]{:S(2)}) collective-permute-start(bf16[256,256]{1,0:T(8,128)(2,1)S(1)} %get-tuple-element.52), channel_id=1, source_target_pairs={{0,2},{2,0},{4,6},{6,4},{8,10},{10,8},{12,14},{14,12},{16,18},{18,... | collective-permute-start | bytes 393224 | tf_op jit(solution)/shard_map/ppermute | solution.py:31
  53.6 1.4 %collective-permute-start.12 = (bf16[256,256]{1,0:T(8,128)(2,1)S(1)}, bf16[256,256]{1,0:T(8,128)(2,1)S(1)}, u32[]{:S(2)}, u32[]{:S(2)}) collective-permute-start(bf16[256,256]{1,0:T(8,128)(2,1)S(1)} %get-tuple-element.53), channel_id=1, source_target_pairs={{0,4},{2,6},{4,0},{6,2},{8,12},{10,14},{12,8},{14,10},{16,20},{18,... | collective-permute-start | bytes 393224 | tf_op jit(solution)/shard_map/ppermute | solution.py:31
  55.0 0.6 collective-permute-start.13
  55.6 0.6 shard_map.88
  56.2 1.6 %collective-permute-start.19 = (bf16[256,128]{1,0:T(8,128)(2,1)S(1)}, bf16[256,128]{1,0:T(8,128)(2,1)S(1)}, u32[]{:S(2)}, u32[]{:S(2)}) collective-permute-start(bf16[256,128]{1,0:T(8,128)(2,1)S(1)} %get-tuple-element.64), channel_id=1, source_target_pairs={{0,2},{2,0},{4,6},{6,4},{8,10},{10,8},{12,14},{14,12},{16,18},{18,... | collective-permute-start | bytes 196616 | tf_op jit(solution)/shard_map/ppermute | solution.py:31
  57.7 2.6 %collective-permute-done.14.refs_1_ = bf16[4,256,128]{2,1,0:T(8,128)(2,1)S(1)} collective-permute-done((bf16[4,256,128]{2,1,0:T(8,128)(2,1)S(1)}, bf16[4,256,128]{2,1,0:T(8,128)(2,1)S(1)}, u32[]{:S(2)}, u32[]{:S(2)}) %collective-permute-start.14) | collective-permute-done | bytes 262176 | tf_op jit(solution)/shard_map/ppermute | solution.py:26
  60.3 1.8 %collective-permute-start.20 = (bf16[256,128]{1,0:T(8,128)(2,1)S(1)}, bf16[256,128]{1,0:T(8,128)(2,1)S(1)}, u32[]{:S(2)}, u32[]{:S(2)}) collective-permute-start(bf16[256,128]{1,0:T(8,128)(2,1)S(1)} %get-tuple-element.65), channel_id=1, source_target_pairs={{0,4},{2,6},{4,0},{6,2},{8,12},{10,14},{12,8},{14,10},{16,20},{18,... | collective-permute-start | bytes 196616 | tf_op jit(solution)/shard_map/ppermute | solution.py:31
  62.7 1.2 %collective-permute-start.21 = (bf16[256,128]{1,0:T(8,128)(2,1)S(1)}, bf16[256,128]{1,0:T(8,128)(2,1)S(1)}, u32[]{:S(2)}, u32[]{:S(2)}) collective-permute-start(bf16[256,128]{1,0:T(8,128)(2,1)S(1)} %get-tuple-element.66), channel_id=1, source_target_pairs={{0,6},{2,4},{4,2},{6,0},{8,14},{10,12},{12,10},{14,8},{16,22},{18,... | collective-permute-start | bytes 196616 | tf_op jit(solution)/shard_map/ppermute | solution.py:31
  64.5 1.8 %collective-permute-start.16 = (bf16[256,128]{1,0:T(8,128)(2,1)S(1)}, bf16[256,128]{1,0:T(8,128)(2,1)S(1)}, u32[]{:S(2)}, u32[]{:S(2)}) collective-permute-start(bf16[256,128]{1,0:T(8,128)(2,1)S(1)} %get-tuple-element.59), channel_id=1, source_target_pairs={{0,4},{2,6},{4,0},{6,2},{8,12},{10,14},{12,8},{14,10},{16,20},{18,... | collective-permute-start | bytes 196616 | tf_op jit(solution)/shard_map/ppermute | solution.py:31
  66.3 1.2 %collective-permute-start.17 = (bf16[256,128]{1,0:T(8,128)(2,1)S(1)}, bf16[256,128]{1,0:T(8,128)(2,1)S(1)}, u32[]{:S(2)}, u32[]{:S(2)}) collective-permute-start(bf16[256,128]{1,0:T(8,128)(2,1)S(1)} %get-tuple-element.60), channel_id=1, source_target_pairs={{0,6},{2,4},{4,2},{6,0},{8,14},{10,12},{12,10},{14,8},{16,22},{18,... | collective-permute-start | bytes 196616 | tf_op jit(solution)/shard_map/ppermute | solution.py:31
  67.5 1.4 %shard_map.85 = bf16[256,1024]{1,0:T(8,128)(2,1)} custom-call(s32[2]{0:T(128)S(1)} %copy-done.3, bf16[256,256]{1,0:T(8,128)(2,1)S(1)} %get-tuple-element.51.refs_0_, bf16[256,256]{1,0:T(8,128)(2,1)S(1)} %collective-permute-done.11.refs_1_, bf16[256,256]{1,0:T(8,128)(2,1)S(1)} %collective-permute-done.12.refs_2_, ...), custom_call_target="tpu_custom_call" | custom-call | bytes 1048584 | tf_op jit(solution)/shard_map/pallas_call | solution.py:38
  68.9 1.3 %shard_map.89 = bf16[256,512]{1,0:T(8,128)(2,1)} custom-call(s32[2]{0:T(128)S(1)} %copy-done.3, bf16[256,128]{1,0:T(8,128)(2,1)S(1)} %get-tuple-element.63.refs_0_, bf16[256,128]{1,0:T(8,128)(2,1)S(1)} %collective-permute-done.19.refs_1_, bf16[256,128]{1,0:T(8,128)(2,1)S(1)} %collective-permute-done.20.refs_2_, ...), custom_call_target="tpu_custom_call" | custom-call | bytes 524296 | tf_op jit(solution)/shard_map/pallas_call | solution.py:38
  70.2 1.3 %collective-permute-done.17.refs_3_ = bf16[256,128]{1,0:T(8,128)(2,1)S(1)} collective-permute-done((bf16[256,128]{1,0:T(8,128)(2,1)S(1)}, bf16[256,128]{1,0:T(8,128)(2,1)S(1)}, u32[]{:S(2)}, u32[]{:S(2)}) %collective-permute-start.17) | collective-permute-done | bytes 65568 | tf_op jit(solution)/shard_map/ppermute | solution.py:31
  71.4 1.3 %shard_map.87 = bf16[256,512]{1,0:T(8,128)(2,1)} custom-call(s32[2]{0:T(128)S(1)} %copy-done.3, bf16[256,128]{1,0:T(8,128)(2,1)S(1)} %get-tuple-element.57.refs_0_, bf16[256,128]{1,0:T(8,128)(2,1)S(1)} %collective-permute-done.15.refs_1_, bf16[256,128]{1,0:T(8,128)(2,1)S(1)} %collective-permute-done.16.refs_2_, ...), custom_call_target="tpu_custom_call" | custom-call | bytes 524296 | tf_op jit(solution)/shard_map/pallas_call | solution.py:38
  (35 shorter events, 4.3 us)
Async XLA Ops:
  3.8 10.7 %collective-permute-start = (bf16[256,256]{1,0:T(8,128)(2,1)}, bf16[256,256]{1,0:T(8,128)(2,1)S(1)}, u32[]{:S(2)}, u32[]{:S(2)}) collective-permute-start(bf16[256,256]{1,0:T(8,128)(2,1)} %get-tuple-element.36), channel_id=1, source_target_pairs={{0,2},{2,0},{4,6},{6,4},{8,10},{10,8},{12,14},{14,12},{16,18},{18,... | collective-permute-start | bytes 393224 | tf_op jit(solution)/shard_map/ppermute | solution.py:31
  6.8 8.0 %collective-permute-start.1 = (bf16[256,256]{1,0:T(8,128)(2,1)}, bf16[256,256]{1,0:T(8,128)(2,1)S(1)}, u32[]{:S(2)}, u32[]{:S(2)}) collective-permute-start(bf16[256,256]{1,0:T(8,128)(2,1)} %get-tuple-element.37), channel_id=1, source_target_pairs={{0,4},{2,6},{4,0},{6,2},{8,12},{10,14},{12,8},{14,10},{16,20},{18,... | collective-permute-start | bytes 393224 | tf_op jit(solution)/shard_map/ppermute | solution.py:31
  8.4 6.5 %collective-permute-start.2 = (bf16[256,256]{1,0:T(8,128)(2,1)}, bf16[256,256]{1,0:T(8,128)(2,1)S(1)}, u32[]{:S(2)}, u32[]{:S(2)}) collective-permute-start(bf16[256,256]{1,0:T(8,128)(2,1)} %get-tuple-element.38), channel_id=1, source_target_pairs={{0,6},{2,4},{4,2},{6,0},{8,14},{10,12},{12,10},{14,8},{16,22},{18,... | collective-permute-start | bytes 393224 | tf_op jit(solution)/shard_map/ppermute | solution.py:31
  8.4 6.5 %copy-start.2 = (bf16[256,256]{1,0:T(8,128)(2,1)S(1)}, bf16[256,256]{1,0:T(8,128)(2,1)}, u32[]{:S(2)}) copy-start(bf16[256,256]{1,0:T(8,128)(2,1)} %get-tuple-element.35.refs_0_) | copy-start | bytes 393220
  8.4 6.5 %copy-start.3 = (s32[2]{0:T(128)S(1)}, s32[2]{0:T(128)}, u32[]{:S(2)}) copy-start(s32[2]{0:T(128)} %pad_add_fusion.ids_ref) | copy-start | bytes 28
  8.4 10.7 %copy-start.1 = (bf16[256,1024]{1,0:T(8,128)(2,1)S(1)}, bf16[256,1024]{1,0:T(8,128)(2,1)}, u32[]{:S(2)}) copy-start(bf16[256,1024]{1,0:T(8,128)(2,1)} %q_ref.1) | copy-start | bytes 1572868
  14.4 14.9 %collective-permute-start.7 = (bf16[1024,256]{1,0:T(8,128)(2,1)}, bf16[1024,256]{1,0:T(8,128)(2,1)S(1)}, u32[]{:S(2)}, u32[]{:S(2)}) collective-permute-start(bf16[1024,256]{1,0:T(8,128)(2,1)} %shard_map.81), channel_id=1, source_target_pairs={{0,1},{1,0},{2,3},{3,2},{4,5},{5,4},{6,7},{7,6},{8,9},{9,8},{10,11... | collective-permute-start | bytes 1572872 | tf_op jit(solution)/shard_map/ppermute | solution.py:31
  15.4 19.1 %collective-permute-start.3 = (bf16[4,256,256]{2,1,0:T(8,128)(2,1)S(1)}, bf16[4,256,256]{2,1,0:T(8,128)(2,1)S(1)}, u32[]{:S(2)}, u32[]{:S(2)}) collective-permute-start(bf16[4,256,256]{2,1,0:T(8,128)(2,1)S(1)} %shard_map.77.refs_0_.own_ref), channel_id=1, source_target_pairs={{0,8},{2,10},{4,12},{6,14},{8,16},{10,18},{12,20},{14,22},{16,24},... | collective-permute-start | bytes 1572872 | tf_op jit(solution)/shard_map/ppermute | solution.py:26
  19.7 13.8 %collective-permute-start.4 = (bf16[256,256]{1,0:T(8,128)(2,1)S(1)}, bf16[256,256]{1,0:T(8,128)(2,1)S(1)}, u32[]{:S(2)}, u32[]{:S(2)}) collective-permute-start(bf16[256,256]{1,0:T(8,128)(2,1)S(1)} %get-tuple-element.40), channel_id=1, source_target_pairs={{0,2},{2,0},{4,6},{6,4},{8,10},{10,8},{12,14},{14,12},{16,18},{18,... | collective-permute-start | bytes 393224 | tf_op jit(solution)/shard_map/ppermute | solution.py:31
  21.3 12.8 %collective-permute-start.5 = (bf16[256,256]{1,0:T(8,128)(2,1)S(1)}, bf16[256,256]{1,0:T(8,128)(2,1)S(1)}, u32[]{:S(2)}, u32[]{:S(2)}) collective-permute-start(bf16[256,256]{1,0:T(8,128)(2,1)S(1)} %get-tuple-element.41), channel_id=1, source_target_pairs={{0,4},{2,6},{4,0},{6,2},{8,12},{10,14},{12,8},{14,10},{16,20},{18,... | collective-permute-start | bytes 393224 | tf_op jit(solution)/shard_map/ppermute | solution.py:31
  22.8 11.7 %collective-permute-start.6 = (bf16[256,256]{1,0:T(8,128)(2,1)S(1)}, bf16[256,256]{1,0:T(8,128)(2,1)S(1)}, u32[]{:S(2)}, u32[]{:S(2)}) collective-permute-start(bf16[256,256]{1,0:T(8,128)(2,1)S(1)} %get-tuple-element.42), channel_id=1, source_target_pairs={{0,6},{2,4},{4,2},{6,0},{8,14},{10,12},{12,10},{14,8},{16,22},{18,... | collective-permute-start | bytes 393224 | tf_op jit(solution)/shard_map/ppermute | solution.py:31
  29.3 1.0 %copy-start = (bf16[1024,256]{1,0:T(8,128)(2,1)S(1)}, bf16[1024,256]{1,0:T(8,128)(2,1)}, u32[]{:S(2)}) copy-start(bf16[1024,256]{1,0:T(8,128)(2,1)} %shard_map.80.refs_0_) | copy-start | bytes 1572868
  31.0 8.1 %collective-permute-start.10 = (bf16[256,256]{1,0:T(8,128)(2,1)S(1)}, bf16[256,256]{1,0:T(8,128)(2,1)S(1)}, u32[]{:S(2)}, u32[]{:S(2)}) collective-permute-start(bf16[256,256]{1,0:T(8,128)(2,1)S(1)} %get-tuple-element.49), channel_id=1, source_target_pairs={{0,6},{2,4},{4,2},{6,0},{8,14},{10,12},{12,10},{14,8},{16,22},{18,... | collective-permute-start | bytes 393224 | tf_op jit(solution)/shard_map/ppermute | solution.py:31
  33.5 6.1 %collective-permute-start.8 = (bf16[256,256]{1,0:T(8,128)(2,1)S(1)}, bf16[256,256]{1,0:T(8,128)(2,1)S(1)}, u32[]{:S(2)}, u32[]{:S(2)}) collective-permute-start(bf16[256,256]{1,0:T(8,128)(2,1)S(1)} %get-tuple-element.47), channel_id=1, source_target_pairs={{0,2},{2,0},{4,6},{6,4},{8,10},{10,8},{12,14},{14,12},{16,18},{18,... | collective-permute-start | bytes 393224 | tf_op jit(solution)/shard_map/ppermute | solution.py:31
  34.1 5.6 %collective-permute-start.9 = (bf16[256,256]{1,0:T(8,128)(2,1)S(1)}, bf16[256,256]{1,0:T(8,128)(2,1)S(1)}, u32[]{:S(2)}, u32[]{:S(2)}) collective-permute-start(bf16[256,256]{1,0:T(8,128)(2,1)S(1)} %get-tuple-element.48), channel_id=1, source_target_pairs={{0,4},{2,6},{4,0},{6,2},{8,12},{10,14},{12,8},{14,10},{16,20},{18,... | collective-permute-start | bytes 393224 | tf_op jit(solution)/shard_map/ppermute | solution.py:31
  42.4 13.2 %collective-permute-start.18 = (bf16[4,256,128]{2,1,0:T(8,128)(2,1)S(1)}, bf16[4,256,128]{2,1,0:T(8,128)(2,1)S(1)}, u32[]{:S(2)}, u32[]{:S(2)}) collective-permute-start(bf16[4,256,128]{2,1,0:T(8,128)(2,1)S(1)} %get-tuple-element.62), channel_id=1, source_target_pairs={{8,0},{10,2},{12,4},{14,6},{16,8},{18,10},{20,12},{22,14},{24,16},... | collective-permute-start | bytes 786440 | tf_op jit(solution)/shard_map/ppermute | solution.py:26
  50.7 9.6 %collective-permute-start.14 = (bf16[4,256,128]{2,1,0:T(8,128)(2,1)S(1)}, bf16[4,256,128]{2,1,0:T(8,128)(2,1)S(1)}, u32[]{:S(2)}, u32[]{:S(2)}) collective-permute-start(bf16[4,256,128]{2,1,0:T(8,128)(2,1)S(1)} %get-tuple-element.56), channel_id=1, source_target_pairs={{8,0},{10,2},{12,4},{14,6},{16,8},{18,10},{20,12},{22,14},{24,16},... | collective-permute-start | bytes 786440 | tf_op jit(solution)/shard_map/ppermute | solution.py:26
  52.0 10.7 %collective-permute-start.11 = (bf16[256,256]{1,0:T(8,128)(2,1)S(1)}, bf16[256,256]{1,0:T(8,128)(2,1)S(1)}, u32[]{:S(2)}, u32[]{:S(2)}) collective-permute-start(bf16[256,256]{1,0:T(8,128)(2,1)S(1)} %get-tuple-element.52), channel_id=1, source_target_pairs={{0,2},{2,0},{4,6},{6,4},{8,10},{10,8},{12,14},{14,12},{16,18},{18,... | collective-permute-start | bytes 393224 | tf_op jit(solution)/shard_map/ppermute | solution.py:31
  53.6 10.4 %collective-permute-start.12 = (bf16[256,256]{1,0:T(8,128)(2,1)S(1)}, bf16[256,256]{1,0:T(8,128)(2,1)S(1)}, u32[]{:S(2)}, u32[]{:S(2)}) collective-permute-start(bf16[256,256]{1,0:T(8,128)(2,1)S(1)} %get-tuple-element.53), channel_id=1, source_target_pairs={{0,4},{2,6},{4,0},{6,2},{8,12},{10,14},{12,8},{14,10},{16,20},{18,... | collective-permute-start | bytes 393224 | tf_op jit(solution)/shard_map/ppermute | solution.py:31
  55.0 9.5 %collective-permute-start.13 = (bf16[256,256]{1,0:T(8,128)(2,1)S(1)}, bf16[256,256]{1,0:T(8,128)(2,1)S(1)}, u32[]{:S(2)}, u32[]{:S(2)}) collective-permute-start(bf16[256,256]{1,0:T(8,128)(2,1)S(1)} %get-tuple-element.54), channel_id=1, source_target_pairs={{0,6},{2,4},{4,2},{6,0},{8,14},{10,12},{12,10},{14,8},{16,22},{18,... | collective-permute-start | bytes 393224 | tf_op jit(solution)/shard_map/ppermute | solution.py:31
  56.2 10.1 %collective-permute-start.19 = (bf16[256,128]{1,0:T(8,128)(2,1)S(1)}, bf16[256,128]{1,0:T(8,128)(2,1)S(1)}, u32[]{:S(2)}, u32[]{:S(2)}) collective-permute-start(bf16[256,128]{1,0:T(8,128)(2,1)S(1)} %get-tuple-element.64), channel_id=1, source_target_pairs={{0,2},{2,0},{4,6},{6,4},{8,10},{10,8},{12,14},{14,12},{16,18},{18,... | collective-permute-start | bytes 196616 | tf_op jit(solution)/shard_map/ppermute | solution.py:31
  60.3 8.5 %collective-permute-start.20 = (bf16[256,128]{1,0:T(8,128)(2,1)S(1)}, bf16[256,128]{1,0:T(8,128)(2,1)S(1)}, u32[]{:S(2)}, u32[]{:S(2)}) collective-permute-start(bf16[256,128]{1,0:T(8,128)(2,1)S(1)} %get-tuple-element.65), channel_id=1, source_target_pairs={{0,4},{2,6},{4,0},{6,2},{8,12},{10,14},{12,8},{14,10},{16,20},{18,... | collective-permute-start | bytes 196616 | tf_op jit(solution)/shard_map/ppermute | solution.py:31
  62.7 6.2 %collective-permute-start.21 = (bf16[256,128]{1,0:T(8,128)(2,1)S(1)}, bf16[256,128]{1,0:T(8,128)(2,1)S(1)}, u32[]{:S(2)}, u32[]{:S(2)}) collective-permute-start(bf16[256,128]{1,0:T(8,128)(2,1)S(1)} %get-tuple-element.66), channel_id=1, source_target_pairs={{0,6},{2,4},{4,2},{6,0},{8,14},{10,12},{12,10},{14,8},{16,22},{18,... | collective-permute-start | bytes 196616 | tf_op jit(solution)/shard_map/ppermute | solution.py:31
  64.0 6.2 %collective-permute-start.15 = (bf16[256,128]{1,0:T(8,128)(2,1)S(1)}, bf16[256,128]{1,0:T(8,128)(2,1)S(1)}, u32[]{:S(2)}, u32[]{:S(2)}) collective-permute-start(bf16[256,128]{1,0:T(8,128)(2,1)S(1)} %get-tuple-element.58), channel_id=1, source_target_pairs={{0,2},{2,0},{4,6},{6,4},{8,10},{10,8},{12,14},{14,12},{16,18},{18,... | collective-permute-start | bytes 196616 | tf_op jit(solution)/shard_map/ppermute | solution.py:31
  64.5 5.7 %collective-permute-start.16 = (bf16[256,128]{1,0:T(8,128)(2,1)S(1)}, bf16[256,128]{1,0:T(8,128)(2,1)S(1)}, u32[]{:S(2)}, u32[]{:S(2)}) collective-permute-start(bf16[256,128]{1,0:T(8,128)(2,1)S(1)} %get-tuple-element.59), channel_id=1, source_target_pairs={{0,4},{2,6},{4,0},{6,2},{8,12},{10,14},{12,8},{14,10},{16,20},{18,... | collective-permute-start | bytes 196616 | tf_op jit(solution)/shard_map/ppermute | solution.py:31
  66.3 5.2 %collective-permute-start.17 = (bf16[256,128]{1,0:T(8,128)(2,1)S(1)}, bf16[256,128]{1,0:T(8,128)(2,1)S(1)}, u32[]{:S(2)}, u32[]{:S(2)}) collective-permute-start(bf16[256,128]{1,0:T(8,128)(2,1)S(1)} %get-tuple-element.60), channel_id=1, source_target_pairs={{0,6},{2,4},{4,2},{6,0},{8,14},{10,12},{12,10},{14,8},{16,22},{18,... | collective-permute-start | bytes 196616 | tf_op jit(solution)/shard_map/ppermute | solution.py:31

commit v4 on v3

v4 whole, which is shorter than its diff:
```python
import functools

import jax
import jax.numpy as jnp
from jax import lax
from jax.experimental import pallas as pl
from jax.experimental.pallas import tpu as pltpu
from jax.sharding import PartitionSpec as P

HEAD_SIZE = 128
WINDOW_LENGTH = 1024
LOG2_E = 1.4426950408889634
AHEAD = 10**10

score_scale = 168.0 ** (-0.5)

VMEM = pl.BlockSpec(memory_space=pltpu.VMEM)
ANY = pl.BlockSpec(memory_space=pl.ANY)
SMEM = pl.BlockSpec(memory_space=pltpu.SMEM)
NT = (((1,), (1,)), ((), ()))
NN = (((1,), (0,)), ((), ()))


def shifted(value, axis, steps):
    count = lax.axis_size(axis)
    leading, last = (max(0, -steps), min(count, count - steps))
    return lax.ppermute(value, axis, [(source, source + steps) for source in range(leading, last)])


def swapped(value, axis, bits):
    count = lax.axis_size(axis)
    return lax.ppermute(value, axis, [(source, source ^ bits) for source in range(count)])


def call(body, outs, scratch=(), flops=0, exps=0, specs=None, vmem=32):
    def run(*args):
        moved = sum(a.size * a.dtype.itemsize for a in args)
        moved += sum(o.size * o.dtype.itemsize for o in outs)
        return pl.pallas_call(
            body,
            out_shape=tuple(outs),
            in_specs=specs or [SMEM if a.dtype == jnp.int32 else VMEM for a in args],
            out_specs=tuple(VMEM for _ in outs),
            scratch_shapes=list(scratch),
            compiler_params=pltpu.CompilerParams(vmem_limit_bytes=vmem * 1024 * 1024),
            cost_estimate=pl.CostEstimate(flops=flops, bytes_accessed=moved, transcendentals=exps),
        )(*args)

    return run


def spot(group):
    index = lax.axis_index("ctx")
    place = lax.rem(index, group)
    return place, index - place


def lanes(index, width):
    return pl.ds(pl.multiple_of(index * width, width), width)


def pack_kv(group, keys, values):
    tokens, width = keys.shape[0], keys.shape[1] // group

    def body(k_ref, v_ref, *refs):
        for r in range(group):
            member = spot(group)[0] ^ r
            refs[r][:, :width] = k_ref[:, lanes(member, width)]
            refs[r][:, width:] = v_ref[:, lanes(member, width)]

    outs = [jax.ShapeDtypeStruct((tokens, 2 * width), jnp.bfloat16)] * group
    return call(body, outs, flops=AHEAD)(keys, values)


def pack_queries(group, queries, before):
    tokens, width = queries.shape[0], queries.shape[1] // group

    def body(q_ref, before_ref, *out_refs):
        for r in range(group):
            out_refs[r][...] = q_ref[:, lanes(spot(group)[0] ^ r, width)]

    outs = [jax.ShapeDtypeStruct((tokens, width), jnp.bfloat16)] * group
    return call(body, outs, specs=[VMEM, ANY])(queries, before)


def order_pieces(group, pieces):
    def body(*refs):
        for r in range(group):
            refs[group][spot(group)[0] ^ r] = refs[r][...]

    outs = [jax.ShapeDtypeStruct((group,) + pieces[0].shape, jnp.bfloat16)]
    return call(body, outs)(*pieces)[0]


def head_product(parts, part, out_weight, layer_cotangent, before):
    tokens, depth = layer_cotangent.shape
    rows = out_weight.shape[0] // parts
    tile = min(rows, 512)

    def body(w_ref, c_ref, *refs):
        first = (lax.axis_index("tp") ^ part) * rows if parts > 1 else 0

        @pl.loop(0, rows // tile)
        def _(i):
            here = pl.ds(pl.multiple_of(i * tile, tile), tile)
            there = pl.ds(pl.multiple_of(first + i * tile, tile), tile)
            refs[-1][here, :] = lax.dot_general(
                w_ref[there, :], c_ref[...], NT, preferred_element_type=jnp.float32
            ).astype(jnp.bfloat16)

    outs = [jax.ShapeDtypeStruct((rows, tokens), jnp.bfloat16)]
    specs = [VMEM, VMEM] + [ANY] * len(before)
    return call(body, outs, flops=2 * rows * tokens * depth, specs=specs, vmem=16)(
        out_weight, layer_cotangent, *before
    )[0]


def pack_grads(group, terms):
    rows, tokens = terms[0].shape
    rows //= group

    def body(*refs):
        for r in range(group):
            there = lanes(spot(group)[0] ^ r, rows)
            total = refs[0][there, :]
            if len(terms) > 1:
                total = total.astype(jnp.float32)
                for term in refs[1 : len(terms)]:
                    total = total + term[there, :].astype(jnp.float32)
            refs[len(terms) + r][...] = total.astype(jnp.bfloat16)

    outs = [jax.ShapeDtypeStruct((rows, tokens), jnp.bfloat16)] * group
    return call(body, outs)(*terms)


class Shape:
    def __init__(self, group, steps, heads, per_head, tokens):
        self.group, self.steps, self.heads, self.per_head, self.tokens = group, steps, heads, per_head, tokens
        self.back = steps * group
        self.span = self.back + 1
        self.total = self.back + group
        self.wide = per_head * tokens
        self.width = heads * per_head * HEAD_SIZE
        self.kv_width = heads * HEAD_SIZE
        self.entries = group * heads * self.wide * self.span * tokens

    def block(self, own_ref, earlier_refs, number):
        if number < self.back:
            return earlier_refs[number // self.group].at[number % self.group]
        return own_ref.at[number - self.back]


def turn_queries(z, pieces):
    def body(*refs):
        for head in range(z.heads):
            for r in range(z.group):
                for j in range(z.per_head):
                    lower = (head * z.per_head + j) * HEAD_SIZE
                    refs[z.group][head, spot(z.group)[0] ^ r, :, j * z.tokens : (j + 1) * z.tokens] = refs[r][
                        :, lower : lower + HEAD_SIZE
                    ].T

    outs = [jax.ShapeDtypeStruct((z.heads, z.group, HEAD_SIZE, z.wide), jnp.bfloat16)]
    return call(body, outs)(*pieces)[0]


def softmax(z, kv_own, kv_earlier, qt):
    factor = score_scale * LOG2_E

    def body(*refs):
        own_ref, earlier_refs = refs[0], refs[1 : 1 + z.steps]
        qt_ref, e_ref, inverse_ref, k_all, s_all = refs[1 + z.steps :]
        first = spot(z.group)[1]
        key_id = lax.broadcasted_iota(jnp.int32, (z.tokens, z.wide), 0)
        query_id = lax.broadcasted_iota(jnp.int32, (z.tokens, z.wide), 1) & (z.tokens - 1)
        for head in range(z.heads):
            at_k = slice(head * HEAD_SIZE, (head + 1) * HEAD_SIZE)
            for number in range(z.total):
                k_all[number] = z.block(own_ref, earlier_refs, number)[:, at_k]

            @pl.loop(0, z.group)
            def _(b):
                qt = qt_ref[head, b]
                top = None
                for c in range(z.span):
                    s = lax.dot_general(k_all[b + c], qt, NN, preferred_element_type=jnp.float32)
                    if c == 0:
                        s = jnp.where(key_id > query_id, s, -jnp.inf)
                    if c == z.back:
                        s = jnp.where(key_id <= query_id, s, -jnp.inf)
                    s_all[c] = s
                    here = jnp.max(s, axis=0, keepdims=True)
                    if c < z.back:
                        here = jnp.where(first + b + c >= z.back, here, -jnp.inf)
                    top = here if top is None else jnp.maximum(top, here)
                norm = jnp.zeros((1, z.wide), jnp.float32)
                for c in range(z.span):
                    base = top
                    if c < z.back:
                        base = jnp.where(first + b + c >= z.back, top, jnp.inf)
                    e = jnp.exp2((s_all[c] - base) * factor)
                    norm = norm + jnp.sum(e, axis=0, keepdims=True)
                    e_ref[head, b, c] = e.astype(jnp.bfloat16)
                inverse_ref[head, b] = 1.0 / norm

    outs = [
        jax.ShapeDtypeStruct((z.heads, z.group, z.span, z.tokens, z.wide), jnp.bfloat16),
        jax.ShapeDtypeStruct((z.heads, z.group, 1, z.wide), jnp.float32),
    ]
    scratch = [
        pltpu.VMEM((z.total, z.tokens, HEAD_SIZE), jnp.bfloat16),
        pltpu.VMEM((z.span, z.tokens, z.wide), jnp.float32),
    ]
    return call(body, outs, scratch, flops=2 * z.entries * HEAD_SIZE, exps=z.entries)(
        kv_own, *kv_earlier, qt
    )


def value_terms(z, e, inverse, grads):
    def body(e_ref, inverse_ref, *refs):
        g_refs, (g_ref, own_ref), earlier_refs = (
            refs[: z.group],
            refs[z.group : z.group + 2],
            refs[z.group + 2 : z.group + 2 + z.steps],
        )
        dv_all = refs[-1]
        place = spot(z.group)[0]
        for head in range(z.heads):
            at = slice(head * HEAD_SIZE, (head + 1) * HEAD_SIZE)
            for r in range(z.group):
                for j in range(z.per_head):
                    lower = (head * z.per_head + j) * HEAD_SIZE
                    g_ref[head, place ^ r, :, j * z.tokens : (j + 1) * z.tokens] = g_refs[r][
                        lower : lower + HEAD_SIZE, :
                    ]
            dv_all[...] = jnp.zeros_like(dv_all)

            @pl.loop(0, z.group)
            def _(b):
                g = (g_ref[head, b].astype(jnp.float32) * inverse_ref[head, b]).astype(jnp.bfloat16)
                for c in range(z.span):
                    dv_all[b + c] += lax.dot_general(
                        e_ref[head, b, c], g, NT, preferred_element_type=jnp.float32
                    )

            for number in range(z.total):
                part = dv_all[number]
                z.block(own_ref, earlier_refs, number)[:, at] = part.astype(own_ref.dtype if number >= z.back else jnp.bfloat16)

    outs = [
        jax.ShapeDtypeStruct((z.heads, z.group, HEAD_SIZE, z.wide), jnp.bfloat16),
        jax.ShapeDtypeStruct((z.group, z.tokens, z.kv_width), jnp.float32),
    ]
    outs += [jax.ShapeDtypeStruct((z.group, z.tokens, z.kv_width), jnp.bfloat16)] * z.steps
    scratch = [pltpu.VMEM((z.total, z.tokens, HEAD_SIZE), jnp.float32)]
    results = call(body, outs, scratch, flops=2 * z.entries * HEAD_SIZE)(e, inverse, *grads)
    return results[0], results[1], results[2:]


def key_terms(z, e, inverse, qt, g, kv_own, kv_earlier):
    def body(e_ref, inverse_ref, qt_ref, g_ref, own_ref, *refs):
        earlier_refs, ds_ref = refs[: z.steps], refs[z.steps]
        dk_own, dk_earlier = refs[z.steps + 1], refs[z.steps + 2 : 2 * z.steps + 2]
        v_all, dk_all, dp_all = refs[2 * z.steps + 2 :]
        for head in range(z.heads):
            at = slice(head * HEAD_SIZE, (head + 1) * HEAD_SIZE)
            at_v = slice(z.kv_width + head * HEAD_SIZE, z.kv_width + (head + 1) * HEAD_SIZE)
            for number in range(z.total):
                v_all[number] = z.block(own_ref, earlier_refs, number)[:, at_v]
            dk_all[...] = jnp.zeros_like(dk_all)

            @pl.loop(0, z.group)
            def _(b):
                g = g_ref[head, b]
                inverse = inverse_ref[head, b]
                delta = jnp.zeros((1, z.wide), jnp.float32)
                for c in range(z.span):
                    dp = lax.dot_general(v_all[b + c], g, NN, preferred_element_type=jnp.float32)
                    delta = delta + jnp.sum(e_ref[head, b, c].astype(jnp.float32) * dp, axis=0, keepdims=True)
                    dp_all[c] = dp
                delta = delta * inverse
                q = (qt_ref[head, b].astype(jnp.float32) * inverse).astype(jnp.bfloat16)
                for c in range(z.span):
                    ds = (e_ref[head, b, c].astype(jnp.float32) * (dp_all[c] - delta)).astype(jnp.bfloat16)
                    ds_ref[head, b, c] = ds
                    dk_all[b + c] += lax.dot_general(ds, q, NT, preferred_element_type=jnp.float32)

            for number in range(z.total):
                part = dk_all[number] * score_scale
                z.block(dk_own, dk_earlier, number)[:, at] = part.astype(
                    dk_own.dtype if number >= z.back else jnp.bfloat16
                )

    outs = [jax.ShapeDtypeStruct(e.shape, jnp.bfloat16)]
    outs += [jax.ShapeDtypeStruct((z.group, z.tokens, z.kv_width), jnp.float32)]
    outs += [jax.ShapeDtypeStruct((z.group, z.tokens, z.kv_width), jnp.bfloat16)] * z.steps
    scratch = [
        pltpu.VMEM((z.total, z.tokens, HEAD_SIZE), jnp.bfloat16),
        pltpu.VMEM((z.total, z.tokens, HEAD_SIZE), jnp.float32),
        pltpu.VMEM((z.span, z.tokens, z.wide), jnp.float32),
    ]
    results = call(body, outs, scratch, flops=4 * z.entries * HEAD_SIZE)(
        e, inverse, qt, g, kv_own, *kv_earlier
    )
    return results[0], results[1], results[2:]


def query_terms(z, ds, inverse, kv_own, kv_earlier, dv_terms):
    def body(ds_ref, inverse_ref, own_ref, *refs):
        earlier_refs, term_refs, dv_ref = refs[: z.steps], refs[z.steps : 2 * z.steps + 1], refs[2 * z.steps + 1]
        dq_refs = refs[2 * z.steps + 2 : 2 * z.steps + 2 + z.group]
        kt_all, dq_all = refs[2 * z.steps + 2 + z.group :]
        dv = term_refs[0][...]
        for term in term_refs[1:]:
            dv = dv + term[...].astype(jnp.float32)
        dv_ref[...] = dv.astype(jnp.bfloat16)
        for head in range(z.heads):
            at = slice(head * HEAD_SIZE, (head + 1) * HEAD_SIZE)
            for number in range(z.total):
                kt_all[number] = z.block(own_ref, earlier_refs, number)[:, at].T

            @pl.loop(0, z.group)
            def _(b):
                dqt = jnp.zeros((HEAD_SIZE, z.wide), jnp.float32)
                for c in range(z.span):
                    dqt = dqt + lax.dot_general(
                        kt_all[b + c], ds_ref[head, b, c], NN, preferred_element_type=jnp.float32
                    )
                dqt = dqt * (inverse_ref[head, b] * score_scale)
                for j in range(z.per_head):
                    lower = (head * z.per_head + j) * HEAD_SIZE
                    dq_all[b, :, lower : lower + HEAD_SIZE] = (
                        dqt[:, j * z.tokens : (j + 1) * z.tokens].T.astype(jnp.bfloat16)
                    )

        for r in range(z.group):
            dq_refs[r][...] = dq_all[spot(z.group)[0] ^ r]

    outs = [jax.ShapeDtypeStruct((z.group, z.tokens, z.kv_width), jnp.bfloat16)]
    outs += [jax.ShapeDtypeStruct((z.tokens, z.width), jnp.bfloat16)] * z.group
    scratch = [
        pltpu.VMEM((z.total, HEAD_SIZE, z.tokens), jnp.bfloat16),
        pltpu.VMEM((z.group, z.tokens, z.width), jnp.bfloat16),
    ]
    results = call(body, outs, scratch, flops=2 * z.entries * HEAD_SIZE)(
        ds, inverse, kv_own, *kv_earlier, *dv_terms
    )
    return results[0], results[1:]


def pack_terms(group, sums):
    tokens, width = sums[0][0].shape[1:]
    flat = [term for terms in sums for term in terms]

    def body(*refs):
        for r in range(group):
            member = spot(group)[0] ^ r
            number = 0
            for column, terms in enumerate(sums):
                total = refs[number][member].astype(jnp.float32)
                for term in refs[number + 1 : number + len(terms)]:
                    total = total + term[member].astype(jnp.float32)
                refs[len(flat) + r][:, column * width : (column + 1) * width] = total.astype(jnp.bfloat16)
                number += len(terms)

    outs = [jax.ShapeDtypeStruct((tokens, len(sums) * width), jnp.bfloat16)] * group
    return call(body, outs)(*flat)


def unpack(group, pieces, widths):
    tokens = pieces[0].shape[0]

    def body(*refs):
        for r in range(group):
            lower = 0
            for number, width in enumerate(widths):
                refs[group + number][:, lanes(spot(group)[0] ^ r, width)] = refs[r][:, lower : lower + width]
                lower += width

    outs = [jax.ShapeDtypeStruct((tokens, group * width), jnp.bfloat16) for width in widths]
    return call(body, outs)(*pieces)


def local(layer_cotangent, out_weight, queries, keys, values):
    tokens = queries.shape[0]
    kv_heads = keys.shape[1] // HEAD_SIZE
    per_head = queries.shape[1] // keys.shape[1]
    count, tp_count = lax.axis_size("ctx"), lax.axis_size("tp")
    group = 1
    while (
        kv_heads % (2 * group) == 0
        and count % (2 * group) == 0
        and WINDOW_LENGTH % (2 * group * tokens) == 0
    ):
        group *= 2
    heads = kv_heads // group
    kv_width = heads * HEAD_SIZE
    back_groups = WINDOW_LENGTH // (group * tokens)
    def trade(sent):
        return [sent[0]] + [swapped(sent[r], "ctx", r) for r in range(1, group)]

    def returned(earlier):
        return [
            shifted(earlier[number], "ctx", -group * (back_groups - number)) for number in range(back_groups)
        ]

    sent = pack_kv(group, keys, values)
    kv_own = order_pieces(group, trade(sent))
    kv_earlier = [shifted(kv_own, "ctx", group * step) for step in range(back_groups, 0, -1)]
    z = Shape(group, back_groups, heads, per_head, tokens)
    query_sent = pack_queries(group, queries, sent[0])
    qt = turn_queries(z, trade(query_sent))
    if tp_count == 2:
        other = head_product(2, 1, out_weight, layer_cotangent, [query_sent[0]])
        terms = [head_product(2, 0, out_weight, layer_cotangent, [kv_own, other]), swapped(other, "tp", 1)]
    else:
        product = head_product(1, 0, out_weight, layer_cotangent, [query_sent[0]])
        terms = [lax.psum_scatter(product, "tp", scatter_dimension=0, tiled=True)]
    grads = trade(pack_grads(group, terms))
    e, inverse = softmax(z, kv_own, kv_earlier, qt)
    g, dv_own, dv_earlier = value_terms(z, e, inverse, grads)
    dv_terms = [dv_own] + returned(dv_earlier)
    ds, dk_own, dk_earlier = key_terms(z, e, inverse, qt, g, kv_own, kv_earlier)
    dk_terms = [dk_own] + returned(dk_earlier)
    dv, dq = query_terms(z, ds, inverse, kv_own, kv_earlier, dv_terms)
    dq = trade(dq)
    dkv = trade(pack_terms(group, [dk_terms, [dv]]))
    (query_grads,) = unpack(group, dq, [dq[0].shape[1]])
    key_gradients, value_gradients = unpack(group, dkv, [kv_width, kv_width])
    return (query_grads, key_gradients, value_gradients)


def solution(mesh):
    in_specs = (P("ctx", "tp"), P(None, "tp"), P("ctx", "tp"), P("ctx", "tp"), P("ctx", "tp"))
    out_specs = (P("ctx", "tp"), P("ctx", "tp"), P("ctx", "tp"))
    return jax.shard_map(local, mesh=mesh, in_specs=in_specs, out_specs=out_specs, check_vma=False)
```

time: 73 us -> 58.9 us (0.81)
  the two profiles are of different devices: /device:TPU:0 before, /device:TPU:24 now
where the time goes in v4:
time: 58.9 us; the launch traced here: 58.3 us
  starting transfers between devices  25.2 us (43%)
  Pallas kernels  19.7 us (33%)
  waiting for transfers between devices  9.84 us (17%)
  local copies, waits for them, and re-layouts  2.74 us (5%)
  between operations  0.81 us (1%)
    pallas_call x14, Pallas kernels, run(): pl.pallas_call(body, out_shape=tuple(outs), in_specs=specs or [SMEM if a....  19.7 us
    ppermute x16, starting transfers between devices, swapped(): lax.ppermute(value, axis, [(source, source ^ bits) for source in range(co...  19.2 us
    ppermute x16, waiting for transfers between devices, swapped(): lax.ppermute(value, axis, [(source, source ^ bits) for source in range(co...  7.48 us
    ppermute x3, starting transfers between devices, shifted(): lax.ppermute(value, axis, [(source, source + steps) for source in range(l...  6.03 us
    unnamed x10, local copies, waits for them, and re-layouts  2.74 us
    ppermute x3, waiting for transfers between devices, shifted(): lax.ppermute(value, axis, [(source, source + steps) for source in range(l...  2.36 us
  transfers between devices with their start and end apart: 19, of which 6 were waited for; matrix products, arithmetic and copies ran while one was open for 0% of the time, Pallas kernels for 28%

profile of v4, /device:TPU:24, one launch (start us, length us, event | category | flops | bytes accessed | tf_op | source)
XLA Modules:
  0.0 58.3 jit_solution(9450934952764642590)
XLA Ops:
  0.7 1.0 %copy-done.3 = bf16[256,512]{1,0:T(8,128)(2,1)S(1)} copy-done((bf16[256,512]{1,0:T(8,128)(2,1)S(1)}, bf16[256,512]{1,0:T(8,128)(2,1)}, u32[]{:S(2)}) %copy-start.3) | copy-done | bytes 262168
  1.7 0.9 %copy-done.4 = bf16[256,512]{1,0:T(8,128)(2,1)S(1)} copy-done((bf16[256,512]{1,0:T(8,128)(2,1)S(1)}, bf16[256,512]{1,0:T(8,128)(2,1)}, u32[]{:S(2)}) %copy-start.4) | copy-done | bytes 262168
  2.7 1.6 %collective-permute-start = (bf16[256,256]{1,0:T(8,128)(2,1)S(1)}, bf16[256,256]{1,0:T(8,128)(2,1)S(1)}, u32[]{:S(2)}, u32[]{:S(2)}) collective-permute-start(bf16[256,256]{1,0:T(8,128)(2,1)S(1)} %get-tuple-element.35), channel_id=1, source_target_pairs={{0,2},{2,0},{4,6},{6,4},{8,10},{10,8},{12,14},{14,12},{16,18},{18,... | collective-permute-start | bytes 393224 | tf_op jit(solution)/shard_map/ppermute | solution.py:32
  4.3 1.5 %collective-permute-start.1 = (bf16[256,256]{1,0:T(8,128)(2,1)S(1)}, bf16[256,256]{1,0:T(8,128)(2,1)S(1)}, u32[]{:S(2)}, u32[]{:S(2)}) collective-permute-start(bf16[256,256]{1,0:T(8,128)(2,1)S(1)} %get-tuple-element.36), channel_id=1, source_target_pairs={{0,4},{2,6},{4,0},{6,2},{8,12},{10,14},{12,8},{14,10},{16,20},{18,... | collective-permute-start | bytes 393224 | tf_op jit(solution)/shard_map/ppermute | solution.py:32
  7.1 1.9 %shard_map.81.refs_1_ = bf16[1024,256]{1,0:T(8,128)(2,1)S(1)} custom-call(bf16[2048,2688]{1,0:T(8,128)(2,1)S(1)} %copy-done, bf16[256,2688]{1,0:T(8,128)(2,1)S(1)} %copy-done.1, bf16[256,256]{1,0:T(8,128)(2,1)S(1)} %get-tuple-element.38.refs_0_), custom_call_target="tpu_custom_call" | custom-call | flops 1409286144 | bytes 13041664 | tf_op jit(solution)/shard_map/pallas_call | solution.py:39
  9.1 2.9 %collective-permute-done.1.refs_2_ = bf16[256,256]{1,0:T(8,128)(2,1)S(1)} collective-permute-done((bf16[256,256]{1,0:T(8,128)(2,1)S(1)}, bf16[256,256]{1,0:T(8,128)(2,1)S(1)}, u32[]{:S(2)}, u32[]{:S(2)}) %collective-permute-start.1) | collective-permute-done | bytes 131104 | tf_op jit(solution)/shard_map/ppermute | solution.py:32
  12.1 1.3 %collective-permute-start.3 = (bf16[4,256,256]{2,1,0:T(8,128)(2,1)S(1)}, bf16[4,256,256]{2,1,0:T(8,128)(2,1)S(1)}, u32[]{:S(2)}, u32[]{:S(2)}) collective-permute-start(bf16[4,256,256]{2,1,0:T(8,128)(2,1)S(1)} %shard_map.77.refs_0_.own_ref), channel_id=1, source_target_pairs={{0,8},{2,10},{4,12},{6,14},{8,16},{10,18},{12,20},{14,22},{16,24},... | collective-permute-start | bytes 1572872 | tf_op jit(solution)/shard_map/ppermute | solution.py:27
  13.4 1.3 %collective-permute-start.4 = (bf16[256,256]{1,0:T(8,128)(2,1)S(1)}, bf16[256,256]{1,0:T(8,128)(2,1)S(1)}, u32[]{:S(2)}, u32[]{:S(2)}) collective-permute-start(bf16[256,256]{1,0:T(8,128)(2,1)S(1)} %get-tuple-element.39), channel_id=1, source_target_pairs={{0,2},{2,0},{4,6},{6,4},{8,10},{10,8},{12,14},{14,12},{16,18},{18,... | collective-permute-start | bytes 393224 | tf_op jit(solution)/shard_map/ppermute | solution.py:32
  14.7 0.8 %collective-permute-start.5 = (bf16[256,256]{1,0:T(8,128)(2,1)S(1)}, bf16[256,256]{1,0:T(8,128)(2,1)S(1)}, u32[]{:S(2)}, u32[]{:S(2)}) collective-permute-start(bf16[256,256]{1,0:T(8,128)(2,1)S(1)} %get-tuple-element.40), channel_id=1, source_target_pairs={{0,4},{2,6},{4,0},{6,2},{8,12},{10,14},{12,8},{14,10},{16,20},{18,... | collective-permute-start | bytes 393224 | tf_op jit(solution)/shard_map/ppermute | solution.py:32
  15.5 1.4 %collective-permute-start.6 = (bf16[256,256]{1,0:T(8,128)(2,1)S(1)}, bf16[256,256]{1,0:T(8,128)(2,1)S(1)}, u32[]{:S(2)}, u32[]{:S(2)}) collective-permute-start(bf16[256,256]{1,0:T(8,128)(2,1)S(1)} %get-tuple-element.41), channel_id=1, source_target_pairs={{0,6},{2,4},{4,2},{6,0},{8,14},{10,12},{12,10},{14,8},{16,22},{18,... | collective-permute-start | bytes 393224 | tf_op jit(solution)/shard_map/ppermute | solution.py:32
  16.9 1.9 %shard_map.82.refs_0_ = bf16[1024,256]{1,0:T(8,128)(2,1)S(1)} custom-call(bf16[2048,2688]{1,0:T(8,128)(2,1)S(1)} %copy-done, bf16[256,2688]{1,0:T(8,128)(2,1)S(1)} %copy-done.1, bf16[4,256,256]{2,1,0:T(8,128)(2,1)S(1)} %shard_map.77.refs_0_.own_ref, bf16[1024,256]{1,0:T(8,128)(2,1)S(1)} %shard_map.81.refs_1_), custom_call_target="tpu_custom_call" | custom-call | flops 1409286144 | bytes 13959168 | tf_op jit(solution)/shard_map/pallas_call | solution.py:39
  19.0 1.3 %collective-permute-start.8 = (bf16[256,256]{1,0:T(8,128)(2,1)S(1)}, bf16[256,256]{1,0:T(8,128)(2,1)S(1)}, u32[]{:S(2)}, u32[]{:S(2)}) collective-permute-start(bf16[256,256]{1,0:T(8,128)(2,1)S(1)} %get-tuple-element.45), channel_id=1, source_target_pairs={{0,2},{2,0},{4,6},{6,4},{8,10},{10,8},{12,14},{14,12},{16,18},{18,... | collective-permute-start | bytes 393224 | tf_op jit(solution)/shard_map/ppermute | solution.py:32
  20.3 0.8 %collective-permute-start.9 = (bf16[256,256]{1,0:T(8,128)(2,1)S(1)}, bf16[256,256]{1,0:T(8,128)(2,1)S(1)}, u32[]{:S(2)}, u32[]{:S(2)}) collective-permute-start(bf16[256,256]{1,0:T(8,128)(2,1)S(1)} %get-tuple-element.46), channel_id=1, source_target_pairs={{0,4},{2,6},{4,0},{6,2},{8,12},{10,14},{12,8},{14,10},{16,20},{18,... | collective-permute-start | bytes 393224 | tf_op jit(solution)/shard_map/ppermute | solution.py:32
  21.1 2.7 %collective-permute-start.10 = (bf16[256,256]{1,0:T(8,128)(2,1)S(1)}, bf16[256,256]{1,0:T(8,128)(2,1)S(1)}, u32[]{:S(2)}, u32[]{:S(2)}) collective-permute-start(bf16[256,256]{1,0:T(8,128)(2,1)S(1)} %get-tuple-element.47), channel_id=1, source_target_pairs={{0,6},{2,4},{4,2},{6,0},{8,14},{10,12},{12,10},{14,8},{16,22},{18,... | collective-permute-start | bytes 393224 | tf_op jit(solution)/shard_map/ppermute | solution.py:32
  24.0 2.4 %collective-permute-done.3.refs_1_.refs_0_ = bf16[4,256,256]{2,1,0:T(8,128)(2,1)S(1)} collective-permute-done((bf16[4,256,256]{2,1,0:T(8,128)(2,1)S(1)}, bf16[4,256,256]{2,1,0:T(8,128)(2,1)S(1)}, u32[]{:S(2)}, u32[]{:S(2)}) %collective-permute-start.3) | collective-permute-done | bytes 524320 | tf_op jit(solution)/shard_map/ppermute | solution.py:27
  26.4 3.8 %shard_map.80 = (bf16[1,4,5,256,512]{4,3,2,1,0:T(8,128)(2,1)S(1)}, f32[1,4,1,512]{3,2,1,0:T(1,128)S(1)}) custom-call(bf16[4,256,256]{2,1,0:T(8,128)(2,1)S(1)} %shard_map.77.refs_0_.own_ref, bf16[4,256,256]{2,1,0:T(8,128)(2,1)S(1)} %collective-permute-done.3.refs_1_.refs_0_, bf16[1,4,128,512]{3,2,1,0:T(8,128)(2,1)S(1)} %shard_map.79.refs_2_.qt_ref), custom_call_target="tpu_custom_call" | custom-call | flops 671088640 | bytes 6823936 | tf_op jit(solution)/shard_map/pallas_call | solution.py:39
  30.2 2.2 %shard_map.84 = (bf16[1,4,128,512]{3,2,1,0:T(8,128)(2,1)S(1)}, f32[4,256,128]{2,1,0:T(8,128)S(1)}, bf16[4,256,128]{2,1,0:T(8,128)(2,1)S(1)}) custom-call(bf16[1,4,5,256,512]{4,3,2,1,0:T(8,128)(2,1)S(1)} %get-tuple-element.42.e_ref, f32[1,4,1,512]{3,2,1,0:T(1,128)S(1)} %get-tuple-element.43.inverse_ref, bf16[256,256]{1,0:T(8,128)(2,1)S(1)} %get-tuple-element.44.refs_0_, ...), custom_call_target="tpu_custom_call" | custom-call | flops 671088640 | bytes 7086080 | tf_op jit(solution)/shard_map/pallas_call | solution.py:39
  32.4 2.4 %collective-permute-start.11 = (bf16[4,256,128]{2,1,0:T(8,128)(2,1)S(1)}, bf16[4,256,128]{2,1,0:T(8,128)(2,1)S(1)}, u32[]{:S(2)}, u32[]{:S(2)}) collective-permute-start(bf16[4,256,128]{2,1,0:T(8,128)(2,1)S(1)} %get-tuple-element.51), channel_id=1, source_target_pairs={{8,0},{10,2},{12,4},{14,6},{16,8},{18,10},{20,12},{22,14},{24,16},... | collective-permute-start | bytes 786440 | tf_op jit(solution)/shard_map/ppermute | solution.py:27
  34.8 5.6 %shard_map.85 = (bf16[1,4,5,256,512]{4,3,2,1,0:T(8,128)(2,1)S(1)}, f32[4,256,128]{2,1,0:T(8,128)S(1)}, bf16[4,256,128]{2,1,0:T(8,128)(2,1)S(1)}) custom-call(bf16[1,4,5,256,512]{4,3,2,1,0:T(8,128)(2,1)S(1)} %get-tuple-element.42.e_ref, f32[1,4,1,512]{3,2,1,0:T(1,128)S(1)} %get-tuple-element.43.inverse_ref, ...), custom_call_target="tpu_custom_call" | custom-call | flops 1342177280 | bytes 13377536 | tf_op jit(solution)/shard_map/pallas_call | solution.py:39
  40.4 2.4 %collective-permute-start.15 = (bf16[4,256,128]{2,1,0:T(8,128)(2,1)S(1)}, bf16[4,256,128]{2,1,0:T(8,128)(2,1)S(1)}, u32[]{:S(2)}, u32[]{:S(2)}) collective-permute-start(bf16[4,256,128]{2,1,0:T(8,128)(2,1)S(1)} %get-tuple-element.57), channel_id=1, source_target_pairs={{8,0},{10,2},{12,4},{14,6},{16,8},{18,10},{20,12},{22,14},{24,16},... | collective-permute-start | bytes 786440 | tf_op jit(solution)/shard_map/ppermute | solution.py:27
  42.8 1.9 %shard_map.86 = (bf16[4,256,128]{2,1,0:T(8,128)(2,1)S(1)}, bf16[256,256]{1,0:T(8,128)(2,1)S(1)}, bf16[256,256]{1,0:T(8,128)(2,1)S(1)}, bf16[256,256]{1,0:T(8,128)(2,1)S(1)}, bf16[256,256]{1,0:T(8,128)(2,1)S(1)}) custom-call(bf16[1,4,5,256,512]{4,3,2,1,0:T(8,128)(2,1)S(1)} %get-tuple-element.49.ds_ref, f32[1,4,1,512]{3,2,1,0:T(1,128)S(1)} %get-tuple-element.43.inverse_ref, ...), custom_call_target="tpu_custom_call" | custom-call | flops 671088640 | bytes 7872512 | tf_op jit(solution)/shard_map/pallas_call | solution.py:39
  44.7 1.7 %collective-permute-start.12 = (bf16[256,256]{1,0:T(8,128)(2,1)S(1)}, bf16[256,256]{1,0:T(8,128)(2,1)S(1)}, u32[]{:S(2)}, u32[]{:S(2)}) collective-permute-start(bf16[256,256]{1,0:T(8,128)(2,1)S(1)} %get-tuple-element.53), channel_id=1, source_target_pairs={{0,2},{2,0},{4,6},{6,4},{8,10},{10,8},{12,14},{14,12},{16,18},{18,... | collective-permute-start | bytes 393224 | tf_op jit(solution)/shard_map/ppermute | solution.py:32
  46.4 0.5 collective-permute-start.13
  46.9 1.3 %collective-permute-start.14 = (bf16[256,256]{1,0:T(8,128)(2,1)S(1)}, bf16[256,256]{1,0:T(8,128)(2,1)S(1)}, u32[]{:S(2)}, u32[]{:S(2)}) collective-permute-start(bf16[256,256]{1,0:T(8,128)(2,1)S(1)} %get-tuple-element.55), channel_id=1, source_target_pairs={{0,6},{2,4},{4,2},{6,0},{8,14},{10,12},{12,10},{14,8},{16,22},{18,... | collective-permute-start | bytes 393224 | tf_op jit(solution)/shard_map/ppermute | solution.py:32
  48.4 1.7 %collective-permute-start.16 = (bf16[256,256]{1,0:T(8,128)(2,1)S(1)}, bf16[256,256]{1,0:T(8,128)(2,1)S(1)}, u32[]{:S(2)}, u32[]{:S(2)}) collective-permute-start(bf16[256,256]{1,0:T(8,128)(2,1)S(1)} %get-tuple-element.60), channel_id=1, source_target_pairs={{0,2},{2,0},{4,6},{6,4},{8,10},{10,8},{12,14},{14,12},{16,18},{18,... | collective-permute-start | bytes 393224 | tf_op jit(solution)/shard_map/ppermute | solution.py:32
  50.1 0.5 collective-permute-start.17
  50.6 0.6 collective-permute-done.12.refs_1_
  51.1 1.5 %collective-permute-start.18 = (bf16[256,256]{1,0:T(8,128)(2,1)S(1)}, bf16[256,256]{1,0:T(8,128)(2,1)S(1)}, u32[]{:S(2)}, u32[]{:S(2)}) collective-permute-start(bf16[256,256]{1,0:T(8,128)(2,1)S(1)} %get-tuple-element.62), channel_id=1, source_target_pairs={{0,6},{2,4},{4,2},{6,0},{8,14},{10,12},{12,10},{14,8},{16,22},{18,... | collective-permute-start | bytes 393224 | tf_op jit(solution)/shard_map/ppermute | solution.py:32
  52.6 2.0 %collective-permute-done.13.refs_2_ = bf16[256,256]{1,0:T(8,128)(2,1)S(1)} collective-permute-done((bf16[256,256]{1,0:T(8,128)(2,1)S(1)}, bf16[256,256]{1,0:T(8,128)(2,1)S(1)}, u32[]{:S(2)}, u32[]{:S(2)}) %collective-permute-start.13) | collective-permute-done | bytes 131104 | tf_op jit(solution)/shard_map/ppermute | solution.py:32
  54.6 0.9 %shard_map.87 = bf16[256,1024]{1,0:T(8,128)(2,1)} custom-call(bf16[256,256]{1,0:T(8,128)(2,1)S(1)} %get-tuple-element.52.refs_0_, bf16[256,256]{1,0:T(8,128)(2,1)S(1)} %collective-permute-done.12.refs_1_, bf16[256,256]{1,0:T(8,128)(2,1)S(1)} %collective-permute-done.13.refs_2_, bf16[256,256]{1,0:T(8,128)(2,1)S(1)} %collective-permute-done.14.refs_3_), custom_call_target="tpu_custom_call" | custom-call | bytes 1048576 | tf_op jit(solution)/shard_map/pallas_call | solution.py:39
  55.8 1.6 %collective-permute-done.17.refs_2_ = bf16[256,256]{1,0:T(8,128)(2,1)S(1)} collective-permute-done((bf16[256,256]{1,0:T(8,128)(2,1)S(1)}, bf16[256,256]{1,0:T(8,128)(2,1)S(1)}, u32[]{:S(2)}, u32[]{:S(2)}) %collective-permute-start.17) | collective-permute-done | bytes 131104 | tf_op jit(solution)/shard_map/ppermute | solution.py:32
  57.4 0.9 %shard_map.89 = (bf16[256,512]{1,0:T(8,128)(2,1)}, bf16[256,512]{1,0:T(8,128)(2,1)}) custom-call(bf16[256,256]{1,0:T(8,128)(2,1)S(1)} %get-tuple-element.59.refs_0_, bf16[256,256]{1,0:T(8,128)(2,1)S(1)} %collective-permute-done.16.refs_1_, bf16[256,256]{1,0:T(8,128)(2,1)S(1)} %collective-permute-done.17.refs_2_, ...), custom_call_target="tpu_custom_call" | custom-call | bytes 1048576 | tf_op jit(solution)/shard_map/pallas_call | solution.py:39
  (30 shorter events, 2.3 us)
Async XLA Ops:
  0.6 5.6 %copy-start.2 = (bf16[256,1024]{1,0:T(8,128)(2,1)S(1)}, bf16[256,1024]{1,0:T(8,128)(2,1)}, u32[]{:S(2)}) copy-start(bf16[256,1024]{1,0:T(8,128)(2,1)} %q_ref.1) | copy-start | bytes 1572868
  0.6 1.0 %copy-start.3 = (bf16[256,512]{1,0:T(8,128)(2,1)S(1)}, bf16[256,512]{1,0:T(8,128)(2,1)}, u32[]{:S(2)}) copy-start(bf16[256,512]{1,0:T(8,128)(2,1)} %k_ref.1) | copy-start | bytes 786436
  1.6 0.9 %copy-start.4 = (bf16[256,512]{1,0:T(8,128)(2,1)S(1)}, bf16[256,512]{1,0:T(8,128)(2,1)}, u32[]{:S(2)}) copy-start(bf16[256,512]{1,0:T(8,128)(2,1)} %v_ref.1) | copy-start | bytes 786436
  2.6 4.1 %copy-start = (bf16[2048,2688]{1,0:T(8,128)(2,1)S(1)}, bf16[2048,2688]{1,0:T(8,128)(2,1)}, u32[]{:S(2)}) copy-start(bf16[2048,2688]{1,0:T(8,128)(2,1)} %w_ref.3) | copy-start | bytes 33030148
  2.6 4.5 %copy-start.1 = (bf16[256,2688]{1,0:T(8,128)(2,1)S(1)}, bf16[256,2688]{1,0:T(8,128)(2,1)}, u32[]{:S(2)}) copy-start(bf16[256,2688]{1,0:T(8,128)(2,1)} %c_ref.3) | copy-start | bytes 4128772
  2.7 6.4 %collective-permute-start = (bf16[256,256]{1,0:T(8,128)(2,1)S(1)}, bf16[256,256]{1,0:T(8,128)(2,1)S(1)}, u32[]{:S(2)}, u32[]{:S(2)}) collective-permute-start(bf16[256,256]{1,0:T(8,128)(2,1)S(1)} %get-tuple-element.35), channel_id=1, source_target_pairs={{0,2},{2,0},{4,6},{6,4},{8,10},{10,8},{12,14},{14,12},{16,18},{18,... | collective-permute-start | bytes 393224 | tf_op jit(solution)/shard_map/ppermute | solution.py:32
  4.3 7.8 %collective-permute-start.1 = (bf16[256,256]{1,0:T(8,128)(2,1)S(1)}, bf16[256,256]{1,0:T(8,128)(2,1)S(1)}, u32[]{:S(2)}, u32[]{:S(2)}) collective-permute-start(bf16[256,256]{1,0:T(8,128)(2,1)S(1)} %get-tuple-element.36), channel_id=1, source_target_pairs={{0,4},{2,6},{4,0},{6,2},{8,12},{10,14},{12,8},{14,10},{16,20},{18,... | collective-permute-start | bytes 393224 | tf_op jit(solution)/shard_map/ppermute | solution.py:32
  5.8 6.3 %collective-permute-start.2 = (bf16[256,256]{1,0:T(8,128)(2,1)S(1)}, bf16[256,256]{1,0:T(8,128)(2,1)S(1)}, u32[]{:S(2)}, u32[]{:S(2)}) collective-permute-start(bf16[256,256]{1,0:T(8,128)(2,1)S(1)} %get-tuple-element.37), channel_id=1, source_target_pairs={{0,6},{2,4},{4,2},{6,0},{8,14},{10,12},{12,10},{14,8},{16,22},{18,... | collective-permute-start | bytes 393224 | tf_op jit(solution)/shard_map/ppermute | solution.py:32
  9.0 9.8 %collective-permute-start.7 = (bf16[1024,256]{1,0:T(8,128)(2,1)S(1)}, bf16[1024,256]{1,0:T(8,128)(2,1)S(1)}, u32[]{:S(2)}, u32[]{:S(2)}) collective-permute-start(bf16[1024,256]{1,0:T(8,128)(2,1)S(1)} %shard_map.81.refs_1_), channel_id=1, source_target_pairs={{0,1},{1,0},{2,3},{3,2},{4,5},{5,4},{6,7},{7,6},{8,9},{9,8},{10,11... | collective-permute-start | bytes 1572872 | tf_op jit(solution)/shard_map/ppermute | solution.py:32
  12.1 14.3 %collective-permute-start.3 = (bf16[4,256,256]{2,1,0:T(8,128)(2,1)S(1)}, bf16[4,256,256]{2,1,0:T(8,128)(2,1)S(1)}, u32[]{:S(2)}, u32[]{:S(2)}) collective-permute-start(bf16[4,256,256]{2,1,0:T(8,128)(2,1)S(1)} %shard_map.77.refs_0_.own_ref), channel_id=1, source_target_pairs={{0,8},{2,10},{4,12},{6,14},{8,16},{10,18},{12,20},{14,22},{16,24},... | collective-permute-start | bytes 1572872 | tf_op jit(solution)/shard_map/ppermute | solution.py:27
  13.4 6.9 %collective-permute-start.4 = (bf16[256,256]{1,0:T(8,128)(2,1)S(1)}, bf16[256,256]{1,0:T(8,128)(2,1)S(1)}, u32[]{:S(2)}, u32[]{:S(2)}) collective-permute-start(bf16[256,256]{1,0:T(8,128)(2,1)S(1)} %get-tuple-element.39), channel_id=1, source_target_pairs={{0,2},{2,0},{4,6},{6,4},{8,10},{10,8},{12,14},{14,12},{16,18},{18,... | collective-permute-start | bytes 393224 | tf_op jit(solution)/shard_map/ppermute | solution.py:32
  14.7 6.4 %collective-permute-start.5 = (bf16[256,256]{1,0:T(8,128)(2,1)S(1)}, bf16[256,256]{1,0:T(8,128)(2,1)S(1)}, u32[]{:S(2)}, u32[]{:S(2)}) collective-permute-start(bf16[256,256]{1,0:T(8,128)(2,1)S(1)} %get-tuple-element.40), channel_id=1, source_target_pairs={{0,4},{2,6},{4,0},{6,2},{8,12},{10,14},{12,8},{14,10},{16,20},{18,... | collective-permute-start | bytes 393224 | tf_op jit(solution)/shard_map/ppermute | solution.py:32
  15.5 8.3 %collective-permute-start.6 = (bf16[256,256]{1,0:T(8,128)(2,1)S(1)}, bf16[256,256]{1,0:T(8,128)(2,1)S(1)}, u32[]{:S(2)}, u32[]{:S(2)}) collective-permute-start(bf16[256,256]{1,0:T(8,128)(2,1)S(1)} %get-tuple-element.41), channel_id=1, source_target_pairs={{0,6},{2,4},{4,2},{6,0},{8,14},{10,12},{12,10},{14,8},{16,22},{18,... | collective-permute-start | bytes 393224 | tf_op jit(solution)/shard_map/ppermute | solution.py:32
  19.0 11.2 %collective-permute-start.8 = (bf16[256,256]{1,0:T(8,128)(2,1)S(1)}, bf16[256,256]{1,0:T(8,128)(2,1)S(1)}, u32[]{:S(2)}, u32[]{:S(2)}) collective-permute-start(bf16[256,256]{1,0:T(8,128)(2,1)S(1)} %get-tuple-element.45), channel_id=1, source_target_pairs={{0,2},{2,0},{4,6},{6,4},{8,10},{10,8},{12,14},{14,12},{16,18},{18,... | collective-permute-start | bytes 393224 | tf_op jit(solution)/shard_map/ppermute | solution.py:32
  20.3 9.9 %collective-permute-start.9 = (bf16[256,256]{1,0:T(8,128)(2,1)S(1)}, bf16[256,256]{1,0:T(8,128)(2,1)S(1)}, u32[]{:S(2)}, u32[]{:S(2)}) collective-permute-start(bf16[256,256]{1,0:T(8,128)(2,1)S(1)} %get-tuple-element.46), channel_id=1, source_target_pairs={{0,4},{2,6},{4,0},{6,2},{8,12},{10,14},{12,8},{14,10},{16,20},{18,... | collective-permute-start | bytes 393224 | tf_op jit(solution)/shard_map/ppermute | solution.py:32
  21.1 9.1 %collective-permute-start.10 = (bf16[256,256]{1,0:T(8,128)(2,1)S(1)}, bf16[256,256]{1,0:T(8,128)(2,1)S(1)}, u32[]{:S(2)}, u32[]{:S(2)}) collective-permute-start(bf16[256,256]{1,0:T(8,128)(2,1)S(1)} %get-tuple-element.47), channel_id=1, source_target_pairs={{0,6},{2,4},{4,2},{6,0},{8,14},{10,12},{12,10},{14,8},{16,22},{18,... | collective-permute-start | bytes 393224 | tf_op jit(solution)/shard_map/ppermute | solution.py:32
  32.4 10.4 %collective-permute-start.11 = (bf16[4,256,128]{2,1,0:T(8,128)(2,1)S(1)}, bf16[4,256,128]{2,1,0:T(8,128)(2,1)S(1)}, u32[]{:S(2)}, u32[]{:S(2)}) collective-permute-start(bf16[4,256,128]{2,1,0:T(8,128)(2,1)S(1)} %get-tuple-element.51), channel_id=1, source_target_pairs={{8,0},{10,2},{12,4},{14,6},{16,8},{18,10},{20,12},{22,14},{24,16},... | collective-permute-start | bytes 786440 | tf_op jit(solution)/shard_map/ppermute | solution.py:27
  40.4 7.9 %collective-permute-start.15 = (bf16[4,256,128]{2,1,0:T(8,128)(2,1)S(1)}, bf16[4,256,128]{2,1,0:T(8,128)(2,1)S(1)}, u32[]{:S(2)}, u32[]{:S(2)}) collective-permute-start(bf16[4,256,128]{2,1,0:T(8,128)(2,1)S(1)} %get-tuple-element.57), channel_id=1, source_target_pairs={{8,0},{10,2},{12,4},{14,6},{16,8},{18,10},{20,12},{22,14},{24,16},... | collective-permute-start | bytes 786440 | tf_op jit(solution)/shard_map/ppermute | solution.py:27
  44.7 6.4 %collective-permute-start.12 = (bf16[256,256]{1,0:T(8,128)(2,1)S(1)}, bf16[256,256]{1,0:T(8,128)(2,1)S(1)}, u32[]{:S(2)}, u32[]{:S(2)}) collective-permute-start(bf16[256,256]{1,0:T(8,128)(2,1)S(1)} %get-tuple-element.53), channel_id=1, source_target_pairs={{0,2},{2,0},{4,6},{6,4},{8,10},{10,8},{12,14},{14,12},{16,18},{18,... | collective-permute-start | bytes 393224 | tf_op jit(solution)/shard_map/ppermute | solution.py:32
  46.4 8.2 %collective-permute-start.13 = (bf16[256,256]{1,0:T(8,128)(2,1)S(1)}, bf16[256,256]{1,0:T(8,128)(2,1)S(1)}, u32[]{:S(2)}, u32[]{:S(2)}) collective-permute-start(bf16[256,256]{1,0:T(8,128)(2,1)S(1)} %get-tuple-element.54), channel_id=1, source_target_pairs={{0,4},{2,6},{4,0},{6,2},{8,12},{10,14},{12,8},{14,10},{16,20},{18,... | collective-permute-start | bytes 393224 | tf_op jit(solution)/shard_map/ppermute | solution.py:32
  46.9 7.7 %collective-permute-start.14 = (bf16[256,256]{1,0:T(8,128)(2,1)S(1)}, bf16[256,256]{1,0:T(8,128)(2,1)S(1)}, u32[]{:S(2)}, u32[]{:S(2)}) collective-permute-start(bf16[256,256]{1,0:T(8,128)(2,1)S(1)} %get-tuple-element.55), channel_id=1, source_target_pairs={{0,6},{2,4},{4,2},{6,0},{8,14},{10,12},{12,10},{14,8},{16,22},{18,... | collective-permute-start | bytes 393224 | tf_op jit(solution)/shard_map/ppermute | solution.py:32
  48.4 7.5 %collective-permute-start.16 = (bf16[256,256]{1,0:T(8,128)(2,1)S(1)}, bf16[256,256]{1,0:T(8,128)(2,1)S(1)}, u32[]{:S(2)}, u32[]{:S(2)}) collective-permute-start(bf16[256,256]{1,0:T(8,128)(2,1)S(1)} %get-tuple-element.60), channel_id=1, source_target_pairs={{0,2},{2,0},{4,6},{6,4},{8,10},{10,8},{12,14},{14,12},{16,18},{18,... | collective-permute-start | bytes 393224 | tf_op jit(solution)/shard_map/ppermute | solution.py:32
  50.1 7.4 %collective-permute-start.17 = (bf16[256,256]{1,0:T(8,128)(2,1)S(1)}, bf16[256,256]{1,0:T(8,128)(2,1)S(1)}, u32[]{:S(2)}, u32[]{:S(2)}) collective-permute-start(bf16[256,256]{1,0:T(8,128)(2,1)S(1)} %get-tuple-element.61), channel_id=1, source_target_pairs={{0,4},{2,6},{4,0},{6,2},{8,12},{10,14},{12,8},{14,10},{16,20},{18,... | collective-permute-start | bytes 393224 | tf_op jit(solution)/shard_map/ppermute | solution.py:32
  51.1 6.3 %collective-permute-start.18 = (bf16[256,256]{1,0:T(8,128)(2,1)S(1)}, bf16[256,256]{1,0:T(8,128)(2,1)S(1)}, u32[]{:S(2)}, u32[]{:S(2)}) collective-permute-start(bf16[256,256]{1,0:T(8,128)(2,1)S(1)} %get-tuple-element.62), channel_id=1, source_target_pairs={{0,6},{2,4},{4,2},{6,0},{8,14},{10,12},{12,10},{14,8},{16,22},{18,... | collective-permute-start | bytes 393224 | tf_op jit(solution)/shard_map/ppermute | solution.py:32

commit v5 on v4

--- a/solution.py
+++ b/solution.py
@@ -59,17 +59,24 @@
     return pl.ds(pl.multiple_of(index * width, width), width)
 
 
-def pack_kv(group, keys, values):
+def begin():
+    def body(out_ref):
+        out_ref[...] = jnp.zeros_like(out_ref)
+
+    return call(body, [jax.ShapeDtypeStruct((8, 128), jnp.float32)], flops=AHEAD)()[0]
+
+
+def pack_kv(group, keys, values, before):
     tokens, width = keys.shape[0], keys.shape[1] // group
 
-    def body(k_ref, v_ref, *refs):
+    def body(k_ref, v_ref, before_ref, *refs):
         for r in range(group):
             member = spot(group)[0] ^ r
             refs[r][:, :width] = k_ref[:, lanes(member, width)]
             refs[r][:, width:] = v_ref[:, lanes(member, width)]
 
     outs = [jax.ShapeDtypeStruct((tokens, 2 * width), jnp.bfloat16)] * group
-    return call(body, outs, flops=AHEAD)(keys, values)
+    return call(body, outs, flops=AHEAD, specs=[VMEM, VMEM, ANY])(keys, values, before)
 
 
 def pack_queries(group, queries, before):
@@ -83,13 +90,13 @@
     return call(body, outs, specs=[VMEM, ANY])(queries, before)
 
 
-def order_pieces(group, pieces):
-    def body(*refs):
-        for r in range(group):
-            refs[group][spot(group)[0] ^ r] = refs[r][...]
+def order_pieces(group, pieces, before):
+    def body(*refs):
+        for r in range(group):
+            refs[-1][spot(group)[0] ^ r] = refs[r][...]
 
     outs = [jax.ShapeDtypeStruct((group,) + pieces[0].shape, jnp.bfloat16)]
-    return call(body, outs)(*pieces)[0]
+    return call(body, outs, specs=[VMEM] * group + [ANY])(*pieces, before)[0]
 
 
 def head_product(parts, part, out_weight, layer_cotangent, before):
@@ -169,7 +176,7 @@
 
     def body(*refs):
         own_ref, earlier_refs = refs[0], refs[1 : 1 + z.steps]
-        qt_ref, e_ref, inverse_ref, k_all, s_all = refs[1 + z.steps :]
+        qt_ref, e_ref, inverse_ref, k_all, s_all, tops = refs[1 + z.steps :]
         first = spot(z.group)[1]
         key_id = lax.broadcasted_iota(jnp.int32, (z.tokens, z.wide), 0)
         query_id = lax.broadcasted_iota(jnp.int32, (z.tokens, z.wide), 1) & (z.tokens - 1)
@@ -178,30 +185,48 @@
             for number in range(z.total):
                 k_all[number] = z.block(own_ref, earlier_refs, number)[:, at_k]
 
-            @pl.loop(0, z.group)
-            def _(b):
-                qt = qt_ref[head, b]
-                top = None
+            def score(b, slot, c, top):
+                s = lax.dot_general(k_all[b + c], qt_ref[head, b], NN, preferred_element_type=jnp.float32)
+                if c == 0:
+                    s = jnp.where(key_id > query_id, s, -jnp.inf)
+                if c == z.back:
+                    s = jnp.where(key_id <= query_id, s, -jnp.inf)
+                s_all[slot, c] = s
+                here = jnp.max(s, axis=0, keepdims=True)
+                if c < z.back:
+                    here = jnp.where(first + b + c >= z.back, here, -jnp.inf)
+                return here if top is None else jnp.maximum(top, here)
+
+            def expo(b, slot, c, norm):
+                base = tops[slot]
+                if c < z.back:
+                    base = jnp.where(first + b + c >= z.back, base, jnp.inf)
+                e = jnp.exp2((s_all[slot, c] - base) * factor)
+                e_ref[head, b, c] = e.astype(jnp.bfloat16)
+                here = jnp.sum(e, axis=0, keepdims=True)
+                return here if norm is None else norm + here
+
+            def both(b, slot, ahead):
+                top = norm = None
                 for c in range(z.span):
-                    s = lax.dot_general(k_all[b + c], qt, NN, preferred_element_type=jnp.float32)
-                    if c == 0:
-                        s = jnp.where(key_id > query_id, s, -jnp.inf)
-                    if c == z.back:
-                        s = jnp.where(key_id <= query_id, s, -jnp.inf)
-                    s_all[c] = s
-                    here = jnp.max(s, axis=0, keepdims=True)
-                    if c < z.back:
-                        here = jnp.where(first + b + c >= z.back, here, -jnp.inf)
-                    top = here if top is None else jnp.maximum(top, here)
-                norm = jnp.zeros((1, z.wide), jnp.float32)
-                for c in range(z.span):
-                    base = top
-                    if c < z.back:
-                        base = jnp.where(first + b + c >= z.back, top, jnp.inf)
-                    e = jnp.exp2((s_all[c] - base) * factor)
-                    norm = norm + jnp.sum(e, axis=0, keepdims=True)
-                    e_ref[head, b, c] = e.astype(jnp.bfloat16)
+                    if ahead:
+                        top = score(b + 1, 1 - slot, c, top)
+                    norm = expo(b, slot, c, norm)
+                if ahead:
+                    tops[1 - slot] = top
                 inverse_ref[head, b] = 1.0 / norm
+
+            top = None
+            for c in range(z.span):
+                top = score(0, 0, c, top)
+            tops[0] = top
+            if z.group > 1:
+
+                @pl.loop(0, z.group - 1)
+                def _(b):
+                    both(b, b & 1, True)
+
+            both(z.group - 1, (z.group - 1) & 1, False)
 
     outs = [
         jax.ShapeDtypeStruct((z.heads, z.group, z.span, z.tokens, z.wide), jnp.bfloat16),
@@ -209,7 +234,8 @@
     ]
     scratch = [
         pltpu.VMEM((z.total, z.tokens, HEAD_SIZE), jnp.bfloat16),
-        pltpu.VMEM((z.span, z.tokens, z.wide), jnp.float32),
+        pltpu.VMEM((2, z.span, z.tokens, z.wide), jnp.float32),
+        pltpu.VMEM((2, 1, z.wide), jnp.float32),
     ]
     return call(body, outs, scratch, flops=2 * z.entries * HEAD_SIZE, exps=z.entries)(
         kv_own, *kv_earlier, qt
@@ -238,13 +264,13 @@
             @pl.loop(0, z.group)
             def _(b):
                 g = (g_ref[head, b].astype(jnp.float32) * inverse_ref[head, b]).astype(jnp.bfloat16)
-                for c in range(z.span):
-                    dv_all[b + c] += lax.dot_general(
-                        e_ref[head, b, c], g, NT, preferred_element_type=jnp.float32
-                    )
+                window = pl.ds(pl.multiple_of(b * z.tokens, z.tokens), z.span * z.tokens)
+                dv_all[window, :] += lax.dot_general(
+                    e_ref[head, b].reshape(z.span * z.tokens, z.wide), g, NT, preferred_element_type=jnp.float32
+                )
 
             for number in range(z.total):
-                part = dv_all[number]
+                part = dv_all[number * z.tokens : (number + 1) * z.tokens, :]
                 z.block(own_ref, earlier_refs, number)[:, at] = part.astype(own_ref.dtype if number >= z.back else jnp.bfloat16)
 
     outs = [
@@ -252,7 +278,7 @@
         jax.ShapeDtypeStruct((z.group, z.tokens, z.kv_width), jnp.float32),
     ]
     outs += [jax.ShapeDtypeStruct((z.group, z.tokens, z.kv_width), jnp.bfloat16)] * z.steps
-    scratch = [pltpu.VMEM((z.total, z.tokens, HEAD_SIZE), jnp.float32)]
+    scratch = [pltpu.VMEM((z.total * z.tokens, HEAD_SIZE), jnp.float32)]
     results = call(body, outs, scratch, flops=2 * z.entries * HEAD_SIZE)(e, inverse, *grads)
     return results[0], results[1], results[2:]
 
@@ -261,7 +287,7 @@
     def body(e_ref, inverse_ref, qt_ref, g_ref, own_ref, *refs):
         earlier_refs, ds_ref = refs[: z.steps], refs[z.steps]
         dk_own, dk_earlier = refs[z.steps + 1], refs[z.steps + 2 : 2 * z.steps + 2]
-        v_all, dk_all, dp_all = refs[2 * z.steps + 2 :]
+        v_all, dk_all, dp_all, deltas = refs[2 * z.steps + 2 :]
         for head in range(z.heads):
             at = slice(head * HEAD_SIZE, (head + 1) * HEAD_SIZE)
             at_v = slice(z.kv_width + head * HEAD_SIZE, z.kv_width + (head + 1) * HEAD_SIZE)
@@ -269,21 +295,37 @@
                 v_all[number] = z.block(own_ref, earlier_refs, number)[:, at_v]
             dk_all[...] = jnp.zeros_like(dk_all)
 
-            @pl.loop(0, z.group)
-            def _(b):
-                g = g_ref[head, b]
-                inverse = inverse_ref[head, b]
-                delta = jnp.zeros((1, z.wide), jnp.float32)
+            def product(b, slot, c, delta):
+                dp = lax.dot_general(v_all[b + c], g_ref[head, b], NN, preferred_element_type=jnp.float32)
+                dp_all[slot, c] = dp
+                here = jnp.sum(e_ref[head, b, c].astype(jnp.float32) * dp, axis=0, keepdims=True)
+                return here if delta is None else delta + here
+
+            def both(b, slot, ahead):
+                delta = None
+                q = (qt_ref[head, b].astype(jnp.float32) * inverse_ref[head, b]).astype(jnp.bfloat16)
                 for c in range(z.span):
-                    dp = lax.dot_general(v_all[b + c], g, NN, preferred_element_type=jnp.float32)
-                    delta = delta + jnp.sum(e_ref[head, b, c].astype(jnp.float32) * dp, axis=0, keepdims=True)
-                    dp_all[c] = dp
-                delta = delta * inverse
-                q = (qt_ref[head, b].astype(jnp.float32) * inverse).astype(jnp.bfloat16)
-                for c in range(z.span):
-                    ds = (e_ref[head, b, c].astype(jnp.float32) * (dp_all[c] - delta)).astype(jnp.bfloat16)
+                    if ahead:
+                        delta = product(b + 1, 1 - slot, c, delta)
+                    ds = (e_ref[head, b, c].astype(jnp.float32) * (dp_all[slot, c] - deltas[slot])).astype(
+                        jnp.bfloat16
+                    )
                     ds_ref[head, b, c] = ds
                     dk_all[b + c] += lax.dot_general(ds, q, NT, preferred_element_type=jnp.float32)
+                if ahead:
+                    deltas[1 - slot] = delta * inverse_ref[head, b + 1]
+
+            delta = None
+            for c in range(z.span):
+                delta = product(0, 0, c, delta)
+            deltas[0] = delta * inverse_ref[head, 0]
+            if z.group > 1:
+
+                @pl.loop(0, z.group - 1)
+                def _(b):
+                    both(b, b & 1, True)
+
+            both(z.group - 1, (z.group - 1) & 1, False)
 
             for number in range(z.total):
                 part = dk_all[number] * score_scale
@@ -297,7 +339,8 @@
     scratch = [
         pltpu.VMEM((z.total, z.tokens, HEAD_SIZE), jnp.bfloat16),
         pltpu.VMEM((z.total, z.tokens, HEAD_SIZE), jnp.float32),
-        pltpu.VMEM((z.span, z.tokens, z.wide), jnp.float32),
+        pltpu.VMEM((2, z.span, z.tokens, z.wide), jnp.float32),
+        pltpu.VMEM((2, 1, z.wide), jnp.float32),
     ]
     results = call(body, outs, scratch, flops=4 * z.entries * HEAD_SIZE)(
         e, inverse, qt, g, kv_own, *kv_earlier
@@ -404,18 +447,20 @@
             shifted(earlier[number], "ctx", -group * (back_groups - number)) for number in range(back_groups)
         ]
 
-    sent = pack_kv(group, keys, values)
-    kv_own = order_pieces(group, trade(sent))
-    kv_earlier = [shifted(kv_own, "ctx", group * step) for step in range(back_groups, 0, -1)]
+    sent = pack_kv(group, keys, values, begin())
+    kv_pieces = trade(sent)
     z = Shape(group, back_groups, heads, per_head, tokens)
     query_sent = pack_queries(group, queries, sent[0])
-    qt = turn_queries(z, trade(query_sent))
     if tp_count == 2:
         other = head_product(2, 1, out_weight, layer_cotangent, [query_sent[0]])
-        terms = [head_product(2, 0, out_weight, layer_cotangent, [kv_own, other]), swapped(other, "tp", 1)]
+        mine = head_product(2, 0, out_weight, layer_cotangent, [other])
+        terms = [mine, swapped(other, "tp", 1)]
     else:
-        product = head_product(1, 0, out_weight, layer_cotangent, [query_sent[0]])
-        terms = [lax.psum_scatter(product, "tp", scatter_dimension=0, tiled=True)]
+        mine = head_product(1, 0, out_weight, layer_cotangent, [query_sent[0]])
+        terms = [lax.psum_scatter(mine, "tp", scatter_dimension=0, tiled=True)]
+    kv_own = order_pieces(group, kv_pieces, mine)
+    kv_earlier = [shifted(kv_own, "ctx", group * step) for step in range(back_groups, 0, -1)]
+    qt = turn_queries(z, trade(query_sent))
     grads = trade(pack_grads(group, terms))
     e, inverse = softmax(z, kv_own, kv_earlier, qt)
     g, dv_own, dv_earlier = value_terms(z, e, inverse, grads)

time: 58.9 us -> 62.3 us (1.058)
  waiting for transfers between devices: 9.84 us -> 13.2 us
  Pallas kernels: 19.7 us -> 21.9 us
  local copies, waits for them, and re-layouts: 2.74 us -> 1.28 us
    ppermute x16, waiting for transfers between devices: 7.48 us -> 9.93 us  [swapped(): lax.ppermute(value, axis, [(source, source ^ bits) for source in range(co...]
    pallas_call x14 -> x15, Pallas kernels: 19.7 us -> 21.9 us  [run(): pl.pallas_call(body, out_shape=tuple(outs), in_specs=specs or [SMEM if a....]
    unnamed x10 -> x14, local copies, waits for them, and re-layouts: 2.74 us -> 1.28 us
    ppermute x3, waiting for transfers between devices: 2.36 us -> 3.22 us  [shifted(): lax.ppermute(value, axis, [(source, source + steps) for source in range(l...]
  transfers between devices with their start and end apart: 19 -> 19, of which waited for: 6 -> 7; matrix products, arithmetic and copies ran while one was open for 0% -> 0% of each run, Pallas kernels for 28% -> 30%
where the time goes in v5:
time: 62.3 us; the launch traced here: 62 us
  starting transfers between devices  24.8 us (40%)
  Pallas kernels  21.9 us (35%)
  waiting for transfers between devices  13.2 us (21%)
  local copies, waits for them, and re-layouts  1.28 us (2%)
  between operations  0.85 us (1%)
    pallas_call x15, Pallas kernels, run(): pl.pallas_call(body, out_shape=tuple(outs), in_specs=specs or [SMEM if a....  21.9 us
    ppermute x16, starting transfers between devices, swapped(): lax.ppermute(value, axis, [(source, source ^ bits) for source in range(co...  18.8 us
    ppermute x16, waiting for transfers between devices, swapped(): lax.ppermute(value, axis, [(source, source ^ bits) for source in range(co...  9.93 us
    ppermute x3, starting transfers between devices, shifted(): lax.ppermute(value, axis, [(source, source + steps) for source in range(l...  6.02 us
    ppermute x3, waiting for transfers between devices, shifted(): lax.ppermute(value, axis, [(source, source + steps) for source in range(l...  3.22 us
    unnamed x14, local copies, waits for them, and re-layouts  1.28 us
  transfers between devices with their start and end apart: 19, of which 7 were waited for; matrix products, arithmetic and copies ran while one was open for 0% of the time, Pallas kernels for 30%

profile of v5, /device:TPU:24, one launch (start us, length us, event | category | flops | bytes accessed | tf_op | source)
XLA Modules:
  0.0 62.0 jit_solution(15116826231340061737)
XLA Ops:
  0.7 0.9 %copy-done.3 = bf16[256,512]{1,0:T(8,128)(2,1)S(1)} copy-done((bf16[256,512]{1,0:T(8,128)(2,1)S(1)}, bf16[256,512]{1,0:T(8,128)(2,1)}, u32[]{:S(2)}) %copy-start.3) | copy-done | bytes 262168
  1.8 1.6 %collective-permute-start = (bf16[256,256]{1,0:T(8,128)(2,1)S(1)}, bf16[256,256]{1,0:T(8,128)(2,1)S(1)}, u32[]{:S(2)}, u32[]{:S(2)}) collective-permute-start(bf16[256,256]{1,0:T(8,128)(2,1)S(1)} %get-tuple-element.35), channel_id=1, source_target_pairs={{0,2},{2,0},{4,6},{6,4},{8,10},{10,8},{12,14},{14,12},{16,18},{18,... | collective-permute-start | bytes 393224 | tf_op jit(solution)/shard_map/ppermute | solution.py:32
  3.3 1.5 %collective-permute-start.1 = (bf16[256,256]{1,0:T(8,128)(2,1)S(1)}, bf16[256,256]{1,0:T(8,128)(2,1)S(1)}, u32[]{:S(2)}, u32[]{:S(2)}) collective-permute-start(bf16[256,256]{1,0:T(8,128)(2,1)S(1)} %get-tuple-element.36), channel_id=1, source_target_pairs={{0,4},{2,6},{4,0},{6,2},{8,12},{10,14},{12,8},{14,10},{16,20},{18,... | collective-permute-start | bytes 393224 | tf_op jit(solution)/shard_map/ppermute | solution.py:32
  4.8 0.5 collective-permute-start.2
  5.7 1.9 %shard_map.79.refs_0_ = bf16[1024,256]{1,0:T(8,128)(2,1)S(1)} custom-call(bf16[2048,2688]{1,0:T(8,128)(2,1)S(1)} %bitcast.1, bf16[256,2688]{1,0:T(8,128)(2,1)S(1)} %copy-done, bf16[256,256]{1,0:T(8,128)(2,1)S(1)} %get-tuple-element.38.refs_0_), custom_call_target="tpu_custom_call" | custom-call | flops 1409286144 | bytes 13041664 | tf_op jit(solution)/shard_map/pallas_call | solution.py:39
  7.7 1.9 %shard_map.80.refs_4_.refs_0_ = bf16[1024,256]{1,0:T(8,128)(2,1)S(1)} custom-call(bf16[2048,2688]{1,0:T(8,128)(2,1)S(1)} %bitcast.1, bf16[256,2688]{1,0:T(8,128)(2,1)S(1)} %copy-done, bf16[1024,256]{1,0:T(8,128)(2,1)S(1)} %shard_map.79.refs_0_), custom_call_target="tpu_custom_call" | custom-call | flops 1409286144 | bytes 13434880 | tf_op jit(solution)/shard_map/pallas_call | solution.py:39
  9.6 1.5 %collective-permute-done.1.refs_2_ = bf16[256,256]{1,0:T(8,128)(2,1)S(1)} collective-permute-done((bf16[256,256]{1,0:T(8,128)(2,1)S(1)}, bf16[256,256]{1,0:T(8,128)(2,1)S(1)}, u32[]{:S(2)}, u32[]{:S(2)}) %collective-permute-start.1) | collective-permute-done | bytes 131104 | tf_op jit(solution)/shard_map/ppermute | solution.py:32
  11.2 1.3 %collective-permute-start.3 = (bf16[4,256,256]{2,1,0:T(8,128)(2,1)S(1)}, bf16[4,256,256]{2,1,0:T(8,128)(2,1)S(1)}, u32[]{:S(2)}, u32[]{:S(2)}) collective-permute-start(bf16[4,256,256]{2,1,0:T(8,128)(2,1)S(1)} %shard_map.81.refs_0_.own_ref), channel_id=1, source_target_pairs={{0,8},{2,10},{4,12},{6,14},{8,16},{10,18},{12,20},{14,22},{16,24},... | collective-permute-start | bytes 1572872 | tf_op jit(solution)/shard_map/ppermute | solution.py:27
  12.5 1.3 %collective-permute-start.4 = (bf16[256,256]{1,0:T(8,128)(2,1)S(1)}, bf16[256,256]{1,0:T(8,128)(2,1)S(1)}, u32[]{:S(2)}, u32[]{:S(2)}) collective-permute-start(bf16[256,256]{1,0:T(8,128)(2,1)S(1)} %get-tuple-element.39), channel_id=1, source_target_pairs={{0,2},{2,0},{4,6},{6,4},{8,10},{10,8},{12,14},{14,12},{16,18},{18,... | collective-permute-start | bytes 393224 | tf_op jit(solution)/shard_map/ppermute | solution.py:32
  13.7 0.8 %collective-permute-start.5 = (bf16[256,256]{1,0:T(8,128)(2,1)S(1)}, bf16[256,256]{1,0:T(8,128)(2,1)S(1)}, u32[]{:S(2)}, u32[]{:S(2)}) collective-permute-start(bf16[256,256]{1,0:T(8,128)(2,1)S(1)} %get-tuple-element.40), channel_id=1, source_target_pairs={{0,4},{2,6},{4,0},{6,2},{8,12},{10,14},{12,8},{14,10},{16,20},{18,... | collective-permute-start | bytes 393224 | tf_op jit(solution)/shard_map/ppermute | solution.py:32
  14.6 1.4 %collective-permute-start.6 = (bf16[256,256]{1,0:T(8,128)(2,1)S(1)}, bf16[256,256]{1,0:T(8,128)(2,1)S(1)}, u32[]{:S(2)}, u32[]{:S(2)}) collective-permute-start(bf16[256,256]{1,0:T(8,128)(2,1)S(1)} %get-tuple-element.41), channel_id=1, source_target_pairs={{0,6},{2,4},{4,2},{6,0},{8,14},{10,12},{12,10},{14,8},{16,22},{18,... | collective-permute-start | bytes 393224 | tf_op jit(solution)/shard_map/ppermute | solution.py:32
  16.1 1.3 %collective-permute-start.8 = (bf16[256,256]{1,0:T(8,128)(2,1)S(1)}, bf16[256,256]{1,0:T(8,128)(2,1)S(1)}, u32[]{:S(2)}, u32[]{:S(2)}) collective-permute-start(bf16[256,256]{1,0:T(8,128)(2,1)S(1)} %get-tuple-element.45), channel_id=1, source_target_pairs={{0,2},{2,0},{4,6},{6,4},{8,10},{10,8},{12,14},{14,12},{16,18},{18,... | collective-permute-start | bytes 393224 | tf_op jit(solution)/shard_map/ppermute | solution.py:32
  17.4 1.1 %collective-permute-done.4.refs_1_ = bf16[256,256]{1,0:T(8,128)(2,1)S(1)} collective-permute-done((bf16[256,256]{1,0:T(8,128)(2,1)S(1)}, bf16[256,256]{1,0:T(8,128)(2,1)S(1)}, u32[]{:S(2)}, u32[]{:S(2)}) %collective-permute-start.4) | collective-permute-done | bytes 131104 | tf_op jit(solution)/shard_map/ppermute | solution.py:32
  18.6 1.5 %collective-permute-start.9 = (bf16[256,256]{1,0:T(8,128)(2,1)S(1)}, bf16[256,256]{1,0:T(8,128)(2,1)S(1)}, u32[]{:S(2)}, u32[]{:S(2)}) collective-permute-start(bf16[256,256]{1,0:T(8,128)(2,1)S(1)} %get-tuple-element.46), channel_id=1, source_target_pairs={{0,4},{2,6},{4,0},{6,2},{8,12},{10,14},{12,8},{14,10},{16,20},{18,... | collective-permute-start | bytes 393224 | tf_op jit(solution)/shard_map/ppermute | solution.py:32
  20.0 2.4 %collective-permute-done.5.refs_2_ = bf16[256,256]{1,0:T(8,128)(2,1)S(1)} collective-permute-done((bf16[256,256]{1,0:T(8,128)(2,1)S(1)}, bf16[256,256]{1,0:T(8,128)(2,1)S(1)}, u32[]{:S(2)}, u32[]{:S(2)}) %collective-permute-start.5) | collective-permute-done | bytes 131104 | tf_op jit(solution)/shard_map/ppermute | solution.py:32
  22.7 3.2 %collective-permute-done.3.refs_1_.refs_0_ = bf16[4,256,256]{2,1,0:T(8,128)(2,1)S(1)} collective-permute-done((bf16[4,256,256]{2,1,0:T(8,128)(2,1)S(1)}, bf16[4,256,256]{2,1,0:T(8,128)(2,1)S(1)}, u32[]{:S(2)}, u32[]{:S(2)}) %collective-permute-start.3) | collective-permute-done | bytes 524320 | tf_op jit(solution)/shard_map/ppermute | solution.py:27
  25.9 5.0 %shard_map.83 = (bf16[1,4,5,256,512]{4,3,2,1,0:T(8,128)(2,1)S(1)}, f32[1,4,1,512]{3,2,1,0:T(1,128)S(1)}) custom-call(bf16[4,256,256]{2,1,0:T(8,128)(2,1)S(1)} %shard_map.81.refs_0_.own_ref, bf16[4,256,256]{2,1,0:T(8,128)(2,1)S(1)} %collective-permute-done.3.refs_1_.refs_0_, bf16[1,4,128,512]{3,2,1,0:T(8,128)(2,1)S(1)} %shard_map.82.refs_2_.qt_ref), custom_call_target="tpu_custom_call" | custom-call | flops 671088640 | bytes 6823936 | tf_op jit(solution)/shard_map/pallas_call | solution.py:39
  30.9 2.2 %shard_map.85 = (bf16[1,4,128,512]{3,2,1,0:T(8,128)(2,1)S(1)}, f32[4,256,128]{2,1,0:T(8,128)S(1)}, bf16[4,256,128]{2,1,0:T(8,128)(2,1)S(1)}) custom-call(bf16[1,4,5,256,512]{4,3,2,1,0:T(8,128)(2,1)S(1)} %get-tuple-element.42.e_ref, f32[1,4,1,512]{3,2,1,0:T(1,128)S(1)} %get-tuple-element.43.inverse_ref, bf16[256,256]{1,0:T(8,128)(2,1)S(1)} %get-tuple-element.44.refs_0_, ...), custom_call_target="tpu_custom_call" | custom-call | flops 671088640 | bytes 7086080 | tf_op jit(solution)/shard_map/pallas_call | solution.py:39
  33.1 2.4 %collective-permute-start.11 = (bf16[4,256,128]{2,1,0:T(8,128)(2,1)S(1)}, bf16[4,256,128]{2,1,0:T(8,128)(2,1)S(1)}, u32[]{:S(2)}, u32[]{:S(2)}) collective-permute-start(bf16[4,256,128]{2,1,0:T(8,128)(2,1)S(1)} %get-tuple-element.51), channel_id=1, source_target_pairs={{8,0},{10,2},{12,4},{14,6},{16,8},{18,10},{20,12},{22,14},{24,16},... | collective-permute-start | bytes 786440 | tf_op jit(solution)/shard_map/ppermute | solution.py:27
  35.5 6.6 %shard_map.86 = (bf16[1,4,5,256,512]{4,3,2,1,0:T(8,128)(2,1)S(1)}, f32[4,256,128]{2,1,0:T(8,128)S(1)}, bf16[4,256,128]{2,1,0:T(8,128)(2,1)S(1)}) custom-call(bf16[1,4,5,256,512]{4,3,2,1,0:T(8,128)(2,1)S(1)} %get-tuple-element.42.e_ref, f32[1,4,1,512]{3,2,1,0:T(1,128)S(1)} %get-tuple-element.43.inverse_ref, ...), custom_call_target="tpu_custom_call" | custom-call | flops 1342177280 | bytes 13377536 | tf_op jit(solution)/shard_map/pallas_call | solution.py:39
  42.1 2.3 %collective-permute-start.15 = (bf16[4,256,128]{2,1,0:T(8,128)(2,1)S(1)}, bf16[4,256,128]{2,1,0:T(8,128)(2,1)S(1)}, u32[]{:S(2)}, u32[]{:S(2)}) collective-permute-start(bf16[4,256,128]{2,1,0:T(8,128)(2,1)S(1)} %get-tuple-element.57), channel_id=1, source_target_pairs={{8,0},{10,2},{12,4},{14,6},{16,8},{18,10},{20,12},{22,14},{24,16},... | collective-permute-start | bytes 786440 | tf_op jit(solution)/shard_map/ppermute | solution.py:27
  44.5 1.9 %shard_map.87 = (bf16[4,256,128]{2,1,0:T(8,128)(2,1)S(1)}, bf16[256,256]{1,0:T(8,128)(2,1)S(1)}, bf16[256,256]{1,0:T(8,128)(2,1)S(1)}, bf16[256,256]{1,0:T(8,128)(2,1)S(1)}, bf16[256,256]{1,0:T(8,128)(2,1)S(1)}) custom-call(bf16[1,4,5,256,512]{4,3,2,1,0:T(8,128)(2,1)S(1)} %get-tuple-element.49.ds_ref, f32[1,4,1,512]{3,2,1,0:T(1,128)S(1)} %get-tuple-element.43.inverse_ref, ...), custom_call_target="tpu_custom_call" | custom-call | flops 671088640 | bytes 7872512 | tf_op jit(solution)/shard_map/pallas_call | solution.py:39
  46.4 1.6 %collective-permute-start.12 = (bf16[256,256]{1,0:T(8,128)(2,1)S(1)}, bf16[256,256]{1,0:T(8,128)(2,1)S(1)}, u32[]{:S(2)}, u32[]{:S(2)}) collective-permute-start(bf16[256,256]{1,0:T(8,128)(2,1)S(1)} %get-tuple-element.53), channel_id=1, source_target_pairs={{0,2},{2,0},{4,6},{6,4},{8,10},{10,8},{12,14},{14,12},{16,18},{18,... | collective-permute-start | bytes 393224 | tf_op jit(solution)/shard_map/ppermute | solution.py:32
  48.0 1.5 %collective-permute-start.13 = (bf16[256,256]{1,0:T(8,128)(2,1)S(1)}, bf16[256,256]{1,0:T(8,128)(2,1)S(1)}, u32[]{:S(2)}, u32[]{:S(2)}) collective-permute-start(bf16[256,256]{1,0:T(8,128)(2,1)S(1)} %get-tuple-element.54), channel_id=1, source_target_pairs={{0,4},{2,6},{4,0},{6,2},{8,12},{10,14},{12,8},{14,10},{16,20},{18,... | collective-permute-start | bytes 393224 | tf_op jit(solution)/shard_map/ppermute | solution.py:32
  49.5 0.5 collective-permute-start.14
  50.1 1.6 %collective-permute-start.16 = (bf16[256,256]{1,0:T(8,128)(2,1)S(1)}, bf16[256,256]{1,0:T(8,128)(2,1)S(1)}, u32[]{:S(2)}, u32[]{:S(2)}) collective-permute-start(bf16[256,256]{1,0:T(8,128)(2,1)S(1)} %get-tuple-element.60), channel_id=1, source_target_pairs={{0,2},{2,0},{4,6},{6,4},{8,10},{10,8},{12,14},{14,12},{16,18},{18,... | collective-permute-start | bytes 393224 | tf_op jit(solution)/shard_map/ppermute | solution.py:32
  51.7 1.5 %collective-permute-start.17 = (bf16[256,256]{1,0:T(8,128)(2,1)S(1)}, bf16[256,256]{1,0:T(8,128)(2,1)S(1)}, u32[]{:S(2)}, u32[]{:S(2)}) collective-permute-start(bf16[256,256]{1,0:T(8,128)(2,1)S(1)} %get-tuple-element.61), channel_id=1, source_target_pairs={{0,4},{2,6},{4,0},{6,2},{8,12},{10,14},{12,8},{14,10},{16,20},{18,... | collective-permute-start | bytes 393224 | tf_op jit(solution)/shard_map/ppermute | solution.py:32
  53.2 2.2 %collective-permute-start.18 = (bf16[256,256]{1,0:T(8,128)(2,1)S(1)}, bf16[256,256]{1,0:T(8,128)(2,1)S(1)}, u32[]{:S(2)}, u32[]{:S(2)}) collective-permute-start(bf16[256,256]{1,0:T(8,128)(2,1)S(1)} %get-tuple-element.62), channel_id=1, source_target_pairs={{0,6},{2,4},{4,2},{6,0},{8,14},{10,12},{12,10},{14,8},{16,22},{18,... | collective-permute-start | bytes 393224 | tf_op jit(solution)/shard_map/ppermute | solution.py:32
  55.4 1.9 %collective-permute-done.13.refs_2_ = bf16[256,256]{1,0:T(8,128)(2,1)S(1)} collective-permute-done((bf16[256,256]{1,0:T(8,128)(2,1)S(1)}, bf16[256,256]{1,0:T(8,128)(2,1)S(1)}, u32[]{:S(2)}, u32[]{:S(2)}) %collective-permute-start.13) | collective-permute-done | bytes 131104 | tf_op jit(solution)/shard_map/ppermute | solution.py:32
  57.3 0.9 %shard_map.88 = bf16[256,1024]{1,0:T(8,128)(2,1)} custom-call(bf16[256,256]{1,0:T(8,128)(2,1)S(1)} %get-tuple-element.52.refs_0_, bf16[256,256]{1,0:T(8,128)(2,1)S(1)} %collective-permute-done.12.refs_1_, bf16[256,256]{1,0:T(8,128)(2,1)S(1)} %collective-permute-done.13.refs_2_, bf16[256,256]{1,0:T(8,128)(2,1)S(1)} %collective-permute-done.14.refs_3_), custom_call_target="tpu_custom_call" | custom-call | bytes 1048576 | tf_op jit(solution)/shard_map/pallas_call | solution.py:39
  58.3 2.8 %collective-permute-done.17.refs_2_ = bf16[256,256]{1,0:T(8,128)(2,1)S(1)} collective-permute-done((bf16[256,256]{1,0:T(8,128)(2,1)S(1)}, bf16[256,256]{1,0:T(8,128)(2,1)S(1)}, u32[]{:S(2)}, u32[]{:S(2)}) %collective-permute-start.17) | collective-permute-done | bytes 131104 | tf_op jit(solution)/shard_map/ppermute | solution.py:32
  61.1 0.9 %shard_map.90 = (bf16[256,512]{1,0:T(8,128)(2,1)}, bf16[256,512]{1,0:T(8,128)(2,1)}) custom-call(bf16[256,256]{1,0:T(8,128)(2,1)S(1)} %get-tuple-element.59.refs_0_, bf16[256,256]{1,0:T(8,128)(2,1)S(1)} %collective-permute-done.16.refs_1_, bf16[256,256]{1,0:T(8,128)(2,1)S(1)} %collective-permute-done.17.refs_2_, ...), custom_call_target="tpu_custom_call" | custom-call | bytes 1048576 | tf_op jit(solution)/shard_map/pallas_call | solution.py:39
  (36 shorter events, 1.2 us)
Async XLA Ops:
  0.6 1.0 %copy-start.3 = (bf16[256,512]{1,0:T(8,128)(2,1)S(1)}, bf16[256,512]{1,0:T(8,128)(2,1)}, u32[]{:S(2)}) copy-start(bf16[256,512]{1,0:T(8,128)(2,1)} %v_ref.1) | copy-start | bytes 786436
  0.6 1.0 %copy-start.2 = (bf16[256,512]{1,0:T(8,128)(2,1)S(1)}, bf16[256,512]{1,0:T(8,128)(2,1)}, u32[]{:S(2)}) copy-start(bf16[256,512]{1,0:T(8,128)(2,1)} %k_ref.1) | copy-start | bytes 786436
  0.7 4.7 %slice-start = ((s8[11010048]{0:T(1024)(128)(4,1)}), s8[4194304]{0:T(1024)(128)(4,1)S(1)}, s32[]{:S(2)}) async-start(s8[11010048]{0:T(1024)(128)(4,1)} %bitcast), calls=%async_computation | async-start | bytes 8388608
  0.7 4.7 %slice-start.1 = ((s8[11010048]{0:T(1024)(128)(4,1)}), s8[4194304]{0:T(1024)(128)(4,1)S(1)}, s32[]{:S(2)}) async-start(s8[11010048]{0:T(1024)(128)(4,1)} %bitcast), calls=%async_computation.1 | async-start | bytes 8388608
  1.7 3.7 %copy-start.1 = (bf16[256,1024]{1,0:T(8,128)(2,1)S(1)}, bf16[256,1024]{1,0:T(8,128)(2,1)}, u32[]{:S(2)}) copy-start(bf16[256,1024]{1,0:T(8,128)(2,1)} %q_ref.1) | copy-start | bytes 1572868
  1.7 3.8 %slice-start.2 = ((s8[11010048]{0:T(1024)(128)(4,1)}), s8[2621440]{0:T(1024)(128)(4,1)S(1)}, s32[]{:S(2)}) async-start(s8[11010048]{0:T(1024)(128)(4,1)} %bitcast), calls=%async_computation.2 | async-start | bytes 5242880
  1.7 4.0 %copy-start = (bf16[256,2688]{1,0:T(8,128)(2,1)S(1)}, bf16[256,2688]{1,0:T(8,128)(2,1)}, u32[]{:S(2)}) copy-start(bf16[256,2688]{1,0:T(8,128)(2,1)} %c_ref.3) | copy-start | bytes 4128772
  1.8 7.8 %collective-permute-start = (bf16[256,256]{1,0:T(8,128)(2,1)S(1)}, bf16[256,256]{1,0:T(8,128)(2,1)S(1)}, u32[]{:S(2)}, u32[]{:S(2)}) collective-permute-start(bf16[256,256]{1,0:T(8,128)(2,1)S(1)} %get-tuple-element.35), channel_id=1, source_target_pairs={{0,2},{2,0},{4,6},{6,4},{8,10},{10,8},{12,14},{14,12},{16,18},{18,... | collective-permute-start | bytes 393224 | tf_op jit(solution)/shard_map/ppermute | solution.py:32
  3.3 7.8 %collective-permute-start.1 = (bf16[256,256]{1,0:T(8,128)(2,1)S(1)}, bf16[256,256]{1,0:T(8,128)(2,1)S(1)}, u32[]{:S(2)}, u32[]{:S(2)}) collective-permute-start(bf16[256,256]{1,0:T(8,128)(2,1)S(1)} %get-tuple-element.36), channel_id=1, source_target_pairs={{0,4},{2,6},{4,0},{6,2},{8,12},{10,14},{12,8},{14,10},{16,20},{18,... | collective-permute-start | bytes 393224 | tf_op jit(solution)/shard_map/ppermute | solution.py:32
  4.8 6.3 %collective-permute-start.2 = (bf16[256,256]{1,0:T(8,128)(2,1)S(1)}, bf16[256,256]{1,0:T(8,128)(2,1)S(1)}, u32[]{:S(2)}, u32[]{:S(2)}) collective-permute-start(bf16[256,256]{1,0:T(8,128)(2,1)S(1)} %get-tuple-element.37), channel_id=1, source_target_pairs={{0,6},{2,4},{4,2},{6,0},{8,14},{10,12},{12,10},{14,8},{16,22},{18,... | collective-permute-start | bytes 393224 | tf_op jit(solution)/shard_map/ppermute | solution.py:32
  7.6 8.4 %collective-permute-start.7 = (bf16[1024,256]{1,0:T(8,128)(2,1)S(1)}, bf16[1024,256]{1,0:T(8,128)(2,1)S(1)}, u32[]{:S(2)}, u32[]{:S(2)}) collective-permute-start(bf16[1024,256]{1,0:T(8,128)(2,1)S(1)} %shard_map.79.refs_0_), channel_id=1, source_target_pairs={{0,1},{1,0},{2,3},{3,2},{4,5},{5,4},{6,7},{7,6},{8,9},{9,8},{10,11... | collective-permute-start | bytes 1572872 | tf_op jit(solution)/shard_map/ppermute | solution.py:32
  11.2 14.7 %collective-permute-start.3 = (bf16[4,256,256]{2,1,0:T(8,128)(2,1)S(1)}, bf16[4,256,256]{2,1,0:T(8,128)(2,1)S(1)}, u32[]{:S(2)}, u32[]{:S(2)}) collective-permute-start(bf16[4,256,256]{2,1,0:T(8,128)(2,1)S(1)} %shard_map.81.refs_0_.own_ref), channel_id=1, source_target_pairs={{0,8},{2,10},{4,12},{6,14},{8,16},{10,18},{12,20},{14,22},{16,24},... | collective-permute-start | bytes 1572872 | tf_op jit(solution)/shard_map/ppermute | solution.py:27
  12.5 6.1 %collective-permute-start.4 = (bf16[256,256]{1,0:T(8,128)(2,1)S(1)}, bf16[256,256]{1,0:T(8,128)(2,1)S(1)}, u32[]{:S(2)}, u32[]{:S(2)}) collective-permute-start(bf16[256,256]{1,0:T(8,128)(2,1)S(1)} %get-tuple-element.39), channel_id=1, source_target_pairs={{0,2},{2,0},{4,6},{6,4},{8,10},{10,8},{12,14},{14,12},{16,18},{18,... | collective-permute-start | bytes 393224 | tf_op jit(solution)/shard_map/ppermute | solution.py:32
  13.7 8.7 %collective-permute-start.5 = (bf16[256,256]{1,0:T(8,128)(2,1)S(1)}, bf16[256,256]{1,0:T(8,128)(2,1)S(1)}, u32[]{:S(2)}, u32[]{:S(2)}) collective-permute-start(bf16[256,256]{1,0:T(8,128)(2,1)S(1)} %get-tuple-element.40), channel_id=1, source_target_pairs={{0,4},{2,6},{4,0},{6,2},{8,12},{10,14},{12,8},{14,10},{16,20},{18,... | collective-permute-start | bytes 393224 | tf_op jit(solution)/shard_map/ppermute | solution.py:32
  14.6 7.9 %collective-permute-start.6 = (bf16[256,256]{1,0:T(8,128)(2,1)S(1)}, bf16[256,256]{1,0:T(8,128)(2,1)S(1)}, u32[]{:S(2)}, u32[]{:S(2)}) collective-permute-start(bf16[256,256]{1,0:T(8,128)(2,1)S(1)} %get-tuple-element.41), channel_id=1, source_target_pairs={{0,6},{2,4},{4,2},{6,0},{8,14},{10,12},{12,10},{14,8},{16,22},{18,... | collective-permute-start | bytes 393224 | tf_op jit(solution)/shard_map/ppermute | solution.py:32
  16.1 14.7 %collective-permute-start.8 = (bf16[256,256]{1,0:T(8,128)(2,1)S(1)}, bf16[256,256]{1,0:T(8,128)(2,1)S(1)}, u32[]{:S(2)}, u32[]{:S(2)}) collective-permute-start(bf16[256,256]{1,0:T(8,128)(2,1)S(1)} %get-tuple-element.45), channel_id=1, source_target_pairs={{0,2},{2,0},{4,6},{6,4},{8,10},{10,8},{12,14},{14,12},{16,18},{18,... | collective-permute-start | bytes 393224 | tf_op jit(solution)/shard_map/ppermute | solution.py:32
  18.6 12.3 %collective-permute-start.9 = (bf16[256,256]{1,0:T(8,128)(2,1)S(1)}, bf16[256,256]{1,0:T(8,128)(2,1)S(1)}, u32[]{:S(2)}, u32[]{:S(2)}) collective-permute-start(bf16[256,256]{1,0:T(8,128)(2,1)S(1)} %get-tuple-element.46), channel_id=1, source_target_pairs={{0,4},{2,6},{4,0},{6,2},{8,12},{10,14},{12,8},{14,10},{16,20},{18,... | collective-permute-start | bytes 393224 | tf_op jit(solution)/shard_map/ppermute | solution.py:32
  22.5 8.4 %collective-permute-start.10 = (bf16[256,256]{1,0:T(8,128)(2,1)S(1)}, bf16[256,256]{1,0:T(8,128)(2,1)S(1)}, u32[]{:S(2)}, u32[]{:S(2)}) collective-permute-start(bf16[256,256]{1,0:T(8,128)(2,1)S(1)} %get-tuple-element.47), channel_id=1, source_target_pairs={{0,6},{2,4},{4,2},{6,0},{8,14},{10,12},{12,10},{14,8},{16,22},{18,... | collective-permute-start | bytes 393224 | tf_op jit(solution)/shard_map/ppermute | solution.py:32
  33.1 11.4 %collective-permute-start.11 = (bf16[4,256,128]{2,1,0:T(8,128)(2,1)S(1)}, bf16[4,256,128]{2,1,0:T(8,128)(2,1)S(1)}, u32[]{:S(2)}, u32[]{:S(2)}) collective-permute-start(bf16[4,256,128]{2,1,0:T(8,128)(2,1)S(1)} %get-tuple-element.51), channel_id=1, source_target_pairs={{8,0},{10,2},{12,4},{14,6},{16,8},{18,10},{20,12},{22,14},{24,16},... | collective-permute-start | bytes 786440 | tf_op jit(solution)/shard_map/ppermute | solution.py:27
  42.1 7.8 %collective-permute-start.15 = (bf16[4,256,128]{2,1,0:T(8,128)(2,1)S(1)}, bf16[4,256,128]{2,1,0:T(8,128)(2,1)S(1)}, u32[]{:S(2)}, u32[]{:S(2)}) collective-permute-start(bf16[4,256,128]{2,1,0:T(8,128)(2,1)S(1)} %get-tuple-element.57), channel_id=1, source_target_pairs={{8,0},{10,2},{12,4},{14,6},{16,8},{18,10},{20,12},{22,14},{24,16},... | collective-permute-start | bytes 786440 | tf_op jit(solution)/shard_map/ppermute | solution.py:27
  46.4 6.8 %collective-permute-start.12 = (bf16[256,256]{1,0:T(8,128)(2,1)S(1)}, bf16[256,256]{1,0:T(8,128)(2,1)S(1)}, u32[]{:S(2)}, u32[]{:S(2)}) collective-permute-start(bf16[256,256]{1,0:T(8,128)(2,1)S(1)} %get-tuple-element.53), channel_id=1, source_target_pairs={{0,2},{2,0},{4,6},{6,4},{8,10},{10,8},{12,14},{14,12},{16,18},{18,... | collective-permute-start | bytes 393224 | tf_op jit(solution)/shard_map/ppermute | solution.py:32
  48.0 9.3 %collective-permute-start.13 = (bf16[256,256]{1,0:T(8,128)(2,1)S(1)}, bf16[256,256]{1,0:T(8,128)(2,1)S(1)}, u32[]{:S(2)}, u32[]{:S(2)}) collective-permute-start(bf16[256,256]{1,0:T(8,128)(2,1)S(1)} %get-tuple-element.54), channel_id=1, source_target_pairs={{0,4},{2,6},{4,0},{6,2},{8,12},{10,14},{12,8},{14,10},{16,20},{18,... | collective-permute-start | bytes 393224 | tf_op jit(solution)/shard_map/ppermute | solution.py:32
  49.5 7.8 %collective-permute-start.14 = (bf16[256,256]{1,0:T(8,128)(2,1)S(1)}, bf16[256,256]{1,0:T(8,128)(2,1)S(1)}, u32[]{:S(2)}, u32[]{:S(2)}) collective-permute-start(bf16[256,256]{1,0:T(8,128)(2,1)S(1)} %get-tuple-element.55), channel_id=1, source_target_pairs={{0,6},{2,4},{4,2},{6,0},{8,14},{10,12},{12,10},{14,8},{16,22},{18,... | collective-permute-start | bytes 393224 | tf_op jit(solution)/shard_map/ppermute | solution.py:32
  50.1 8.2 %collective-permute-start.16 = (bf16[256,256]{1,0:T(8,128)(2,1)S(1)}, bf16[256,256]{1,0:T(8,128)(2,1)S(1)}, u32[]{:S(2)}, u32[]{:S(2)}) collective-permute-start(bf16[256,256]{1,0:T(8,128)(2,1)S(1)} %get-tuple-element.60), channel_id=1, source_target_pairs={{0,2},{2,0},{4,6},{6,4},{8,10},{10,8},{12,14},{14,12},{16,18},{18,... | collective-permute-start | bytes 393224 | tf_op jit(solution)/shard_map/ppermute | solution.py:32
  51.7 9.4 %collective-permute-start.17 = (bf16[256,256]{1,0:T(8,128)(2,1)S(1)}, bf16[256,256]{1,0:T(8,128)(2,1)S(1)}, u32[]{:S(2)}, u32[]{:S(2)}) collective-permute-start(bf16[256,256]{1,0:T(8,128)(2,1)S(1)} %get-tuple-element.61), channel_id=1, source_target_pairs={{0,4},{2,6},{4,0},{6,2},{8,12},{10,14},{12,8},{14,10},{16,20},{18,... | collective-permute-start | bytes 393224 | tf_op jit(solution)/shard_map/ppermute | solution.py:32
  53.2 7.9 %collective-permute-start.18 = (bf16[256,256]{1,0:T(8,128)(2,1)S(1)}, bf16[256,256]{1,0:T(8,128)(2,1)S(1)}, u32[]{:S(2)}, u32[]{:S(2)}) collective-permute-start(bf16[256,256]{1,0:T(8,128)(2,1)S(1)} %get-tuple-element.62), channel_id=1, source_target_pairs={{0,6},{2,4},{4,2},{6,0},{8,14},{10,12},{12,10},{14,8},{16,22},{18,... | collective-permute-start | bytes 393224 | tf_op jit(solution)/shard_map/ppermute | solution.py:32

commit v6 on v4

--- a/solution.py
+++ b/solution.py
@@ -11,6 +11,7 @@
 WINDOW_LENGTH = 1024
 LOG2_E = 1.4426950408889634
 AHEAD = 10**10
+ONES = 16
 
 score_scale = 168.0 ** (-0.5)
 
@@ -59,17 +60,24 @@
     return pl.ds(pl.multiple_of(index * width, width), width)
 
 
-def pack_kv(group, keys, values):
+def begin():
+    def body(out_ref):
+        out_ref[...] = jnp.zeros_like(out_ref)
+
+    return call(body, [jax.ShapeDtypeStruct((8, 128), jnp.float32)], flops=AHEAD)()[0]
+
+
+def pack_kv(group, keys, values, before):
     tokens, width = keys.shape[0], keys.shape[1] // group
 
-    def body(k_ref, v_ref, *refs):
+    def body(k_ref, v_ref, before_ref, *refs):
         for r in range(group):
             member = spot(group)[0] ^ r
             refs[r][:, :width] = k_ref[:, lanes(member, width)]
             refs[r][:, width:] = v_ref[:, lanes(member, width)]
 
     outs = [jax.ShapeDtypeStruct((tokens, 2 * width), jnp.bfloat16)] * group
-    return call(body, outs, flops=AHEAD)(keys, values)
+    return call(body, outs, flops=AHEAD, specs=[VMEM, VMEM, ANY])(keys, values, before)
 
 
 def pack_queries(group, queries, before):
@@ -83,13 +91,18 @@
     return call(body, outs, specs=[VMEM, ANY])(queries, before)
 
 
-def order_pieces(group, pieces):
+def order_kv(group, pieces, before):
+    tokens, width = pieces[0].shape
+    width //= 2
+
     def body(*refs):
         for r in range(group):
-            refs[group][spot(group)[0] ^ r] = refs[r][...]
-
-    outs = [jax.ShapeDtypeStruct((group,) + pieces[0].shape, jnp.bfloat16)]
-    return call(body, outs)(*pieces)[0]
+            member = spot(group)[0] ^ r
+            refs[-2][member] = refs[r][:, :width]
+            refs[-1][member] = refs[r][:, width:]
+
+    outs = [jax.ShapeDtypeStruct((group, tokens, width), jnp.bfloat16)] * 2
+    return call(body, outs, flops=AHEAD, specs=[VMEM] * group + [ANY])(*pieces, before)
 
 
 def head_product(parts, part, out_weight, layer_cotangent, before):
@@ -115,7 +128,7 @@
     )[0]
 
 
-def pack_grads(group, terms):
+def pack_grads(group, terms, before):
     rows, tokens = terms[0].shape
     rows //= group
 
@@ -127,10 +140,10 @@
                 total = total.astype(jnp.float32)
                 for term in refs[1 : len(terms)]:
                     total = total + term[there, :].astype(jnp.float32)
-            refs[len(terms) + r][...] = total.astype(jnp.bfloat16)
+            refs[len(terms) + 1 + r][...] = total.astype(jnp.bfloat16)
 
     outs = [jax.ShapeDtypeStruct((rows, tokens), jnp.bfloat16)] * group
-    return call(body, outs)(*terms)
+    return call(body, outs, specs=[VMEM] * len(terms) + [ANY])(*terms, before)
 
 
 class Shape:
@@ -164,19 +177,19 @@
     return call(body, outs)(*pieces)[0]
 
 
-def softmax(z, kv_own, kv_earlier, qt):
+def softmax(z, k_own, k_earlier, qt):
     factor = score_scale * LOG2_E
 
-    def body(*refs):
-        own_ref, earlier_refs = refs[0], refs[1 : 1 + z.steps]
-        qt_ref, e_ref, inverse_ref, k_all, s_all = refs[1 + z.steps :]
+    def body(own_ref, *refs):
+        earlier_refs = refs[: z.steps]
+        qt_ref, e_ref, k_all, s_all = refs[z.steps :]
         first = spot(z.group)[1]
         key_id = lax.broadcasted_iota(jnp.int32, (z.tokens, z.wide), 0)
         query_id = lax.broadcasted_iota(jnp.int32, (z.tokens, z.wide), 1) & (z.tokens - 1)
         for head in range(z.heads):
-            at_k = slice(head * HEAD_SIZE, (head + 1) * HEAD_SIZE)
-            for number in range(z.total):
-                k_all[number] = z.block(own_ref, earlier_refs, number)[:, at_k]
+            at = slice(head * HEAD_SIZE, (head + 1) * HEAD_SIZE)
+            for number in range(z.total):
+                k_all[number] = z.block(own_ref, earlier_refs, number)[:, at]
 
             @pl.loop(0, z.group)
             def _(b):
@@ -193,40 +206,33 @@
                     if c < z.back:
                         here = jnp.where(first + b + c >= z.back, here, -jnp.inf)
                     top = here if top is None else jnp.maximum(top, here)
-                norm = jnp.zeros((1, z.wide), jnp.float32)
                 for c in range(z.span):
                     base = top
                     if c < z.back:
                         base = jnp.where(first + b + c >= z.back, top, jnp.inf)
-                    e = jnp.exp2((s_all[c] - base) * factor)
-                    norm = norm + jnp.sum(e, axis=0, keepdims=True)
-                    e_ref[head, b, c] = e.astype(jnp.bfloat16)
-                inverse_ref[head, b] = 1.0 / norm
-
-    outs = [
-        jax.ShapeDtypeStruct((z.heads, z.group, z.span, z.tokens, z.wide), jnp.bfloat16),
-        jax.ShapeDtypeStruct((z.heads, z.group, 1, z.wide), jnp.float32),
-    ]
+                    e_ref[head, b, c] = jnp.exp2((s_all[c] - base) * factor).astype(jnp.bfloat16)
+
+    outs = [jax.ShapeDtypeStruct((z.heads, z.group, z.span, z.tokens, z.wide), jnp.bfloat16)]
     scratch = [
         pltpu.VMEM((z.total, z.tokens, HEAD_SIZE), jnp.bfloat16),
         pltpu.VMEM((z.span, z.tokens, z.wide), jnp.float32),
     ]
     return call(body, outs, scratch, flops=2 * z.entries * HEAD_SIZE, exps=z.entries)(
-        kv_own, *kv_earlier, qt
-    )
-
-
-def value_terms(z, e, inverse, grads):
-    def body(e_ref, inverse_ref, *refs):
-        g_refs, (g_ref, own_ref), earlier_refs = (
-            refs[: z.group],
-            refs[z.group : z.group + 2],
-            refs[z.group + 2 : z.group + 2 + z.steps],
-        )
-        dv_all = refs[-1]
+        k_own, *k_earlier, qt
+    )[0]
+
+
+def value_terms(z, e, grads, v_own, v_earlier):
+    def body(e_ref, own_ref, *refs):
+        earlier_refs, g_refs = refs[: z.steps], refs[z.steps : z.steps + z.group]
+        g_ref, inverse_ref, delta_ref, dv_own = refs[z.steps + z.group : z.steps + z.group + 4]
+        dv_earlier, (vt_all, dv_all) = refs[z.steps + z.group + 4 : -2], refs[-2:]
         place = spot(z.group)[0]
+        vt_all[:, HEAD_SIZE:, :] = jnp.ones((z.total, ONES, z.tokens), jnp.bfloat16)
         for head in range(z.heads):
             at = slice(head * HEAD_SIZE, (head + 1) * HEAD_SIZE)
+            for number in range(z.total):
+                vt_all[number, :HEAD_SIZE, :] = z.block(own_ref, earlier_refs, number)[:, at].T
             for r in range(z.group):
                 for j in range(z.per_head):
                     lower = (head * z.per_head + j) * HEAD_SIZE
@@ -237,51 +243,56 @@
 
             @pl.loop(0, z.group)
             def _(b):
-                g = (g_ref[head, b].astype(jnp.float32) * inverse_ref[head, b]).astype(jnp.bfloat16)
-                for c in range(z.span):
-                    dv_all[b + c] += lax.dot_general(
-                        e_ref[head, b, c], g, NT, preferred_element_type=jnp.float32
-                    )
-
-            for number in range(z.total):
-                part = dv_all[number]
-                z.block(own_ref, earlier_refs, number)[:, at] = part.astype(own_ref.dtype if number >= z.back else jnp.bfloat16)
+                out = None
+                for c in range(z.span):
+                    term = lax.dot_general(vt_all[b + c], e_ref[head, b, c], NN, preferred_element_type=jnp.float32)
+                    out = term if out is None else out + term
+                inverse = 1.0 / out[HEAD_SIZE : HEAD_SIZE + 1, :]
+                g = g_ref[head, b].astype(jnp.float32)
+                inverse_ref[head, b] = inverse
+                delta_ref[head, b] = jnp.sum(out[:HEAD_SIZE, :] * g, axis=0, keepdims=True) * inverse
+                g = (g * inverse).astype(jnp.bfloat16)
+                for c in range(z.span):
+                    dv_all[b + c] += lax.dot_general(e_ref[head, b, c], g, NT, preferred_element_type=jnp.float32)
+
+            for number in range(z.total):
+                z.block(dv_own, dv_earlier, number)[:, at] = dv_all[number].astype(
+                    dv_own.dtype if number >= z.back else jnp.bfloat16
+                )
 
     outs = [
         jax.ShapeDtypeStruct((z.heads, z.group, HEAD_SIZE, z.wide), jnp.bfloat16),
+        jax.ShapeDtypeStruct((z.heads, z.group, 1, z.wide), jnp.float32),
+        jax.ShapeDtypeStruct((z.heads, z.group, 1, z.wide), jnp.float32),
         jax.ShapeDtypeStruct((z.group, z.tokens, z.kv_width), jnp.float32),
     ]
     outs += [jax.ShapeDtypeStruct((z.group, z.tokens, z.kv_width), jnp.bfloat16)] * z.steps
-    scratch = [pltpu.VMEM((z.total, z.tokens, HEAD_SIZE), jnp.float32)]
-    results = call(body, outs, scratch, flops=2 * z.entries * HEAD_SIZE)(e, inverse, *grads)
-    return results[0], results[1], results[2:]
-
-
-def key_terms(z, e, inverse, qt, g, kv_own, kv_earlier):
-    def body(e_ref, inverse_ref, qt_ref, g_ref, own_ref, *refs):
+    scratch = [
+        pltpu.VMEM((z.total, HEAD_SIZE + ONES, z.tokens), jnp.bfloat16),
+        pltpu.VMEM((z.total, z.tokens, HEAD_SIZE), jnp.float32),
+    ]
+    results = call(body, outs, scratch, flops=4 * z.entries * HEAD_SIZE)(e, v_own, *v_earlier, *grads)
+    return results[:3], results[3], results[4:]
+
+
+def key_terms(z, e, inverse, delta, qt, g, v_own, v_earlier):
+    def body(e_ref, inverse_ref, delta_ref, qt_ref, g_ref, own_ref, *refs):
         earlier_refs, ds_ref = refs[: z.steps], refs[z.steps]
         dk_own, dk_earlier = refs[z.steps + 1], refs[z.steps + 2 : 2 * z.steps + 2]
-        v_all, dk_all, dp_all = refs[2 * z.steps + 2 :]
+        v_all, dk_all = refs[2 * z.steps + 2 :]
         for head in range(z.heads):
             at = slice(head * HEAD_SIZE, (head + 1) * HEAD_SIZE)
-            at_v = slice(z.kv_width + head * HEAD_SIZE, z.kv_width + (head + 1) * HEAD_SIZE)
-            for number in range(z.total):
-                v_all[number] = z.block(own_ref, earlier_refs, number)[:, at_v]
+            for number in range(z.total):
+                v_all[number] = z.block(own_ref, earlier_refs, number)[:, at]
             dk_all[...] = jnp.zeros_like(dk_all)
 
             @pl.loop(0, z.group)
             def _(b):
                 g = g_ref[head, b]
-                inverse = inverse_ref[head, b]
-                delta = jnp.zeros((1, z.wide), jnp.float32)
+                q = (qt_ref[head, b].astype(jnp.float32) * inverse_ref[head, b]).astype(jnp.bfloat16)
                 for c in range(z.span):
                     dp = lax.dot_general(v_all[b + c], g, NN, preferred_element_type=jnp.float32)
-                    delta = delta + jnp.sum(e_ref[head, b, c].astype(jnp.float32) * dp, axis=0, keepdims=True)
-                    dp_all[c] = dp
-                delta = delta * inverse
-                q = (qt_ref[head, b].astype(jnp.float32) * inverse).astype(jnp.bfloat16)
-                for c in range(z.span):
-                    ds = (e_ref[head, b, c].astype(jnp.float32) * (dp_all[c] - delta)).astype(jnp.bfloat16)
+                    ds = e_ref[head, b, c] * (dp - delta_ref[head, b]).astype(jnp.bfloat16)
                     ds_ref[head, b, c] = ds
                     dk_all[b + c] += lax.dot_general(ds, q, NT, preferred_element_type=jnp.float32)
 
@@ -297,15 +308,14 @@
     scratch = [
         pltpu.VMEM((z.total, z.tokens, HEAD_SIZE), jnp.bfloat16),
         pltpu.VMEM((z.total, z.tokens, HEAD_SIZE), jnp.float32),
-        pltpu.VMEM((z.span, z.tokens, z.wide), jnp.float32),
     ]
     results = call(body, outs, scratch, flops=4 * z.entries * HEAD_SIZE)(
-        e, inverse, qt, g, kv_own, *kv_earlier
+        e, inverse, delta, qt, g, v_own, *v_earlier
     )
     return results[0], results[1], results[2:]
 
 
-def query_terms(z, ds, inverse, kv_own, kv_earlier, dv_terms):
+def query_terms(z, ds, inverse, k_own, k_earlier, dv_terms):
     def body(ds_ref, inverse_ref, own_ref, *refs):
         earlier_refs, term_refs, dv_ref = refs[: z.steps], refs[z.steps : 2 * z.steps + 1], refs[2 * z.steps + 1]
         dq_refs = refs[2 * z.steps + 2 : 2 * z.steps + 2 + z.group]
@@ -343,7 +353,7 @@
         pltpu.VMEM((z.group, z.tokens, z.width), jnp.bfloat16),
     ]
     results = call(body, outs, scratch, flops=2 * z.entries * HEAD_SIZE)(
-        ds, inverse, kv_own, *kv_earlier, *dv_terms
+        ds, inverse, k_own, *k_earlier, *dv_terms
     )
     return results[0], results[1:]
 
@@ -404,25 +414,30 @@
             shifted(earlier[number], "ctx", -group * (back_groups - number)) for number in range(back_groups)
         ]
 
-    sent = pack_kv(group, keys, values)
-    kv_own = order_pieces(group, trade(sent))
-    kv_earlier = [shifted(kv_own, "ctx", group * step) for step in range(back_groups, 0, -1)]
+    sent = pack_kv(group, keys, values, begin())
+    kv_pieces = trade(sent)
     z = Shape(group, back_groups, heads, per_head, tokens)
     query_sent = pack_queries(group, queries, sent[0])
-    qt = turn_queries(z, trade(query_sent))
+    query_pieces = trade(query_sent)
     if tp_count == 2:
         other = head_product(2, 1, out_weight, layer_cotangent, [query_sent[0]])
-        terms = [head_product(2, 0, out_weight, layer_cotangent, [kv_own, other]), swapped(other, "tp", 1)]
+        mine = head_product(2, 0, out_weight, layer_cotangent, [other])
+        terms = [mine, swapped(other, "tp", 1)]
     else:
-        product = head_product(1, 0, out_weight, layer_cotangent, [query_sent[0]])
-        terms = [lax.psum_scatter(product, "tp", scatter_dimension=0, tiled=True)]
-    grads = trade(pack_grads(group, terms))
-    e, inverse = softmax(z, kv_own, kv_earlier, qt)
-    g, dv_own, dv_earlier = value_terms(z, e, inverse, grads)
+        mine = head_product(1, 0, out_weight, layer_cotangent, [query_sent[0]])
+        terms = [lax.psum_scatter(mine, "tp", scatter_dimension=0, tiled=True)]
+    k_own, v_own = order_kv(group, kv_pieces, mine)
+    k_earlier, v_earlier = (
+        [shifted(own, "ctx", group * step) for step in range(back_groups, 0, -1)] for own in (k_own, v_own)
+    )
+    qt = turn_queries(z, query_pieces)
+    grads = trade(pack_grads(group, terms, k_own))
+    e = softmax(z, k_own, k_earlier, qt)
+    (g, inverse, delta), dv_own, dv_earlier = value_terms(z, e, grads, v_own, v_earlier)
     dv_terms = [dv_own] + returned(dv_earlier)
-    ds, dk_own, dk_earlier = key_terms(z, e, inverse, qt, g, kv_own, kv_earlier)
+    ds, dk_own, dk_earlier = key_terms(z, e, inverse, delta, qt, g, v_own, v_earlier)
     dk_terms = [dk_own] + returned(dk_earlier)
-    dv, dq = query_terms(z, ds, inverse, kv_own, kv_earlier, dv_terms)
+    dv, dq = query_terms(z, ds, inverse, k_own, k_earlier, dv_terms)
     dq = trade(dq)
     dkv = trade(pack_terms(group, [dk_terms, [dv]]))
     (query_grads,) = unpack(group, dq, [dq[0].shape[1]])

time: 58.9 us -> 61.8 us (1.049)
  starting transfers between devices: 25.2 us -> 28.9 us
  local copies, waits for them, and re-layouts: 2.74 us -> 1.28 us
    ppermute x3 -> x4, starting transfers between devices: 6.03 us -> 11.1 us  [shifted(): lax.ppermute(value, axis, [(source, source + steps) for source in range(l...]
    ppermute x16, waiting for transfers between devices: 7.48 us -> 9.96 us  [swapped(): lax.ppermute(value, axis, [(source, source ^ bits) for source in range(co...]
    ppermute x3 -> x4, waiting for transfers between devices: 2.36 us -> 0.01 us  [shifted(): lax.ppermute(value, axis, [(source, source + steps) for source in range(l...]
    unnamed x10 -> x14, local copies, waits for them, and re-layouts: 2.74 us -> 1.28 us
    ppermute x16, starting transfers between devices: 19.2 us -> 17.8 us  [swapped(): lax.ppermute(value, axis, [(source, source ^ bits) for source in range(co...]
    pallas_call x14 -> x15, Pallas kernels: 19.7 us -> 20.3 us  [run(): pl.pallas_call(body, out_shape=tuple(outs), in_specs=specs or [SMEM if a....]
  transfers between devices with their start and end apart: 19 -> 20, of which waited for: 6 -> 7; matrix products, arithmetic and copies ran while one was open for 0% -> 0% of each run, Pallas kernels for 28% -> 25%
where the time goes in v6:
time: 61.8 us; the launch traced here: 61.3 us
  starting transfers between devices  28.9 us (47%)
  Pallas kernels  20.3 us (33%)
  waiting for transfers between devices  9.97 us (16%)
  local copies, waits for them, and re-layouts  1.28 us (2%)
  between operations  0.88 us (1%)
    pallas_call x15, Pallas kernels, run(): pl.pallas_call(body, out_shape=tuple(outs), in_specs=specs or [SMEM if a....  20.3 us
    ppermute x16, starting transfers between devices, swapped(): lax.ppermute(value, axis, [(source, source ^ bits) for source in range(co...  17.8 us
    ppermute x4, starting transfers between devices, shifted(): lax.ppermute(value, axis, [(source, source + steps) for source in range(l...  11.1 us
    ppermute x16, waiting for transfers between devices, swapped(): lax.ppermute(value, axis, [(source, source ^ bits) for source in range(co...  9.96 us
    unnamed x14, local copies, waits for them, and re-layouts  1.28 us
  transfers between devices with their start and end apart: 20, of which 7 were waited for; matrix products, arithmetic and copies ran while one was open for 0% of the time, Pallas kernels for 25%

profile of v6, /device:TPU:24, one launch (start us, length us, event | category | flops | bytes accessed | tf_op | source)
XLA Modules:
  0.0 61.3 jit_solution(3494972509008875970)
XLA Ops:
  0.7 0.9 %copy-done.3 = bf16[256,512]{1,0:T(8,128)(2,1)S(1)} copy-done((bf16[256,512]{1,0:T(8,128)(2,1)S(1)}, bf16[256,512]{1,0:T(8,128)(2,1)}, u32[]{:S(2)}) %copy-start.3) | copy-done | bytes 262168
  1.8 1.6 %collective-permute-start = (bf16[256,256]{1,0:T(8,128)(2,1)S(1)}, bf16[256,256]{1,0:T(8,128)(2,1)S(1)}, u32[]{:S(2)}, u32[]{:S(2)}) collective-permute-start(bf16[256,256]{1,0:T(8,128)(2,1)S(1)} %get-tuple-element.37), channel_id=1, source_target_pairs={{0,2},{2,0},{4,6},{6,4},{8,10},{10,8},{12,14},{14,12},{16,18},{18,... | collective-permute-start | bytes 393224 | tf_op jit(solution)/shard_map/ppermute | solution.py:33
  3.3 1.5 %collective-permute-start.1 = (bf16[256,256]{1,0:T(8,128)(2,1)S(1)}, bf16[256,256]{1,0:T(8,128)(2,1)S(1)}, u32[]{:S(2)}, u32[]{:S(2)}) collective-permute-start(bf16[256,256]{1,0:T(8,128)(2,1)S(1)} %get-tuple-element.38), channel_id=1, source_target_pairs={{0,4},{2,6},{4,0},{6,2},{8,12},{10,14},{12,8},{14,10},{16,20},{18,... | collective-permute-start | bytes 393224 | tf_op jit(solution)/shard_map/ppermute | solution.py:33
  5.7 1.9 %shard_map.79.refs_0_ = bf16[1024,256]{1,0:T(8,128)(2,1)S(1)} custom-call(bf16[2048,2688]{1,0:T(8,128)(2,1)S(1)} %bitcast.1, bf16[256,2688]{1,0:T(8,128)(2,1)S(1)} %copy-done, bf16[256,256]{1,0:T(8,128)(2,1)S(1)} %get-tuple-element.40.refs_0_), custom_call_target="tpu_custom_call" | custom-call | flops 1409286144 | bytes 13041664 | tf_op jit(solution)/shard_map/pallas_call | solution.py:40
  7.7 1.9 %shard_map.80.refs_4_.refs_0_ = bf16[1024,256]{1,0:T(8,128)(2,1)S(1)} custom-call(bf16[2048,2688]{1,0:T(8,128)(2,1)S(1)} %bitcast.1, bf16[256,2688]{1,0:T(8,128)(2,1)S(1)} %copy-done, bf16[1024,256]{1,0:T(8,128)(2,1)S(1)} %shard_map.79.refs_0_), custom_call_target="tpu_custom_call" | custom-call | flops 1409286144 | bytes 13434880 | tf_op jit(solution)/shard_map/pallas_call | solution.py:40
  9.6 1.5 %collective-permute-done.1.refs_2_ = bf16[256,256]{1,0:T(8,128)(2,1)S(1)} collective-permute-done((bf16[256,256]{1,0:T(8,128)(2,1)S(1)}, bf16[256,256]{1,0:T(8,128)(2,1)S(1)}, u32[]{:S(2)}, u32[]{:S(2)}) %collective-permute-start.1) | collective-permute-done | bytes 131104 | tf_op jit(solution)/shard_map/ppermute | solution.py:33
  11.2 1.3 %collective-permute-start.3 = (bf16[4,256,128]{2,1,0:T(8,128)(2,1)S(1)}, bf16[4,256,128]{2,1,0:T(8,128)(2,1)S(1)}, u32[]{:S(2)}, u32[]{:S(2)}) collective-permute-start(bf16[4,256,128]{2,1,0:T(8,128)(2,1)S(1)} %get-tuple-element.41.own_ref.refs_2_), channel_id=1, source_target_pairs={{0,8},{2,10},{4,12},{6,14},{8,16},{10,18},{12,20},{14,22},{16,24},... | collective-permute-start | bytes 786440 | tf_op jit(solution)/shard_map/ppermute | solution.py:28
  12.5 1.3 %collective-permute-start.4 = (bf16[256,256]{1,0:T(8,128)(2,1)S(1)}, bf16[256,256]{1,0:T(8,128)(2,1)S(1)}, u32[]{:S(2)}, u32[]{:S(2)}) collective-permute-start(bf16[256,256]{1,0:T(8,128)(2,1)S(1)} %get-tuple-element.42), channel_id=1, source_target_pairs={{0,2},{2,0},{4,6},{6,4},{8,10},{10,8},{12,14},{14,12},{16,18},{18,... | collective-permute-start | bytes 393224 | tf_op jit(solution)/shard_map/ppermute | solution.py:33
  13.8 0.8 %collective-permute-start.5 = (bf16[256,256]{1,0:T(8,128)(2,1)S(1)}, bf16[256,256]{1,0:T(8,128)(2,1)S(1)}, u32[]{:S(2)}, u32[]{:S(2)}) collective-permute-start(bf16[256,256]{1,0:T(8,128)(2,1)S(1)} %get-tuple-element.43), channel_id=1, source_target_pairs={{0,4},{2,6},{4,0},{6,2},{8,12},{10,14},{12,8},{14,10},{16,20},{18,... | collective-permute-start | bytes 393224 | tf_op jit(solution)/shard_map/ppermute | solution.py:33
  14.6 1.3 %collective-permute-start.7 = (bf16[4,256,128]{2,1,0:T(8,128)(2,1)S(1)}, bf16[4,256,128]{2,1,0:T(8,128)(2,1)S(1)}, u32[]{:S(2)}, u32[]{:S(2)}) collective-permute-start(bf16[4,256,128]{2,1,0:T(8,128)(2,1)S(1)} %get-tuple-element.45.own_ref), channel_id=1, source_target_pairs={{0,8},{2,10},{4,12},{6,14},{8,16},{10,18},{12,20},{14,22},{16,24},... | collective-permute-start | bytes 786440 | tf_op jit(solution)/shard_map/ppermute | solution.py:28
  15.9 1.5 %collective-permute-start.6 = (bf16[256,256]{1,0:T(8,128)(2,1)S(1)}, bf16[256,256]{1,0:T(8,128)(2,1)S(1)}, u32[]{:S(2)}, u32[]{:S(2)}) collective-permute-start(bf16[256,256]{1,0:T(8,128)(2,1)S(1)} %get-tuple-element.44), channel_id=1, source_target_pairs={{0,6},{2,4},{4,2},{6,0},{8,14},{10,12},{12,10},{14,8},{16,22},{18,... | collective-permute-start | bytes 393224 | tf_op jit(solution)/shard_map/ppermute | solution.py:33
  17.6 1.5 %collective-permute-start.9 = (bf16[256,256]{1,0:T(8,128)(2,1)S(1)}, bf16[256,256]{1,0:T(8,128)(2,1)S(1)}, u32[]{:S(2)}, u32[]{:S(2)}) collective-permute-start(bf16[256,256]{1,0:T(8,128)(2,1)S(1)} %get-tuple-element.47), channel_id=1, source_target_pairs={{0,2},{2,0},{4,6},{6,4},{8,10},{10,8},{12,14},{14,12},{16,18},{18,... | collective-permute-start | bytes 393224 | tf_op jit(solution)/shard_map/ppermute | solution.py:33
  19.0 2.1 %collective-permute-start.10 = (bf16[256,256]{1,0:T(8,128)(2,1)S(1)}, bf16[256,256]{1,0:T(8,128)(2,1)S(1)}, u32[]{:S(2)}, u32[]{:S(2)}) collective-permute-start(bf16[256,256]{1,0:T(8,128)(2,1)S(1)} %get-tuple-element.48), channel_id=1, source_target_pairs={{0,4},{2,6},{4,0},{6,2},{8,12},{10,14},{12,8},{14,10},{16,20},{18,... | collective-permute-start | bytes 393224 | tf_op jit(solution)/shard_map/ppermute | solution.py:33
  21.1 2.0 %collective-permute-done.6.refs_3_ = bf16[256,256]{1,0:T(8,128)(2,1)S(1)} collective-permute-done((bf16[256,256]{1,0:T(8,128)(2,1)S(1)}, bf16[256,256]{1,0:T(8,128)(2,1)S(1)}, u32[]{:S(2)}, u32[]{:S(2)}) %collective-permute-start.6) | collective-permute-done | bytes 131104 | tf_op jit(solution)/shard_map/ppermute | solution.py:33
  23.1 0.9 %collective-permute-start.11 = (bf16[256,256]{1,0:T(8,128)(2,1)S(1)}, bf16[256,256]{1,0:T(8,128)(2,1)S(1)}, u32[]{:S(2)}, u32[]{:S(2)}) collective-permute-start(bf16[256,256]{1,0:T(8,128)(2,1)S(1)} %get-tuple-element.49), channel_id=1, source_target_pairs={{0,6},{2,4},{4,2},{6,0},{8,14},{10,12},{12,10},{14,8},{16,22},{18,... | collective-permute-start | bytes 393224 | tf_op jit(solution)/shard_map/ppermute | solution.py:33
  24.2 3.3 %shard_map.83.e_ref = bf16[1,4,5,256,512]{4,3,2,1,0:T(8,128)(2,1)S(1)} custom-call(bf16[4,256,128]{2,1,0:T(8,128)(2,1)S(1)} %get-tuple-element.41.own_ref.refs_2_, bf16[4,256,128]{2,1,0:T(8,128)(2,1)S(1)} %collective-permute-done.3.refs_0_, bf16[1,4,128,512]{3,2,1,0:T(8,128)(2,1)S(1)} %shard_map.82.refs_1_.qt_ref), custom_call_target="tpu_custom_call" | custom-call | flops 671088640 | bytes 6291456 | tf_op jit(solution)/shard_map/pallas_call | solution.py:40
  27.6 1.4 %collective-permute-done.11.refs_4_ = bf16[256,256]{1,0:T(8,128)(2,1)S(1)} collective-permute-done((bf16[256,256]{1,0:T(8,128)(2,1)S(1)}, bf16[256,256]{1,0:T(8,128)(2,1)S(1)}, u32[]{:S(2)}, u32[]{:S(2)}) %collective-permute-start.11) | collective-permute-done | bytes 131104 | tf_op jit(solution)/shard_map/ppermute | solution.py:33
  29.0 3.8 %shard_map.85 = (bf16[1,4,128,512]{3,2,1,0:T(8,128)(2,1)S(1)}, f32[1,4,1,512]{3,2,1,0:T(1,128)S(1)}, f32[1,4,1,512]{3,2,1,0:T(1,128)S(1)}, f32[4,256,128]{2,1,0:T(8,128)S(1)}, bf16[4,256,128]{2,1,0:T(8,128)(2,1)S(1)}) custom-call(bf16[1,4,5,256,512]{4,3,2,1,0:T(8,128)(2,1)S(1)} %shard_map.83.e_ref, bf16[4,256,128]{2,1,0:T(8,128)(2,1)S(1)} %get-tuple-element.45.own_ref, ...), custom_call_target="tpu_custom_call" | custom-call | flops 1342177280 | bytes 7618560 | tf_op jit(solution)/shard_map/pallas_call | solution.py:40
  32.8 4.9 %collective-permute-start.12 = (bf16[4,256,128]{2,1,0:T(8,128)(2,1)S(1)}, bf16[4,256,128]{2,1,0:T(8,128)(2,1)S(1)}, u32[]{:S(2)}, u32[]{:S(2)}) collective-permute-start(bf16[4,256,128]{2,1,0:T(8,128)(2,1)S(1)} %get-tuple-element.55), channel_id=1, source_target_pairs={{8,0},{10,2},{12,4},{14,6},{16,8},{18,10},{20,12},{22,14},{24,16},... | collective-permute-start | bytes 786440 | tf_op jit(solution)/shard_map/ppermute | solution.py:28
  37.8 5.0 %shard_map.86 = (bf16[1,4,5,256,512]{4,3,2,1,0:T(8,128)(2,1)S(1)}, f32[4,256,128]{2,1,0:T(8,128)S(1)}, bf16[4,256,128]{2,1,0:T(8,128)(2,1)S(1)}) custom-call(bf16[1,4,5,256,512]{4,3,2,1,0:T(8,128)(2,1)S(1)} %shard_map.83.e_ref, f32[1,4,1,512]{3,2,1,0:T(1,128)S(1)} %get-tuple-element.50.inverse_ref, f32[1,4,1,512]{3,2,1,0:T(1,128)S(1)} %get-tuple-element.51.delta_ref, ...), custom_call_target="tpu_custom_call" | custom-call | flops 1342177280 | bytes 12861440 | tf_op jit(solution)/shard_map/pallas_call | solution.py:40
  42.8 3.6 %collective-permute-start.16 = (bf16[4,256,128]{2,1,0:T(8,128)(2,1)S(1)}, bf16[4,256,128]{2,1,0:T(8,128)(2,1)S(1)}, u32[]{:S(2)}, u32[]{:S(2)}) collective-permute-start(bf16[4,256,128]{2,1,0:T(8,128)(2,1)S(1)} %get-tuple-element.61), channel_id=1, source_target_pairs={{8,0},{10,2},{12,4},{14,6},{16,8},{18,10},{20,12},{22,14},{24,16},... | collective-permute-start | bytes 786440 | tf_op jit(solution)/shard_map/ppermute | solution.py:28
  46.5 1.9 %shard_map.87 = (bf16[4,256,128]{2,1,0:T(8,128)(2,1)S(1)}, bf16[256,256]{1,0:T(8,128)(2,1)S(1)}, bf16[256,256]{1,0:T(8,128)(2,1)S(1)}, bf16[256,256]{1,0:T(8,128)(2,1)S(1)}, bf16[256,256]{1,0:T(8,128)(2,1)S(1)}) custom-call(bf16[1,4,5,256,512]{4,3,2,1,0:T(8,128)(2,1)S(1)} %get-tuple-element.53.ds_ref, f32[1,4,1,512]{3,2,1,0:T(1,128)S(1)} %get-tuple-element.50.inverse_ref, ...), custom_call_target="tpu_custom_call" | custom-call | flops 671088640 | bytes 7348224 | tf_op jit(solution)/shard_map/pallas_call | solution.py:40
  48.4 0.9 %collective-permute-start.13 = (bf16[256,256]{1,0:T(8,128)(2,1)S(1)}, bf16[256,256]{1,0:T(8,128)(2,1)S(1)}, u32[]{:S(2)}, u32[]{:S(2)}) collective-permute-start(bf16[256,256]{1,0:T(8,128)(2,1)S(1)} %get-tuple-element.57), channel_id=1, source_target_pairs={{0,2},{2,0},{4,6},{6,4},{8,10},{10,8},{12,14},{14,12},{16,18},{18,... | collective-permute-start | bytes 393224 | tf_op jit(solution)/shard_map/ppermute | solution.py:33
  49.2 0.6 collective-permute-start.14
  49.8 2.1 %collective-permute-start.15 = (bf16[256,256]{1,0:T(8,128)(2,1)S(1)}, bf16[256,256]{1,0:T(8,128)(2,1)S(1)}, u32[]{:S(2)}, u32[]{:S(2)}) collective-permute-start(bf16[256,256]{1,0:T(8,128)(2,1)S(1)} %get-tuple-element.59), channel_id=1, source_target_pairs={{0,6},{2,4},{4,2},{6,0},{8,14},{10,12},{12,10},{14,8},{16,22},{18,... | collective-permute-start | bytes 393224 | tf_op jit(solution)/shard_map/ppermute | solution.py:33
  52.0 0.9 %collective-permute-start.17 = (bf16[256,256]{1,0:T(8,128)(2,1)S(1)}, bf16[256,256]{1,0:T(8,128)(2,1)S(1)}, u32[]{:S(2)}, u32[]{:S(2)}) collective-permute-start(bf16[256,256]{1,0:T(8,128)(2,1)S(1)} %get-tuple-element.64), channel_id=1, source_target_pairs={{0,2},{2,0},{4,6},{6,4},{8,10},{10,8},{12,14},{14,12},{16,18},{18,... | collective-permute-start | bytes 393224 | tf_op jit(solution)/shard_map/ppermute | solution.py:33
  53.5 1.1 %collective-permute-done.13.refs_1_ = bf16[256,256]{1,0:T(8,128)(2,1)S(1)} collective-permute-done((bf16[256,256]{1,0:T(8,128)(2,1)S(1)}, bf16[256,256]{1,0:T(8,128)(2,1)S(1)}, u32[]{:S(2)}, u32[]{:S(2)}) %collective-permute-start.13) | collective-permute-done | bytes 131104 | tf_op jit(solution)/shard_map/ppermute | solution.py:33
  54.6 1.1 %collective-permute-start.19 = (bf16[256,256]{1,0:T(8,128)(2,1)S(1)}, bf16[256,256]{1,0:T(8,128)(2,1)S(1)}, u32[]{:S(2)}, u32[]{:S(2)}) collective-permute-start(bf16[256,256]{1,0:T(8,128)(2,1)S(1)} %get-tuple-element.66), channel_id=1, source_target_pairs={{0,6},{2,4},{4,2},{6,0},{8,14},{10,12},{12,10},{14,8},{16,22},{18,... | collective-permute-start | bytes 393224 | tf_op jit(solution)/shard_map/ppermute | solution.py:33
  55.7 0.9 %collective-permute-done.14.refs_2_ = bf16[256,256]{1,0:T(8,128)(2,1)S(1)} collective-permute-done((bf16[256,256]{1,0:T(8,128)(2,1)S(1)}, bf16[256,256]{1,0:T(8,128)(2,1)S(1)}, u32[]{:S(2)}, u32[]{:S(2)}) %collective-permute-start.14) | collective-permute-done | bytes 131104 | tf_op jit(solution)/shard_map/ppermute | solution.py:33
  56.5 0.9 %shard_map.88 = bf16[256,1024]{1,0:T(8,128)(2,1)} custom-call(bf16[256,256]{1,0:T(8,128)(2,1)S(1)} %get-tuple-element.56.refs_0_, bf16[256,256]{1,0:T(8,128)(2,1)S(1)} %collective-permute-done.13.refs_1_, bf16[256,256]{1,0:T(8,128)(2,1)S(1)} %collective-permute-done.14.refs_2_, bf16[256,256]{1,0:T(8,128)(2,1)S(1)} %collective-permute-done.15.refs_3_), custom_call_target="tpu_custom_call" | custom-call | bytes 1048576 | tf_op jit(solution)/shard_map/pallas_call | solution.py:40
  57.9 2.5 %collective-permute-done.19.refs_3_ = bf16[256,256]{1,0:T(8,128)(2,1)S(1)} collective-permute-done((bf16[256,256]{1,0:T(8,128)(2,1)S(1)}, bf16[256,256]{1,0:T(8,128)(2,1)S(1)}, u32[]{:S(2)}, u32[]{:S(2)}) %collective-permute-start.19) | collective-permute-done | bytes 131104 | tf_op jit(solution)/shard_map/ppermute | solution.py:33
  60.4 0.9 %shard_map.90 = (bf16[256,512]{1,0:T(8,128)(2,1)}, bf16[256,512]{1,0:T(8,128)(2,1)}) custom-call(bf16[256,256]{1,0:T(8,128)(2,1)S(1)} %get-tuple-element.63.refs_0_, bf16[256,256]{1,0:T(8,128)(2,1)S(1)} %collective-permute-done.17.refs_1_, bf16[256,256]{1,0:T(8,128)(2,1)S(1)} %collective-permute-done.18.refs_2_, ...), custom_call_target="tpu_custom_call" | custom-call | bytes 1048576 | tf_op jit(solution)/shard_map/pallas_call | solution.py:40
  (38 shorter events, 2.7 us)
Async XLA Ops:
  0.6 1.0 %copy-start.3 = (bf16[256,512]{1,0:T(8,128)(2,1)S(1)}, bf16[256,512]{1,0:T(8,128)(2,1)}, u32[]{:S(2)}) copy-start(bf16[256,512]{1,0:T(8,128)(2,1)} %v_ref.1) | copy-start | bytes 786436
  0.6 1.0 %copy-start.2 = (bf16[256,512]{1,0:T(8,128)(2,1)S(1)}, bf16[256,512]{1,0:T(8,128)(2,1)}, u32[]{:S(2)}) copy-start(bf16[256,512]{1,0:T(8,128)(2,1)} %k_ref.1) | copy-start | bytes 786436
  0.7 4.7 %slice-start = ((s8[11010048]{0:T(1024)(128)(4,1)}), s8[4194304]{0:T(1024)(128)(4,1)S(1)}, s32[]{:S(2)}) async-start(s8[11010048]{0:T(1024)(128)(4,1)} %bitcast), calls=%async_computation | async-start | bytes 8388608
  0.7 4.7 %slice-start.1 = ((s8[11010048]{0:T(1024)(128)(4,1)}), s8[4194304]{0:T(1024)(128)(4,1)S(1)}, s32[]{:S(2)}) async-start(s8[11010048]{0:T(1024)(128)(4,1)} %bitcast), calls=%async_computation.1 | async-start | bytes 8388608
  1.7 3.7 %copy-start.1 = (bf16[256,1024]{1,0:T(8,128)(2,1)S(1)}, bf16[256,1024]{1,0:T(8,128)(2,1)}, u32[]{:S(2)}) copy-start(bf16[256,1024]{1,0:T(8,128)(2,1)} %q_ref.1) | copy-start | bytes 1572868
  1.7 3.8 %slice-start.2 = ((s8[11010048]{0:T(1024)(128)(4,1)}), s8[2621440]{0:T(1024)(128)(4,1)S(1)}, s32[]{:S(2)}) async-start(s8[11010048]{0:T(1024)(128)(4,1)} %bitcast), calls=%async_computation.2 | async-start | bytes 5242880
  1.7 4.0 %copy-start = (bf16[256,2688]{1,0:T(8,128)(2,1)S(1)}, bf16[256,2688]{1,0:T(8,128)(2,1)}, u32[]{:S(2)}) copy-start(bf16[256,2688]{1,0:T(8,128)(2,1)} %c_ref.3) | copy-start | bytes 4128772
  1.8 7.8 %collective-permute-start = (bf16[256,256]{1,0:T(8,128)(2,1)S(1)}, bf16[256,256]{1,0:T(8,128)(2,1)S(1)}, u32[]{:S(2)}, u32[]{:S(2)}) collective-permute-start(bf16[256,256]{1,0:T(8,128)(2,1)S(1)} %get-tuple-element.37), channel_id=1, source_target_pairs={{0,2},{2,0},{4,6},{6,4},{8,10},{10,8},{12,14},{14,12},{16,18},{18,... | collective-permute-start | bytes 393224 | tf_op jit(solution)/shard_map/ppermute | solution.py:33
  3.3 7.8 %collective-permute-start.1 = (bf16[256,256]{1,0:T(8,128)(2,1)S(1)}, bf16[256,256]{1,0:T(8,128)(2,1)S(1)}, u32[]{:S(2)}, u32[]{:S(2)}) collective-permute-start(bf16[256,256]{1,0:T(8,128)(2,1)S(1)} %get-tuple-element.38), channel_id=1, source_target_pairs={{0,4},{2,6},{4,0},{6,2},{8,12},{10,14},{12,8},{14,10},{16,20},{18,... | collective-permute-start | bytes 393224 | tf_op jit(solution)/shard_map/ppermute | solution.py:33
  4.8 6.3 %collective-permute-start.2 = (bf16[256,256]{1,0:T(8,128)(2,1)S(1)}, bf16[256,256]{1,0:T(8,128)(2,1)S(1)}, u32[]{:S(2)}, u32[]{:S(2)}) collective-permute-start(bf16[256,256]{1,0:T(8,128)(2,1)S(1)} %get-tuple-element.39), channel_id=1, source_target_pairs={{0,6},{2,4},{4,2},{6,0},{8,14},{10,12},{12,10},{14,8},{16,22},{18,... | collective-permute-start | bytes 393224 | tf_op jit(solution)/shard_map/ppermute | solution.py:33
  7.6 8.3 %collective-permute-start.8 = (bf16[1024,256]{1,0:T(8,128)(2,1)S(1)}, bf16[1024,256]{1,0:T(8,128)(2,1)S(1)}, u32[]{:S(2)}, u32[]{:S(2)}) collective-permute-start(bf16[1024,256]{1,0:T(8,128)(2,1)S(1)} %shard_map.79.refs_0_), channel_id=1, source_target_pairs={{0,1},{1,0},{2,3},{3,2},{4,5},{5,4},{6,7},{7,6},{8,9},{9,8},{10,11... | collective-permute-start | bytes 1572872 | tf_op jit(solution)/shard_map/ppermute | solution.py:33
  11.2 13.0 %collective-permute-start.3 = (bf16[4,256,128]{2,1,0:T(8,128)(2,1)S(1)}, bf16[4,256,128]{2,1,0:T(8,128)(2,1)S(1)}, u32[]{:S(2)}, u32[]{:S(2)}) collective-permute-start(bf16[4,256,128]{2,1,0:T(8,128)(2,1)S(1)} %get-tuple-element.41.own_ref.refs_2_), channel_id=1, source_target_pairs={{0,8},{2,10},{4,12},{6,14},{8,16},{10,18},{12,20},{14,22},{16,24},... | collective-permute-start | bytes 786440 | tf_op jit(solution)/shard_map/ppermute | solution.py:28
  12.5 5.0 %collective-permute-start.4 = (bf16[256,256]{1,0:T(8,128)(2,1)S(1)}, bf16[256,256]{1,0:T(8,128)(2,1)S(1)}, u32[]{:S(2)}, u32[]{:S(2)}) collective-permute-start(bf16[256,256]{1,0:T(8,128)(2,1)S(1)} %get-tuple-element.42), channel_id=1, source_target_pairs={{0,2},{2,0},{4,6},{6,4},{8,10},{10,8},{12,14},{14,12},{16,18},{18,... | collective-permute-start | bytes 393224 | tf_op jit(solution)/shard_map/ppermute | solution.py:33
  13.8 5.3 %collective-permute-start.5 = (bf16[256,256]{1,0:T(8,128)(2,1)S(1)}, bf16[256,256]{1,0:T(8,128)(2,1)S(1)}, u32[]{:S(2)}, u32[]{:S(2)}) collective-permute-start(bf16[256,256]{1,0:T(8,128)(2,1)S(1)} %get-tuple-element.43), channel_id=1, source_target_pairs={{0,4},{2,6},{4,0},{6,2},{8,12},{10,14},{12,8},{14,10},{16,20},{18,... | collective-permute-start | bytes 393224 | tf_op jit(solution)/shard_map/ppermute | solution.py:33
  14.6 12.9 %collective-permute-start.7 = (bf16[4,256,128]{2,1,0:T(8,128)(2,1)S(1)}, bf16[4,256,128]{2,1,0:T(8,128)(2,1)S(1)}, u32[]{:S(2)}, u32[]{:S(2)}) collective-permute-start(bf16[4,256,128]{2,1,0:T(8,128)(2,1)S(1)} %get-tuple-element.45.own_ref), channel_id=1, source_target_pairs={{0,8},{2,10},{4,12},{6,14},{8,16},{10,18},{12,20},{14,22},{16,24},... | collective-permute-start | bytes 786440 | tf_op jit(solution)/shard_map/ppermute | solution.py:28
  15.9 7.2 %collective-permute-start.6 = (bf16[256,256]{1,0:T(8,128)(2,1)S(1)}, bf16[256,256]{1,0:T(8,128)(2,1)S(1)}, u32[]{:S(2)}, u32[]{:S(2)}) collective-permute-start(bf16[256,256]{1,0:T(8,128)(2,1)S(1)} %get-tuple-element.44), channel_id=1, source_target_pairs={{0,6},{2,4},{4,2},{6,0},{8,14},{10,12},{12,10},{14,8},{16,22},{18,... | collective-permute-start | bytes 393224 | tf_op jit(solution)/shard_map/ppermute | solution.py:33
  17.6 10.0 %collective-permute-start.9 = (bf16[256,256]{1,0:T(8,128)(2,1)S(1)}, bf16[256,256]{1,0:T(8,128)(2,1)S(1)}, u32[]{:S(2)}, u32[]{:S(2)}) collective-permute-start(bf16[256,256]{1,0:T(8,128)(2,1)S(1)} %get-tuple-element.47), channel_id=1, source_target_pairs={{0,2},{2,0},{4,6},{6,4},{8,10},{10,8},{12,14},{14,12},{16,18},{18,... | collective-permute-start | bytes 393224 | tf_op jit(solution)/shard_map/ppermute | solution.py:33
  19.0 8.5 %collective-permute-start.10 = (bf16[256,256]{1,0:T(8,128)(2,1)S(1)}, bf16[256,256]{1,0:T(8,128)(2,1)S(1)}, u32[]{:S(2)}, u32[]{:S(2)}) collective-permute-start(bf16[256,256]{1,0:T(8,128)(2,1)S(1)} %get-tuple-element.48), channel_id=1, source_target_pairs={{0,4},{2,6},{4,0},{6,2},{8,12},{10,14},{12,8},{14,10},{16,20},{18,... | collective-permute-start | bytes 393224 | tf_op jit(solution)/shard_map/ppermute | solution.py:33
  23.1 5.9 %collective-permute-start.11 = (bf16[256,256]{1,0:T(8,128)(2,1)S(1)}, bf16[256,256]{1,0:T(8,128)(2,1)S(1)}, u32[]{:S(2)}, u32[]{:S(2)}) collective-permute-start(bf16[256,256]{1,0:T(8,128)(2,1)S(1)} %get-tuple-element.49), channel_id=1, source_target_pairs={{0,6},{2,4},{4,2},{6,0},{8,14},{10,12},{12,10},{14,8},{16,22},{18,... | collective-permute-start | bytes 393224 | tf_op jit(solution)/shard_map/ppermute | solution.py:33
  32.8 13.6 %collective-permute-start.12 = (bf16[4,256,128]{2,1,0:T(8,128)(2,1)S(1)}, bf16[4,256,128]{2,1,0:T(8,128)(2,1)S(1)}, u32[]{:S(2)}, u32[]{:S(2)}) collective-permute-start(bf16[4,256,128]{2,1,0:T(8,128)(2,1)S(1)} %get-tuple-element.55), channel_id=1, source_target_pairs={{8,0},{10,2},{12,4},{14,6},{16,8},{18,10},{20,12},{22,14},{24,16},... | collective-permute-start | bytes 786440 | tf_op jit(solution)/shard_map/ppermute | solution.py:28
  42.8 9.1 %collective-permute-start.16 = (bf16[4,256,128]{2,1,0:T(8,128)(2,1)S(1)}, bf16[4,256,128]{2,1,0:T(8,128)(2,1)S(1)}, u32[]{:S(2)}, u32[]{:S(2)}) collective-permute-start(bf16[4,256,128]{2,1,0:T(8,128)(2,1)S(1)} %get-tuple-element.61), channel_id=1, source_target_pairs={{8,0},{10,2},{12,4},{14,6},{16,8},{18,10},{20,12},{22,14},{24,16},... | collective-permute-start | bytes 786440 | tf_op jit(solution)/shard_map/ppermute | solution.py:28
  48.4 6.2 %collective-permute-start.13 = (bf16[256,256]{1,0:T(8,128)(2,1)S(1)}, bf16[256,256]{1,0:T(8,128)(2,1)S(1)}, u32[]{:S(2)}, u32[]{:S(2)}) collective-permute-start(bf16[256,256]{1,0:T(8,128)(2,1)S(1)} %get-tuple-element.57), channel_id=1, source_target_pairs={{0,2},{2,0},{4,6},{6,4},{8,10},{10,8},{12,14},{14,12},{16,18},{18,... | collective-permute-start | bytes 393224 | tf_op jit(solution)/shard_map/ppermute | solution.py:33
  49.2 7.3 %collective-permute-start.14 = (bf16[256,256]{1,0:T(8,128)(2,1)S(1)}, bf16[256,256]{1,0:T(8,128)(2,1)S(1)}, u32[]{:S(2)}, u32[]{:S(2)}) collective-permute-start(bf16[256,256]{1,0:T(8,128)(2,1)S(1)} %get-tuple-element.58), channel_id=1, source_target_pairs={{0,4},{2,6},{4,0},{6,2},{8,12},{10,14},{12,8},{14,10},{16,20},{18,... | collective-permute-start | bytes 393224 | tf_op jit(solution)/shard_map/ppermute | solution.py:33
  49.8 6.7 %collective-permute-start.15 = (bf16[256,256]{1,0:T(8,128)(2,1)S(1)}, bf16[256,256]{1,0:T(8,128)(2,1)S(1)}, u32[]{:S(2)}, u32[]{:S(2)}) collective-permute-start(bf16[256,256]{1,0:T(8,128)(2,1)S(1)} %get-tuple-element.59), channel_id=1, source_target_pairs={{0,6},{2,4},{4,2},{6,0},{8,14},{10,12},{12,10},{14,8},{16,22},{18,... | collective-permute-start | bytes 393224 | tf_op jit(solution)/shard_map/ppermute | solution.py:33
  52.0 5.4 %collective-permute-start.17 = (bf16[256,256]{1,0:T(8,128)(2,1)S(1)}, bf16[256,256]{1,0:T(8,128)(2,1)S(1)}, u32[]{:S(2)}, u32[]{:S(2)}) collective-permute-start(bf16[256,256]{1,0:T(8,128)(2,1)S(1)} %get-tuple-element.64), channel_id=1, source_target_pairs={{0,2},{2,0},{4,6},{6,4},{8,10},{10,8},{12,14},{14,12},{16,18},{18,... | collective-permute-start | bytes 393224 | tf_op jit(solution)/shard_map/ppermute | solution.py:33
  52.9 5.0 %collective-permute-start.18 = (bf16[256,256]{1,0:T(8,128)(2,1)S(1)}, bf16[256,256]{1,0:T(8,128)(2,1)S(1)}, u32[]{:S(2)}, u32[]{:S(2)}) collective-permute-start(bf16[256,256]{1,0:T(8,128)(2,1)S(1)} %get-tuple-element.65), channel_id=1, source_target_pairs={{0,4},{2,6},{4,0},{6,2},{8,12},{10,14},{12,8},{14,10},{16,20},{18,... | collective-permute-start | bytes 393224 | tf_op jit(solution)/shard_map/ppermute | solution.py:33
  54.6 5.9 %collective-permute-start.19 = (bf16[256,256]{1,0:T(8,128)(2,1)S(1)}, bf16[256,256]{1,0:T(8,128)(2,1)S(1)}, u32[]{:S(2)}, u32[]{:S(2)}) collective-permute-start(bf16[256,256]{1,0:T(8,128)(2,1)S(1)} %get-tuple-element.66), channel_id=1, source_target_pairs={{0,6},{2,4},{4,2},{6,0},{8,14},{10,12},{12,10},{14,8},{16,22},{18,... | collective-permute-start | bytes 393224 | tf_op jit(solution)/shard_map/ppermute | solution.py:33

commit v7 on v4

--- a/solution.py
+++ b/solution.py
@@ -59,17 +59,24 @@
     return pl.ds(pl.multiple_of(index * width, width), width)
 
 
-def pack_kv(group, keys, values):
+def begin():
+    def body(out_ref):
+        out_ref[...] = jnp.zeros_like(out_ref)
+
+    return call(body, [jax.ShapeDtypeStruct((8, 128), jnp.float32)], flops=AHEAD)()[0]
+
+
+def pack_kv(group, keys, values, before):
     tokens, width = keys.shape[0], keys.shape[1] // group
 
-    def body(k_ref, v_ref, *refs):
+    def body(k_ref, v_ref, before_ref, *refs):
         for r in range(group):
             member = spot(group)[0] ^ r
             refs[r][:, :width] = k_ref[:, lanes(member, width)]
             refs[r][:, width:] = v_ref[:, lanes(member, width)]
 
     outs = [jax.ShapeDtypeStruct((tokens, 2 * width), jnp.bfloat16)] * group
-    return call(body, outs, flops=AHEAD)(keys, values)
+    return call(body, outs, flops=AHEAD, specs=[VMEM, VMEM, ANY])(keys, values, before)
 
 
 def pack_queries(group, queries, before):
@@ -83,13 +90,18 @@
     return call(body, outs, specs=[VMEM, ANY])(queries, before)
 
 
-def order_pieces(group, pieces):
+def order_kv(group, pieces, before):
+    tokens, width = pieces[0].shape
+    width //= 2
+
     def body(*refs):
         for r in range(group):
-            refs[group][spot(group)[0] ^ r] = refs[r][...]
-
-    outs = [jax.ShapeDtypeStruct((group,) + pieces[0].shape, jnp.bfloat16)]
-    return call(body, outs)(*pieces)[0]
+            member = spot(group)[0] ^ r
+            refs[-2][member] = refs[r][:, :width]
+            refs[-1][member] = refs[r][:, width:]
+
+    outs = [jax.ShapeDtypeStruct((group, tokens, width), jnp.bfloat16)] * 2
+    return call(body, outs, flops=AHEAD, specs=[VMEM] * group + [ANY])(*pieces, before)
 
 
 def head_product(parts, part, out_weight, layer_cotangent, before):
@@ -115,7 +127,7 @@
     )[0]
 
 
-def pack_grads(group, terms):
+def pack_grads(group, terms, before):
     rows, tokens = terms[0].shape
     rows //= group
 
@@ -127,10 +139,10 @@
                 total = total.astype(jnp.float32)
                 for term in refs[1 : len(terms)]:
                     total = total + term[there, :].astype(jnp.float32)
-            refs[len(terms) + r][...] = total.astype(jnp.bfloat16)
+            refs[len(terms) + 1 + r][...] = total.astype(jnp.bfloat16)
 
     outs = [jax.ShapeDtypeStruct((rows, tokens), jnp.bfloat16)] * group
-    return call(body, outs)(*terms)
+    return call(body, outs, specs=[VMEM] * len(terms) + [ANY])(*terms, before)
 
 
 class Shape:
@@ -164,19 +176,19 @@
     return call(body, outs)(*pieces)[0]
 
 
-def softmax(z, kv_own, kv_earlier, qt):
+def softmax(z, k_own, k_earlier, qt):
     factor = score_scale * LOG2_E
 
-    def body(*refs):
-        own_ref, earlier_refs = refs[0], refs[1 : 1 + z.steps]
-        qt_ref, e_ref, inverse_ref, k_all, s_all = refs[1 + z.steps :]
+    def body(own_ref, *refs):
+        earlier_refs = refs[: z.steps]
+        qt_ref, e_ref, inverse_ref, k_all, s_all = refs[z.steps :]
         first = spot(z.group)[1]
         key_id = lax.broadcasted_iota(jnp.int32, (z.tokens, z.wide), 0)
         query_id = lax.broadcasted_iota(jnp.int32, (z.tokens, z.wide), 1) & (z.tokens - 1)
         for head in range(z.heads):
-            at_k = slice(head * HEAD_SIZE, (head + 1) * HEAD_SIZE)
+            at = slice(head * HEAD_SIZE, (head + 1) * HEAD_SIZE)
             for number in range(z.total):
-                k_all[number] = z.block(own_ref, earlier_refs, number)[:, at_k]
+                k_all[number] = z.block(own_ref, earlier_refs, number)[:, at]
 
             @pl.loop(0, z.group)
             def _(b):
@@ -212,7 +224,7 @@
         pltpu.VMEM((z.span, z.tokens, z.wide), jnp.float32),
     ]
     return call(body, outs, scratch, flops=2 * z.entries * HEAD_SIZE, exps=z.entries)(
-        kv_own, *kv_earlier, qt
+        k_own, *k_earlier, qt
     )
 
 
@@ -244,8 +256,9 @@
                     )
 
             for number in range(z.total):
-                part = dv_all[number]
-                z.block(own_ref, earlier_refs, number)[:, at] = part.astype(own_ref.dtype if number >= z.back else jnp.bfloat16)
+                z.block(own_ref, earlier_refs, number)[:, at] = dv_all[number].astype(
+                    own_ref.dtype if number >= z.back else jnp.bfloat16
+                )
 
     outs = [
         jax.ShapeDtypeStruct((z.heads, z.group, HEAD_SIZE, z.wide), jnp.bfloat16),
@@ -257,16 +270,15 @@
     return results[0], results[1], results[2:]
 
 
-def key_terms(z, e, inverse, qt, g, kv_own, kv_earlier):
+def key_terms(z, e, inverse, qt, g, v_own, v_earlier):
     def body(e_ref, inverse_ref, qt_ref, g_ref, own_ref, *refs):
         earlier_refs, ds_ref = refs[: z.steps], refs[z.steps]
         dk_own, dk_earlier = refs[z.steps + 1], refs[z.steps + 2 : 2 * z.steps + 2]
         v_all, dk_all, dp_all = refs[2 * z.steps + 2 :]
         for head in range(z.heads):
             at = slice(head * HEAD_SIZE, (head + 1) * HEAD_SIZE)
-            at_v = slice(z.kv_width + head * HEAD_SIZE, z.kv_width + (head + 1) * HEAD_SIZE)
             for number in range(z.total):
-                v_all[number] = z.block(own_ref, earlier_refs, number)[:, at_v]
+                v_all[number] = z.block(own_ref, earlier_refs, number)[:, at]
             dk_all[...] = jnp.zeros_like(dk_all)
 
             @pl.loop(0, z.group)
@@ -281,7 +293,7 @@
                 delta = delta * inverse
                 q = (qt_ref[head, b].astype(jnp.float32) * inverse).astype(jnp.bfloat16)
                 for c in range(z.span):
-                    ds = (e_ref[head, b, c].astype(jnp.float32) * (dp_all[c] - delta)).astype(jnp.bfloat16)
+                    ds = e_ref[head, b, c] * (dp_all[c] - delta).astype(jnp.bfloat16)
                     ds_ref[head, b, c] = ds
                     dk_all[b + c] += lax.dot_general(ds, q, NT, preferred_element_type=jnp.float32)
 
@@ -300,12 +312,12 @@
         pltpu.VMEM((z.span, z.tokens, z.wide), jnp.float32),
     ]
     results = call(body, outs, scratch, flops=4 * z.entries * HEAD_SIZE)(
-        e, inverse, qt, g, kv_own, *kv_earlier
+        e, inverse, qt, g, v_own, *v_earlier
     )
     return results[0], results[1], results[2:]
 
 
-def query_terms(z, ds, inverse, kv_own, kv_earlier, dv_terms):
+def query_terms(z, ds, inverse, k_own, k_earlier, dv_terms):
     def body(ds_ref, inverse_ref, own_ref, *refs):
         earlier_refs, term_refs, dv_ref = refs[: z.steps], refs[z.steps : 2 * z.steps + 1], refs[2 * z.steps + 1]
         dq_refs = refs[2 * z.steps + 2 : 2 * z.steps + 2 + z.group]
@@ -343,7 +355,7 @@
         pltpu.VMEM((z.group, z.tokens, z.width), jnp.bfloat16),
     ]
     results = call(body, outs, scratch, flops=2 * z.entries * HEAD_SIZE)(
-        ds, inverse, kv_own, *kv_earlier, *dv_terms
+        ds, inverse, k_own, *k_earlier, *dv_terms
     )
     return results[0], results[1:]
 
@@ -404,25 +416,30 @@
             shifted(earlier[number], "ctx", -group * (back_groups - number)) for number in range(back_groups)
         ]
 
-    sent = pack_kv(group, keys, values)
-    kv_own = order_pieces(group, trade(sent))
-    kv_earlier = [shifted(kv_own, "ctx", group * step) for step in range(back_groups, 0, -1)]
+    sent = pack_kv(group, keys, values, begin())
+    kv_pieces = trade(sent)
     z = Shape(group, back_groups, heads, per_head, tokens)
     query_sent = pack_queries(group, queries, sent[0])
-    qt = turn_queries(z, trade(query_sent))
+    query_pieces = trade(query_sent)
+    qt = turn_queries(z, query_pieces)
     if tp_count == 2:
         other = head_product(2, 1, out_weight, layer_cotangent, [query_sent[0]])
-        terms = [head_product(2, 0, out_weight, layer_cotangent, [kv_own, other]), swapped(other, "tp", 1)]
+        mine = head_product(2, 0, out_weight, layer_cotangent, [other, qt])
+        terms = [mine, swapped(other, "tp", 1)]
     else:
-        product = head_product(1, 0, out_weight, layer_cotangent, [query_sent[0]])
-        terms = [lax.psum_scatter(product, "tp", scatter_dimension=0, tiled=True)]
-    grads = trade(pack_grads(group, terms))
-    e, inverse = softmax(z, kv_own, kv_earlier, qt)
+        other = head_product(1, 0, out_weight, layer_cotangent, [query_sent[0]])
+        terms = [lax.psum_scatter(other, "tp", scatter_dimension=0, tiled=True)]
+    k_own, v_own = order_kv(group, kv_pieces, other)
+    k_earlier, v_earlier = (
+        [shifted(own, "ctx", group * step) for step in range(back_groups, 0, -1)] for own in (k_own, v_own)
+    )
+    grads = trade(pack_grads(group, terms, qt))
+    e, inverse = softmax(z, k_own, k_earlier, qt)
     g, dv_own, dv_earlier = value_terms(z, e, inverse, grads)
     dv_terms = [dv_own] + returned(dv_earlier)
-    ds, dk_own, dk_earlier = key_terms(z, e, inverse, qt, g, kv_own, kv_earlier)
+    ds, dk_own, dk_earlier = key_terms(z, e, inverse, qt, g, v_own, v_earlier)
     dk_terms = [dk_own] + returned(dk_earlier)
-    dv, dq = query_terms(z, ds, inverse, kv_own, kv_earlier, dv_terms)
+    dv, dq = query_terms(z, ds, inverse, k_own, k_earlier, dv_terms)
     dq = trade(dq)
     dkv = trade(pack_terms(group, [dk_terms, [dv]]))
     (query_grads,) = unpack(group, dq, [dq[0].shape[1]])

time: 58.9 us -> 61 us (1.036)
  starting transfers between devices: 25.2 us -> 29.4 us
  local copies, waits for them, and re-layouts: 2.74 us -> 1 us
    ppermute x3 -> x4, starting transfers between devices: 6.03 us -> 11 us  [shifted(): lax.ppermute(value, axis, [(source, source + steps) for source in range(l...]
    unnamed x10 -> x14, local copies, waits for them, and re-layouts: 2.74 us -> 1 us
    ppermute x16, waiting for transfers between devices: 7.48 us -> 8.99 us  [swapped(): lax.ppermute(value, axis, [(source, source ^ bits) for source in range(co...]
    ppermute x3 -> x4, waiting for transfers between devices: 2.36 us -> 0.88 us  [shifted(): lax.ppermute(value, axis, [(source, source + steps) for source in range(l...]
    ppermute x16, starting transfers between devices: 19.2 us -> 18.3 us  [swapped(): lax.ppermute(value, axis, [(source, source ^ bits) for source in range(co...]
    pallas_call x14 -> x15, Pallas kernels: 19.7 us -> 19.4 us  [run(): pl.pallas_call(body, out_shape=tuple(outs), in_specs=specs or [SMEM if a....]
  transfers between devices with their start and end apart: 19 -> 20, of which waited for: 6 -> 10; matrix products, arithmetic and copies ran while one was open for 0% -> 0% of each run, Pallas kernels for 28% -> 30%
where the time goes in v7:
time: 61 us; the launch traced here: 60.5 us
  starting transfers between devices  29.4 us (48%)
  Pallas kernels  19.4 us (32%)
  waiting for transfers between devices  9.87 us (16%)
  local copies, waits for them, and re-layouts  1 us (2%)
  between operations  0.84 us (1%)
    pallas_call x15, Pallas kernels, run(): pl.pallas_call(body, out_shape=tuple(outs), in_specs=specs or [SMEM if a....  19.4 us
    ppermute x16, starting transfers between devices, swapped(): lax.ppermute(value, axis, [(source, source ^ bits) for source in range(co...  18.3 us
    ppermute x4, starting transfers between devices, shifted(): lax.ppermute(value, axis, [(source, source + steps) for source in range(l...  11 us
    ppermute x16, waiting for transfers between devices, swapped(): lax.ppermute(value, axis, [(source, source ^ bits) for source in range(co...  8.99 us
  transfers between devices with their start and end apart: 20, of which 10 were waited for; matrix products, arithmetic and copies ran while one was open for 0% of the time, Pallas kernels for 30%

profile of v7, /device:TPU:24, one launch (start us, length us, event | category | flops | bytes accessed | tf_op | source)
XLA Modules:
  0.0 60.5 jit_solution(17288700702870533636)
XLA Ops:
  0.7 0.9 %copy-done.3 = bf16[256,512]{1,0:T(8,128)(2,1)S(1)} copy-done((bf16[256,512]{1,0:T(8,128)(2,1)S(1)}, bf16[256,512]{1,0:T(8,128)(2,1)}, u32[]{:S(2)}) %copy-start.3) | copy-done | bytes 262168
  1.8 1.6 %collective-permute-start = (bf16[256,256]{1,0:T(8,128)(2,1)S(1)}, bf16[256,256]{1,0:T(8,128)(2,1)S(1)}, u32[]{:S(2)}, u32[]{:S(2)}) collective-permute-start(bf16[256,256]{1,0:T(8,128)(2,1)S(1)} %get-tuple-element.37), channel_id=1, source_target_pairs={{0,2},{2,0},{4,6},{6,4},{8,10},{10,8},{12,14},{14,12},{16,18},{18,... | collective-permute-start | bytes 393224 | tf_op jit(solution)/shard_map/ppermute | solution.py:32
  3.3 1.5 %collective-permute-start.1 = (bf16[256,256]{1,0:T(8,128)(2,1)S(1)}, bf16[256,256]{1,0:T(8,128)(2,1)S(1)}, u32[]{:S(2)}, u32[]{:S(2)}) collective-permute-start(bf16[256,256]{1,0:T(8,128)(2,1)S(1)} %get-tuple-element.38), channel_id=1, source_target_pairs={{0,4},{2,6},{4,0},{6,2},{8,12},{10,14},{12,8},{14,10},{16,20},{18,... | collective-permute-start | bytes 393224 | tf_op jit(solution)/shard_map/ppermute | solution.py:32
  5.4 1.6 %collective-permute-start.4 = (bf16[256,256]{1,0:T(8,128)(2,1)S(1)}, bf16[256,256]{1,0:T(8,128)(2,1)S(1)}, u32[]{:S(2)}, u32[]{:S(2)}) collective-permute-start(bf16[256,256]{1,0:T(8,128)(2,1)S(1)} %get-tuple-element.42), channel_id=1, source_target_pairs={{0,2},{2,0},{4,6},{6,4},{8,10},{10,8},{12,14},{14,12},{16,18},{18,... | collective-permute-start | bytes 393224 | tf_op jit(solution)/shard_map/ppermute | solution.py:32
  7.0 1.5 %collective-permute-start.5 = (bf16[256,256]{1,0:T(8,128)(2,1)S(1)}, bf16[256,256]{1,0:T(8,128)(2,1)S(1)}, u32[]{:S(2)}, u32[]{:S(2)}) collective-permute-start(bf16[256,256]{1,0:T(8,128)(2,1)S(1)} %get-tuple-element.43), channel_id=1, source_target_pairs={{0,4},{2,6},{4,0},{6,2},{8,12},{10,14},{12,8},{14,10},{16,20},{18,... | collective-permute-start | bytes 393224 | tf_op jit(solution)/shard_map/ppermute | solution.py:32
  8.5 1.9 %shard_map.79.refs_4_.refs_0_ = bf16[1024,256]{1,0:T(8,128)(2,1)S(1)} custom-call(bf16[2048,2688]{1,0:T(8,128)(2,1)S(1)} %bitcast.1, bf16[256,2688]{1,0:T(8,128)(2,1)S(1)} %copy-done, bf16[256,256]{1,0:T(8,128)(2,1)S(1)} %get-tuple-element.40.refs_0_), custom_call_target="tpu_custom_call" | custom-call | flops 1409286144 | bytes 13041664 | tf_op jit(solution)/shard_map/pallas_call | solution.py:39
  10.9 0.6 %collective-permute-done.1.refs_2_ = bf16[256,256]{1,0:T(8,128)(2,1)S(1)} collective-permute-done((bf16[256,256]{1,0:T(8,128)(2,1)S(1)}, bf16[256,256]{1,0:T(8,128)(2,1)S(1)}, u32[]{:S(2)}, u32[]{:S(2)}) %collective-permute-start.1) | collective-permute-done | bytes 131104 | tf_op jit(solution)/shard_map/ppermute | solution.py:32
  12.3 1.3 %collective-permute-start.3 = (bf16[4,256,128]{2,1,0:T(8,128)(2,1)S(1)}, bf16[4,256,128]{2,1,0:T(8,128)(2,1)S(1)}, u32[]{:S(2)}, u32[]{:S(2)}) collective-permute-start(bf16[4,256,128]{2,1,0:T(8,128)(2,1)S(1)} %get-tuple-element.41.own_ref), channel_id=1, source_target_pairs={{0,8},{2,10},{4,12},{6,14},{8,16},{10,18},{12,20},{14,22},{16,24},... | collective-permute-start | bytes 786440 | tf_op jit(solution)/shard_map/ppermute | solution.py:27
  13.9 1.3 %collective-permute-start.11 = (bf16[4,256,128]{2,1,0:T(8,128)(2,1)S(1)}, bf16[4,256,128]{2,1,0:T(8,128)(2,1)S(1)}, u32[]{:S(2)}, u32[]{:S(2)}) collective-permute-start(bf16[4,256,128]{2,1,0:T(8,128)(2,1)S(1)} %get-tuple-element.52.own_ref), channel_id=1, source_target_pairs={{0,8},{2,10},{4,12},{6,14},{8,16},{10,18},{12,20},{14,22},{16,24},... | collective-permute-start | bytes 786440 | tf_op jit(solution)/shard_map/ppermute | solution.py:27
  15.2 1.5 %collective-permute-done.5.refs_2_ = bf16[256,256]{1,0:T(8,128)(2,1)S(1)} collective-permute-done((bf16[256,256]{1,0:T(8,128)(2,1)S(1)}, bf16[256,256]{1,0:T(8,128)(2,1)S(1)}, u32[]{:S(2)}, u32[]{:S(2)}) %collective-permute-start.5) | collective-permute-done | bytes 131104 | tf_op jit(solution)/shard_map/ppermute | solution.py:32
  16.9 1.9 %shard_map.83.refs_0_ = bf16[1024,256]{1,0:T(8,128)(2,1)S(1)} custom-call(bf16[2048,2688]{1,0:T(8,128)(2,1)S(1)} %bitcast.1, bf16[256,2688]{1,0:T(8,128)(2,1)S(1)} %copy-done, bf16[1024,256]{1,0:T(8,128)(2,1)S(1)} %shard_map.79.refs_4_.refs_0_, bf16[1,4,128,512]{3,2,1,0:T(8,128)(2,1)S(1)} %shard_map.81.refs_1_.refs_2_.qt_ref), custom_call_target="tpu_custom_call" | custom-call | flops 1409286144 | bytes 13959168 | tf_op jit(solution)/shard_map/pallas_call | solution.py:39
  19.0 1.3 %collective-permute-start.8 = (bf16[256,256]{1,0:T(8,128)(2,1)S(1)}, bf16[256,256]{1,0:T(8,128)(2,1)S(1)}, u32[]{:S(2)}, u32[]{:S(2)}) collective-permute-start(bf16[256,256]{1,0:T(8,128)(2,1)S(1)} %get-tuple-element.48), channel_id=1, source_target_pairs={{0,2},{2,0},{4,6},{6,4},{8,10},{10,8},{12,14},{14,12},{16,18},{18,... | collective-permute-start | bytes 393224 | tf_op jit(solution)/shard_map/ppermute | solution.py:32
  20.3 0.8 %collective-permute-start.9 = (bf16[256,256]{1,0:T(8,128)(2,1)S(1)}, bf16[256,256]{1,0:T(8,128)(2,1)S(1)}, u32[]{:S(2)}, u32[]{:S(2)}) collective-permute-start(bf16[256,256]{1,0:T(8,128)(2,1)S(1)} %get-tuple-element.49), channel_id=1, source_target_pairs={{0,4},{2,6},{4,0},{6,2},{8,12},{10,14},{12,8},{14,10},{16,20},{18,... | collective-permute-start | bytes 393224 | tf_op jit(solution)/shard_map/ppermute | solution.py:32
  21.1 1.5 %collective-permute-start.10 = (bf16[256,256]{1,0:T(8,128)(2,1)S(1)}, bf16[256,256]{1,0:T(8,128)(2,1)S(1)}, u32[]{:S(2)}, u32[]{:S(2)}) collective-permute-start(bf16[256,256]{1,0:T(8,128)(2,1)S(1)} %get-tuple-element.50), channel_id=1, source_target_pairs={{0,6},{2,4},{4,2},{6,0},{8,14},{10,12},{12,10},{14,8},{16,22},{18,... | collective-permute-start | bytes 393224 | tf_op jit(solution)/shard_map/ppermute | solution.py:32
  22.5 0.9 %collective-permute-done.3.refs_0_ = bf16[4,256,128]{2,1,0:T(8,128)(2,1)S(1)} collective-permute-done((bf16[4,256,128]{2,1,0:T(8,128)(2,1)S(1)}, bf16[4,256,128]{2,1,0:T(8,128)(2,1)S(1)}, u32[]{:S(2)}, u32[]{:S(2)}) %collective-permute-start.3) | collective-permute-done | bytes 262176 | tf_op jit(solution)/shard_map/ppermute | solution.py:27
  23.4 3.7 %shard_map.82 = (bf16[1,4,5,256,512]{4,3,2,1,0:T(8,128)(2,1)S(1)}, f32[1,4,1,512]{3,2,1,0:T(1,128)S(1)}) custom-call(bf16[4,256,128]{2,1,0:T(8,128)(2,1)S(1)} %get-tuple-element.41.own_ref, bf16[4,256,128]{2,1,0:T(8,128)(2,1)S(1)} %collective-permute-done.3.refs_0_, bf16[1,4,128,512]{3,2,1,0:T(8,128)(2,1)S(1)} %shard_map.81.refs_1_.refs_2_.qt_ref), custom_call_target="tpu_custom_call" | custom-call | flops 671088640 | bytes 6299648 | tf_op jit(solution)/shard_map/pallas_call | solution.py:39
  27.1 0.7 %collective-permute-done.9.refs_2_ = bf16[256,256]{1,0:T(8,128)(2,1)S(1)} collective-permute-done((bf16[256,256]{1,0:T(8,128)(2,1)S(1)}, bf16[256,256]{1,0:T(8,128)(2,1)S(1)}, u32[]{:S(2)}, u32[]{:S(2)}) %collective-permute-start.9) | collective-permute-done | bytes 131104 | tf_op jit(solution)/shard_map/ppermute | solution.py:32
  27.9 2.2 %shard_map.85 = (bf16[1,4,128,512]{3,2,1,0:T(8,128)(2,1)S(1)}, f32[4,256,128]{2,1,0:T(8,128)S(1)}, bf16[4,256,128]{2,1,0:T(8,128)(2,1)S(1)}) custom-call(bf16[1,4,5,256,512]{4,3,2,1,0:T(8,128)(2,1)S(1)} %get-tuple-element.45.e_ref, f32[1,4,1,512]{3,2,1,0:T(1,128)S(1)} %get-tuple-element.46.inverse_ref, bf16[256,256]{1,0:T(8,128)(2,1)S(1)} %get-tuple-element.47.refs_0_, ...), custom_call_target="tpu_custom_call" | custom-call | flops 671088640 | bytes 7086080 | tf_op jit(solution)/shard_map/pallas_call | solution.py:39
  30.1 4.8 %collective-permute-start.12 = (bf16[4,256,128]{2,1,0:T(8,128)(2,1)S(1)}, bf16[4,256,128]{2,1,0:T(8,128)(2,1)S(1)}, u32[]{:S(2)}, u32[]{:S(2)}) collective-permute-start(bf16[4,256,128]{2,1,0:T(8,128)(2,1)S(1)} %get-tuple-element.55), channel_id=1, source_target_pairs={{8,0},{10,2},{12,4},{14,6},{16,8},{18,10},{20,12},{22,14},{24,16},... | collective-permute-start | bytes 786440 | tf_op jit(solution)/shard_map/ppermute | solution.py:27
  34.9 5.3 %shard_map.86 = (bf16[1,4,5,256,512]{4,3,2,1,0:T(8,128)(2,1)S(1)}, f32[4,256,128]{2,1,0:T(8,128)S(1)}, bf16[4,256,128]{2,1,0:T(8,128)(2,1)S(1)}) custom-call(bf16[1,4,5,256,512]{4,3,2,1,0:T(8,128)(2,1)S(1)} %get-tuple-element.45.e_ref, f32[1,4,1,512]{3,2,1,0:T(1,128)S(1)} %get-tuple-element.46.inverse_ref, ...), custom_call_target="tpu_custom_call" | custom-call | flops 1342177280 | bytes 12853248 | tf_op jit(solution)/shard_map/pallas_call | solution.py:39
  40.2 3.7 %collective-permute-start.16 = (bf16[4,256,128]{2,1,0:T(8,128)(2,1)S(1)}, bf16[4,256,128]{2,1,0:T(8,128)(2,1)S(1)}, u32[]{:S(2)}, u32[]{:S(2)}) collective-permute-start(bf16[4,256,128]{2,1,0:T(8,128)(2,1)S(1)} %get-tuple-element.61), channel_id=1, source_target_pairs={{8,0},{10,2},{12,4},{14,6},{16,8},{18,10},{20,12},{22,14},{24,16},... | collective-permute-start | bytes 786440 | tf_op jit(solution)/shard_map/ppermute | solution.py:27
  43.9 1.9 %shard_map.87 = (bf16[4,256,128]{2,1,0:T(8,128)(2,1)S(1)}, bf16[256,256]{1,0:T(8,128)(2,1)S(1)}, bf16[256,256]{1,0:T(8,128)(2,1)S(1)}, bf16[256,256]{1,0:T(8,128)(2,1)S(1)}, bf16[256,256]{1,0:T(8,128)(2,1)S(1)}) custom-call(bf16[1,4,5,256,512]{4,3,2,1,0:T(8,128)(2,1)S(1)} %get-tuple-element.53.ds_ref, f32[1,4,1,512]{3,2,1,0:T(1,128)S(1)} %get-tuple-element.46.inverse_ref, ...), custom_call_target="tpu_custom_call" | custom-call | flops 671088640 | bytes 7348224 | tf_op jit(solution)/shard_map/pallas_call | solution.py:39
  45.8 0.6 %collective-permute-start.13 = (bf16[256,256]{1,0:T(8,128)(2,1)S(1)}, bf16[256,256]{1,0:T(8,128)(2,1)S(1)}, u32[]{:S(2)}, u32[]{:S(2)}) collective-permute-start(bf16[256,256]{1,0:T(8,128)(2,1)S(1)} %get-tuple-element.57), channel_id=1, source_target_pairs={{0,2},{2,0},{4,6},{6,4},{8,10},{10,8},{12,14},{14,12},{16,18},{18,... | collective-permute-start | bytes 393224 | tf_op jit(solution)/shard_map/ppermute | solution.py:32
  46.5 1.7 %collective-permute-start.14 = (bf16[256,256]{1,0:T(8,128)(2,1)S(1)}, bf16[256,256]{1,0:T(8,128)(2,1)S(1)}, u32[]{:S(2)}, u32[]{:S(2)}) collective-permute-start(bf16[256,256]{1,0:T(8,128)(2,1)S(1)} %get-tuple-element.58), channel_id=1, source_target_pairs={{0,4},{2,6},{4,0},{6,2},{8,12},{10,14},{12,8},{14,10},{16,20},{18,... | collective-permute-start | bytes 393224 | tf_op jit(solution)/shard_map/ppermute | solution.py:32
  48.2 1.2 %collective-permute-start.15 = (bf16[256,256]{1,0:T(8,128)(2,1)S(1)}, bf16[256,256]{1,0:T(8,128)(2,1)S(1)}, u32[]{:S(2)}, u32[]{:S(2)}) collective-permute-start(bf16[256,256]{1,0:T(8,128)(2,1)S(1)} %get-tuple-element.59), channel_id=1, source_target_pairs={{0,6},{2,4},{4,2},{6,0},{8,14},{10,12},{12,10},{14,8},{16,22},{18,... | collective-permute-start | bytes 393224 | tf_op jit(solution)/shard_map/ppermute | solution.py:32
  49.5 0.6 %collective-permute-start.17 = (bf16[256,256]{1,0:T(8,128)(2,1)S(1)}, bf16[256,256]{1,0:T(8,128)(2,1)S(1)}, u32[]{:S(2)}, u32[]{:S(2)}) collective-permute-start(bf16[256,256]{1,0:T(8,128)(2,1)S(1)} %get-tuple-element.64), channel_id=1, source_target_pairs={{0,2},{2,0},{4,6},{6,4},{8,10},{10,8},{12,14},{14,12},{16,18},{18,... | collective-permute-start | bytes 393224 | tf_op jit(solution)/shard_map/ppermute | solution.py:32
  50.1 1.7 %collective-permute-start.18 = (bf16[256,256]{1,0:T(8,128)(2,1)S(1)}, bf16[256,256]{1,0:T(8,128)(2,1)S(1)}, u32[]{:S(2)}, u32[]{:S(2)}) collective-permute-start(bf16[256,256]{1,0:T(8,128)(2,1)S(1)} %get-tuple-element.65), channel_id=1, source_target_pairs={{0,4},{2,6},{4,0},{6,2},{8,12},{10,14},{12,8},{14,10},{16,20},{18,... | collective-permute-start | bytes 393224 | tf_op jit(solution)/shard_map/ppermute | solution.py:32
  52.3 1.7 %collective-permute-start.19 = (bf16[256,256]{1,0:T(8,128)(2,1)S(1)}, bf16[256,256]{1,0:T(8,128)(2,1)S(1)}, u32[]{:S(2)}, u32[]{:S(2)}) collective-permute-start(bf16[256,256]{1,0:T(8,128)(2,1)S(1)} %get-tuple-element.66), channel_id=1, source_target_pairs={{0,6},{2,4},{4,2},{6,0},{8,14},{10,12},{12,10},{14,8},{16,22},{18,... | collective-permute-start | bytes 393224 | tf_op jit(solution)/shard_map/ppermute | solution.py:32
  54.0 2.0 %collective-permute-done.14.refs_2_ = bf16[256,256]{1,0:T(8,128)(2,1)S(1)} collective-permute-done((bf16[256,256]{1,0:T(8,128)(2,1)S(1)}, bf16[256,256]{1,0:T(8,128)(2,1)S(1)}, u32[]{:S(2)}, u32[]{:S(2)}) %collective-permute-start.14) | collective-permute-done | bytes 131104 | tf_op jit(solution)/shard_map/ppermute | solution.py:32
  56.0 0.9 %shard_map.88 = bf16[256,1024]{1,0:T(8,128)(2,1)} custom-call(bf16[256,256]{1,0:T(8,128)(2,1)S(1)} %get-tuple-element.56.refs_0_, bf16[256,256]{1,0:T(8,128)(2,1)S(1)} %collective-permute-done.13.refs_1_, bf16[256,256]{1,0:T(8,128)(2,1)S(1)} %collective-permute-done.14.refs_2_, bf16[256,256]{1,0:T(8,128)(2,1)S(1)} %collective-permute-done.15.refs_3_), custom_call_target="tpu_custom_call" | custom-call | bytes 1048576 | tf_op jit(solution)/shard_map/pallas_call | solution.py:39
  56.9 2.6 %collective-permute-done.18.refs_2_ = bf16[256,256]{1,0:T(8,128)(2,1)S(1)} collective-permute-done((bf16[256,256]{1,0:T(8,128)(2,1)S(1)}, bf16[256,256]{1,0:T(8,128)(2,1)S(1)}, u32[]{:S(2)}, u32[]{:S(2)}) %collective-permute-start.18) | collective-permute-done | bytes 131104 | tf_op jit(solution)/shard_map/ppermute | solution.py:32
  59.6 0.9 %shard_map.90 = (bf16[256,512]{1,0:T(8,128)(2,1)}, bf16[256,512]{1,0:T(8,128)(2,1)}) custom-call(bf16[256,256]{1,0:T(8,128)(2,1)S(1)} %get-tuple-element.63.refs_0_, bf16[256,256]{1,0:T(8,128)(2,1)S(1)} %collective-permute-done.17.refs_1_, bf16[256,256]{1,0:T(8,128)(2,1)S(1)} %collective-permute-done.18.refs_2_, ...), custom_call_target="tpu_custom_call" | custom-call | bytes 1048576 | tf_op jit(solution)/shard_map/pallas_call | solution.py:39
  (38 shorter events, 3.3 us)
Async XLA Ops:
  0.6 1.0 %copy-start.3 = (bf16[256,512]{1,0:T(8,128)(2,1)S(1)}, bf16[256,512]{1,0:T(8,128)(2,1)}, u32[]{:S(2)}) copy-start(bf16[256,512]{1,0:T(8,128)(2,1)} %v_ref.1) | copy-start | bytes 786436
  0.6 1.0 %copy-start.2 = (bf16[256,512]{1,0:T(8,128)(2,1)S(1)}, bf16[256,512]{1,0:T(8,128)(2,1)}, u32[]{:S(2)}) copy-start(bf16[256,512]{1,0:T(8,128)(2,1)} %k_ref.1) | copy-start | bytes 786436
  0.7 7.8 %slice-start = ((s8[11010048]{0:T(1024)(128)(4,1)}), s8[4194304]{0:T(1024)(128)(4,1)S(1)}, s32[]{:S(2)}) async-start(s8[11010048]{0:T(1024)(128)(4,1)} %bitcast), calls=%async_computation | async-start | bytes 8388608
  0.7 7.8 %slice-start.1 = ((s8[11010048]{0:T(1024)(128)(4,1)}), s8[4194304]{0:T(1024)(128)(4,1)S(1)}, s32[]{:S(2)}) async-start(s8[11010048]{0:T(1024)(128)(4,1)} %bitcast), calls=%async_computation.1 | async-start | bytes 8388608
  1.7 3.7 %copy-start.1 = (bf16[256,1024]{1,0:T(8,128)(2,1)S(1)}, bf16[256,1024]{1,0:T(8,128)(2,1)}, u32[]{:S(2)}) copy-start(bf16[256,1024]{1,0:T(8,128)(2,1)} %q_ref.1) | copy-start | bytes 1572868
  1.7 6.8 %slice-start.2 = ((s8[11010048]{0:T(1024)(128)(4,1)}), s8[2621440]{0:T(1024)(128)(4,1)S(1)}, s32[]{:S(2)}) async-start(s8[11010048]{0:T(1024)(128)(4,1)} %bitcast), calls=%async_computation.2 | async-start | bytes 5242880
  1.7 6.8 %copy-start = (bf16[256,2688]{1,0:T(8,128)(2,1)S(1)}, bf16[256,2688]{1,0:T(8,128)(2,1)}, u32[]{:S(2)}) copy-start(bf16[256,2688]{1,0:T(8,128)(2,1)} %c_ref.3) | copy-start | bytes 4128772
  1.8 8.6 %collective-permute-start = (bf16[256,256]{1,0:T(8,128)(2,1)S(1)}, bf16[256,256]{1,0:T(8,128)(2,1)S(1)}, u32[]{:S(2)}, u32[]{:S(2)}) collective-permute-start(bf16[256,256]{1,0:T(8,128)(2,1)S(1)} %get-tuple-element.37), channel_id=1, source_target_pairs={{0,2},{2,0},{4,6},{6,4},{8,10},{10,8},{12,14},{14,12},{16,18},{18,... | collective-permute-start | bytes 393224 | tf_op jit(solution)/shard_map/ppermute | solution.py:32
  3.3 8.3 %collective-permute-start.1 = (bf16[256,256]{1,0:T(8,128)(2,1)S(1)}, bf16[256,256]{1,0:T(8,128)(2,1)S(1)}, u32[]{:S(2)}, u32[]{:S(2)}) collective-permute-start(bf16[256,256]{1,0:T(8,128)(2,1)S(1)} %get-tuple-element.38), channel_id=1, source_target_pairs={{0,4},{2,6},{4,0},{6,2},{8,12},{10,14},{12,8},{14,10},{16,20},{18,... | collective-permute-start | bytes 393224 | tf_op jit(solution)/shard_map/ppermute | solution.py:32
  4.8 7.4 %collective-permute-start.2 = (bf16[256,256]{1,0:T(8,128)(2,1)S(1)}, bf16[256,256]{1,0:T(8,128)(2,1)S(1)}, u32[]{:S(2)}, u32[]{:S(2)}) collective-permute-start(bf16[256,256]{1,0:T(8,128)(2,1)S(1)} %get-tuple-element.39), channel_id=1, source_target_pairs={{0,6},{2,4},{4,2},{6,0},{8,14},{10,12},{12,10},{14,8},{16,22},{18,... | collective-permute-start | bytes 393224 | tf_op jit(solution)/shard_map/ppermute | solution.py:32
  5.4 8.5 %collective-permute-start.4 = (bf16[256,256]{1,0:T(8,128)(2,1)S(1)}, bf16[256,256]{1,0:T(8,128)(2,1)S(1)}, u32[]{:S(2)}, u32[]{:S(2)}) collective-permute-start(bf16[256,256]{1,0:T(8,128)(2,1)S(1)} %get-tuple-element.42), channel_id=1, source_target_pairs={{0,2},{2,0},{4,6},{6,4},{8,10},{10,8},{12,14},{14,12},{16,18},{18,... | collective-permute-start | bytes 393224 | tf_op jit(solution)/shard_map/ppermute | solution.py:32
  7.0 9.8 %collective-permute-start.5 = (bf16[256,256]{1,0:T(8,128)(2,1)S(1)}, bf16[256,256]{1,0:T(8,128)(2,1)S(1)}, u32[]{:S(2)}, u32[]{:S(2)}) collective-permute-start(bf16[256,256]{1,0:T(8,128)(2,1)S(1)} %get-tuple-element.43), channel_id=1, source_target_pairs={{0,4},{2,6},{4,0},{6,2},{8,12},{10,14},{12,8},{14,10},{16,20},{18,... | collective-permute-start | bytes 393224 | tf_op jit(solution)/shard_map/ppermute | solution.py:32
  10.4 6.3 %collective-permute-start.6 = (bf16[256,256]{1,0:T(8,128)(2,1)S(1)}, bf16[256,256]{1,0:T(8,128)(2,1)S(1)}, u32[]{:S(2)}, u32[]{:S(2)}) collective-permute-start(bf16[256,256]{1,0:T(8,128)(2,1)S(1)} %get-tuple-element.44), channel_id=1, source_target_pairs={{0,6},{2,4},{4,2},{6,0},{8,14},{10,12},{12,10},{14,8},{16,22},{18,... | collective-permute-start | bytes 393224 | tf_op jit(solution)/shard_map/ppermute | solution.py:32
  11.6 7.2 %collective-permute-start.7 = (bf16[1024,256]{1,0:T(8,128)(2,1)S(1)}, bf16[1024,256]{1,0:T(8,128)(2,1)S(1)}, u32[]{:S(2)}, u32[]{:S(2)}) collective-permute-start(bf16[1024,256]{1,0:T(8,128)(2,1)S(1)} %shard_map.79.refs_4_.refs_0_), channel_id=1, source_target_pairs={{0,1},{1,0},{2,3},{3,2},{4,5},{5,4},{6,7},{7,6},{8,9},{9,8},{10,11... | collective-permute-start | bytes 1572872 | tf_op jit(solution)/shard_map/ppermute | solution.py:32
  12.3 11.1 %collective-permute-start.3 = (bf16[4,256,128]{2,1,0:T(8,128)(2,1)S(1)}, bf16[4,256,128]{2,1,0:T(8,128)(2,1)S(1)}, u32[]{:S(2)}, u32[]{:S(2)}) collective-permute-start(bf16[4,256,128]{2,1,0:T(8,128)(2,1)S(1)} %get-tuple-element.41.own_ref), channel_id=1, source_target_pairs={{0,8},{2,10},{4,12},{6,14},{8,16},{10,18},{12,20},{14,22},{16,24},... | collective-permute-start | bytes 786440 | tf_op jit(solution)/shard_map/ppermute | solution.py:27
  13.9 21.0 %collective-permute-start.11 = (bf16[4,256,128]{2,1,0:T(8,128)(2,1)S(1)}, bf16[4,256,128]{2,1,0:T(8,128)(2,1)S(1)}, u32[]{:S(2)}, u32[]{:S(2)}) collective-permute-start(bf16[4,256,128]{2,1,0:T(8,128)(2,1)S(1)} %get-tuple-element.52.own_ref), channel_id=1, source_target_pairs={{0,8},{2,10},{4,12},{6,14},{8,16},{10,18},{12,20},{14,22},{16,24},... | collective-permute-start | bytes 786440 | tf_op jit(solution)/shard_map/ppermute | solution.py:27
  19.0 8.2 %collective-permute-start.8 = (bf16[256,256]{1,0:T(8,128)(2,1)S(1)}, bf16[256,256]{1,0:T(8,128)(2,1)S(1)}, u32[]{:S(2)}, u32[]{:S(2)}) collective-permute-start(bf16[256,256]{1,0:T(8,128)(2,1)S(1)} %get-tuple-element.48), channel_id=1, source_target_pairs={{0,2},{2,0},{4,6},{6,4},{8,10},{10,8},{12,14},{14,12},{16,18},{18,... | collective-permute-start | bytes 393224 | tf_op jit(solution)/shard_map/ppermute | solution.py:32
  20.3 7.6 %collective-permute-start.9 = (bf16[256,256]{1,0:T(8,128)(2,1)S(1)}, bf16[256,256]{1,0:T(8,128)(2,1)S(1)}, u32[]{:S(2)}, u32[]{:S(2)}) collective-permute-start(bf16[256,256]{1,0:T(8,128)(2,1)S(1)} %get-tuple-element.49), channel_id=1, source_target_pairs={{0,4},{2,6},{4,0},{6,2},{8,12},{10,14},{12,8},{14,10},{16,20},{18,... | collective-permute-start | bytes 393224 | tf_op jit(solution)/shard_map/ppermute | solution.py:32
  21.1 6.8 %collective-permute-start.10 = (bf16[256,256]{1,0:T(8,128)(2,1)S(1)}, bf16[256,256]{1,0:T(8,128)(2,1)S(1)}, u32[]{:S(2)}, u32[]{:S(2)}) collective-permute-start(bf16[256,256]{1,0:T(8,128)(2,1)S(1)} %get-tuple-element.50), channel_id=1, source_target_pairs={{0,6},{2,4},{4,2},{6,0},{8,14},{10,12},{12,10},{14,8},{16,22},{18,... | collective-permute-start | bytes 393224 | tf_op jit(solution)/shard_map/ppermute | solution.py:32
  30.1 13.8 %collective-permute-start.12 = (bf16[4,256,128]{2,1,0:T(8,128)(2,1)S(1)}, bf16[4,256,128]{2,1,0:T(8,128)(2,1)S(1)}, u32[]{:S(2)}, u32[]{:S(2)}) collective-permute-start(bf16[4,256,128]{2,1,0:T(8,128)(2,1)S(1)} %get-tuple-element.55), channel_id=1, source_target_pairs={{8,0},{10,2},{12,4},{14,6},{16,8},{18,10},{20,12},{22,14},{24,16},... | collective-permute-start | bytes 786440 | tf_op jit(solution)/shard_map/ppermute | solution.py:27
  40.2 9.2 %collective-permute-start.16 = (bf16[4,256,128]{2,1,0:T(8,128)(2,1)S(1)}, bf16[4,256,128]{2,1,0:T(8,128)(2,1)S(1)}, u32[]{:S(2)}, u32[]{:S(2)}) collective-permute-start(bf16[4,256,128]{2,1,0:T(8,128)(2,1)S(1)} %get-tuple-element.61), channel_id=1, source_target_pairs={{8,0},{10,2},{12,4},{14,6},{16,8},{18,10},{20,12},{22,14},{24,16},... | collective-permute-start | bytes 786440 | tf_op jit(solution)/shard_map/ppermute | solution.py:27
  45.8 6.5 %collective-permute-start.13 = (bf16[256,256]{1,0:T(8,128)(2,1)S(1)}, bf16[256,256]{1,0:T(8,128)(2,1)S(1)}, u32[]{:S(2)}, u32[]{:S(2)}) collective-permute-start(bf16[256,256]{1,0:T(8,128)(2,1)S(1)} %get-tuple-element.57), channel_id=1, source_target_pairs={{0,2},{2,0},{4,6},{6,4},{8,10},{10,8},{12,14},{14,12},{16,18},{18,... | collective-permute-start | bytes 393224 | tf_op jit(solution)/shard_map/ppermute | solution.py:32
  46.5 9.5 %collective-permute-start.14 = (bf16[256,256]{1,0:T(8,128)(2,1)S(1)}, bf16[256,256]{1,0:T(8,128)(2,1)S(1)}, u32[]{:S(2)}, u32[]{:S(2)}) collective-permute-start(bf16[256,256]{1,0:T(8,128)(2,1)S(1)} %get-tuple-element.58), channel_id=1, source_target_pairs={{0,4},{2,6},{4,0},{6,2},{8,12},{10,14},{12,8},{14,10},{16,20},{18,... | collective-permute-start | bytes 393224 | tf_op jit(solution)/shard_map/ppermute | solution.py:32
  48.2 7.8 %collective-permute-start.15 = (bf16[256,256]{1,0:T(8,128)(2,1)S(1)}, bf16[256,256]{1,0:T(8,128)(2,1)S(1)}, u32[]{:S(2)}, u32[]{:S(2)}) collective-permute-start(bf16[256,256]{1,0:T(8,128)(2,1)S(1)} %get-tuple-element.59), channel_id=1, source_target_pairs={{0,6},{2,4},{4,2},{6,0},{8,14},{10,12},{12,10},{14,8},{16,22},{18,... | collective-permute-start | bytes 393224 | tf_op jit(solution)/shard_map/ppermute | solution.py:32
  49.5 7.5 %collective-permute-start.17 = (bf16[256,256]{1,0:T(8,128)(2,1)S(1)}, bf16[256,256]{1,0:T(8,128)(2,1)S(1)}, u32[]{:S(2)}, u32[]{:S(2)}) collective-permute-start(bf16[256,256]{1,0:T(8,128)(2,1)S(1)} %get-tuple-element.64), channel_id=1, source_target_pairs={{0,2},{2,0},{4,6},{6,4},{8,10},{10,8},{12,14},{14,12},{16,18},{18,... | collective-permute-start | bytes 393224 | tf_op jit(solution)/shard_map/ppermute | solution.py:32
  50.1 9.5 %collective-permute-start.18 = (bf16[256,256]{1,0:T(8,128)(2,1)S(1)}, bf16[256,256]{1,0:T(8,128)(2,1)S(1)}, u32[]{:S(2)}, u32[]{:S(2)}) collective-permute-start(bf16[256,256]{1,0:T(8,128)(2,1)S(1)} %get-tuple-element.65), channel_id=1, source_target_pairs={{0,4},{2,6},{4,0},{6,2},{8,12},{10,14},{12,8},{14,10},{16,20},{18,... | collective-permute-start | bytes 393224 | tf_op jit(solution)/shard_map/ppermute | solution.py:32
  52.3 7.3 %collective-permute-start.19 = (bf16[256,256]{1,0:T(8,128)(2,1)S(1)}, bf16[256,256]{1,0:T(8,128)(2,1)S(1)}, u32[]{:S(2)}, u32[]{:S(2)}) collective-permute-start(bf16[256,256]{1,0:T(8,128)(2,1)S(1)} %get-tuple-element.66), channel_id=1, source_target_pairs={{0,6},{2,4},{4,2},{6,0},{8,14},{10,12},{12,10},{14,8},{16,22},{18,... | collective-permute-start | bytes 393224 | tf_op jit(solution)/shard_map/ppermute | solution.py:32

commit v8 on v4

--- a/solution.py
+++ b/solution.py
@@ -59,17 +59,24 @@
     return pl.ds(pl.multiple_of(index * width, width), width)
 
 
-def pack_kv(group, keys, values):
+def begin():
+    def body(out_ref):
+        out_ref[...] = jnp.zeros_like(out_ref)
+
+    return call(body, [jax.ShapeDtypeStruct((8, 128), jnp.float32)], flops=AHEAD)()[0]
+
+
+def pack_kv(group, keys, values, before):
     tokens, width = keys.shape[0], keys.shape[1] // group
 
-    def body(k_ref, v_ref, *refs):
+    def body(k_ref, v_ref, before_ref, *refs):
         for r in range(group):
             member = spot(group)[0] ^ r
             refs[r][:, :width] = k_ref[:, lanes(member, width)]
             refs[r][:, width:] = v_ref[:, lanes(member, width)]
 
     outs = [jax.ShapeDtypeStruct((tokens, 2 * width), jnp.bfloat16)] * group
-    return call(body, outs, flops=AHEAD)(keys, values)
+    return call(body, outs, flops=AHEAD, specs=[VMEM, VMEM, ANY])(keys, values, before)
 
 
 def pack_queries(group, queries, before):
@@ -83,13 +90,13 @@
     return call(body, outs, specs=[VMEM, ANY])(queries, before)
 
 
-def order_pieces(group, pieces):
-    def body(*refs):
-        for r in range(group):
-            refs[group][spot(group)[0] ^ r] = refs[r][...]
+def order_pieces(group, pieces, before):
+    def body(*refs):
+        for r in range(group):
+            refs[-1][spot(group)[0] ^ r] = refs[r][...]
 
     outs = [jax.ShapeDtypeStruct((group,) + pieces[0].shape, jnp.bfloat16)]
-    return call(body, outs)(*pieces)[0]
+    return call(body, outs, specs=[VMEM] * group + [ANY])(*pieces, before)[0]
 
 
 def head_product(parts, part, out_weight, layer_cotangent, before):
@@ -281,7 +288,7 @@
                 delta = delta * inverse
                 q = (qt_ref[head, b].astype(jnp.float32) * inverse).astype(jnp.bfloat16)
                 for c in range(z.span):
-                    ds = (e_ref[head, b, c].astype(jnp.float32) * (dp_all[c] - delta)).astype(jnp.bfloat16)
+                    ds = e_ref[head, b, c] * (dp_all[c] - delta).astype(jnp.bfloat16)
                     ds_ref[head, b, c] = ds
                     dk_all[b + c] += lax.dot_general(ds, q, NT, preferred_element_type=jnp.float32)
 
@@ -404,18 +411,20 @@
             shifted(earlier[number], "ctx", -group * (back_groups - number)) for number in range(back_groups)
         ]
 
-    sent = pack_kv(group, keys, values)
-    kv_own = order_pieces(group, trade(sent))
-    kv_earlier = [shifted(kv_own, "ctx", group * step) for step in range(back_groups, 0, -1)]
+    sent = pack_kv(group, keys, values, begin())
+    kv_pieces = trade(sent)
     z = Shape(group, back_groups, heads, per_head, tokens)
     query_sent = pack_queries(group, queries, sent[0])
-    qt = turn_queries(z, trade(query_sent))
     if tp_count == 2:
         other = head_product(2, 1, out_weight, layer_cotangent, [query_sent[0]])
-        terms = [head_product(2, 0, out_weight, layer_cotangent, [kv_own, other]), swapped(other, "tp", 1)]
+        mine = head_product(2, 0, out_weight, layer_cotangent, [other])
+        terms = [mine, swapped(other, "tp", 1)]
     else:
-        product = head_product(1, 0, out_weight, layer_cotangent, [query_sent[0]])
-        terms = [lax.psum_scatter(product, "tp", scatter_dimension=0, tiled=True)]
+        mine = head_product(1, 0, out_weight, layer_cotangent, [query_sent[0]])
+        terms = [lax.psum_scatter(mine, "tp", scatter_dimension=0, tiled=True)]
+    kv_own = order_pieces(group, kv_pieces, mine)
+    kv_earlier = [shifted(kv_own, "ctx", group * step) for step in range(back_groups, 0, -1)]
+    qt = turn_queries(z, trade(query_sent))
     grads = trade(pack_grads(group, terms))
     e, inverse = softmax(z, kv_own, kv_earlier, qt)
     g, dv_own, dv_earlier = value_terms(z, e, inverse, grads)

time: 58.9 us -> 60 us (1.019)
  waiting for transfers between devices: 9.84 us -> 13.7 us
  local copies, waits for them, and re-layouts: 2.74 us -> 1.28 us
  starting transfers between devices: 25.2 us -> 24.2 us
    ppermute x16, waiting for transfers between devices: 7.48 us -> 10.5 us  [swapped(): lax.ppermute(value, axis, [(source, source ^ bits) for source in range(co...]
    ppermute x16, starting transfers between devices: 19.2 us -> 17.3 us  [swapped(): lax.ppermute(value, axis, [(source, source ^ bits) for source in range(co...]
    unnamed x10 -> x14, local copies, waits for them, and re-layouts: 2.74 us -> 1.28 us
    ppermute x3, starting transfers between devices: 6.03 us -> 6.92 us  [shifted(): lax.ppermute(value, axis, [(source, source + steps) for source in range(l...]
    ppermute x3, waiting for transfers between devices: 2.36 us -> 3.22 us  [shifted(): lax.ppermute(value, axis, [(source, source + steps) for source in range(l...]
    pallas_call x14 -> x15, Pallas kernels: 19.7 us -> 19.4 us  [run(): pl.pallas_call(body, out_shape=tuple(outs), in_specs=specs or [SMEM if a....]
  transfers between devices with their start and end apart: 19 -> 19, of which waited for: 6 -> 8; matrix products, arithmetic and copies ran while one was open for 0% -> 0% of each run, Pallas kernels for 28% -> 27%
where the time goes in v8:
time: 60 us; the launch traced here: 59.5 us
  starting transfers between devices  24.2 us (40%)
  Pallas kernels  19.4 us (32%)
  waiting for transfers between devices  13.7 us (23%)
  local copies, waits for them, and re-layouts  1.28 us (2%)
  between operations  0.85 us (1%)
    pallas_call x15, Pallas kernels, run(): pl.pallas_call(body, out_shape=tuple(outs), in_specs=specs or [SMEM if a....  19.4 us
    ppermute x16, starting transfers between devices, swapped(): lax.ppermute(value, axis, [(source, source ^ bits) for source in range(co...  17.3 us
    ppermute x16, waiting for transfers between devices, swapped(): lax.ppermute(value, axis, [(source, source ^ bits) for source in range(co...  10.5 us
    ppermute x3, starting transfers between devices, shifted(): lax.ppermute(value, axis, [(source, source + steps) for source in range(l...  6.92 us
    ppermute x3, waiting for transfers between devices, shifted(): lax.ppermute(value, axis, [(source, source + steps) for source in range(l...  3.22 us
    unnamed x14, local copies, waits for them, and re-layouts  1.28 us
  transfers between devices with their start and end apart: 19, of which 8 were waited for; matrix products, arithmetic and copies ran while one was open for 0% of the time, Pallas kernels for 27%

profile of v8, /device:TPU:24, one launch (start us, length us, event | category | flops | bytes accessed | tf_op | source)
XLA Modules:
  0.0 59.5 jit_solution(13994232362826565381)
XLA Ops:
  0.7 0.9 %copy-done.3 = bf16[256,512]{1,0:T(8,128)(2,1)S(1)} copy-done((bf16[256,512]{1,0:T(8,128)(2,1)S(1)}, bf16[256,512]{1,0:T(8,128)(2,1)}, u32[]{:S(2)}) %copy-start.3) | copy-done | bytes 262168
  1.8 1.6 %collective-permute-start = (bf16[256,256]{1,0:T(8,128)(2,1)S(1)}, bf16[256,256]{1,0:T(8,128)(2,1)S(1)}, u32[]{:S(2)}, u32[]{:S(2)}) collective-permute-start(bf16[256,256]{1,0:T(8,128)(2,1)S(1)} %get-tuple-element.35), channel_id=1, source_target_pairs={{0,2},{2,0},{4,6},{6,4},{8,10},{10,8},{12,14},{14,12},{16,18},{18,... | collective-permute-start | bytes 393224 | tf_op jit(solution)/shard_map/ppermute | solution.py:32
  3.3 1.5 %collective-permute-start.1 = (bf16[256,256]{1,0:T(8,128)(2,1)S(1)}, bf16[256,256]{1,0:T(8,128)(2,1)S(1)}, u32[]{:S(2)}, u32[]{:S(2)}) collective-permute-start(bf16[256,256]{1,0:T(8,128)(2,1)S(1)} %get-tuple-element.36), channel_id=1, source_target_pairs={{0,4},{2,6},{4,0},{6,2},{8,12},{10,14},{12,8},{14,10},{16,20},{18,... | collective-permute-start | bytes 393224 | tf_op jit(solution)/shard_map/ppermute | solution.py:32
  5.7 1.9 %shard_map.79.refs_0_ = bf16[1024,256]{1,0:T(8,128)(2,1)S(1)} custom-call(bf16[2048,2688]{1,0:T(8,128)(2,1)S(1)} %bitcast.1, bf16[256,2688]{1,0:T(8,128)(2,1)S(1)} %copy-done, bf16[256,256]{1,0:T(8,128)(2,1)S(1)} %get-tuple-element.38.refs_0_), custom_call_target="tpu_custom_call" | custom-call | flops 1409286144 | bytes 13041664 | tf_op jit(solution)/shard_map/pallas_call | solution.py:39
  7.7 1.9 %shard_map.80.refs_4_.refs_0_ = bf16[1024,256]{1,0:T(8,128)(2,1)S(1)} custom-call(bf16[2048,2688]{1,0:T(8,128)(2,1)S(1)} %bitcast.1, bf16[256,2688]{1,0:T(8,128)(2,1)S(1)} %copy-done, bf16[1024,256]{1,0:T(8,128)(2,1)S(1)} %shard_map.79.refs_0_), custom_call_target="tpu_custom_call" | custom-call | flops 1409286144 | bytes 13434880 | tf_op jit(solution)/shard_map/pallas_call | solution.py:39
  9.6 1.5 %collective-permute-done.1.refs_2_ = bf16[256,256]{1,0:T(8,128)(2,1)S(1)} collective-permute-done((bf16[256,256]{1,0:T(8,128)(2,1)S(1)}, bf16[256,256]{1,0:T(8,128)(2,1)S(1)}, u32[]{:S(2)}, u32[]{:S(2)}) %collective-permute-start.1) | collective-permute-done | bytes 131104 | tf_op jit(solution)/shard_map/ppermute | solution.py:32
  11.2 1.3 %collective-permute-start.3 = (bf16[4,256,256]{2,1,0:T(8,128)(2,1)S(1)}, bf16[4,256,256]{2,1,0:T(8,128)(2,1)S(1)}, u32[]{:S(2)}, u32[]{:S(2)}) collective-permute-start(bf16[4,256,256]{2,1,0:T(8,128)(2,1)S(1)} %shard_map.81.refs_0_.own_ref), channel_id=1, source_target_pairs={{0,8},{2,10},{4,12},{6,14},{8,16},{10,18},{12,20},{14,22},{16,24},... | collective-permute-start | bytes 1572872 | tf_op jit(solution)/shard_map/ppermute | solution.py:27
  12.5 1.3 %collective-permute-start.4 = (bf16[256,256]{1,0:T(8,128)(2,1)S(1)}, bf16[256,256]{1,0:T(8,128)(2,1)S(1)}, u32[]{:S(2)}, u32[]{:S(2)}) collective-permute-start(bf16[256,256]{1,0:T(8,128)(2,1)S(1)} %get-tuple-element.39), channel_id=1, source_target_pairs={{0,2},{2,0},{4,6},{6,4},{8,10},{10,8},{12,14},{14,12},{16,18},{18,... | collective-permute-start | bytes 393224 | tf_op jit(solution)/shard_map/ppermute | solution.py:32
  13.7 0.8 %collective-permute-start.5 = (bf16[256,256]{1,0:T(8,128)(2,1)S(1)}, bf16[256,256]{1,0:T(8,128)(2,1)S(1)}, u32[]{:S(2)}, u32[]{:S(2)}) collective-permute-start(bf16[256,256]{1,0:T(8,128)(2,1)S(1)} %get-tuple-element.40), channel_id=1, source_target_pairs={{0,4},{2,6},{4,0},{6,2},{8,12},{10,14},{12,8},{14,10},{16,20},{18,... | collective-permute-start | bytes 393224 | tf_op jit(solution)/shard_map/ppermute | solution.py:32
  14.6 1.4 %collective-permute-start.6 = (bf16[256,256]{1,0:T(8,128)(2,1)S(1)}, bf16[256,256]{1,0:T(8,128)(2,1)S(1)}, u32[]{:S(2)}, u32[]{:S(2)}) collective-permute-start(bf16[256,256]{1,0:T(8,128)(2,1)S(1)} %get-tuple-element.41), channel_id=1, source_target_pairs={{0,6},{2,4},{4,2},{6,0},{8,14},{10,12},{12,10},{14,8},{16,22},{18,... | collective-permute-start | bytes 393224 | tf_op jit(solution)/shard_map/ppermute | solution.py:32
  16.1 1.3 %collective-permute-start.8 = (bf16[256,256]{1,0:T(8,128)(2,1)S(1)}, bf16[256,256]{1,0:T(8,128)(2,1)S(1)}, u32[]{:S(2)}, u32[]{:S(2)}) collective-permute-start(bf16[256,256]{1,0:T(8,128)(2,1)S(1)} %get-tuple-element.45), channel_id=1, source_target_pairs={{0,2},{2,0},{4,6},{6,4},{8,10},{10,8},{12,14},{14,12},{16,18},{18,... | collective-permute-start | bytes 393224 | tf_op jit(solution)/shard_map/ppermute | solution.py:32
  17.4 1.1 %collective-permute-done.4.refs_1_ = bf16[256,256]{1,0:T(8,128)(2,1)S(1)} collective-permute-done((bf16[256,256]{1,0:T(8,128)(2,1)S(1)}, bf16[256,256]{1,0:T(8,128)(2,1)S(1)}, u32[]{:S(2)}, u32[]{:S(2)}) %collective-permute-start.4) | collective-permute-done | bytes 131104 | tf_op jit(solution)/shard_map/ppermute | solution.py:32
  18.6 1.5 %collective-permute-start.9 = (bf16[256,256]{1,0:T(8,128)(2,1)S(1)}, bf16[256,256]{1,0:T(8,128)(2,1)S(1)}, u32[]{:S(2)}, u32[]{:S(2)}) collective-permute-start(bf16[256,256]{1,0:T(8,128)(2,1)S(1)} %get-tuple-element.46), channel_id=1, source_target_pairs={{0,4},{2,6},{4,0},{6,2},{8,12},{10,14},{12,8},{14,10},{16,20},{18,... | collective-permute-start | bytes 393224 | tf_op jit(solution)/shard_map/ppermute | solution.py:32
  20.0 2.4 %collective-permute-done.5.refs_2_ = bf16[256,256]{1,0:T(8,128)(2,1)S(1)} collective-permute-done((bf16[256,256]{1,0:T(8,128)(2,1)S(1)}, bf16[256,256]{1,0:T(8,128)(2,1)S(1)}, u32[]{:S(2)}, u32[]{:S(2)}) %collective-permute-start.5) | collective-permute-done | bytes 131104 | tf_op jit(solution)/shard_map/ppermute | solution.py:32
  22.7 3.2 %collective-permute-done.3.refs_1_.refs_0_ = bf16[4,256,256]{2,1,0:T(8,128)(2,1)S(1)} collective-permute-done((bf16[4,256,256]{2,1,0:T(8,128)(2,1)S(1)}, bf16[4,256,256]{2,1,0:T(8,128)(2,1)S(1)}, u32[]{:S(2)}, u32[]{:S(2)}) %collective-permute-start.3) | collective-permute-done | bytes 524320 | tf_op jit(solution)/shard_map/ppermute | solution.py:27
  25.9 3.8 %shard_map.83 = (bf16[1,4,5,256,512]{4,3,2,1,0:T(8,128)(2,1)S(1)}, f32[1,4,1,512]{3,2,1,0:T(1,128)S(1)}) custom-call(bf16[4,256,256]{2,1,0:T(8,128)(2,1)S(1)} %shard_map.81.refs_0_.own_ref, bf16[4,256,256]{2,1,0:T(8,128)(2,1)S(1)} %collective-permute-done.3.refs_1_.refs_0_, bf16[1,4,128,512]{3,2,1,0:T(8,128)(2,1)S(1)} %shard_map.82.refs_2_.qt_ref), custom_call_target="tpu_custom_call" | custom-call | flops 671088640 | bytes 6823936 | tf_op jit(solution)/shard_map/pallas_call | solution.py:39
  29.7 2.2 %shard_map.85 = (bf16[1,4,128,512]{3,2,1,0:T(8,128)(2,1)S(1)}, f32[4,256,128]{2,1,0:T(8,128)S(1)}, bf16[4,256,128]{2,1,0:T(8,128)(2,1)S(1)}) custom-call(bf16[1,4,5,256,512]{4,3,2,1,0:T(8,128)(2,1)S(1)} %get-tuple-element.42.e_ref, f32[1,4,1,512]{3,2,1,0:T(1,128)S(1)} %get-tuple-element.43.inverse_ref, bf16[256,256]{1,0:T(8,128)(2,1)S(1)} %get-tuple-element.44.refs_0_, ...), custom_call_target="tpu_custom_call" | custom-call | flops 671088640 | bytes 7086080 | tf_op jit(solution)/shard_map/pallas_call | solution.py:39
  31.9 3.3 %collective-permute-start.11 = (bf16[4,256,128]{2,1,0:T(8,128)(2,1)S(1)}, bf16[4,256,128]{2,1,0:T(8,128)(2,1)S(1)}, u32[]{:S(2)}, u32[]{:S(2)}) collective-permute-start(bf16[4,256,128]{2,1,0:T(8,128)(2,1)S(1)} %get-tuple-element.51), channel_id=1, source_target_pairs={{8,0},{10,2},{12,4},{14,6},{16,8},{18,10},{20,12},{22,14},{24,16},... | collective-permute-start | bytes 786440 | tf_op jit(solution)/shard_map/ppermute | solution.py:27
  35.2 5.4 %shard_map.86 = (bf16[1,4,5,256,512]{4,3,2,1,0:T(8,128)(2,1)S(1)}, f32[4,256,128]{2,1,0:T(8,128)S(1)}, bf16[4,256,128]{2,1,0:T(8,128)(2,1)S(1)}) custom-call(bf16[1,4,5,256,512]{4,3,2,1,0:T(8,128)(2,1)S(1)} %get-tuple-element.42.e_ref, f32[1,4,1,512]{3,2,1,0:T(1,128)S(1)} %get-tuple-element.43.inverse_ref, ...), custom_call_target="tpu_custom_call" | custom-call | flops 1342177280 | bytes 13377536 | tf_op jit(solution)/shard_map/pallas_call | solution.py:39
  40.5 2.4 %collective-permute-start.15 = (bf16[4,256,128]{2,1,0:T(8,128)(2,1)S(1)}, bf16[4,256,128]{2,1,0:T(8,128)(2,1)S(1)}, u32[]{:S(2)}, u32[]{:S(2)}) collective-permute-start(bf16[4,256,128]{2,1,0:T(8,128)(2,1)S(1)} %get-tuple-element.57), channel_id=1, source_target_pairs={{8,0},{10,2},{12,4},{14,6},{16,8},{18,10},{20,12},{22,14},{24,16},... | collective-permute-start | bytes 786440 | tf_op jit(solution)/shard_map/ppermute | solution.py:27
  42.9 1.9 %shard_map.87 = (bf16[4,256,128]{2,1,0:T(8,128)(2,1)S(1)}, bf16[256,256]{1,0:T(8,128)(2,1)S(1)}, bf16[256,256]{1,0:T(8,128)(2,1)S(1)}, bf16[256,256]{1,0:T(8,128)(2,1)S(1)}, bf16[256,256]{1,0:T(8,128)(2,1)S(1)}) custom-call(bf16[1,4,5,256,512]{4,3,2,1,0:T(8,128)(2,1)S(1)} %get-tuple-element.49.ds_ref, f32[1,4,1,512]{3,2,1,0:T(1,128)S(1)} %get-tuple-element.43.inverse_ref, ...), custom_call_target="tpu_custom_call" | custom-call | flops 671088640 | bytes 7872512 | tf_op jit(solution)/shard_map/pallas_call | solution.py:39
  44.9 0.7 %collective-permute-start.12 = (bf16[256,256]{1,0:T(8,128)(2,1)S(1)}, bf16[256,256]{1,0:T(8,128)(2,1)S(1)}, u32[]{:S(2)}, u32[]{:S(2)}) collective-permute-start(bf16[256,256]{1,0:T(8,128)(2,1)S(1)} %get-tuple-element.53), channel_id=1, source_target_pairs={{0,2},{2,0},{4,6},{6,4},{8,10},{10,8},{12,14},{14,12},{16,18},{18,... | collective-permute-start | bytes 393224 | tf_op jit(solution)/shard_map/ppermute | solution.py:32
  45.5 1.5 %collective-permute-start.13 = (bf16[256,256]{1,0:T(8,128)(2,1)S(1)}, bf16[256,256]{1,0:T(8,128)(2,1)S(1)}, u32[]{:S(2)}, u32[]{:S(2)}) collective-permute-start(bf16[256,256]{1,0:T(8,128)(2,1)S(1)} %get-tuple-element.54), channel_id=1, source_target_pairs={{0,4},{2,6},{4,0},{6,2},{8,12},{10,14},{12,8},{14,10},{16,20},{18,... | collective-permute-start | bytes 393224 | tf_op jit(solution)/shard_map/ppermute | solution.py:32
  47.0 1.4 %collective-permute-start.14 = (bf16[256,256]{1,0:T(8,128)(2,1)S(1)}, bf16[256,256]{1,0:T(8,128)(2,1)S(1)}, u32[]{:S(2)}, u32[]{:S(2)}) collective-permute-start(bf16[256,256]{1,0:T(8,128)(2,1)S(1)} %get-tuple-element.55), channel_id=1, source_target_pairs={{0,6},{2,4},{4,2},{6,0},{8,14},{10,12},{12,10},{14,8},{16,22},{18,... | collective-permute-start | bytes 393224 | tf_op jit(solution)/shard_map/ppermute | solution.py:32
  48.5 0.7 %collective-permute-start.16 = (bf16[256,256]{1,0:T(8,128)(2,1)S(1)}, bf16[256,256]{1,0:T(8,128)(2,1)S(1)}, u32[]{:S(2)}, u32[]{:S(2)}) collective-permute-start(bf16[256,256]{1,0:T(8,128)(2,1)S(1)} %get-tuple-element.60), channel_id=1, source_target_pairs={{0,2},{2,0},{4,6},{6,4},{8,10},{10,8},{12,14},{14,12},{16,18},{18,... | collective-permute-start | bytes 393224 | tf_op jit(solution)/shard_map/ppermute | solution.py:32
  49.2 1.5 %collective-permute-start.17 = (bf16[256,256]{1,0:T(8,128)(2,1)S(1)}, bf16[256,256]{1,0:T(8,128)(2,1)S(1)}, u32[]{:S(2)}, u32[]{:S(2)}) collective-permute-start(bf16[256,256]{1,0:T(8,128)(2,1)S(1)} %get-tuple-element.61), channel_id=1, source_target_pairs={{0,4},{2,6},{4,0},{6,2},{8,12},{10,14},{12,8},{14,10},{16,20},{18,... | collective-permute-start | bytes 393224 | tf_op jit(solution)/shard_map/ppermute | solution.py:32
  50.7 0.6 collective-permute-done.12.refs_1_
  51.3 1.6 %collective-permute-start.18 = (bf16[256,256]{1,0:T(8,128)(2,1)S(1)}, bf16[256,256]{1,0:T(8,128)(2,1)S(1)}, u32[]{:S(2)}, u32[]{:S(2)}) collective-permute-start(bf16[256,256]{1,0:T(8,128)(2,1)S(1)} %get-tuple-element.62), channel_id=1, source_target_pairs={{0,6},{2,4},{4,2},{6,0},{8,14},{10,12},{12,10},{14,8},{16,22},{18,... | collective-permute-start | bytes 393224 | tf_op jit(solution)/shard_map/ppermute | solution.py:32
  52.9 1.9 %collective-permute-done.13.refs_2_ = bf16[256,256]{1,0:T(8,128)(2,1)S(1)} collective-permute-done((bf16[256,256]{1,0:T(8,128)(2,1)S(1)}, bf16[256,256]{1,0:T(8,128)(2,1)S(1)}, u32[]{:S(2)}, u32[]{:S(2)}) %collective-permute-start.13) | collective-permute-done | bytes 131104 | tf_op jit(solution)/shard_map/ppermute | solution.py:32
  54.8 0.9 %shard_map.88 = bf16[256,1024]{1,0:T(8,128)(2,1)} custom-call(bf16[256,256]{1,0:T(8,128)(2,1)S(1)} %get-tuple-element.52.refs_0_, bf16[256,256]{1,0:T(8,128)(2,1)S(1)} %collective-permute-done.12.refs_1_, bf16[256,256]{1,0:T(8,128)(2,1)S(1)} %collective-permute-done.13.refs_2_, bf16[256,256]{1,0:T(8,128)(2,1)S(1)} %collective-permute-done.14.refs_3_), custom_call_target="tpu_custom_call" | custom-call | bytes 1048576 | tf_op jit(solution)/shard_map/pallas_call | solution.py:39
  55.9 2.7 %collective-permute-done.17.refs_2_ = bf16[256,256]{1,0:T(8,128)(2,1)S(1)} collective-permute-done((bf16[256,256]{1,0:T(8,128)(2,1)S(1)}, bf16[256,256]{1,0:T(8,128)(2,1)S(1)}, u32[]{:S(2)}, u32[]{:S(2)}) %collective-permute-start.17) | collective-permute-done | bytes 131104 | tf_op jit(solution)/shard_map/ppermute | solution.py:32
  58.6 0.9 %shard_map.90 = (bf16[256,512]{1,0:T(8,128)(2,1)}, bf16[256,512]{1,0:T(8,128)(2,1)}) custom-call(bf16[256,256]{1,0:T(8,128)(2,1)S(1)} %get-tuple-element.59.refs_0_, bf16[256,256]{1,0:T(8,128)(2,1)S(1)} %collective-permute-done.16.refs_1_, bf16[256,256]{1,0:T(8,128)(2,1)S(1)} %collective-permute-done.17.refs_2_, ...), custom_call_target="tpu_custom_call" | custom-call | bytes 1048576 | tf_op jit(solution)/shard_map/pallas_call | solution.py:39
  (36 shorter events, 1.8 us)
Async XLA Ops:
  0.6 1.0 %copy-start.3 = (bf16[256,512]{1,0:T(8,128)(2,1)S(1)}, bf16[256,512]{1,0:T(8,128)(2,1)}, u32[]{:S(2)}) copy-start(bf16[256,512]{1,0:T(8,128)(2,1)} %v_ref.1) | copy-start | bytes 786436
  0.6 1.0 %copy-start.2 = (bf16[256,512]{1,0:T(8,128)(2,1)S(1)}, bf16[256,512]{1,0:T(8,128)(2,1)}, u32[]{:S(2)}) copy-start(bf16[256,512]{1,0:T(8,128)(2,1)} %k_ref.1) | copy-start | bytes 786436
  0.7 4.7 %slice-start = ((s8[11010048]{0:T(1024)(128)(4,1)}), s8[4194304]{0:T(1024)(128)(4,1)S(1)}, s32[]{:S(2)}) async-start(s8[11010048]{0:T(1024)(128)(4,1)} %bitcast), calls=%async_computation | async-start | bytes 8388608
  0.7 4.7 %slice-start.1 = ((s8[11010048]{0:T(1024)(128)(4,1)}), s8[4194304]{0:T(1024)(128)(4,1)S(1)}, s32[]{:S(2)}) async-start(s8[11010048]{0:T(1024)(128)(4,1)} %bitcast), calls=%async_computation.1 | async-start | bytes 8388608
  1.7 3.7 %copy-start.1 = (bf16[256,1024]{1,0:T(8,128)(2,1)S(1)}, bf16[256,1024]{1,0:T(8,128)(2,1)}, u32[]{:S(2)}) copy-start(bf16[256,1024]{1,0:T(8,128)(2,1)} %q_ref.1) | copy-start | bytes 1572868
  1.7 3.8 %slice-start.2 = ((s8[11010048]{0:T(1024)(128)(4,1)}), s8[2621440]{0:T(1024)(128)(4,1)S(1)}, s32[]{:S(2)}) async-start(s8[11010048]{0:T(1024)(128)(4,1)} %bitcast), calls=%async_computation.2 | async-start | bytes 5242880
  1.7 4.0 %copy-start = (bf16[256,2688]{1,0:T(8,128)(2,1)S(1)}, bf16[256,2688]{1,0:T(8,128)(2,1)}, u32[]{:S(2)}) copy-start(bf16[256,2688]{1,0:T(8,128)(2,1)} %c_ref.3) | copy-start | bytes 4128772
  1.8 7.8 %collective-permute-start = (bf16[256,256]{1,0:T(8,128)(2,1)S(1)}, bf16[256,256]{1,0:T(8,128)(2,1)S(1)}, u32[]{:S(2)}, u32[]{:S(2)}) collective-permute-start(bf16[256,256]{1,0:T(8,128)(2,1)S(1)} %get-tuple-element.35), channel_id=1, source_target_pairs={{0,2},{2,0},{4,6},{6,4},{8,10},{10,8},{12,14},{14,12},{16,18},{18,... | collective-permute-start | bytes 393224 | tf_op jit(solution)/shard_map/ppermute | solution.py:32
  3.3 7.8 %collective-permute-start.1 = (bf16[256,256]{1,0:T(8,128)(2,1)S(1)}, bf16[256,256]{1,0:T(8,128)(2,1)S(1)}, u32[]{:S(2)}, u32[]{:S(2)}) collective-permute-start(bf16[256,256]{1,0:T(8,128)(2,1)S(1)} %get-tuple-element.36), channel_id=1, source_target_pairs={{0,4},{2,6},{4,0},{6,2},{8,12},{10,14},{12,8},{14,10},{16,20},{18,... | collective-permute-start | bytes 393224 | tf_op jit(solution)/shard_map/ppermute | solution.py:32
  4.8 6.3 %collective-permute-start.2 = (bf16[256,256]{1,0:T(8,128)(2,1)S(1)}, bf16[256,256]{1,0:T(8,128)(2,1)S(1)}, u32[]{:S(2)}, u32[]{:S(2)}) collective-permute-start(bf16[256,256]{1,0:T(8,128)(2,1)S(1)} %get-tuple-element.37), channel_id=1, source_target_pairs={{0,6},{2,4},{4,2},{6,0},{8,14},{10,12},{12,10},{14,8},{16,22},{18,... | collective-permute-start | bytes 393224 | tf_op jit(solution)/shard_map/ppermute | solution.py:32
  7.6 8.4 %collective-permute-start.7 = (bf16[1024,256]{1,0:T(8,128)(2,1)S(1)}, bf16[1024,256]{1,0:T(8,128)(2,1)S(1)}, u32[]{:S(2)}, u32[]{:S(2)}) collective-permute-start(bf16[1024,256]{1,0:T(8,128)(2,1)S(1)} %shard_map.79.refs_0_), channel_id=1, source_target_pairs={{0,1},{1,0},{2,3},{3,2},{4,5},{5,4},{6,7},{7,6},{8,9},{9,8},{10,11... | collective-permute-start | bytes 1572872 | tf_op jit(solution)/shard_map/ppermute | solution.py:32
  11.2 14.7 %collective-permute-start.3 = (bf16[4,256,256]{2,1,0:T(8,128)(2,1)S(1)}, bf16[4,256,256]{2,1,0:T(8,128)(2,1)S(1)}, u32[]{:S(2)}, u32[]{:S(2)}) collective-permute-start(bf16[4,256,256]{2,1,0:T(8,128)(2,1)S(1)} %shard_map.81.refs_0_.own_ref), channel_id=1, source_target_pairs={{0,8},{2,10},{4,12},{6,14},{8,16},{10,18},{12,20},{14,22},{16,24},... | collective-permute-start | bytes 1572872 | tf_op jit(solution)/shard_map/ppermute | solution.py:27
  12.5 6.1 %collective-permute-start.4 = (bf16[256,256]{1,0:T(8,128)(2,1)S(1)}, bf16[256,256]{1,0:T(8,128)(2,1)S(1)}, u32[]{:S(2)}, u32[]{:S(2)}) collective-permute-start(bf16[256,256]{1,0:T(8,128)(2,1)S(1)} %get-tuple-element.39), channel_id=1, source_target_pairs={{0,2},{2,0},{4,6},{6,4},{8,10},{10,8},{12,14},{14,12},{16,18},{18,... | collective-permute-start | bytes 393224 | tf_op jit(solution)/shard_map/ppermute | solution.py:32
  13.7 8.7 %collective-permute-start.5 = (bf16[256,256]{1,0:T(8,128)(2,1)S(1)}, bf16[256,256]{1,0:T(8,128)(2,1)S(1)}, u32[]{:S(2)}, u32[]{:S(2)}) collective-permute-start(bf16[256,256]{1,0:T(8,128)(2,1)S(1)} %get-tuple-element.40), channel_id=1, source_target_pairs={{0,4},{2,6},{4,0},{6,2},{8,12},{10,14},{12,8},{14,10},{16,20},{18,... | collective-permute-start | bytes 393224 | tf_op jit(solution)/shard_map/ppermute | solution.py:32
  14.6 7.9 %collective-permute-start.6 = (bf16[256,256]{1,0:T(8,128)(2,1)S(1)}, bf16[256,256]{1,0:T(8,128)(2,1)S(1)}, u32[]{:S(2)}, u32[]{:S(2)}) collective-permute-start(bf16[256,256]{1,0:T(8,128)(2,1)S(1)} %get-tuple-element.41), channel_id=1, source_target_pairs={{0,6},{2,4},{4,2},{6,0},{8,14},{10,12},{12,10},{14,8},{16,22},{18,... | collective-permute-start | bytes 393224 | tf_op jit(solution)/shard_map/ppermute | solution.py:32
  16.1 13.5 %collective-permute-start.8 = (bf16[256,256]{1,0:T(8,128)(2,1)S(1)}, bf16[256,256]{1,0:T(8,128)(2,1)S(1)}, u32[]{:S(2)}, u32[]{:S(2)}) collective-permute-start(bf16[256,256]{1,0:T(8,128)(2,1)S(1)} %get-tuple-element.45), channel_id=1, source_target_pairs={{0,2},{2,0},{4,6},{6,4},{8,10},{10,8},{12,14},{14,12},{16,18},{18,... | collective-permute-start | bytes 393224 | tf_op jit(solution)/shard_map/ppermute | solution.py:32
  18.6 11.1 %collective-permute-start.9 = (bf16[256,256]{1,0:T(8,128)(2,1)S(1)}, bf16[256,256]{1,0:T(8,128)(2,1)S(1)}, u32[]{:S(2)}, u32[]{:S(2)}) collective-permute-start(bf16[256,256]{1,0:T(8,128)(2,1)S(1)} %get-tuple-element.46), channel_id=1, source_target_pairs={{0,4},{2,6},{4,0},{6,2},{8,12},{10,14},{12,8},{14,10},{16,20},{18,... | collective-permute-start | bytes 393224 | tf_op jit(solution)/shard_map/ppermute | solution.py:32
  22.5 7.2 %collective-permute-start.10 = (bf16[256,256]{1,0:T(8,128)(2,1)S(1)}, bf16[256,256]{1,0:T(8,128)(2,1)S(1)}, u32[]{:S(2)}, u32[]{:S(2)}) collective-permute-start(bf16[256,256]{1,0:T(8,128)(2,1)S(1)} %get-tuple-element.47), channel_id=1, source_target_pairs={{0,6},{2,4},{4,2},{6,0},{8,14},{10,12},{12,10},{14,8},{16,22},{18,... | collective-permute-start | bytes 393224 | tf_op jit(solution)/shard_map/ppermute | solution.py:32
  31.9 11.0 %collective-permute-start.11 = (bf16[4,256,128]{2,1,0:T(8,128)(2,1)S(1)}, bf16[4,256,128]{2,1,0:T(8,128)(2,1)S(1)}, u32[]{:S(2)}, u32[]{:S(2)}) collective-permute-start(bf16[4,256,128]{2,1,0:T(8,128)(2,1)S(1)} %get-tuple-element.51), channel_id=1, source_target_pairs={{8,0},{10,2},{12,4},{14,6},{16,8},{18,10},{20,12},{22,14},{24,16},... | collective-permute-start | bytes 786440 | tf_op jit(solution)/shard_map/ppermute | solution.py:27
  40.5 7.9 %collective-permute-start.15 = (bf16[4,256,128]{2,1,0:T(8,128)(2,1)S(1)}, bf16[4,256,128]{2,1,0:T(8,128)(2,1)S(1)}, u32[]{:S(2)}, u32[]{:S(2)}) collective-permute-start(bf16[4,256,128]{2,1,0:T(8,128)(2,1)S(1)} %get-tuple-element.57), channel_id=1, source_target_pairs={{8,0},{10,2},{12,4},{14,6},{16,8},{18,10},{20,12},{22,14},{24,16},... | collective-permute-start | bytes 786440 | tf_op jit(solution)/shard_map/ppermute | solution.py:27
  44.9 6.4 %collective-permute-start.12 = (bf16[256,256]{1,0:T(8,128)(2,1)S(1)}, bf16[256,256]{1,0:T(8,128)(2,1)S(1)}, u32[]{:S(2)}, u32[]{:S(2)}) collective-permute-start(bf16[256,256]{1,0:T(8,128)(2,1)S(1)} %get-tuple-element.53), channel_id=1, source_target_pairs={{0,2},{2,0},{4,6},{6,4},{8,10},{10,8},{12,14},{14,12},{16,18},{18,... | collective-permute-start | bytes 393224 | tf_op jit(solution)/shard_map/ppermute | solution.py:32
  45.5 9.3 %collective-permute-start.13 = (bf16[256,256]{1,0:T(8,128)(2,1)S(1)}, bf16[256,256]{1,0:T(8,128)(2,1)S(1)}, u32[]{:S(2)}, u32[]{:S(2)}) collective-permute-start(bf16[256,256]{1,0:T(8,128)(2,1)S(1)} %get-tuple-element.54), channel_id=1, source_target_pairs={{0,4},{2,6},{4,0},{6,2},{8,12},{10,14},{12,8},{14,10},{16,20},{18,... | collective-permute-start | bytes 393224 | tf_op jit(solution)/shard_map/ppermute | solution.py:32
  47.0 7.8 %collective-permute-start.14 = (bf16[256,256]{1,0:T(8,128)(2,1)S(1)}, bf16[256,256]{1,0:T(8,128)(2,1)S(1)}, u32[]{:S(2)}, u32[]{:S(2)}) collective-permute-start(bf16[256,256]{1,0:T(8,128)(2,1)S(1)} %get-tuple-element.55), channel_id=1, source_target_pairs={{0,6},{2,4},{4,2},{6,0},{8,14},{10,12},{12,10},{14,8},{16,22},{18,... | collective-permute-start | bytes 393224 | tf_op jit(solution)/shard_map/ppermute | solution.py:32
  48.5 7.4 %collective-permute-start.16 = (bf16[256,256]{1,0:T(8,128)(2,1)S(1)}, bf16[256,256]{1,0:T(8,128)(2,1)S(1)}, u32[]{:S(2)}, u32[]{:S(2)}) collective-permute-start(bf16[256,256]{1,0:T(8,128)(2,1)S(1)} %get-tuple-element.60), channel_id=1, source_target_pairs={{0,2},{2,0},{4,6},{6,4},{8,10},{10,8},{12,14},{14,12},{16,18},{18,... | collective-permute-start | bytes 393224 | tf_op jit(solution)/shard_map/ppermute | solution.py:32
  49.2 9.4 %collective-permute-start.17 = (bf16[256,256]{1,0:T(8,128)(2,1)S(1)}, bf16[256,256]{1,0:T(8,128)(2,1)S(1)}, u32[]{:S(2)}, u32[]{:S(2)}) collective-permute-start(bf16[256,256]{1,0:T(8,128)(2,1)S(1)} %get-tuple-element.61), channel_id=1, source_target_pairs={{0,4},{2,6},{4,0},{6,2},{8,12},{10,14},{12,8},{14,10},{16,20},{18,... | collective-permute-start | bytes 393224 | tf_op jit(solution)/shard_map/ppermute | solution.py:32
  51.3 7.3 %collective-permute-start.18 = (bf16[256,256]{1,0:T(8,128)(2,1)S(1)}, bf16[256,256]{1,0:T(8,128)(2,1)S(1)}, u32[]{:S(2)}, u32[]{:S(2)}) collective-permute-start(bf16[256,256]{1,0:T(8,128)(2,1)S(1)} %get-tuple-element.62), channel_id=1, source_target_pairs={{0,6},{2,4},{4,2},{6,0},{8,14},{10,12},{12,10},{14,8},{16,22},{18,... | collective-permute-start | bytes 393224 | tf_op jit(solution)/shard_map/ppermute | solution.py:32

commit v9 on v8

--- a/solution.py
+++ b/solution.py
@@ -55,6 +55,10 @@
     return place, index - place
 
 
+def hop(group, r):
+    return group - r if r else 0
+
+
 def lanes(index, width):
     return pl.ds(pl.multiple_of(index * width, width), width)
 
@@ -71,7 +75,7 @@
 
     def body(k_ref, v_ref, before_ref, *refs):
         for r in range(group):
-            member = spot(group)[0] ^ r
+            member = spot(group)[0] ^ hop(group, r)
             refs[r][:, :width] = k_ref[:, lanes(member, width)]
             refs[r][:, width:] = v_ref[:, lanes(member, width)]
 
@@ -84,7 +88,7 @@
 
     def body(q_ref, before_ref, *out_refs):
         for r in range(group):
-            out_refs[r][...] = q_ref[:, lanes(spot(group)[0] ^ r, width)]
+            out_refs[r][...] = q_ref[:, lanes(spot(group)[0] ^ hop(group, r), width)]
 
     outs = [jax.ShapeDtypeStruct((tokens, width), jnp.bfloat16)] * group
     return call(body, outs, specs=[VMEM, ANY])(queries, before)
@@ -93,7 +97,7 @@
 def order_pieces(group, pieces, before):
     def body(*refs):
         for r in range(group):
-            refs[-1][spot(group)[0] ^ r] = refs[r][...]
+            refs[-1][spot(group)[0] ^ hop(group, r)] = refs[r][...]
 
     outs = [jax.ShapeDtypeStruct((group,) + pieces[0].shape, jnp.bfloat16)]
     return call(body, outs, specs=[VMEM] * group + [ANY])(*pieces, before)[0]
@@ -122,22 +126,22 @@
     )[0]
 
 
-def pack_grads(group, terms):
+def pack_grads(group, terms, before):
     rows, tokens = terms[0].shape
     rows //= group
 
     def body(*refs):
         for r in range(group):
-            there = lanes(spot(group)[0] ^ r, rows)
+            there = lanes(spot(group)[0] ^ hop(group, r), rows)
             total = refs[0][there, :]
             if len(terms) > 1:
                 total = total.astype(jnp.float32)
                 for term in refs[1 : len(terms)]:
                     total = total + term[there, :].astype(jnp.float32)
-            refs[len(terms) + r][...] = total.astype(jnp.bfloat16)
+            refs[len(terms) + 1 + r][...] = total.astype(jnp.bfloat16)
 
     outs = [jax.ShapeDtypeStruct((rows, tokens), jnp.bfloat16)] * group
-    return call(body, outs)(*terms)
+    return call(body, outs, specs=[VMEM] * len(terms) + [ANY])(*terms, before)
 
 
 class Shape:
@@ -163,7 +167,7 @@
             for r in range(z.group):
                 for j in range(z.per_head):
                     lower = (head * z.per_head + j) * HEAD_SIZE
-                    refs[z.group][head, spot(z.group)[0] ^ r, :, j * z.tokens : (j + 1) * z.tokens] = refs[r][
+                    refs[z.group][head, spot(z.group)[0] ^ hop(z.group, r), :, j * z.tokens : (j + 1) * z.tokens] = refs[r][
                         :, lower : lower + HEAD_SIZE
                     ].T
 
@@ -237,7 +241,7 @@
             for r in range(z.group):
                 for j in range(z.per_head):
                     lower = (head * z.per_head + j) * HEAD_SIZE
-                    g_ref[head, place ^ r, :, j * z.tokens : (j + 1) * z.tokens] = g_refs[r][
+                    g_ref[head, place ^ hop(z.group, r), :, j * z.tokens : (j + 1) * z.tokens] = g_refs[r][
                         lower : lower + HEAD_SIZE, :
                     ]
             dv_all[...] = jnp.zeros_like(dv_all)
@@ -314,13 +318,9 @@
 
 def query_terms(z, ds, inverse, kv_own, kv_earlier, dv_terms):
     def body(ds_ref, inverse_ref, own_ref, *refs):
-        earlier_refs, term_refs, dv_ref = refs[: z.steps], refs[z.steps : 2 * z.steps + 1], refs[2 * z.steps + 1]
-        dq_refs = refs[2 * z.steps + 2 : 2 * z.steps + 2 + z.group]
-        kt_all, dq_all = refs[2 * z.steps + 2 + z.group :]
-        dv = term_refs[0][...]
-        for term in term_refs[1:]:
-            dv = dv + term[...].astype(jnp.float32)
-        dv_ref[...] = dv.astype(jnp.bfloat16)
+        earlier_refs, term_refs = refs[: z.steps], refs[z.steps : 2 * z.steps + 1]
+        out_refs = refs[2 * z.steps + 1 : 2 * z.steps + 1 + z.group]
+        kt_all, dq_all = refs[2 * z.steps + 1 + z.group :]
         for head in range(z.heads):
             at = slice(head * HEAD_SIZE, (head + 1) * HEAD_SIZE)
             for number in range(z.total):
@@ -341,18 +341,21 @@
                     )
 
         for r in range(z.group):
-            dq_refs[r][...] = dq_all[spot(z.group)[0] ^ r]
-
-    outs = [jax.ShapeDtypeStruct((z.group, z.tokens, z.kv_width), jnp.bfloat16)]
-    outs += [jax.ShapeDtypeStruct((z.tokens, z.width), jnp.bfloat16)] * z.group
+            member = spot(z.group)[0] ^ hop(z.group, r)
+            dv = term_refs[0][member]
+            for term in term_refs[1:]:
+                dv = dv + term[member].astype(jnp.float32)
+            out_refs[r][:, : z.width] = dq_all[member]
+            out_refs[r][:, z.width :] = dv.astype(jnp.bfloat16)
+
+    outs = [jax.ShapeDtypeStruct((z.tokens, z.width + z.kv_width), jnp.bfloat16)] * z.group
     scratch = [
         pltpu.VMEM((z.total, HEAD_SIZE, z.tokens), jnp.bfloat16),
         pltpu.VMEM((z.group, z.tokens, z.width), jnp.bfloat16),
     ]
-    results = call(body, outs, scratch, flops=2 * z.entries * HEAD_SIZE)(
+    return call(body, outs, scratch, flops=2 * z.entries * HEAD_SIZE)(
         ds, inverse, kv_own, *kv_earlier, *dv_terms
     )
-    return results[0], results[1:]
 
 
 def pack_terms(group, sums):
@@ -361,7 +364,7 @@
 
     def body(*refs):
         for r in range(group):
-            member = spot(group)[0] ^ r
+            member = spot(group)[0] ^ hop(group, r)
             number = 0
             for column, terms in enumerate(sums):
                 total = refs[number][member].astype(jnp.float32)
@@ -374,18 +377,19 @@
     return call(body, outs)(*flat)
 
 
-def unpack(group, pieces, widths):
+def unpack(group, pieces, widths, before):
     tokens = pieces[0].shape[0]
 
     def body(*refs):
         for r in range(group):
             lower = 0
             for number, width in enumerate(widths):
-                refs[group + number][:, lanes(spot(group)[0] ^ r, width)] = refs[r][:, lower : lower + width]
+                there = lanes(spot(group)[0] ^ hop(group, r), width)
+                refs[group + 1 + number][:, there] = refs[r][:, lower : lower + width]
                 lower += width
 
     outs = [jax.ShapeDtypeStruct((tokens, group * width), jnp.bfloat16) for width in widths]
-    return call(body, outs)(*pieces)
+    return call(body, outs, specs=[VMEM] * group + [ANY])(*pieces, before)
 
 
 def local(layer_cotangent, out_weight, queries, keys, values):
@@ -403,8 +407,9 @@
     heads = kv_heads // group
     kv_width = heads * HEAD_SIZE
     back_groups = WINDOW_LENGTH // (group * tokens)
+
     def trade(sent):
-        return [sent[0]] + [swapped(sent[r], "ctx", r) for r in range(1, group)]
+        return [sent[0]] + [swapped(sent[r], "ctx", hop(group, r)) for r in range(1, group)]
 
     def returned(earlier):
         return [
@@ -415,27 +420,25 @@
     kv_pieces = trade(sent)
     z = Shape(group, back_groups, heads, per_head, tokens)
     query_sent = pack_queries(group, queries, sent[0])
+    qt = turn_queries(z, trade(query_sent))
     if tp_count == 2:
         other = head_product(2, 1, out_weight, layer_cotangent, [query_sent[0]])
-        mine = head_product(2, 0, out_weight, layer_cotangent, [other])
-        terms = [mine, swapped(other, "tp", 1)]
+        terms = [head_product(2, 0, out_weight, layer_cotangent, [other]), swapped(other, "tp", 1)]
     else:
-        mine = head_product(1, 0, out_weight, layer_cotangent, [query_sent[0]])
-        terms = [lax.psum_scatter(mine, "tp", scatter_dimension=0, tiled=True)]
-    kv_own = order_pieces(group, kv_pieces, mine)
+        other = head_product(1, 0, out_weight, layer_cotangent, [query_sent[0]])
+        terms = [lax.psum_scatter(other, "tp", scatter_dimension=0, tiled=True)]
+    kv_own = order_pieces(group, kv_pieces, terms[0])
     kv_earlier = [shifted(kv_own, "ctx", group * step) for step in range(back_groups, 0, -1)]
-    qt = turn_queries(z, trade(query_sent))
-    grads = trade(pack_grads(group, terms))
+    grads = trade(pack_grads(group, terms, kv_own))
     e, inverse = softmax(z, kv_own, kv_earlier, qt)
     g, dv_own, dv_earlier = value_terms(z, e, inverse, grads)
     dv_terms = [dv_own] + returned(dv_earlier)
     ds, dk_own, dk_earlier = key_terms(z, e, inverse, qt, g, kv_own, kv_earlier)
     dk_terms = [dk_own] + returned(dk_earlier)
-    dv, dq = query_terms(z, ds, inverse, kv_own, kv_earlier, dv_terms)
-    dq = trade(dq)
-    dkv = trade(pack_terms(group, [dk_terms, [dv]]))
-    (query_grads,) = unpack(group, dq, [dq[0].shape[1]])
-    key_gradients, value_gradients = unpack(group, dkv, [kv_width, kv_width])
+    pieces = trade(query_terms(z, ds, inverse, kv_own, kv_earlier, dv_terms))
+    query_grads, value_gradients = unpack(group, pieces, [z.width, kv_width], ds)
+    pieces = trade(pack_terms(group, [dk_terms]))
+    (key_gradients,) = unpack(group, pieces, [kv_width], value_gradients)
     return (query_grads, key_gradients, value_gradients)
 
 

time: 60 us -> 60.9 us (1.015)
  starting transfers between devices: 24.2 us -> 26.5 us
  waiting for transfers between devices: 13.7 us -> 11.7 us
  local copies, waits for them, and re-layouts: 1.28 us -> 2.23 us
    ppermute x16, starting transfers between devices: 17.3 us -> 19.1 us  [swapped(): lax.ppermute(value, axis, [(source, source ^ bits) for source in range(co...]
    ppermute x16, waiting for transfers between devices: 10.5 us -> 9.3 us  [swapped(): lax.ppermute(value, axis, [(source, source ^ bits) for source in range(co...]
    unnamed x14 -> x16, local copies, waits for them, and re-layouts: 1.28 us -> 2.23 us
    ppermute x3, waiting for transfers between devices: 3.22 us -> 2.4 us  [shifted(): lax.ppermute(value, axis, [(source, source + steps) for source in range(l...]
  transfers between devices with their start and end apart: 19 -> 19, of which waited for: 8 -> 10; matrix products, arithmetic and copies ran while one was open for 0% -> 0% of each run, Pallas kernels for 27% -> 27%
where the time goes in v9:
time: 60.9 us; the launch traced here: 60.6 us
  starting transfers between devices  26.5 us (44%)
  Pallas kernels  19.4 us (32%)
  waiting for transfers between devices  11.7 us (19%)
  local copies, waits for them, and re-layouts  2.23 us (4%)
  between operations  0.84 us (1%)
    pallas_call x15, Pallas kernels, run(): pl.pallas_call(body, out_shape=tuple(outs), in_specs=specs or [SMEM if a....  19.4 us
    ppermute x16, starting transfers between devices, swapped(): lax.ppermute(value, axis, [(source, source ^ bits) for source in range(co...  19.1 us
    ppermute x16, waiting for transfers between devices, swapped(): lax.ppermute(value, axis, [(source, source ^ bits) for source in range(co...  9.3 us
    ppermute x3, starting transfers between devices, shifted(): lax.ppermute(value, axis, [(source, source + steps) for source in range(l...  7.36 us
    ppermute x3, waiting for transfers between devices, shifted(): lax.ppermute(value, axis, [(source, source + steps) for source in range(l...  2.4 us
    unnamed x16, local copies, waits for them, and re-layouts  2.23 us
  transfers between devices with their start and end apart: 19, of which 10 were waited for; matrix products, arithmetic and copies ran while one was open for 0% of the time, Pallas kernels for 27%

profile of v9, /device:TPU:24, one launch (start us, length us, event | category | flops | bytes accessed | tf_op | source)
XLA Modules:
  0.0 60.6 jit_solution(13646106335524256073)
XLA Ops:
  0.7 0.9 %copy-done.4 = bf16[256,512]{1,0:T(8,128)(2,1)S(1)} copy-done((bf16[256,512]{1,0:T(8,128)(2,1)S(1)}, bf16[256,512]{1,0:T(8,128)(2,1)}, u32[]{:S(2)}) %copy-start.4) | copy-done | bytes 262168
  1.8 2.5 %collective-permute-start = (bf16[256,256]{1,0:T(8,128)(2,1)S(1)}, bf16[256,256]{1,0:T(8,128)(2,1)S(1)}, u32[]{:S(2)}, u32[]{:S(2)}) collective-permute-start(bf16[256,256]{1,0:T(8,128)(2,1)S(1)} %get-tuple-element.34), channel_id=1, source_target_pairs={{0,6},{2,4},{4,2},{6,0},{8,14},{10,12},{12,10},{14,8},{16,22},{18,... | collective-permute-start | bytes 393224 | tf_op jit(solution)/shard_map/ppermute | solution.py:32
  5.7 1.9 %shard_map.79.refs_0_ = bf16[1024,256]{1,0:T(8,128)(2,1)S(1)} custom-call(bf16[2048,2688]{1,0:T(8,128)(2,1)S(1)} %bitcast.1, bf16[256,2688]{1,0:T(8,128)(2,1)S(1)} %copy-done, bf16[256,256]{1,0:T(8,128)(2,1)S(1)} %get-tuple-element.37.refs_0_), custom_call_target="tpu_custom_call" | custom-call | flops 1409286144 | bytes 13041664 | tf_op jit(solution)/shard_map/pallas_call | solution.py:39
  7.7 1.9 %shard_map.80.refs_4_.refs_0_ = bf16[1024,256]{1,0:T(8,128)(2,1)S(1)} custom-call(bf16[2048,2688]{1,0:T(8,128)(2,1)S(1)} %bitcast.1, bf16[256,2688]{1,0:T(8,128)(2,1)S(1)} %copy-done, bf16[1024,256]{1,0:T(8,128)(2,1)S(1)} %shard_map.79.refs_0_), custom_call_target="tpu_custom_call" | custom-call | flops 1409286144 | bytes 13434880 | tf_op jit(solution)/shard_map/pallas_call | solution.py:39
  9.6 1.2 %collective-permute-done.1.refs_2_ = bf16[256,256]{1,0:T(8,128)(2,1)S(1)} collective-permute-done((bf16[256,256]{1,0:T(8,128)(2,1)S(1)}, bf16[256,256]{1,0:T(8,128)(2,1)S(1)}, u32[]{:S(2)}, u32[]{:S(2)}) %collective-permute-start.1) | collective-permute-done | bytes 131104 | tf_op jit(solution)/shard_map/ppermute | solution.py:32
  10.9 1.3 %collective-permute-start.3 = (bf16[4,256,256]{2,1,0:T(8,128)(2,1)S(1)}, bf16[4,256,256]{2,1,0:T(8,128)(2,1)S(1)}, u32[]{:S(2)}, u32[]{:S(2)}) collective-permute-start(bf16[4,256,256]{2,1,0:T(8,128)(2,1)S(1)} %shard_map.81.refs_0_.refs_2_.own_ref), channel_id=1, source_target_pairs={{0,8},{2,10},{4,12},{6,14},{8,16},{10,18},{12,20},{14,22},{16,24},... | collective-permute-start | bytes 1572872 | tf_op jit(solution)/shard_map/ppermute | solution.py:27
  12.2 1.8 %collective-permute-start.4 = (bf16[256,256]{1,0:T(8,128)(2,1)S(1)}, bf16[256,256]{1,0:T(8,128)(2,1)S(1)}, u32[]{:S(2)}, u32[]{:S(2)}) collective-permute-start(bf16[256,256]{1,0:T(8,128)(2,1)S(1)} %get-tuple-element.38), channel_id=1, source_target_pairs={{0,6},{2,4},{4,2},{6,0},{8,14},{10,12},{12,10},{14,8},{16,22},{18,... | collective-permute-start | bytes 393224 | tf_op jit(solution)/shard_map/ppermute | solution.py:32
  13.9 1.3 %collective-permute-start.5 = (bf16[256,256]{1,0:T(8,128)(2,1)S(1)}, bf16[256,256]{1,0:T(8,128)(2,1)S(1)}, u32[]{:S(2)}, u32[]{:S(2)}) collective-permute-start(bf16[256,256]{1,0:T(8,128)(2,1)S(1)} %get-tuple-element.39), channel_id=1, source_target_pairs={{0,4},{2,6},{4,0},{6,2},{8,12},{10,14},{12,8},{14,10},{16,20},{18,... | collective-permute-start | bytes 393224 | tf_op jit(solution)/shard_map/ppermute | solution.py:32
  15.9 1.8 %collective-permute-start.8 = (bf16[256,256]{1,0:T(8,128)(2,1)S(1)}, bf16[256,256]{1,0:T(8,128)(2,1)S(1)}, u32[]{:S(2)}, u32[]{:S(2)}) collective-permute-start(bf16[256,256]{1,0:T(8,128)(2,1)S(1)} %get-tuple-element.44), channel_id=1, source_target_pairs={{0,6},{2,4},{4,2},{6,0},{8,14},{10,12},{12,10},{14,8},{16,22},{18,... | collective-permute-start | bytes 393224 | tf_op jit(solution)/shard_map/ppermute | solution.py:32
  17.6 1.9 %collective-permute-done.4.refs_1_ = bf16[256,256]{1,0:T(8,128)(2,1)S(1)} collective-permute-done((bf16[256,256]{1,0:T(8,128)(2,1)S(1)}, bf16[256,256]{1,0:T(8,128)(2,1)S(1)}, u32[]{:S(2)}, u32[]{:S(2)}) %collective-permute-start.4) | collective-permute-done | bytes 131104 | tf_op jit(solution)/shard_map/ppermute | solution.py:32
  19.5 1.5 %collective-permute-start.9 = (bf16[256,256]{1,0:T(8,128)(2,1)S(1)}, bf16[256,256]{1,0:T(8,128)(2,1)S(1)}, u32[]{:S(2)}, u32[]{:S(2)}) collective-permute-start(bf16[256,256]{1,0:T(8,128)(2,1)S(1)} %get-tuple-element.45), channel_id=1, source_target_pairs={{0,4},{2,6},{4,0},{6,2},{8,12},{10,14},{12,8},{14,10},{16,20},{18,... | collective-permute-start | bytes 393224 | tf_op jit(solution)/shard_map/ppermute | solution.py:32
  21.0 1.4 %collective-permute-done.5.refs_2_ = bf16[256,256]{1,0:T(8,128)(2,1)S(1)} collective-permute-done((bf16[256,256]{1,0:T(8,128)(2,1)S(1)}, bf16[256,256]{1,0:T(8,128)(2,1)S(1)}, u32[]{:S(2)}, u32[]{:S(2)}) %collective-permute-start.5) | collective-permute-done | bytes 131104 | tf_op jit(solution)/shard_map/ppermute | solution.py:32
  22.4 1.5 %collective-permute-start.10 = (bf16[256,256]{1,0:T(8,128)(2,1)S(1)}, bf16[256,256]{1,0:T(8,128)(2,1)S(1)}, u32[]{:S(2)}, u32[]{:S(2)}) collective-permute-start(bf16[256,256]{1,0:T(8,128)(2,1)S(1)} %get-tuple-element.46), channel_id=1, source_target_pairs={{0,2},{2,0},{4,6},{6,4},{8,10},{10,8},{12,14},{14,12},{16,18},{18,... | collective-permute-start | bytes 393224 | tf_op jit(solution)/shard_map/ppermute | solution.py:32
  24.2 2.4 %collective-permute-done.3.refs_1_.refs_0_ = bf16[4,256,256]{2,1,0:T(8,128)(2,1)S(1)} collective-permute-done((bf16[4,256,256]{2,1,0:T(8,128)(2,1)S(1)}, bf16[4,256,256]{2,1,0:T(8,128)(2,1)S(1)}, u32[]{:S(2)}, u32[]{:S(2)}) %collective-permute-start.3) | collective-permute-done | bytes 524320 | tf_op jit(solution)/shard_map/ppermute | solution.py:27
  26.6 3.8 %shard_map.83 = (bf16[1,4,5,256,512]{4,3,2,1,0:T(8,128)(2,1)S(1)}, f32[1,4,1,512]{3,2,1,0:T(1,128)S(1)}) custom-call(bf16[4,256,256]{2,1,0:T(8,128)(2,1)S(1)} %shard_map.81.refs_0_.refs_2_.own_ref, bf16[4,256,256]{2,1,0:T(8,128)(2,1)S(1)} %collective-permute-done.3.refs_1_.refs_0_, bf16[1,4,128,512]{3,2,1,0:T(8,128)(2,1)S(1)} %shard_map.82.refs_2_.qt_ref), custom_call_target="tpu_custom_call" | custom-call | flops 671088640 | bytes 6823936 | tf_op jit(solution)/shard_map/pallas_call | solution.py:39
  30.4 2.2 %shard_map.85 = (bf16[1,4,128,512]{3,2,1,0:T(8,128)(2,1)S(1)}, f32[4,256,128]{2,1,0:T(8,128)S(1)}, bf16[4,256,128]{2,1,0:T(8,128)(2,1)S(1)}) custom-call(bf16[1,4,5,256,512]{4,3,2,1,0:T(8,128)(2,1)S(1)} %get-tuple-element.41.e_ref, f32[1,4,1,512]{3,2,1,0:T(1,128)S(1)} %get-tuple-element.42.inverse_ref, bf16[256,256]{1,0:T(8,128)(2,1)S(1)} %get-tuple-element.43.refs_0_, ...), custom_call_target="tpu_custom_call" | custom-call | flops 671088640 | bytes 7086080 | tf_op jit(solution)/shard_map/pallas_call | solution.py:39
  32.6 3.7 %collective-permute-start.11 = (bf16[4,256,128]{2,1,0:T(8,128)(2,1)S(1)}, bf16[4,256,128]{2,1,0:T(8,128)(2,1)S(1)}, u32[]{:S(2)}, u32[]{:S(2)}) collective-permute-start(bf16[4,256,128]{2,1,0:T(8,128)(2,1)S(1)} %get-tuple-element.50), channel_id=1, source_target_pairs={{8,0},{10,2},{12,4},{14,6},{16,8},{18,10},{20,12},{22,14},{24,16},... | collective-permute-start | bytes 786440 | tf_op jit(solution)/shard_map/ppermute | solution.py:27
  36.3 5.4 %shard_map.86 = (bf16[1,4,5,256,512]{4,3,2,1,0:T(8,128)(2,1)S(1)}, f32[4,256,128]{2,1,0:T(8,128)S(1)}, bf16[4,256,128]{2,1,0:T(8,128)(2,1)S(1)}) custom-call(bf16[1,4,5,256,512]{4,3,2,1,0:T(8,128)(2,1)S(1)} %get-tuple-element.41.e_ref, f32[1,4,1,512]{3,2,1,0:T(1,128)S(1)} %get-tuple-element.42.inverse_ref, ...), custom_call_target="tpu_custom_call" | custom-call | flops 1342177280 | bytes 13377536 | tf_op jit(solution)/shard_map/pallas_call | solution.py:39
  41.7 2.4 %collective-permute-start.15 = (bf16[4,256,128]{2,1,0:T(8,128)(2,1)S(1)}, bf16[4,256,128]{2,1,0:T(8,128)(2,1)S(1)}, u32[]{:S(2)}, u32[]{:S(2)}) collective-permute-start(bf16[4,256,128]{2,1,0:T(8,128)(2,1)S(1)} %get-tuple-element.57), channel_id=1, source_target_pairs={{8,0},{10,2},{12,4},{14,6},{16,8},{18,10},{20,12},{22,14},{24,16},... | collective-permute-start | bytes 786440 | tf_op jit(solution)/shard_map/ppermute | solution.py:27
  44.0 2.0 %shard_map.87 = (bf16[256,384]{1,0:T(8,128)(2,1)S(1)}, bf16[256,384]{1,0:T(8,128)(2,1)S(1)}, bf16[256,384]{1,0:T(8,128)(2,1)S(1)}, bf16[256,384]{1,0:T(8,128)(2,1)S(1)}) custom-call(bf16[1,4,5,256,512]{4,3,2,1,0:T(8,128)(2,1)S(1)} %get-tuple-element.48.ds_ref.refs_4_, f32[1,4,1,512]{3,2,1,0:T(1,128)S(1)} %get-tuple-element.42.inverse_ref, ...), custom_call_target="tpu_custom_call" | custom-call | flops 671088640 | bytes 7872512 | tf_op jit(solution)/shard_map/pallas_call | solution.py:39
  46.0 1.6 %collective-permute-start.12 = (bf16[256,384]{1,0:T(8,128)(2,1)S(1)}, bf16[256,384]{1,0:T(8,128)(2,1)S(1)}, u32[]{:S(2)}, u32[]{:S(2)}) collective-permute-start(bf16[256,384]{1,0:T(8,128)(2,1)S(1)} %get-tuple-element.52), channel_id=1, source_target_pairs={{0,6},{2,4},{4,2},{6,0},{8,14},{10,12},{12,10},{14,8},{16,22},{18,... | collective-permute-start | bytes 589832 | tf_op jit(solution)/shard_map/ppermute | solution.py:32
  47.6 0.9 %collective-permute-start.13 = (bf16[256,384]{1,0:T(8,128)(2,1)S(1)}, bf16[256,384]{1,0:T(8,128)(2,1)S(1)}, u32[]{:S(2)}, u32[]{:S(2)}) collective-permute-start(bf16[256,384]{1,0:T(8,128)(2,1)S(1)} %get-tuple-element.53), channel_id=1, source_target_pairs={{0,4},{2,6},{4,0},{6,2},{8,12},{10,14},{12,8},{14,10},{16,20},{18,... | collective-permute-start | bytes 589832 | tf_op jit(solution)/shard_map/ppermute | solution.py:32
  48.5 1.1 %collective-permute-start.14 = (bf16[256,384]{1,0:T(8,128)(2,1)S(1)}, bf16[256,384]{1,0:T(8,128)(2,1)S(1)}, u32[]{:S(2)}, u32[]{:S(2)}) collective-permute-start(bf16[256,384]{1,0:T(8,128)(2,1)S(1)} %get-tuple-element.54), channel_id=1, source_target_pairs={{0,2},{2,0},{4,6},{6,4},{8,10},{10,8},{12,14},{14,12},{16,18},{18,... | collective-permute-start | bytes 589832 | tf_op jit(solution)/shard_map/ppermute | solution.py:32
  49.6 1.6 %collective-permute-start.16 = (bf16[256,128]{1,0:T(8,128)(2,1)S(1)}, bf16[256,128]{1,0:T(8,128)(2,1)S(1)}, u32[]{:S(2)}, u32[]{:S(2)}) collective-permute-start(bf16[256,128]{1,0:T(8,128)(2,1)S(1)} %get-tuple-element.59), channel_id=1, source_target_pairs={{0,6},{2,4},{4,2},{6,0},{8,14},{10,12},{12,10},{14,8},{16,22},{18,... | collective-permute-start | bytes 196616 | tf_op jit(solution)/shard_map/ppermute | solution.py:32
  51.2 0.9 %collective-permute-start.17 = (bf16[256,128]{1,0:T(8,128)(2,1)S(1)}, bf16[256,128]{1,0:T(8,128)(2,1)S(1)}, u32[]{:S(2)}, u32[]{:S(2)}) collective-permute-start(bf16[256,128]{1,0:T(8,128)(2,1)S(1)} %get-tuple-element.60), channel_id=1, source_target_pairs={{0,4},{2,6},{4,0},{6,2},{8,12},{10,14},{12,8},{14,10},{16,20},{18,... | collective-permute-start | bytes 196616 | tf_op jit(solution)/shard_map/ppermute | solution.py:32
  52.1 2.6 %collective-permute-done.12.refs_1_ = bf16[256,384]{1,0:T(8,128)(2,1)S(1)} collective-permute-done((bf16[256,384]{1,0:T(8,128)(2,1)S(1)}, bf16[256,384]{1,0:T(8,128)(2,1)S(1)}, u32[]{:S(2)}, u32[]{:S(2)}) %collective-permute-start.12) | collective-permute-done | bytes 196640 | tf_op jit(solution)/shard_map/ppermute | solution.py:32
  54.7 1.1 %collective-permute-start.18 = (bf16[256,128]{1,0:T(8,128)(2,1)S(1)}, bf16[256,128]{1,0:T(8,128)(2,1)S(1)}, u32[]{:S(2)}, u32[]{:S(2)}) collective-permute-start(bf16[256,128]{1,0:T(8,128)(2,1)S(1)} %get-tuple-element.61), channel_id=1, source_target_pairs={{0,2},{2,0},{4,6},{6,4},{8,10},{10,8},{12,14},{14,12},{16,18},{18,... | collective-permute-start | bytes 196616 | tf_op jit(solution)/shard_map/ppermute | solution.py:32
  55.8 0.9 %collective-permute-done.13.refs_2_ = bf16[256,384]{1,0:T(8,128)(2,1)S(1)} collective-permute-done((bf16[256,384]{1,0:T(8,128)(2,1)S(1)}, bf16[256,384]{1,0:T(8,128)(2,1)S(1)}, u32[]{:S(2)}, u32[]{:S(2)}) %collective-permute-start.13) | collective-permute-done | bytes 196640 | tf_op jit(solution)/shard_map/ppermute | solution.py:32
  56.8 1.0 %shard_map.88 = (bf16[256,1024]{1,0:T(8,128)(2,1)}, bf16[256,512]{1,0:T(8,128)(2,1)}) custom-call(bf16[256,384]{1,0:T(8,128)(2,1)S(1)} %get-tuple-element.51.refs_0_, bf16[256,384]{1,0:T(8,128)(2,1)S(1)} %collective-permute-done.12.refs_1_, bf16[256,384]{1,0:T(8,128)(2,1)S(1)} %collective-permute-done.13.refs_2_, ...), custom_call_target="tpu_custom_call" | custom-call | bytes 6815744 | tf_op jit(solution)/shard_map/pallas_call | solution.py:39
  58.1 0.8 %collective-permute-done.18.refs_3_ = bf16[256,128]{1,0:T(8,128)(2,1)S(1)} collective-permute-done((bf16[256,128]{1,0:T(8,128)(2,1)S(1)}, bf16[256,128]{1,0:T(8,128)(2,1)S(1)}, u32[]{:S(2)}, u32[]{:S(2)}) %collective-permute-start.18) | collective-permute-done | bytes 65568 | tf_op jit(solution)/shard_map/ppermute | solution.py:32
  58.9 0.9 %copy-done.2 = bf16[256,512]{1,0:T(8,128)(2,1)S(1)} copy-done((bf16[256,512]{1,0:T(8,128)(2,1)S(1)}, bf16[256,512]{1,0:T(8,128)(2,1)}, u32[]{:S(2)}) %copy-start.2) | copy-done | bytes 262168
  59.9 0.8 %shard_map.90 = bf16[256,512]{1,0:T(8,128)(2,1)} custom-call(bf16[256,128]{1,0:T(8,128)(2,1)S(1)} %get-tuple-element.58.refs_0_, bf16[256,128]{1,0:T(8,128)(2,1)S(1)} %collective-permute-done.16.refs_1_, bf16[256,128]{1,0:T(8,128)(2,1)S(1)} %collective-permute-done.17.refs_2_, bf16[256,128]{1,0:T(8,128)(2,1)S(1)} %collective-permute-done.18.refs_3_, ...), custom_call_target="tpu_custom_call" | custom-call | bytes 786432 | tf_op jit(solution)/shard_map/pallas_call | solution.py:39
  (38 shorter events, 3.1 us)
Async XLA Ops:
  0.6 1.0 %copy-start.4 = (bf16[256,512]{1,0:T(8,128)(2,1)S(1)}, bf16[256,512]{1,0:T(8,128)(2,1)}, u32[]{:S(2)}) copy-start(bf16[256,512]{1,0:T(8,128)(2,1)} %v_ref.1) | copy-start | bytes 786436
  0.6 1.0 %copy-start.3 = (bf16[256,512]{1,0:T(8,128)(2,1)S(1)}, bf16[256,512]{1,0:T(8,128)(2,1)}, u32[]{:S(2)}) copy-start(bf16[256,512]{1,0:T(8,128)(2,1)} %k_ref.1) | copy-start | bytes 786436
  0.7 4.7 %slice-start = ((s8[11010048]{0:T(1024)(128)(4,1)}), s8[4194304]{0:T(1024)(128)(4,1)S(1)}, s32[]{:S(2)}) async-start(s8[11010048]{0:T(1024)(128)(4,1)} %bitcast), calls=%async_computation | async-start | bytes 8388608
  0.7 4.7 %slice-start.1 = ((s8[11010048]{0:T(1024)(128)(4,1)}), s8[4194304]{0:T(1024)(128)(4,1)S(1)}, s32[]{:S(2)}) async-start(s8[11010048]{0:T(1024)(128)(4,1)} %bitcast), calls=%async_computation.1 | async-start | bytes 8388608
  1.7 3.7 %copy-start.1 = (bf16[256,1024]{1,0:T(8,128)(2,1)S(1)}, bf16[256,1024]{1,0:T(8,128)(2,1)}, u32[]{:S(2)}) copy-start(bf16[256,1024]{1,0:T(8,128)(2,1)} %q_ref.1) | copy-start | bytes 1572868
  1.7 3.8 %slice-start.2 = ((s8[11010048]{0:T(1024)(128)(4,1)}), s8[2621440]{0:T(1024)(128)(4,1)S(1)}, s32[]{:S(2)}) async-start(s8[11010048]{0:T(1024)(128)(4,1)} %bitcast), calls=%async_computation.2 | async-start | bytes 5242880
  1.7 4.0 %copy-start = (bf16[256,2688]{1,0:T(8,128)(2,1)S(1)}, bf16[256,2688]{1,0:T(8,128)(2,1)}, u32[]{:S(2)}) copy-start(bf16[256,2688]{1,0:T(8,128)(2,1)} %c_ref.3) | copy-start | bytes 4128772
  1.8 7.8 %collective-permute-start = (bf16[256,256]{1,0:T(8,128)(2,1)S(1)}, bf16[256,256]{1,0:T(8,128)(2,1)S(1)}, u32[]{:S(2)}, u32[]{:S(2)}) collective-permute-start(bf16[256,256]{1,0:T(8,128)(2,1)S(1)} %get-tuple-element.34), channel_id=1, source_target_pairs={{0,6},{2,4},{4,2},{6,0},{8,14},{10,12},{12,10},{14,8},{16,22},{18,... | collective-permute-start | bytes 393224 | tf_op jit(solution)/shard_map/ppermute | solution.py:32
  4.3 6.5 %collective-permute-start.1 = (bf16[256,256]{1,0:T(8,128)(2,1)S(1)}, bf16[256,256]{1,0:T(8,128)(2,1)S(1)}, u32[]{:S(2)}, u32[]{:S(2)}) collective-permute-start(bf16[256,256]{1,0:T(8,128)(2,1)S(1)} %get-tuple-element.35), channel_id=1, source_target_pairs={{0,4},{2,6},{4,0},{6,2},{8,12},{10,14},{12,8},{14,10},{16,20},{18,... | collective-permute-start | bytes 393224 | tf_op jit(solution)/shard_map/ppermute | solution.py:32
  4.8 6.0 %collective-permute-start.2 = (bf16[256,256]{1,0:T(8,128)(2,1)S(1)}, bf16[256,256]{1,0:T(8,128)(2,1)S(1)}, u32[]{:S(2)}, u32[]{:S(2)}) collective-permute-start(bf16[256,256]{1,0:T(8,128)(2,1)S(1)} %get-tuple-element.36), channel_id=1, source_target_pairs={{0,2},{2,0},{4,6},{6,4},{8,10},{10,8},{12,14},{14,12},{16,18},{18,... | collective-permute-start | bytes 393224 | tf_op jit(solution)/shard_map/ppermute | solution.py:32
  7.6 8.2 %collective-permute-start.7 = (bf16[1024,256]{1,0:T(8,128)(2,1)S(1)}, bf16[1024,256]{1,0:T(8,128)(2,1)S(1)}, u32[]{:S(2)}, u32[]{:S(2)}) collective-permute-start(bf16[1024,256]{1,0:T(8,128)(2,1)S(1)} %shard_map.79.refs_0_), channel_id=1, source_target_pairs={{0,1},{1,0},{2,3},{3,2},{4,5},{5,4},{6,7},{7,6},{8,9},{9,8},{10,11... | collective-permute-start | bytes 1572872 | tf_op jit(solution)/shard_map/ppermute | solution.py:32
  10.9 15.7 %collective-permute-start.3 = (bf16[4,256,256]{2,1,0:T(8,128)(2,1)S(1)}, bf16[4,256,256]{2,1,0:T(8,128)(2,1)S(1)}, u32[]{:S(2)}, u32[]{:S(2)}) collective-permute-start(bf16[4,256,256]{2,1,0:T(8,128)(2,1)S(1)} %shard_map.81.refs_0_.refs_2_.own_ref), channel_id=1, source_target_pairs={{0,8},{2,10},{4,12},{6,14},{8,16},{10,18},{12,20},{14,22},{16,24},... | collective-permute-start | bytes 1572872 | tf_op jit(solution)/shard_map/ppermute | solution.py:27
  12.2 7.3 %collective-permute-start.4 = (bf16[256,256]{1,0:T(8,128)(2,1)S(1)}, bf16[256,256]{1,0:T(8,128)(2,1)S(1)}, u32[]{:S(2)}, u32[]{:S(2)}) collective-permute-start(bf16[256,256]{1,0:T(8,128)(2,1)S(1)} %get-tuple-element.38), channel_id=1, source_target_pairs={{0,6},{2,4},{4,2},{6,0},{8,14},{10,12},{12,10},{14,8},{16,22},{18,... | collective-permute-start | bytes 393224 | tf_op jit(solution)/shard_map/ppermute | solution.py:32
  13.9 8.5 %collective-permute-start.5 = (bf16[256,256]{1,0:T(8,128)(2,1)S(1)}, bf16[256,256]{1,0:T(8,128)(2,1)S(1)}, u32[]{:S(2)}, u32[]{:S(2)}) collective-permute-start(bf16[256,256]{1,0:T(8,128)(2,1)S(1)} %get-tuple-element.39), channel_id=1, source_target_pairs={{0,4},{2,6},{4,0},{6,2},{8,12},{10,14},{12,8},{14,10},{16,20},{18,... | collective-permute-start | bytes 393224 | tf_op jit(solution)/shard_map/ppermute | solution.py:32
  15.2 8.7 %collective-permute-start.6 = (bf16[256,256]{1,0:T(8,128)(2,1)S(1)}, bf16[256,256]{1,0:T(8,128)(2,1)S(1)}, u32[]{:S(2)}, u32[]{:S(2)}) collective-permute-start(bf16[256,256]{1,0:T(8,128)(2,1)S(1)} %get-tuple-element.40), channel_id=1, source_target_pairs={{0,2},{2,0},{4,6},{6,4},{8,10},{10,8},{12,14},{14,12},{16,18},{18,... | collective-permute-start | bytes 393224 | tf_op jit(solution)/shard_map/ppermute | solution.py:32
  15.9 14.5 %collective-permute-start.8 = (bf16[256,256]{1,0:T(8,128)(2,1)S(1)}, bf16[256,256]{1,0:T(8,128)(2,1)S(1)}, u32[]{:S(2)}, u32[]{:S(2)}) collective-permute-start(bf16[256,256]{1,0:T(8,128)(2,1)S(1)} %get-tuple-element.44), channel_id=1, source_target_pairs={{0,6},{2,4},{4,2},{6,0},{8,14},{10,12},{12,10},{14,8},{16,22},{18,... | collective-permute-start | bytes 393224 | tf_op jit(solution)/shard_map/ppermute | solution.py:32
  19.5 10.8 %collective-permute-start.9 = (bf16[256,256]{1,0:T(8,128)(2,1)S(1)}, bf16[256,256]{1,0:T(8,128)(2,1)S(1)}, u32[]{:S(2)}, u32[]{:S(2)}) collective-permute-start(bf16[256,256]{1,0:T(8,128)(2,1)S(1)} %get-tuple-element.45), channel_id=1, source_target_pairs={{0,4},{2,6},{4,0},{6,2},{8,12},{10,14},{12,8},{14,10},{16,20},{18,... | collective-permute-start | bytes 393224 | tf_op jit(solution)/shard_map/ppermute | solution.py:32
  22.4 7.9 %collective-permute-start.10 = (bf16[256,256]{1,0:T(8,128)(2,1)S(1)}, bf16[256,256]{1,0:T(8,128)(2,1)S(1)}, u32[]{:S(2)}, u32[]{:S(2)}) collective-permute-start(bf16[256,256]{1,0:T(8,128)(2,1)S(1)} %get-tuple-element.46), channel_id=1, source_target_pairs={{0,2},{2,0},{4,6},{6,4},{8,10},{10,8},{12,14},{14,12},{16,18},{18,... | collective-permute-start | bytes 393224 | tf_op jit(solution)/shard_map/ppermute | solution.py:32
  32.6 11.4 %collective-permute-start.11 = (bf16[4,256,128]{2,1,0:T(8,128)(2,1)S(1)}, bf16[4,256,128]{2,1,0:T(8,128)(2,1)S(1)}, u32[]{:S(2)}, u32[]{:S(2)}) collective-permute-start(bf16[4,256,128]{2,1,0:T(8,128)(2,1)S(1)} %get-tuple-element.50), channel_id=1, source_target_pairs={{8,0},{10,2},{12,4},{14,6},{16,8},{18,10},{20,12},{22,14},{24,16},... | collective-permute-start | bytes 786440 | tf_op jit(solution)/shard_map/ppermute | solution.py:27
  41.7 7.9 %collective-permute-start.15 = (bf16[4,256,128]{2,1,0:T(8,128)(2,1)S(1)}, bf16[4,256,128]{2,1,0:T(8,128)(2,1)S(1)}, u32[]{:S(2)}, u32[]{:S(2)}) collective-permute-start(bf16[4,256,128]{2,1,0:T(8,128)(2,1)S(1)} %get-tuple-element.57), channel_id=1, source_target_pairs={{8,0},{10,2},{12,4},{14,6},{16,8},{18,10},{20,12},{22,14},{24,16},... | collective-permute-start | bytes 786440 | tf_op jit(solution)/shard_map/ppermute | solution.py:27
  46.0 8.6 %collective-permute-start.12 = (bf16[256,384]{1,0:T(8,128)(2,1)S(1)}, bf16[256,384]{1,0:T(8,128)(2,1)S(1)}, u32[]{:S(2)}, u32[]{:S(2)}) collective-permute-start(bf16[256,384]{1,0:T(8,128)(2,1)S(1)} %get-tuple-element.52), channel_id=1, source_target_pairs={{0,6},{2,4},{4,2},{6,0},{8,14},{10,12},{12,10},{14,8},{16,22},{18,... | collective-permute-start | bytes 589832 | tf_op jit(solution)/shard_map/ppermute | solution.py:32
  47.6 9.1 %collective-permute-start.13 = (bf16[256,384]{1,0:T(8,128)(2,1)S(1)}, bf16[256,384]{1,0:T(8,128)(2,1)S(1)}, u32[]{:S(2)}, u32[]{:S(2)}) collective-permute-start(bf16[256,384]{1,0:T(8,128)(2,1)S(1)} %get-tuple-element.53), channel_id=1, source_target_pairs={{0,4},{2,6},{4,0},{6,2},{8,12},{10,14},{12,8},{14,10},{16,20},{18,... | collective-permute-start | bytes 589832 | tf_op jit(solution)/shard_map/ppermute | solution.py:32
  48.5 8.4 %collective-permute-start.14 = (bf16[256,384]{1,0:T(8,128)(2,1)S(1)}, bf16[256,384]{1,0:T(8,128)(2,1)S(1)}, u32[]{:S(2)}, u32[]{:S(2)}) collective-permute-start(bf16[256,384]{1,0:T(8,128)(2,1)S(1)} %get-tuple-element.54), channel_id=1, source_target_pairs={{0,2},{2,0},{4,6},{6,4},{8,10},{10,8},{12,14},{14,12},{16,18},{18,... | collective-permute-start | bytes 589832 | tf_op jit(solution)/shard_map/ppermute | solution.py:32
  49.6 8.2 %collective-permute-start.16 = (bf16[256,128]{1,0:T(8,128)(2,1)S(1)}, bf16[256,128]{1,0:T(8,128)(2,1)S(1)}, u32[]{:S(2)}, u32[]{:S(2)}) collective-permute-start(bf16[256,128]{1,0:T(8,128)(2,1)S(1)} %get-tuple-element.59), channel_id=1, source_target_pairs={{0,6},{2,4},{4,2},{6,0},{8,14},{10,12},{12,10},{14,8},{16,22},{18,... | collective-permute-start | bytes 196616 | tf_op jit(solution)/shard_map/ppermute | solution.py:32
  51.2 6.9 %collective-permute-start.17 = (bf16[256,128]{1,0:T(8,128)(2,1)S(1)}, bf16[256,128]{1,0:T(8,128)(2,1)S(1)}, u32[]{:S(2)}, u32[]{:S(2)}) collective-permute-start(bf16[256,128]{1,0:T(8,128)(2,1)S(1)} %get-tuple-element.60), channel_id=1, source_target_pairs={{0,4},{2,6},{4,0},{6,2},{8,12},{10,14},{12,8},{14,10},{16,20},{18,... | collective-permute-start | bytes 196616 | tf_op jit(solution)/shard_map/ppermute | solution.py:32
  54.7 4.3 %collective-permute-start.18 = (bf16[256,128]{1,0:T(8,128)(2,1)S(1)}, bf16[256,128]{1,0:T(8,128)(2,1)S(1)}, u32[]{:S(2)}, u32[]{:S(2)}) collective-permute-start(bf16[256,128]{1,0:T(8,128)(2,1)S(1)} %get-tuple-element.61), channel_id=1, source_target_pairs={{0,2},{2,0},{4,6},{6,4},{8,10},{10,8},{12,14},{14,12},{16,18},{18,... | collective-permute-start | bytes 196616 | tf_op jit(solution)/shard_map/ppermute | solution.py:32
  58.9 1.0 %copy-start.2 = (bf16[256,512]{1,0:T(8,128)(2,1)S(1)}, bf16[256,512]{1,0:T(8,128)(2,1)}, u32[]{:S(2)}) copy-start(bf16[256,512]{1,0:T(8,128)(2,1)} %get-tuple-element.32.refs_4_) | copy-start | bytes 786436

commit v10 on v9

--- a/solution.py
+++ b/solution.py
@@ -30,6 +30,14 @@
 def swapped(value, axis, bits):
     count = lax.axis_size(axis)
     return lax.ppermute(value, axis, [(source, source ^ bits) for source in range(count)])
+
+
+def exchanged(value, axis, group):
+    if group == 1:
+        return value
+    count = lax.axis_size(axis)
+    groups = [list(range(first, first + group)) for first in range(0, count, group)]
+    return lax.all_to_all(value, axis, 0, 0, axis_index_groups=groups, tiled=True)
 
 
 def call(body, outs, scratch=(), flops=0, exps=0, specs=None, vmem=32):
@@ -83,15 +91,15 @@
     return call(body, outs, flops=AHEAD, specs=[VMEM, VMEM, ANY])(keys, values, before)
 
 
-def pack_queries(group, queries, before):
+def split_queries(group, queries, before):
     tokens, width = queries.shape[0], queries.shape[1] // group
 
-    def body(q_ref, before_ref, *out_refs):
-        for r in range(group):
-            out_refs[r][...] = q_ref[:, lanes(spot(group)[0] ^ hop(group, r), width)]
-
-    outs = [jax.ShapeDtypeStruct((tokens, width), jnp.bfloat16)] * group
-    return call(body, outs, specs=[VMEM, ANY])(queries, before)
+    def body(q_ref, before_ref, out_ref):
+        for member in range(group):
+            out_ref[member] = q_ref[:, member * width : (member + 1) * width]
+
+    outs = [jax.ShapeDtypeStruct((group, tokens, width), jnp.bfloat16)]
+    return call(body, outs, specs=[VMEM, ANY])(queries, before)[0]
 
 
 def order_pieces(group, pieces, before):
@@ -100,7 +108,7 @@
             refs[-1][spot(group)[0] ^ hop(group, r)] = refs[r][...]
 
     outs = [jax.ShapeDtypeStruct((group,) + pieces[0].shape, jnp.bfloat16)]
-    return call(body, outs, specs=[VMEM] * group + [ANY])(*pieces, before)[0]
+    return call(body, outs, flops=AHEAD, specs=[VMEM] * group + [ANY])(*pieces, before)[0]
 
 
 def head_product(parts, part, out_weight, layer_cotangent, before):
@@ -161,18 +169,18 @@
         return own_ref.at[number - self.back]
 
 
-def turn_queries(z, pieces):
-    def body(*refs):
+def turn_queries(z, queries):
+    def body(in_ref, out_ref):
         for head in range(z.heads):
-            for r in range(z.group):
+            for member in range(z.group):
                 for j in range(z.per_head):
                     lower = (head * z.per_head + j) * HEAD_SIZE
-                    refs[z.group][head, spot(z.group)[0] ^ hop(z.group, r), :, j * z.tokens : (j + 1) * z.tokens] = refs[r][
-                        :, lower : lower + HEAD_SIZE
+                    out_ref[head, member, :, j * z.tokens : (j + 1) * z.tokens] = in_ref[
+                        member, :, lower : lower + HEAD_SIZE
                     ].T
 
     outs = [jax.ShapeDtypeStruct((z.heads, z.group, HEAD_SIZE, z.wide), jnp.bfloat16)]
-    return call(body, outs)(*pieces)[0]
+    return call(body, outs)(queries)[0]
 
 
 def softmax(z, kv_own, kv_earlier, qt):
@@ -377,7 +385,7 @@
     return call(body, outs)(*flat)
 
 
-def unpack(group, pieces, widths, before):
+def unpack(group, pieces, widths):
     tokens = pieces[0].shape[0]
 
     def body(*refs):
@@ -385,11 +393,11 @@
             lower = 0
             for number, width in enumerate(widths):
                 there = lanes(spot(group)[0] ^ hop(group, r), width)
-                refs[group + 1 + number][:, there] = refs[r][:, lower : lower + width]
+                refs[group + number][:, there] = refs[r][:, lower : lower + width]
                 lower += width
 
     outs = [jax.ShapeDtypeStruct((tokens, group * width), jnp.bfloat16) for width in widths]
-    return call(body, outs, specs=[VMEM] * group + [ANY])(*pieces, before)
+    return call(body, outs)(*pieces)
 
 
 def local(layer_cotangent, out_weight, queries, keys, values):
@@ -419,13 +427,13 @@
     sent = pack_kv(group, keys, values, begin())
     kv_pieces = trade(sent)
     z = Shape(group, back_groups, heads, per_head, tokens)
-    query_sent = pack_queries(group, queries, sent[0])
-    qt = turn_queries(z, trade(query_sent))
+    query_sent = split_queries(group, queries, sent[0])
+    qt = turn_queries(z, exchanged(query_sent, "ctx", group))
     if tp_count == 2:
-        other = head_product(2, 1, out_weight, layer_cotangent, [query_sent[0]])
+        other = head_product(2, 1, out_weight, layer_cotangent, [query_sent])
         terms = [head_product(2, 0, out_weight, layer_cotangent, [other]), swapped(other, "tp", 1)]
     else:
-        other = head_product(1, 0, out_weight, layer_cotangent, [query_sent[0]])
+        other = head_product(1, 0, out_weight, layer_cotangent, [query_sent])
         terms = [lax.psum_scatter(other, "tp", scatter_dimension=0, tiled=True)]
     kv_own = order_pieces(group, kv_pieces, terms[0])
     kv_earlier = [shifted(kv_own, "ctx", group * step) for step in range(back_groups, 0, -1)]
@@ -436,9 +444,9 @@
     ds, dk_own, dk_earlier = key_terms(z, e, inverse, qt, g, kv_own, kv_earlier)
     dk_terms = [dk_own] + returned(dk_earlier)
     pieces = trade(query_terms(z, ds, inverse, kv_own, kv_earlier, dv_terms))
-    query_grads, value_gradients = unpack(group, pieces, [z.width, kv_width], ds)
+    query_grads, value_gradients = unpack(group, pieces, [z.width, kv_width])
     pieces = trade(pack_terms(group, [dk_terms]))
-    (key_gradients,) = unpack(group, pieces, [kv_width], value_gradients)
+    (key_gradients,) = unpack(group, pieces, [kv_width])
     return (query_grads, key_gradients, value_gradients)
 
 

time: 60.9 us -> 64.8 us (1.064)
  starting transfers between devices: 26.5 us -> 29.1 us
  waiting for transfers between devices: 11.7 us -> 13 us
  local copies, waits for them, and re-layouts: 2.23 us -> 1 us
  Pallas kernels: 19.4 us -> 20.2 us
    all_to_all x0 -> x1, waiting for transfers between devices: none -> 6.58 us  [exchanged(): lax.all_to_all(value, axis, 0, 0, axis_index_groups=groups, tiled=True)]
    all_to_all x0 -> x1, starting transfers between devices: none -> 3.48 us  [exchanged(): lax.all_to_all(value, axis, 0, 0, axis_index_groups=groups, tiled=True)]
    ppermute x16 -> x13, waiting for transfers between devices: 9.3 us -> 5.99 us  [swapped(): lax.ppermute(value, axis, [(source, source ^ bits) for source in range(co...]
    ppermute x3, waiting for transfers between devices: 2.4 us -> 0.39 us  [shifted(): lax.ppermute(value, axis, [(source, source + steps) for source in range(l...]
    ppermute x16 -> x13, starting transfers between devices: 19.1 us -> 17.3 us  [swapped(): lax.ppermute(value, axis, [(source, source ^ bits) for source in range(co...]
    unnamed x16 -> x14, local copies, waits for them, and re-layouts: 2.23 us -> 1 us
    ppermute x3, starting transfers between devices: 7.36 us -> 8.24 us  [shifted(): lax.ppermute(value, axis, [(source, source + steps) for source in range(l...]
    pallas_call x15, Pallas kernels: 19.4 us -> 20.2 us  [run(): pl.pallas_call(body, out_shape=tuple(outs), in_specs=specs or [SMEM if a....]
  transfers between devices with their start and end apart: 19 -> 17, of which waited for: 10 -> 6; matrix products, arithmetic and copies ran while one was open for 0% -> 0% of each run, Pallas kernels for 27% -> 26%
where the time goes in v10:
time: 64.8 us; the launch traced here: 64.1 us
  starting transfers between devices  29.1 us (45%)
  Pallas kernels  20.2 us (31%)
  waiting for transfers between devices  13 us (20%)
  local copies, waits for them, and re-layouts  1 us (2%)
  between operations  0.84 us (1%)
    pallas_call x15, Pallas kernels, run(): pl.pallas_call(body, out_shape=tuple(outs), in_specs=specs or [SMEM if a....  20.2 us
    ppermute x13, starting transfers between devices, swapped(): lax.ppermute(value, axis, [(source, source ^ bits) for source in range(co...  17.3 us
    ppermute x3, starting transfers between devices, shifted(): lax.ppermute(value, axis, [(source, source + steps) for source in range(l...  8.24 us
    all_to_all x1, waiting for transfers between devices, exchanged(): lax.all_to_all(value, axis, 0, 0, axis_index_groups=groups, tiled=True)  6.58 us
    ppermute x13, waiting for transfers between devices, swapped(): lax.ppermute(value, axis, [(source, source ^ bits) for source in range(co...  5.99 us
    all_to_all x1, starting transfers between devices, exchanged(): lax.all_to_all(value, axis, 0, 0, axis_index_groups=groups, tiled=True)  3.48 us
  transfers between devices with their start and end apart: 17, of which 6 were waited for; matrix products, arithmetic and copies ran while one was open for 0% of the time, Pallas kernels for 26%

profile of v10, /device:TPU:24, one launch (start us, length us, event | category | flops | bytes accessed | tf_op | source)
XLA Modules:
  0.0 64.1 jit_solution(18100520001627626373)
XLA Ops:
  0.7 0.9 %copy-done.3 = bf16[256,512]{1,0:T(8,128)(2,1)S(1)} copy-done((bf16[256,512]{1,0:T(8,128)(2,1)S(1)}, bf16[256,512]{1,0:T(8,128)(2,1)}, u32[]{:S(2)}) %copy-start.3) | copy-done | bytes 262168
  1.7 0.1 shard_map.77
  1.8 2.5 %collective-permute-start = (bf16[256,256]{1,0:T(8,128)(2,1)S(1)}, bf16[256,256]{1,0:T(8,128)(2,1)S(1)}, u32[]{:S(2)}, u32[]{:S(2)}) collective-permute-start(bf16[256,256]{1,0:T(8,128)(2,1)S(1)} %get-tuple-element.30), channel_id=1, source_target_pairs={{0,6},{2,4},{4,2},{6,0},{8,14},{10,12},{12,10},{14,8},{16,22},{18,... | collective-permute-start | bytes 393224 | tf_op jit(solution)/shard_map/ppermute | solution.py:32
  4.3 0.5 collective-permute-start.1
  4.8 0.5 collective-permute-start.2
  5.3 0.8 %shard_map.78.refs_0_ = bf16[4,256,256]{2,1,0:T(8,128)(2,1)} custom-call(bf16[256,1024]{1,0:T(8,128)(2,1)S(1)} %copy-done.1, bf16[256,256]{1,0:T(8,128)(2,1)S(1)} %get-tuple-element.29.before_ref.refs_0_), custom_call_target="tpu_custom_call" | custom-call | bytes 1179648 | tf_op jit(solution)/shard_map/pallas_call | solution.py:47
  6.2 1.9 %shard_map.79.refs_0_ = bf16[1024,256]{1,0:T(8,128)(2,1)S(1)} custom-call(bf16[2048,2688]{1,0:T(8,128)(2,1)S(1)} %bitcast.1, bf16[256,2688]{1,0:T(8,128)(2,1)S(1)} %copy-done, bf16[4,256,256]{2,1,0:T(8,128)(2,1)} %shard_map.78.refs_0_), custom_call_target="tpu_custom_call" | custom-call | flops 1409286144 | bytes 13434880 | tf_op jit(solution)/shard_map/pallas_call | solution.py:47
  8.2 1.9 %shard_map.80.refs_4_.refs_0_ = bf16[1024,256]{1,0:T(8,128)(2,1)S(1)} custom-call(bf16[2048,2688]{1,0:T(8,128)(2,1)S(1)} %bitcast.1, bf16[256,2688]{1,0:T(8,128)(2,1)S(1)} %copy-done, bf16[1024,256]{1,0:T(8,128)(2,1)S(1)} %shard_map.79.refs_0_), custom_call_target="tpu_custom_call" | custom-call | flops 1409286144 | bytes 13434880 | tf_op jit(solution)/shard_map/pallas_call | solution.py:47
  10.1 0.7 %collective-permute-done.1.refs_2_ = bf16[256,256]{1,0:T(8,128)(2,1)S(1)} collective-permute-done((bf16[256,256]{1,0:T(8,128)(2,1)S(1)}, bf16[256,256]{1,0:T(8,128)(2,1)S(1)}, u32[]{:S(2)}, u32[]{:S(2)}) %collective-permute-start.1) | collective-permute-done | bytes 131104 | tf_op jit(solution)/shard_map/ppermute | solution.py:32
  10.9 1.3 %collective-permute-start.3 = (bf16[4,256,256]{2,1,0:T(8,128)(2,1)S(1)}, bf16[4,256,256]{2,1,0:T(8,128)(2,1)S(1)}, u32[]{:S(2)}, u32[]{:S(2)}) collective-permute-start(bf16[4,256,256]{2,1,0:T(8,128)(2,1)S(1)} %shard_map.81.refs_0_.refs_2_.own_ref), channel_id=1, source_target_pairs={{0,8},{2,10},{4,12},{6,14},{8,16},{10,18},{12,20},{14,22},{16,24},... | collective-permute-start | bytes 1572872 | tf_op jit(solution)/shard_map/ppermute | solution.py:27
  12.2 3.5 %all-to-all-start = ((bf16[4,256,256]{2,1,0:T(8,128)(2,1)}), bf16[4,256,256]{2,1,0:T(8,128)(2,1)S(1)}, u32[]{:S(2)}, u32[]{:S(2)}) async-start(bf16[4,256,256]{2,1,0:T(8,128)(2,1)} %shard_map.78.refs_0_), calls=%async_computation | async-start | bytes 1048576 | tf_op jit(solution)/shard_map/all_to_all | solution.py:40
  15.7 0.1 shard_map.84
  15.8 2.9 %collective-permute-start.5 = (bf16[256,256]{1,0:T(8,128)(2,1)S(1)}, bf16[256,256]{1,0:T(8,128)(2,1)S(1)}, u32[]{:S(2)}, u32[]{:S(2)}) collective-permute-start(bf16[256,256]{1,0:T(8,128)(2,1)S(1)} %get-tuple-element.36), channel_id=1, source_target_pairs={{0,6},{2,4},{4,2},{6,0},{8,14},{10,12},{12,10},{14,8},{16,22},{18,... | collective-permute-start | bytes 393224 | tf_op jit(solution)/shard_map/ppermute | solution.py:32
  18.8 0.6 collective-permute-start.6
  19.4 6.6 %all-to-all-done.in_ref = bf16[4,256,256]{2,1,0:T(8,128)(2,1)S(1)} async-done(((bf16[4,256,256]{2,1,0:T(8,128)(2,1)}), bf16[4,256,256]{2,1,0:T(8,128)(2,1)S(1)}, u32[]{:S(2)}, u32[]{:S(2)}) %all-to-all-start) | async-done | bytes 524320 | tf_op jit(solution)/shard_map/all_to_all | solution.py:40
  26.0 0.2 shard_map.82.refs_2_.qt_ref
  26.2 0.4 collective-permute-done.3.refs_1_.refs_0_
  26.6 3.8 %shard_map.83 = (bf16[1,4,5,256,512]{4,3,2,1,0:T(8,128)(2,1)S(1)}, f32[1,4,1,512]{3,2,1,0:T(1,128)S(1)}) custom-call(bf16[4,256,256]{2,1,0:T(8,128)(2,1)S(1)} %shard_map.81.refs_0_.refs_2_.own_ref, bf16[4,256,256]{2,1,0:T(8,128)(2,1)S(1)} %collective-permute-done.3.refs_1_.refs_0_, bf16[1,4,128,512]{3,2,1,0:T(8,128)(2,1)S(1)} %shard_map.82.refs_2_.qt_ref), custom_call_target="tpu_custom_call" | custom-call | flops 671088640 | bytes 6823936 | tf_op jit(solution)/shard_map/pallas_call | solution.py:47
  30.4 2.2 %shard_map.85 = (bf16[1,4,128,512]{3,2,1,0:T(8,128)(2,1)S(1)}, f32[4,256,128]{2,1,0:T(8,128)S(1)}, bf16[4,256,128]{2,1,0:T(8,128)(2,1)S(1)}) custom-call(bf16[1,4,5,256,512]{4,3,2,1,0:T(8,128)(2,1)S(1)} %get-tuple-element.33.e_ref, f32[1,4,1,512]{3,2,1,0:T(1,128)S(1)} %get-tuple-element.34.inverse_ref, bf16[256,256]{1,0:T(8,128)(2,1)S(1)} %get-tuple-element.35.refs_0_, ...), custom_call_target="tpu_custom_call" | custom-call | flops 671088640 | bytes 7086080 | tf_op jit(solution)/shard_map/pallas_call | solution.py:47
  32.6 4.6 %collective-permute-start.8 = (bf16[4,256,128]{2,1,0:T(8,128)(2,1)S(1)}, bf16[4,256,128]{2,1,0:T(8,128)(2,1)S(1)}, u32[]{:S(2)}, u32[]{:S(2)}) collective-permute-start(bf16[4,256,128]{2,1,0:T(8,128)(2,1)S(1)} %get-tuple-element.42), channel_id=1, source_target_pairs={{8,0},{10,2},{12,4},{14,6},{16,8},{18,10},{20,12},{22,14},{24,16},... | collective-permute-start | bytes 786440 | tf_op jit(solution)/shard_map/ppermute | solution.py:27
  37.2 5.4 %shard_map.86 = (bf16[1,4,5,256,512]{4,3,2,1,0:T(8,128)(2,1)S(1)}, f32[4,256,128]{2,1,0:T(8,128)S(1)}, bf16[4,256,128]{2,1,0:T(8,128)(2,1)S(1)}) custom-call(bf16[1,4,5,256,512]{4,3,2,1,0:T(8,128)(2,1)S(1)} %get-tuple-element.33.e_ref, f32[1,4,1,512]{3,2,1,0:T(1,128)S(1)} %get-tuple-element.34.inverse_ref, ...), custom_call_target="tpu_custom_call" | custom-call | flops 1342177280 | bytes 13377536 | tf_op jit(solution)/shard_map/pallas_call | solution.py:47
  42.6 2.4 %collective-permute-start.12 = (bf16[4,256,128]{2,1,0:T(8,128)(2,1)S(1)}, bf16[4,256,128]{2,1,0:T(8,128)(2,1)S(1)}, u32[]{:S(2)}, u32[]{:S(2)}) collective-permute-start(bf16[4,256,128]{2,1,0:T(8,128)(2,1)S(1)} %get-tuple-element.49), channel_id=1, source_target_pairs={{8,0},{10,2},{12,4},{14,6},{16,8},{18,10},{20,12},{22,14},{24,16},... | collective-permute-start | bytes 786440 | tf_op jit(solution)/shard_map/ppermute | solution.py:27
  44.9 2.0 %shard_map.87 = (bf16[256,384]{1,0:T(8,128)(2,1)S(1)}, bf16[256,384]{1,0:T(8,128)(2,1)S(1)}, bf16[256,384]{1,0:T(8,128)(2,1)S(1)}, bf16[256,384]{1,0:T(8,128)(2,1)S(1)}) custom-call(bf16[1,4,5,256,512]{4,3,2,1,0:T(8,128)(2,1)S(1)} %get-tuple-element.40.ds_ref, f32[1,4,1,512]{3,2,1,0:T(1,128)S(1)} %get-tuple-element.34.inverse_ref, ...), custom_call_target="tpu_custom_call" | custom-call | flops 671088640 | bytes 7872512 | tf_op jit(solution)/shard_map/pallas_call | solution.py:47
  46.9 3.0 %collective-permute-start.9 = (bf16[256,384]{1,0:T(8,128)(2,1)S(1)}, bf16[256,384]{1,0:T(8,128)(2,1)S(1)}, u32[]{:S(2)}, u32[]{:S(2)}) collective-permute-start(bf16[256,384]{1,0:T(8,128)(2,1)S(1)} %get-tuple-element.44), channel_id=1, source_target_pairs={{0,6},{2,4},{4,2},{6,0},{8,14},{10,12},{12,10},{14,8},{16,22},{18,... | collective-permute-start | bytes 589832 | tf_op jit(solution)/shard_map/ppermute | solution.py:32
  49.9 1.4 %collective-permute-start.10 = (bf16[256,384]{1,0:T(8,128)(2,1)S(1)}, bf16[256,384]{1,0:T(8,128)(2,1)S(1)}, u32[]{:S(2)}, u32[]{:S(2)}) collective-permute-start(bf16[256,384]{1,0:T(8,128)(2,1)S(1)} %get-tuple-element.45), channel_id=1, source_target_pairs={{0,4},{2,6},{4,0},{6,2},{8,12},{10,14},{12,8},{14,10},{16,20},{18,... | collective-permute-start | bytes 589832 | tf_op jit(solution)/shard_map/ppermute | solution.py:32
  51.4 2.1 %collective-permute-start.13 = (bf16[256,128]{1,0:T(8,128)(2,1)S(1)}, bf16[256,128]{1,0:T(8,128)(2,1)S(1)}, u32[]{:S(2)}, u32[]{:S(2)}) collective-permute-start(bf16[256,128]{1,0:T(8,128)(2,1)S(1)} %get-tuple-element.51), channel_id=1, source_target_pairs={{0,6},{2,4},{4,2},{6,0},{8,14},{10,12},{12,10},{14,8},{16,22},{18,... | collective-permute-start | bytes 196616 | tf_op jit(solution)/shard_map/ppermute | solution.py:32
  53.5 1.4 %collective-permute-start.14 = (bf16[256,128]{1,0:T(8,128)(2,1)S(1)}, bf16[256,128]{1,0:T(8,128)(2,1)S(1)}, u32[]{:S(2)}, u32[]{:S(2)}) collective-permute-start(bf16[256,128]{1,0:T(8,128)(2,1)S(1)} %get-tuple-element.52), channel_id=1, source_target_pairs={{0,4},{2,6},{4,0},{6,2},{8,12},{10,14},{12,8},{14,10},{16,20},{18,... | collective-permute-start | bytes 196616 | tf_op jit(solution)/shard_map/ppermute | solution.py:32
  54.9 3.0 %collective-permute-done.13.refs_1_ = bf16[256,128]{1,0:T(8,128)(2,1)S(1)} collective-permute-done((bf16[256,128]{1,0:T(8,128)(2,1)S(1)}, bf16[256,128]{1,0:T(8,128)(2,1)S(1)}, u32[]{:S(2)}, u32[]{:S(2)}) %collective-permute-start.13) | collective-permute-done | bytes 65568 | tf_op jit(solution)/shard_map/ppermute | solution.py:32
  57.9 2.2 %collective-permute-start.15 = (bf16[256,128]{1,0:T(8,128)(2,1)S(1)}, bf16[256,128]{1,0:T(8,128)(2,1)S(1)}, u32[]{:S(2)}, u32[]{:S(2)}) collective-permute-start(bf16[256,128]{1,0:T(8,128)(2,1)S(1)} %get-tuple-element.53), channel_id=1, source_target_pairs={{0,2},{2,0},{4,6},{6,4},{8,10},{10,8},{12,14},{14,12},{16,18},{18,... | collective-permute-start | bytes 196616 | tf_op jit(solution)/shard_map/ppermute | solution.py:32
  60.1 2.2 %collective-permute-done.15.refs_3_ = bf16[256,128]{1,0:T(8,128)(2,1)S(1)} collective-permute-done((bf16[256,128]{1,0:T(8,128)(2,1)S(1)}, bf16[256,128]{1,0:T(8,128)(2,1)S(1)}, u32[]{:S(2)}, u32[]{:S(2)}) %collective-permute-start.15) | collective-permute-done | bytes 65568 | tf_op jit(solution)/shard_map/ppermute | solution.py:32
  62.3 0.8 %shard_map.90 = bf16[256,512]{1,0:T(8,128)(2,1)} custom-call(bf16[256,128]{1,0:T(8,128)(2,1)S(1)} %get-tuple-element.50.refs_0_, bf16[256,128]{1,0:T(8,128)(2,1)S(1)} %collective-permute-done.13.refs_1_, bf16[256,128]{1,0:T(8,128)(2,1)S(1)} %collective-permute-done.14.refs_2_, bf16[256,128]{1,0:T(8,128)(2,1)S(1)} %collective-permute-done.15.refs_3_), custom_call_target="tpu_custom_call" | custom-call | bytes 524288 | tf_op jit(solution)/shard_map/pallas_call | solution.py:47
  63.1 1.0 %shard_map.88 = (bf16[256,1024]{1,0:T(8,128)(2,1)}, bf16[256,512]{1,0:T(8,128)(2,1)}) custom-call(bf16[256,384]{1,0:T(8,128)(2,1)S(1)} %get-tuple-element.43.refs_0_, bf16[256,384]{1,0:T(8,128)(2,1)S(1)} %collective-permute-done.9.refs_1_, bf16[256,384]{1,0:T(8,128)(2,1)S(1)} %collective-permute-done.10.refs_2_, ...), custom_call_target="tpu_custom_call" | custom-call | bytes 1572864 | tf_op jit(solution)/shard_map/pallas_call | solution.py:47
  (32 shorter events, 0.5 us)
Async XLA Ops:
  0.6 1.0 %copy-start.3 = (bf16[256,512]{1,0:T(8,128)(2,1)S(1)}, bf16[256,512]{1,0:T(8,128)(2,1)}, u32[]{:S(2)}) copy-start(bf16[256,512]{1,0:T(8,128)(2,1)} %v_ref.1) | copy-start | bytes 786436
  0.6 1.0 %copy-start.2 = (bf16[256,512]{1,0:T(8,128)(2,1)S(1)}, bf16[256,512]{1,0:T(8,128)(2,1)}, u32[]{:S(2)}) copy-start(bf16[256,512]{1,0:T(8,128)(2,1)} %k_ref.1) | copy-start | bytes 786436
  0.7 5.5 %slice-start = ((s8[11010048]{0:T(1024)(128)(4,1)}), s8[4194304]{0:T(1024)(128)(4,1)S(1)}, s32[]{:S(2)}) async-start(s8[11010048]{0:T(1024)(128)(4,1)} %bitcast), calls=%async_computation.1 | async-start | bytes 8388608
  0.7 5.5 %slice-start.1 = ((s8[11010048]{0:T(1024)(128)(4,1)}), s8[4194304]{0:T(1024)(128)(4,1)S(1)}, s32[]{:S(2)}) async-start(s8[11010048]{0:T(1024)(128)(4,1)} %bitcast), calls=%async_computation.2 | async-start | bytes 8388608
  1.7 3.7 %copy-start.1 = (bf16[256,1024]{1,0:T(8,128)(2,1)S(1)}, bf16[256,1024]{1,0:T(8,128)(2,1)}, u32[]{:S(2)}) copy-start(bf16[256,1024]{1,0:T(8,128)(2,1)} %q_ref.1) | copy-start | bytes 1572868
  1.7 4.5 %slice-start.2 = ((s8[11010048]{0:T(1024)(128)(4,1)}), s8[2621440]{0:T(1024)(128)(4,1)S(1)}, s32[]{:S(2)}) async-start(s8[11010048]{0:T(1024)(128)(4,1)} %bitcast), calls=%async_computation.3 | async-start | bytes 5242880
  1.7 4.5 %copy-start = (bf16[256,2688]{1,0:T(8,128)(2,1)S(1)}, bf16[256,2688]{1,0:T(8,128)(2,1)}, u32[]{:S(2)}) copy-start(bf16[256,2688]{1,0:T(8,128)(2,1)} %c_ref.3) | copy-start | bytes 4128772
  1.8 8.3 %collective-permute-start = (bf16[256,256]{1,0:T(8,128)(2,1)S(1)}, bf16[256,256]{1,0:T(8,128)(2,1)S(1)}, u32[]{:S(2)}, u32[]{:S(2)}) collective-permute-start(bf16[256,256]{1,0:T(8,128)(2,1)S(1)} %get-tuple-element.30), channel_id=1, source_target_pairs={{0,6},{2,4},{4,2},{6,0},{8,14},{10,12},{12,10},{14,8},{16,22},{18,... | collective-permute-start | bytes 393224 | tf_op jit(solution)/shard_map/ppermute | solution.py:32
  4.3 6.5 %collective-permute-start.1 = (bf16[256,256]{1,0:T(8,128)(2,1)S(1)}, bf16[256,256]{1,0:T(8,128)(2,1)S(1)}, u32[]{:S(2)}, u32[]{:S(2)}) collective-permute-start(bf16[256,256]{1,0:T(8,128)(2,1)S(1)} %get-tuple-element.31), channel_id=1, source_target_pairs={{0,4},{2,6},{4,0},{6,2},{8,12},{10,14},{12,8},{14,10},{16,20},{18,... | collective-permute-start | bytes 393224 | tf_op jit(solution)/shard_map/ppermute | solution.py:32
  4.8 6.0 %collective-permute-start.2 = (bf16[256,256]{1,0:T(8,128)(2,1)S(1)}, bf16[256,256]{1,0:T(8,128)(2,1)S(1)}, u32[]{:S(2)}, u32[]{:S(2)}) collective-permute-start(bf16[256,256]{1,0:T(8,128)(2,1)S(1)} %get-tuple-element.32), channel_id=1, source_target_pairs={{0,2},{2,0},{4,6},{6,4},{8,10},{10,8},{12,14},{14,12},{16,18},{18,... | collective-permute-start | bytes 393224 | tf_op jit(solution)/shard_map/ppermute | solution.py:32
  8.1 7.6 %collective-permute-start.4 = (bf16[1024,256]{1,0:T(8,128)(2,1)S(1)}, bf16[1024,256]{1,0:T(8,128)(2,1)S(1)}, u32[]{:S(2)}, u32[]{:S(2)}) collective-permute-start(bf16[1024,256]{1,0:T(8,128)(2,1)S(1)} %shard_map.79.refs_0_), channel_id=1, source_target_pairs={{0,1},{1,0},{2,3},{3,2},{4,5},{5,4},{6,7},{7,6},{8,9},{9,8},{10,11... | collective-permute-start | bytes 1572872 | tf_op jit(solution)/shard_map/ppermute | solution.py:32
  10.9 15.7 %collective-permute-start.3 = (bf16[4,256,256]{2,1,0:T(8,128)(2,1)S(1)}, bf16[4,256,256]{2,1,0:T(8,128)(2,1)S(1)}, u32[]{:S(2)}, u32[]{:S(2)}) collective-permute-start(bf16[4,256,256]{2,1,0:T(8,128)(2,1)S(1)} %shard_map.81.refs_0_.refs_2_.own_ref), channel_id=1, source_target_pairs={{0,8},{2,10},{4,12},{6,14},{8,16},{10,18},{12,20},{14,22},{16,24},... | collective-permute-start | bytes 1572872 | tf_op jit(solution)/shard_map/ppermute | solution.py:27
  12.2 13.8 %all-to-all-start = ((bf16[4,256,256]{2,1,0:T(8,128)(2,1)}), bf16[4,256,256]{2,1,0:T(8,128)(2,1)S(1)}, u32[]{:S(2)}, u32[]{:S(2)}) async-start(bf16[4,256,256]{2,1,0:T(8,128)(2,1)} %shard_map.78.refs_0_), calls=%async_computation | async-start | bytes 1048576 | tf_op jit(solution)/shard_map/all_to_all | solution.py:40
  15.8 14.5 %collective-permute-start.5 = (bf16[256,256]{1,0:T(8,128)(2,1)S(1)}, bf16[256,256]{1,0:T(8,128)(2,1)S(1)}, u32[]{:S(2)}, u32[]{:S(2)}) collective-permute-start(bf16[256,256]{1,0:T(8,128)(2,1)S(1)} %get-tuple-element.36), channel_id=1, source_target_pairs={{0,6},{2,4},{4,2},{6,0},{8,14},{10,12},{12,10},{14,8},{16,22},{18,... | collective-permute-start | bytes 393224 | tf_op jit(solution)/shard_map/ppermute | solution.py:32
  18.8 11.6 %collective-permute-start.6 = (bf16[256,256]{1,0:T(8,128)(2,1)S(1)}, bf16[256,256]{1,0:T(8,128)(2,1)S(1)}, u32[]{:S(2)}, u32[]{:S(2)}) collective-permute-start(bf16[256,256]{1,0:T(8,128)(2,1)S(1)} %get-tuple-element.37), channel_id=1, source_target_pairs={{0,4},{2,6},{4,0},{6,2},{8,12},{10,14},{12,8},{14,10},{16,20},{18,... | collective-permute-start | bytes 393224 | tf_op jit(solution)/shard_map/ppermute | solution.py:32
  19.3 11.1 %collective-permute-start.7 = (bf16[256,256]{1,0:T(8,128)(2,1)S(1)}, bf16[256,256]{1,0:T(8,128)(2,1)S(1)}, u32[]{:S(2)}, u32[]{:S(2)}) collective-permute-start(bf16[256,256]{1,0:T(8,128)(2,1)S(1)} %get-tuple-element.38), channel_id=1, source_target_pairs={{0,2},{2,0},{4,6},{6,4},{8,10},{10,8},{12,14},{14,12},{16,18},{18,... | collective-permute-start | bytes 393224 | tf_op jit(solution)/shard_map/ppermute | solution.py:32
  32.6 12.3 %collective-permute-start.8 = (bf16[4,256,128]{2,1,0:T(8,128)(2,1)S(1)}, bf16[4,256,128]{2,1,0:T(8,128)(2,1)S(1)}, u32[]{:S(2)}, u32[]{:S(2)}) collective-permute-start(bf16[4,256,128]{2,1,0:T(8,128)(2,1)S(1)} %get-tuple-element.42), channel_id=1, source_target_pairs={{8,0},{10,2},{12,4},{14,6},{16,8},{18,10},{20,12},{22,14},{24,16},... | collective-permute-start | bytes 786440 | tf_op jit(solution)/shard_map/ppermute | solution.py:27
  42.6 8.8 %collective-permute-start.12 = (bf16[4,256,128]{2,1,0:T(8,128)(2,1)S(1)}, bf16[4,256,128]{2,1,0:T(8,128)(2,1)S(1)}, u32[]{:S(2)}, u32[]{:S(2)}) collective-permute-start(bf16[4,256,128]{2,1,0:T(8,128)(2,1)S(1)} %get-tuple-element.49), channel_id=1, source_target_pairs={{8,0},{10,2},{12,4},{14,6},{16,8},{18,10},{20,12},{22,14},{24,16},... | collective-permute-start | bytes 786440 | tf_op jit(solution)/shard_map/ppermute | solution.py:27
  46.9 16.2 %collective-permute-start.9 = (bf16[256,384]{1,0:T(8,128)(2,1)S(1)}, bf16[256,384]{1,0:T(8,128)(2,1)S(1)}, u32[]{:S(2)}, u32[]{:S(2)}) collective-permute-start(bf16[256,384]{1,0:T(8,128)(2,1)S(1)} %get-tuple-element.44), channel_id=1, source_target_pairs={{0,6},{2,4},{4,2},{6,0},{8,14},{10,12},{12,10},{14,8},{16,22},{18,... | collective-permute-start | bytes 589832 | tf_op jit(solution)/shard_map/ppermute | solution.py:32
  49.9 13.2 %collective-permute-start.10 = (bf16[256,384]{1,0:T(8,128)(2,1)S(1)}, bf16[256,384]{1,0:T(8,128)(2,1)S(1)}, u32[]{:S(2)}, u32[]{:S(2)}) collective-permute-start(bf16[256,384]{1,0:T(8,128)(2,1)S(1)} %get-tuple-element.45), channel_id=1, source_target_pairs={{0,4},{2,6},{4,0},{6,2},{8,12},{10,14},{12,8},{14,10},{16,20},{18,... | collective-permute-start | bytes 589832 | tf_op jit(solution)/shard_map/ppermute | solution.py:32
  51.3 11.7 %collective-permute-start.11 = (bf16[256,384]{1,0:T(8,128)(2,1)S(1)}, bf16[256,384]{1,0:T(8,128)(2,1)S(1)}, u32[]{:S(2)}, u32[]{:S(2)}) collective-permute-start(bf16[256,384]{1,0:T(8,128)(2,1)S(1)} %get-tuple-element.46), channel_id=1, source_target_pairs={{0,2},{2,0},{4,6},{6,4},{8,10},{10,8},{12,14},{14,12},{16,18},{18,... | collective-permute-start | bytes 589832 | tf_op jit(solution)/shard_map/ppermute | solution.py:32
  51.4 6.5 %collective-permute-start.13 = (bf16[256,128]{1,0:T(8,128)(2,1)S(1)}, bf16[256,128]{1,0:T(8,128)(2,1)S(1)}, u32[]{:S(2)}, u32[]{:S(2)}) collective-permute-start(bf16[256,128]{1,0:T(8,128)(2,1)S(1)} %get-tuple-element.51), channel_id=1, source_target_pairs={{0,6},{2,4},{4,2},{6,0},{8,14},{10,12},{12,10},{14,8},{16,22},{18,... | collective-permute-start | bytes 196616 | tf_op jit(solution)/shard_map/ppermute | solution.py:32
  53.5 6.5 %collective-permute-start.14 = (bf16[256,128]{1,0:T(8,128)(2,1)S(1)}, bf16[256,128]{1,0:T(8,128)(2,1)S(1)}, u32[]{:S(2)}, u32[]{:S(2)}) collective-permute-start(bf16[256,128]{1,0:T(8,128)(2,1)S(1)} %get-tuple-element.52), channel_id=1, source_target_pairs={{0,4},{2,6},{4,0},{6,2},{8,12},{10,14},{12,8},{14,10},{16,20},{18,... | collective-permute-start | bytes 196616 | tf_op jit(solution)/shard_map/ppermute | solution.py:32
  57.9 4.4 %collective-permute-start.15 = (bf16[256,128]{1,0:T(8,128)(2,1)S(1)}, bf16[256,128]{1,0:T(8,128)(2,1)S(1)}, u32[]{:S(2)}, u32[]{:S(2)}) collective-permute-start(bf16[256,128]{1,0:T(8,128)(2,1)S(1)} %get-tuple-element.53), channel_id=1, source_target_pairs={{0,2},{2,0},{4,6},{6,4},{8,10},{10,8},{12,14},{14,12},{16,18},{18,... | collective-permute-start | bytes 196616 | tf_op jit(solution)/shard_map/ppermute | solution.py:32

commit v11 on v9

--- a/solution.py
+++ b/solution.py
@@ -55,8 +55,8 @@
     return place, index - place
 
 
-def hop(group, r):
-    return group - r if r else 0
+def hop(group, r, near=False):
+    return r if near or r == 0 else group - r
 
 
 def lanes(index, width):
@@ -341,7 +341,7 @@
                     )
 
         for r in range(z.group):
-            member = spot(z.group)[0] ^ hop(z.group, r)
+            member = spot(z.group)[0] ^ hop(z.group, r, near=True)
             dv = term_refs[0][member]
             for term in term_refs[1:]:
                 dv = dv + term[member].astype(jnp.float32)
@@ -377,19 +377,22 @@
     return call(body, outs)(*flat)
 
 
-def unpack(group, pieces, widths, before):
+def unpack(group, pieces, widths, before=(), near=False):
     tokens = pieces[0].shape[0]
 
     def body(*refs):
+        out_refs = refs[group + len(before) :]
         for r in range(group):
             lower = 0
             for number, width in enumerate(widths):
-                there = lanes(spot(group)[0] ^ hop(group, r), width)
-                refs[group + 1 + number][:, there] = refs[r][:, lower : lower + width]
+                there = lanes(spot(group)[0] ^ hop(group, r, near), width)
+                out_refs[number][:, there] = refs[r][:, lower : lower + width]
                 lower += width
+        out_refs[-1][...] = jnp.zeros_like(out_refs[-1])
 
     outs = [jax.ShapeDtypeStruct((tokens, group * width), jnp.bfloat16) for width in widths]
-    return call(body, outs, specs=[VMEM] * group + [ANY])(*pieces, before)
+    outs += [jax.ShapeDtypeStruct((8, 128), jnp.float32)]
+    return call(body, outs, specs=[VMEM] * group + [ANY] * len(before))(*pieces, *before)
 
 
 def local(layer_cotangent, out_weight, queries, keys, values):
@@ -408,8 +411,8 @@
     kv_width = heads * HEAD_SIZE
     back_groups = WINDOW_LENGTH // (group * tokens)
 
-    def trade(sent):
-        return [sent[0]] + [swapped(sent[r], "ctx", hop(group, r)) for r in range(1, group)]
+    def trade(sent, near=False):
+        return [sent[0]] + [swapped(sent[r], "ctx", hop(group, r, near)) for r in range(1, group)]
 
     def returned(earlier):
         return [
@@ -420,25 +423,26 @@
     kv_pieces = trade(sent)
     z = Shape(group, back_groups, heads, per_head, tokens)
     query_sent = pack_queries(group, queries, sent[0])
-    qt = turn_queries(z, trade(query_sent))
     if tp_count == 2:
         other = head_product(2, 1, out_weight, layer_cotangent, [query_sent[0]])
-        terms = [head_product(2, 0, out_weight, layer_cotangent, [other]), swapped(other, "tp", 1)]
     else:
         other = head_product(1, 0, out_weight, layer_cotangent, [query_sent[0]])
+    kv_own = order_pieces(group, kv_pieces, other)
+    kv_earlier = [shifted(kv_own, "ctx", group * step) for step in range(back_groups, 0, -1)]
+    if tp_count == 2:
+        terms = [head_product(2, 0, out_weight, layer_cotangent, [kv_own, other]), swapped(other, "tp", 1)]
+    else:
         terms = [lax.psum_scatter(other, "tp", scatter_dimension=0, tiled=True)]
-    kv_own = order_pieces(group, kv_pieces, terms[0])
-    kv_earlier = [shifted(kv_own, "ctx", group * step) for step in range(back_groups, 0, -1)]
+    qt = turn_queries(z, trade(query_sent))
     grads = trade(pack_grads(group, terms, kv_own))
     e, inverse = softmax(z, kv_own, kv_earlier, qt)
     g, dv_own, dv_earlier = value_terms(z, e, inverse, grads)
     dv_terms = [dv_own] + returned(dv_earlier)
     ds, dk_own, dk_earlier = key_terms(z, e, inverse, qt, g, kv_own, kv_earlier)
     dk_terms = [dk_own] + returned(dk_earlier)
-    pieces = trade(query_terms(z, ds, inverse, kv_own, kv_earlier, dv_terms))
-    query_grads, value_gradients = unpack(group, pieces, [z.width, kv_width], ds)
-    pieces = trade(pack_terms(group, [dk_terms]))
-    (key_gradients,) = unpack(group, pieces, [kv_width], value_gradients)
+    pieces = trade(query_terms(z, ds, inverse, kv_own, kv_earlier, dv_terms), near=True)
+    query_grads, value_gradients, done = unpack(group, pieces, [z.width, kv_width], near=True)
+    key_gradients, _ = unpack(group, trade(pack_terms(group, [dk_terms])), [kv_width], [done])
     return (query_grads, key_gradients, value_gradients)
 
 

time: 60.9 us -> 59.3 us (0.974)
  local copies, waits for them, and re-layouts: 2.23 us -> 1.28 us
    unnamed x16 -> x14, local copies, waits for them, and re-layouts: 2.23 us -> 1.28 us
    ppermute x16, waiting for transfers between devices: 9.3 us -> 8.62 us  [swapped(): lax.ppermute(value, axis, [(source, source ^ bits) for source in range(co...]
  transfers between devices with their start and end apart: 19 -> 19, of which waited for: 10 -> 9; matrix products, arithmetic and copies ran while one was open for 0% -> 0% of each run, Pallas kernels for 27% -> 28%
where the time goes in v11:
time: 59.3 us; the launch traced here: 59.1 us
  starting transfers between devices  26.2 us (44%)
  Pallas kernels  19.4 us (33%)
  waiting for transfers between devices  11.3 us (19%)
  local copies, waits for them, and re-layouts  1.28 us (2%)
  between operations  0.84 us (1%)
    pallas_call x15, Pallas kernels, run(): pl.pallas_call(body, out_shape=tuple(outs), in_specs=specs or [SMEM if a....  19.4 us
    ppermute x16, starting transfers between devices, swapped(): lax.ppermute(value, axis, [(source, source ^ bits) for source in range(co...  18.8 us
    ppermute x16, waiting for transfers between devices, swapped(): lax.ppermute(value, axis, [(source, source ^ bits) for source in range(co...  8.62 us
    ppermute x3, starting transfers between devices, shifted(): lax.ppermute(value, axis, [(source, source + steps) for source in range(l...  7.36 us
    ppermute x3, waiting for transfers between devices, shifted(): lax.ppermute(value, axis, [(source, source + steps) for source in range(l...  2.68 us
    unnamed x14, local copies, waits for them, and re-layouts  1.28 us
  transfers between devices with their start and end apart: 19, of which 9 were waited for; matrix products, arithmetic and copies ran while one was open for 0% of the time, Pallas kernels for 28%

profile of v11, /device:TPU:24, one launch (start us, length us, event | category | flops | bytes accessed | tf_op | source)
XLA Modules:
  0.0 59.1 jit_solution(12970807136106448633)
XLA Ops:
  0.7 0.9 %copy-done.3 = bf16[256,512]{1,0:T(8,128)(2,1)S(1)} copy-done((bf16[256,512]{1,0:T(8,128)(2,1)S(1)}, bf16[256,512]{1,0:T(8,128)(2,1)}, u32[]{:S(2)}) %copy-start.3) | copy-done | bytes 262168
  1.8 2.5 %collective-permute-start = (bf16[256,256]{1,0:T(8,128)(2,1)S(1)}, bf16[256,256]{1,0:T(8,128)(2,1)S(1)}, u32[]{:S(2)}, u32[]{:S(2)}) collective-permute-start(bf16[256,256]{1,0:T(8,128)(2,1)S(1)} %get-tuple-element.36), channel_id=1, source_target_pairs={{0,6},{2,4},{4,2},{6,0},{8,14},{10,12},{12,10},{14,8},{16,22},{18,... | collective-permute-start | bytes 393224 | tf_op jit(solution)/shard_map/ppermute | solution.py:32
  4.3 0.5 collective-permute-start.1
  4.8 0.5 collective-permute-start.2
  5.7 1.9 %shard_map.79.refs_4_.refs_1_ = bf16[1024,256]{1,0:T(8,128)(2,1)S(1)} custom-call(bf16[2048,2688]{1,0:T(8,128)(2,1)S(1)} %bitcast.1, bf16[256,2688]{1,0:T(8,128)(2,1)S(1)} %copy-done, bf16[256,256]{1,0:T(8,128)(2,1)S(1)} %get-tuple-element.39.refs_0_), custom_call_target="tpu_custom_call" | custom-call | flops 1409286144 | bytes 13041664 | tf_op jit(solution)/shard_map/pallas_call | solution.py:39
  7.7 0.6 %collective-permute-done.refs_1_ = bf16[256,256]{1,0:T(8,128)(2,1)S(1)} collective-permute-done((bf16[256,256]{1,0:T(8,128)(2,1)S(1)}, bf16[256,256]{1,0:T(8,128)(2,1)S(1)}, u32[]{:S(2)}, u32[]{:S(2)}) %collective-permute-start) | collective-permute-done | bytes 131104 | tf_op jit(solution)/shard_map/ppermute | solution.py:32
  8.3 2.5 %collective-permute-done.1.refs_2_ = bf16[256,256]{1,0:T(8,128)(2,1)S(1)} collective-permute-done((bf16[256,256]{1,0:T(8,128)(2,1)S(1)}, bf16[256,256]{1,0:T(8,128)(2,1)S(1)}, u32[]{:S(2)}, u32[]{:S(2)}) %collective-permute-start.1) | collective-permute-done | bytes 131104 | tf_op jit(solution)/shard_map/ppermute | solution.py:32
  10.9 1.3 %collective-permute-start.3 = (bf16[4,256,256]{2,1,0:T(8,128)(2,1)S(1)}, bf16[4,256,256]{2,1,0:T(8,128)(2,1)S(1)}, u32[]{:S(2)}, u32[]{:S(2)}) collective-permute-start(bf16[4,256,256]{2,1,0:T(8,128)(2,1)S(1)} %shard_map.80.refs_0_.refs_2_.own_ref), channel_id=1, source_target_pairs={{0,8},{2,10},{4,12},{6,14},{8,16},{10,18},{12,20},{14,22},{16,24},... | collective-permute-start | bytes 1572872 | tf_op jit(solution)/shard_map/ppermute | solution.py:27
  12.2 1.8 %collective-permute-start.4 = (bf16[256,256]{1,0:T(8,128)(2,1)S(1)}, bf16[256,256]{1,0:T(8,128)(2,1)S(1)}, u32[]{:S(2)}, u32[]{:S(2)}) collective-permute-start(bf16[256,256]{1,0:T(8,128)(2,1)S(1)} %get-tuple-element.40), channel_id=1, source_target_pairs={{0,6},{2,4},{4,2},{6,0},{8,14},{10,12},{12,10},{14,8},{16,22},{18,... | collective-permute-start | bytes 393224 | tf_op jit(solution)/shard_map/ppermute | solution.py:32
  13.9 1.3 %collective-permute-start.5 = (bf16[256,256]{1,0:T(8,128)(2,1)S(1)}, bf16[256,256]{1,0:T(8,128)(2,1)S(1)}, u32[]{:S(2)}, u32[]{:S(2)}) collective-permute-start(bf16[256,256]{1,0:T(8,128)(2,1)S(1)} %get-tuple-element.41), channel_id=1, source_target_pairs={{0,4},{2,6},{4,0},{6,2},{8,12},{10,14},{12,8},{14,10},{16,20},{18,... | collective-permute-start | bytes 393224 | tf_op jit(solution)/shard_map/ppermute | solution.py:32
  15.7 1.9 %shard_map.83.refs_0_ = bf16[1024,256]{1,0:T(8,128)(2,1)S(1)} custom-call(bf16[2048,2688]{1,0:T(8,128)(2,1)S(1)} %bitcast.1, bf16[256,2688]{1,0:T(8,128)(2,1)S(1)} %copy-done, bf16[4,256,256]{2,1,0:T(8,128)(2,1)S(1)} %shard_map.80.refs_0_.refs_2_.own_ref, bf16[1024,256]{1,0:T(8,128)(2,1)S(1)} %shard_map.79.refs_4_.refs_1_), custom_call_target="tpu_custom_call" | custom-call | flops 1409286144 | bytes 13959168 | tf_op jit(solution)/shard_map/pallas_call | solution.py:39
  17.8 1.8 %collective-permute-start.8 = (bf16[256,256]{1,0:T(8,128)(2,1)S(1)}, bf16[256,256]{1,0:T(8,128)(2,1)S(1)}, u32[]{:S(2)}, u32[]{:S(2)}) collective-permute-start(bf16[256,256]{1,0:T(8,128)(2,1)S(1)} %get-tuple-element.46), channel_id=1, source_target_pairs={{0,6},{2,4},{4,2},{6,0},{8,14},{10,12},{12,10},{14,8},{16,22},{18,... | collective-permute-start | bytes 393224 | tf_op jit(solution)/shard_map/ppermute | solution.py:32
  19.6 1.4 %collective-permute-start.9 = (bf16[256,256]{1,0:T(8,128)(2,1)S(1)}, bf16[256,256]{1,0:T(8,128)(2,1)S(1)}, u32[]{:S(2)}, u32[]{:S(2)}) collective-permute-start(bf16[256,256]{1,0:T(8,128)(2,1)S(1)} %get-tuple-element.47), channel_id=1, source_target_pairs={{0,4},{2,6},{4,0},{6,2},{8,12},{10,14},{12,8},{14,10},{16,20},{18,... | collective-permute-start | bytes 393224 | tf_op jit(solution)/shard_map/ppermute | solution.py:32
  21.0 1.2 %collective-permute-done.5.refs_2_ = bf16[256,256]{1,0:T(8,128)(2,1)S(1)} collective-permute-done((bf16[256,256]{1,0:T(8,128)(2,1)S(1)}, bf16[256,256]{1,0:T(8,128)(2,1)S(1)}, u32[]{:S(2)}, u32[]{:S(2)}) %collective-permute-start.5) | collective-permute-done | bytes 131104 | tf_op jit(solution)/shard_map/ppermute | solution.py:32
  22.2 1.5 %collective-permute-start.10 = (bf16[256,256]{1,0:T(8,128)(2,1)S(1)}, bf16[256,256]{1,0:T(8,128)(2,1)S(1)}, u32[]{:S(2)}, u32[]{:S(2)}) collective-permute-start(bf16[256,256]{1,0:T(8,128)(2,1)S(1)} %get-tuple-element.48), channel_id=1, source_target_pairs={{0,2},{2,0},{4,6},{6,4},{8,10},{10,8},{12,14},{14,12},{16,18},{18,... | collective-permute-start | bytes 393224 | tf_op jit(solution)/shard_map/ppermute | solution.py:32
  23.9 2.7 %collective-permute-done.3.refs_1_.refs_0_ = bf16[4,256,256]{2,1,0:T(8,128)(2,1)S(1)} collective-permute-done((bf16[4,256,256]{2,1,0:T(8,128)(2,1)S(1)}, bf16[4,256,256]{2,1,0:T(8,128)(2,1)S(1)}, u32[]{:S(2)}, u32[]{:S(2)}) %collective-permute-start.3) | collective-permute-done | bytes 524320 | tf_op jit(solution)/shard_map/ppermute | solution.py:27
  26.6 3.8 %shard_map.82 = (bf16[1,4,5,256,512]{4,3,2,1,0:T(8,128)(2,1)S(1)}, f32[1,4,1,512]{3,2,1,0:T(1,128)S(1)}) custom-call(bf16[4,256,256]{2,1,0:T(8,128)(2,1)S(1)} %shard_map.80.refs_0_.refs_2_.own_ref, bf16[4,256,256]{2,1,0:T(8,128)(2,1)S(1)} %collective-permute-done.3.refs_1_.refs_0_, bf16[1,4,128,512]{3,2,1,0:T(8,128)(2,1)S(1)} %shard_map.81.refs_2_.qt_ref), custom_call_target="tpu_custom_call" | custom-call | flops 671088640 | bytes 6823936 | tf_op jit(solution)/shard_map/pallas_call | solution.py:39
  30.4 2.2 %shard_map.85 = (bf16[1,4,128,512]{3,2,1,0:T(8,128)(2,1)S(1)}, f32[4,256,128]{2,1,0:T(8,128)S(1)}, bf16[4,256,128]{2,1,0:T(8,128)(2,1)S(1)}) custom-call(bf16[1,4,5,256,512]{4,3,2,1,0:T(8,128)(2,1)S(1)} %get-tuple-element.43.e_ref, f32[1,4,1,512]{3,2,1,0:T(1,128)S(1)} %get-tuple-element.44.inverse_ref, bf16[256,256]{1,0:T(8,128)(2,1)S(1)} %get-tuple-element.45.refs_0_, ...), custom_call_target="tpu_custom_call" | custom-call | flops 671088640 | bytes 7086080 | tf_op jit(solution)/shard_map/pallas_call | solution.py:39
  32.6 3.7 %collective-permute-start.11 = (bf16[4,256,128]{2,1,0:T(8,128)(2,1)S(1)}, bf16[4,256,128]{2,1,0:T(8,128)(2,1)S(1)}, u32[]{:S(2)}, u32[]{:S(2)}) collective-permute-start(bf16[4,256,128]{2,1,0:T(8,128)(2,1)S(1)} %get-tuple-element.52), channel_id=1, source_target_pairs={{8,0},{10,2},{12,4},{14,6},{16,8},{18,10},{20,12},{22,14},{24,16},... | collective-permute-start | bytes 786440 | tf_op jit(solution)/shard_map/ppermute | solution.py:27
  36.3 5.4 %shard_map.86 = (bf16[1,4,5,256,512]{4,3,2,1,0:T(8,128)(2,1)S(1)}, f32[4,256,128]{2,1,0:T(8,128)S(1)}, bf16[4,256,128]{2,1,0:T(8,128)(2,1)S(1)}) custom-call(bf16[1,4,5,256,512]{4,3,2,1,0:T(8,128)(2,1)S(1)} %get-tuple-element.43.e_ref, f32[1,4,1,512]{3,2,1,0:T(1,128)S(1)} %get-tuple-element.44.inverse_ref, ...), custom_call_target="tpu_custom_call" | custom-call | flops 1342177280 | bytes 13377536 | tf_op jit(solution)/shard_map/pallas_call | solution.py:39
  41.7 2.4 %collective-permute-start.15 = (bf16[4,256,128]{2,1,0:T(8,128)(2,1)S(1)}, bf16[4,256,128]{2,1,0:T(8,128)(2,1)S(1)}, u32[]{:S(2)}, u32[]{:S(2)}) collective-permute-start(bf16[4,256,128]{2,1,0:T(8,128)(2,1)S(1)} %get-tuple-element.59), channel_id=1, source_target_pairs={{8,0},{10,2},{12,4},{14,6},{16,8},{18,10},{20,12},{22,14},{24,16},... | collective-permute-start | bytes 786440 | tf_op jit(solution)/shard_map/ppermute | solution.py:27
  44.0 2.0 %shard_map.87 = (bf16[256,384]{1,0:T(8,128)(2,1)S(1)}, bf16[256,384]{1,0:T(8,128)(2,1)S(1)}, bf16[256,384]{1,0:T(8,128)(2,1)S(1)}, bf16[256,384]{1,0:T(8,128)(2,1)S(1)}) custom-call(bf16[1,4,5,256,512]{4,3,2,1,0:T(8,128)(2,1)S(1)} %get-tuple-element.50.ds_ref, f32[1,4,1,512]{3,2,1,0:T(1,128)S(1)} %get-tuple-element.44.inverse_ref, ...), custom_call_target="tpu_custom_call" | custom-call | flops 671088640 | bytes 7872512 | tf_op jit(solution)/shard_map/pallas_call | solution.py:39
  46.0 1.0 %collective-permute-start.12 = (bf16[256,384]{1,0:T(8,128)(2,1)S(1)}, bf16[256,384]{1,0:T(8,128)(2,1)S(1)}, u32[]{:S(2)}, u32[]{:S(2)}) collective-permute-start(bf16[256,384]{1,0:T(8,128)(2,1)S(1)} %get-tuple-element.54), channel_id=1, source_target_pairs={{0,2},{2,0},{4,6},{6,4},{8,10},{10,8},{12,14},{14,12},{16,18},{18,... | collective-permute-start | bytes 589832 | tf_op jit(solution)/shard_map/ppermute | solution.py:32
  47.0 1.1 %collective-permute-start.13 = (bf16[256,384]{1,0:T(8,128)(2,1)S(1)}, bf16[256,384]{1,0:T(8,128)(2,1)S(1)}, u32[]{:S(2)}, u32[]{:S(2)}) collective-permute-start(bf16[256,384]{1,0:T(8,128)(2,1)S(1)} %get-tuple-element.55), channel_id=1, source_target_pairs={{0,4},{2,6},{4,0},{6,2},{8,12},{10,14},{12,8},{14,10},{16,20},{18,... | collective-permute-start | bytes 589832 | tf_op jit(solution)/shard_map/ppermute | solution.py:32
  48.1 1.4 %collective-permute-start.14 = (bf16[256,384]{1,0:T(8,128)(2,1)S(1)}, bf16[256,384]{1,0:T(8,128)(2,1)S(1)}, u32[]{:S(2)}, u32[]{:S(2)}) collective-permute-start(bf16[256,384]{1,0:T(8,128)(2,1)S(1)} %get-tuple-element.56), channel_id=1, source_target_pairs={{0,6},{2,4},{4,2},{6,0},{8,14},{10,12},{12,10},{14,8},{16,22},{18,... | collective-permute-start | bytes 589832 | tf_op jit(solution)/shard_map/ppermute | solution.py:32
  49.6 1.6 %collective-permute-start.16 = (bf16[256,128]{1,0:T(8,128)(2,1)S(1)}, bf16[256,128]{1,0:T(8,128)(2,1)S(1)}, u32[]{:S(2)}, u32[]{:S(2)}) collective-permute-start(bf16[256,128]{1,0:T(8,128)(2,1)S(1)} %get-tuple-element.61), channel_id=1, source_target_pairs={{0,6},{2,4},{4,2},{6,0},{8,14},{10,12},{12,10},{14,8},{16,22},{18,... | collective-permute-start | bytes 196616 | tf_op jit(solution)/shard_map/ppermute | solution.py:32
  51.2 0.9 %collective-permute-start.17 = (bf16[256,128]{1,0:T(8,128)(2,1)S(1)}, bf16[256,128]{1,0:T(8,128)(2,1)S(1)}, u32[]{:S(2)}, u32[]{:S(2)}) collective-permute-start(bf16[256,128]{1,0:T(8,128)(2,1)S(1)} %get-tuple-element.62), channel_id=1, source_target_pairs={{0,4},{2,6},{4,0},{6,2},{8,12},{10,14},{12,8},{14,10},{16,20},{18,... | collective-permute-start | bytes 196616 | tf_op jit(solution)/shard_map/ppermute | solution.py:32
  52.1 1.8 %collective-permute-done.12.refs_1_ = bf16[256,384]{1,0:T(8,128)(2,1)S(1)} collective-permute-done((bf16[256,384]{1,0:T(8,128)(2,1)S(1)}, bf16[256,384]{1,0:T(8,128)(2,1)S(1)}, u32[]{:S(2)}, u32[]{:S(2)}) %collective-permute-start.12) | collective-permute-done | bytes 196640 | tf_op jit(solution)/shard_map/ppermute | solution.py:32
  53.9 1.0 %collective-permute-start.18 = (bf16[256,128]{1,0:T(8,128)(2,1)S(1)}, bf16[256,128]{1,0:T(8,128)(2,1)S(1)}, u32[]{:S(2)}, u32[]{:S(2)}) collective-permute-start(bf16[256,128]{1,0:T(8,128)(2,1)S(1)} %get-tuple-element.63), channel_id=1, source_target_pairs={{0,2},{2,0},{4,6},{6,4},{8,10},{10,8},{12,14},{14,12},{16,18},{18,... | collective-permute-start | bytes 196616 | tf_op jit(solution)/shard_map/ppermute | solution.py:32
  55.1 1.7 %collective-permute-done.14.refs_3_ = bf16[256,384]{1,0:T(8,128)(2,1)S(1)} collective-permute-done((bf16[256,384]{1,0:T(8,128)(2,1)S(1)}, bf16[256,384]{1,0:T(8,128)(2,1)S(1)}, u32[]{:S(2)}, u32[]{:S(2)}) %collective-permute-start.14) | collective-permute-done | bytes 196640 | tf_op jit(solution)/shard_map/ppermute | solution.py:32
  56.9 1.0 %shard_map.88 = (bf16[256,1024]{1,0:T(8,128)(2,1)}, bf16[256,512]{1,0:T(8,128)(2,1)}, f32[8,128]{1,0:T(8,128)S(1)}) custom-call(bf16[256,384]{1,0:T(8,128)(2,1)S(1)} %get-tuple-element.53.refs_0_, bf16[256,384]{1,0:T(8,128)(2,1)S(1)} %collective-permute-done.12.refs_1_, bf16[256,384]{1,0:T(8,128)(2,1)S(1)} %collective-permute-done.13.refs_2_, ...), custom_call_target="tpu_custom_call" | custom-call | bytes 1576960 | tf_op jit(solution)/shard_map/pallas_call | solution.py:39
  58.3 0.8 %shard_map.90 = (bf16[256,512]{1,0:T(8,128)(2,1)}, f32[8,128]{1,0:T(8,128)}) custom-call(bf16[256,128]{1,0:T(8,128)(2,1)S(1)} %get-tuple-element.60.refs_0_, bf16[256,128]{1,0:T(8,128)(2,1)S(1)} %collective-permute-done.16.refs_1_, bf16[256,128]{1,0:T(8,128)(2,1)S(1)} %collective-permute-done.17.refs_2_, ...), custom_call_target="tpu_custom_call" | custom-call | bytes 532480 | tf_op jit(solution)/shard_map/pallas_call | solution.py:39
  (36 shorter events, 2.3 us)
Async XLA Ops:
  0.6 1.0 %copy-start.3 = (bf16[256,512]{1,0:T(8,128)(2,1)S(1)}, bf16[256,512]{1,0:T(8,128)(2,1)}, u32[]{:S(2)}) copy-start(bf16[256,512]{1,0:T(8,128)(2,1)} %v_ref.1) | copy-start | bytes 786436
  0.6 1.0 %copy-start.2 = (bf16[256,512]{1,0:T(8,128)(2,1)S(1)}, bf16[256,512]{1,0:T(8,128)(2,1)}, u32[]{:S(2)}) copy-start(bf16[256,512]{1,0:T(8,128)(2,1)} %k_ref.1) | copy-start | bytes 786436
  0.7 4.7 %slice-start = ((s8[11010048]{0:T(1024)(128)(4,1)}), s8[4194304]{0:T(1024)(128)(4,1)S(1)}, s32[]{:S(2)}) async-start(s8[11010048]{0:T(1024)(128)(4,1)} %bitcast), calls=%async_computation | async-start | bytes 8388608
  0.7 4.7 %slice-start.1 = ((s8[11010048]{0:T(1024)(128)(4,1)}), s8[4194304]{0:T(1024)(128)(4,1)S(1)}, s32[]{:S(2)}) async-start(s8[11010048]{0:T(1024)(128)(4,1)} %bitcast), calls=%async_computation.1 | async-start | bytes 8388608
  1.7 3.7 %copy-start.1 = (bf16[256,1024]{1,0:T(8,128)(2,1)S(1)}, bf16[256,1024]{1,0:T(8,128)(2,1)}, u32[]{:S(2)}) copy-start(bf16[256,1024]{1,0:T(8,128)(2,1)} %q_ref.1) | copy-start | bytes 1572868
  1.7 3.8 %slice-start.2 = ((s8[11010048]{0:T(1024)(128)(4,1)}), s8[2621440]{0:T(1024)(128)(4,1)S(1)}, s32[]{:S(2)}) async-start(s8[11010048]{0:T(1024)(128)(4,1)} %bitcast), calls=%async_computation.2 | async-start | bytes 5242880
  1.7 4.0 %copy-start = (bf16[256,2688]{1,0:T(8,128)(2,1)S(1)}, bf16[256,2688]{1,0:T(8,128)(2,1)}, u32[]{:S(2)}) copy-start(bf16[256,2688]{1,0:T(8,128)(2,1)} %c_ref.3) | copy-start | bytes 4128772
  1.8 6.5 %collective-permute-start = (bf16[256,256]{1,0:T(8,128)(2,1)S(1)}, bf16[256,256]{1,0:T(8,128)(2,1)S(1)}, u32[]{:S(2)}, u32[]{:S(2)}) collective-permute-start(bf16[256,256]{1,0:T(8,128)(2,1)S(1)} %get-tuple-element.36), channel_id=1, source_target_pairs={{0,6},{2,4},{4,2},{6,0},{8,14},{10,12},{12,10},{14,8},{16,22},{18,... | collective-permute-start | bytes 393224 | tf_op jit(solution)/shard_map/ppermute | solution.py:32
  4.3 6.5 %collective-permute-start.1 = (bf16[256,256]{1,0:T(8,128)(2,1)S(1)}, bf16[256,256]{1,0:T(8,128)(2,1)S(1)}, u32[]{:S(2)}, u32[]{:S(2)}) collective-permute-start(bf16[256,256]{1,0:T(8,128)(2,1)S(1)} %get-tuple-element.37), channel_id=1, source_target_pairs={{0,4},{2,6},{4,0},{6,2},{8,12},{10,14},{12,8},{14,10},{16,20},{18,... | collective-permute-start | bytes 393224 | tf_op jit(solution)/shard_map/ppermute | solution.py:32
  4.8 6.0 %collective-permute-start.2 = (bf16[256,256]{1,0:T(8,128)(2,1)S(1)}, bf16[256,256]{1,0:T(8,128)(2,1)S(1)}, u32[]{:S(2)}, u32[]{:S(2)}) collective-permute-start(bf16[256,256]{1,0:T(8,128)(2,1)S(1)} %get-tuple-element.38), channel_id=1, source_target_pairs={{0,2},{2,0},{4,6},{6,4},{8,10},{10,8},{12,14},{14,12},{16,18},{18,... | collective-permute-start | bytes 393224 | tf_op jit(solution)/shard_map/ppermute | solution.py:32
  7.6 10.1 %collective-permute-start.7 = (bf16[1024,256]{1,0:T(8,128)(2,1)S(1)}, bf16[1024,256]{1,0:T(8,128)(2,1)S(1)}, u32[]{:S(2)}, u32[]{:S(2)}) collective-permute-start(bf16[1024,256]{1,0:T(8,128)(2,1)S(1)} %shard_map.79.refs_4_.refs_1_), channel_id=1, source_target_pairs={{0,1},{1,0},{2,3},{3,2},{4,5},{5,4},{6,7},{7,6},{8,9},{9,8},{10,11... | collective-permute-start | bytes 1572872 | tf_op jit(solution)/shard_map/ppermute | solution.py:32
  10.9 15.7 %collective-permute-start.3 = (bf16[4,256,256]{2,1,0:T(8,128)(2,1)S(1)}, bf16[4,256,256]{2,1,0:T(8,128)(2,1)S(1)}, u32[]{:S(2)}, u32[]{:S(2)}) collective-permute-start(bf16[4,256,256]{2,1,0:T(8,128)(2,1)S(1)} %shard_map.80.refs_0_.refs_2_.own_ref), channel_id=1, source_target_pairs={{0,8},{2,10},{4,12},{6,14},{8,16},{10,18},{12,20},{14,22},{16,24},... | collective-permute-start | bytes 1572872 | tf_op jit(solution)/shard_map/ppermute | solution.py:27
  12.2 7.4 %collective-permute-start.4 = (bf16[256,256]{1,0:T(8,128)(2,1)S(1)}, bf16[256,256]{1,0:T(8,128)(2,1)S(1)}, u32[]{:S(2)}, u32[]{:S(2)}) collective-permute-start(bf16[256,256]{1,0:T(8,128)(2,1)S(1)} %get-tuple-element.40), channel_id=1, source_target_pairs={{0,6},{2,4},{4,2},{6,0},{8,14},{10,12},{12,10},{14,8},{16,22},{18,... | collective-permute-start | bytes 393224 | tf_op jit(solution)/shard_map/ppermute | solution.py:32
  13.9 8.3 %collective-permute-start.5 = (bf16[256,256]{1,0:T(8,128)(2,1)S(1)}, bf16[256,256]{1,0:T(8,128)(2,1)S(1)}, u32[]{:S(2)}, u32[]{:S(2)}) collective-permute-start(bf16[256,256]{1,0:T(8,128)(2,1)S(1)} %get-tuple-element.41), channel_id=1, source_target_pairs={{0,4},{2,6},{4,0},{6,2},{8,12},{10,14},{12,8},{14,10},{16,20},{18,... | collective-permute-start | bytes 393224 | tf_op jit(solution)/shard_map/ppermute | solution.py:32
  15.2 8.5 %collective-permute-start.6 = (bf16[256,256]{1,0:T(8,128)(2,1)S(1)}, bf16[256,256]{1,0:T(8,128)(2,1)S(1)}, u32[]{:S(2)}, u32[]{:S(2)}) collective-permute-start(bf16[256,256]{1,0:T(8,128)(2,1)S(1)} %get-tuple-element.42), channel_id=1, source_target_pairs={{0,2},{2,0},{4,6},{6,4},{8,10},{10,8},{12,14},{14,12},{16,18},{18,... | collective-permute-start | bytes 393224 | tf_op jit(solution)/shard_map/ppermute | solution.py:32
  17.8 12.6 %collective-permute-start.8 = (bf16[256,256]{1,0:T(8,128)(2,1)S(1)}, bf16[256,256]{1,0:T(8,128)(2,1)S(1)}, u32[]{:S(2)}, u32[]{:S(2)}) collective-permute-start(bf16[256,256]{1,0:T(8,128)(2,1)S(1)} %get-tuple-element.46), channel_id=1, source_target_pairs={{0,6},{2,4},{4,2},{6,0},{8,14},{10,12},{12,10},{14,8},{16,22},{18,... | collective-permute-start | bytes 393224 | tf_op jit(solution)/shard_map/ppermute | solution.py:32
  19.6 10.8 %collective-permute-start.9 = (bf16[256,256]{1,0:T(8,128)(2,1)S(1)}, bf16[256,256]{1,0:T(8,128)(2,1)S(1)}, u32[]{:S(2)}, u32[]{:S(2)}) collective-permute-start(bf16[256,256]{1,0:T(8,128)(2,1)S(1)} %get-tuple-element.47), channel_id=1, source_target_pairs={{0,4},{2,6},{4,0},{6,2},{8,12},{10,14},{12,8},{14,10},{16,20},{18,... | collective-permute-start | bytes 393224 | tf_op jit(solution)/shard_map/ppermute | solution.py:32
  22.2 8.2 %collective-permute-start.10 = (bf16[256,256]{1,0:T(8,128)(2,1)S(1)}, bf16[256,256]{1,0:T(8,128)(2,1)S(1)}, u32[]{:S(2)}, u32[]{:S(2)}) collective-permute-start(bf16[256,256]{1,0:T(8,128)(2,1)S(1)} %get-tuple-element.48), channel_id=1, source_target_pairs={{0,2},{2,0},{4,6},{6,4},{8,10},{10,8},{12,14},{14,12},{16,18},{18,... | collective-permute-start | bytes 393224 | tf_op jit(solution)/shard_map/ppermute | solution.py:32
  32.6 11.4 %collective-permute-start.11 = (bf16[4,256,128]{2,1,0:T(8,128)(2,1)S(1)}, bf16[4,256,128]{2,1,0:T(8,128)(2,1)S(1)}, u32[]{:S(2)}, u32[]{:S(2)}) collective-permute-start(bf16[4,256,128]{2,1,0:T(8,128)(2,1)S(1)} %get-tuple-element.52), channel_id=1, source_target_pairs={{8,0},{10,2},{12,4},{14,6},{16,8},{18,10},{20,12},{22,14},{24,16},... | collective-permute-start | bytes 786440 | tf_op jit(solution)/shard_map/ppermute | solution.py:27
  41.7 7.9 %collective-permute-start.15 = (bf16[4,256,128]{2,1,0:T(8,128)(2,1)S(1)}, bf16[4,256,128]{2,1,0:T(8,128)(2,1)S(1)}, u32[]{:S(2)}, u32[]{:S(2)}) collective-permute-start(bf16[4,256,128]{2,1,0:T(8,128)(2,1)S(1)} %get-tuple-element.59), channel_id=1, source_target_pairs={{8,0},{10,2},{12,4},{14,6},{16,8},{18,10},{20,12},{22,14},{24,16},... | collective-permute-start | bytes 786440 | tf_op jit(solution)/shard_map/ppermute | solution.py:27
  46.0 7.8 %collective-permute-start.12 = (bf16[256,384]{1,0:T(8,128)(2,1)S(1)}, bf16[256,384]{1,0:T(8,128)(2,1)S(1)}, u32[]{:S(2)}, u32[]{:S(2)}) collective-permute-start(bf16[256,384]{1,0:T(8,128)(2,1)S(1)} %get-tuple-element.54), channel_id=1, source_target_pairs={{0,2},{2,0},{4,6},{6,4},{8,10},{10,8},{12,14},{14,12},{16,18},{18,... | collective-permute-start | bytes 589832 | tf_op jit(solution)/shard_map/ppermute | solution.py:32
  47.0 8.1 %collective-permute-start.13 = (bf16[256,384]{1,0:T(8,128)(2,1)S(1)}, bf16[256,384]{1,0:T(8,128)(2,1)S(1)}, u32[]{:S(2)}, u32[]{:S(2)}) collective-permute-start(bf16[256,384]{1,0:T(8,128)(2,1)S(1)} %get-tuple-element.55), channel_id=1, source_target_pairs={{0,4},{2,6},{4,0},{6,2},{8,12},{10,14},{12,8},{14,10},{16,20},{18,... | collective-permute-start | bytes 589832 | tf_op jit(solution)/shard_map/ppermute | solution.py:32
  48.1 8.8 %collective-permute-start.14 = (bf16[256,384]{1,0:T(8,128)(2,1)S(1)}, bf16[256,384]{1,0:T(8,128)(2,1)S(1)}, u32[]{:S(2)}, u32[]{:S(2)}) collective-permute-start(bf16[256,384]{1,0:T(8,128)(2,1)S(1)} %get-tuple-element.56), channel_id=1, source_target_pairs={{0,6},{2,4},{4,2},{6,0},{8,14},{10,12},{12,10},{14,8},{16,22},{18,... | collective-permute-start | bytes 589832 | tf_op jit(solution)/shard_map/ppermute | solution.py:32
  49.6 8.2 %collective-permute-start.16 = (bf16[256,128]{1,0:T(8,128)(2,1)S(1)}, bf16[256,128]{1,0:T(8,128)(2,1)S(1)}, u32[]{:S(2)}, u32[]{:S(2)}) collective-permute-start(bf16[256,128]{1,0:T(8,128)(2,1)S(1)} %get-tuple-element.61), channel_id=1, source_target_pairs={{0,6},{2,4},{4,2},{6,0},{8,14},{10,12},{12,10},{14,8},{16,22},{18,... | collective-permute-start | bytes 196616 | tf_op jit(solution)/shard_map/ppermute | solution.py:32
  51.2 7.1 %collective-permute-start.17 = (bf16[256,128]{1,0:T(8,128)(2,1)S(1)}, bf16[256,128]{1,0:T(8,128)(2,1)S(1)}, u32[]{:S(2)}, u32[]{:S(2)}) collective-permute-start(bf16[256,128]{1,0:T(8,128)(2,1)S(1)} %get-tuple-element.62), channel_id=1, source_target_pairs={{0,4},{2,6},{4,0},{6,2},{8,12},{10,14},{12,8},{14,10},{16,20},{18,... | collective-permute-start | bytes 196616 | tf_op jit(solution)/shard_map/ppermute | solution.py:32
  53.9 4.4 %collective-permute-start.18 = (bf16[256,128]{1,0:T(8,128)(2,1)S(1)}, bf16[256,128]{1,0:T(8,128)(2,1)S(1)}, u32[]{:S(2)}, u32[]{:S(2)}) collective-permute-start(bf16[256,128]{1,0:T(8,128)(2,1)S(1)} %get-tuple-element.63), channel_id=1, source_target_pairs={{0,2},{2,0},{4,6},{6,4},{8,10},{10,8},{12,14},{14,12},{16,18},{18,... | collective-permute-start | bytes 196616 | tf_op jit(solution)/shard_map/ppermute | solution.py:32

commit v12 on v11

--- a/solution.py
+++ b/solution.py
@@ -55,10 +55,6 @@
     return place, index - place
 
 
-def hop(group, r, near=False):
-    return r if near or r == 0 else group - r
-
-
 def lanes(index, width):
     return pl.ds(pl.multiple_of(index * width, width), width)
 
@@ -75,7 +71,7 @@
 
     def body(k_ref, v_ref, before_ref, *refs):
         for r in range(group):
-            member = spot(group)[0] ^ hop(group, r)
+            member = spot(group)[0] ^ r
             refs[r][:, :width] = k_ref[:, lanes(member, width)]
             refs[r][:, width:] = v_ref[:, lanes(member, width)]
 
@@ -88,7 +84,7 @@
 
     def body(q_ref, before_ref, *out_refs):
         for r in range(group):
-            out_refs[r][...] = q_ref[:, lanes(spot(group)[0] ^ hop(group, r), width)]
+            out_refs[r][...] = q_ref[:, lanes(spot(group)[0] ^ r, width)]
 
     outs = [jax.ShapeDtypeStruct((tokens, width), jnp.bfloat16)] * group
     return call(body, outs, specs=[VMEM, ANY])(queries, before)
@@ -97,7 +93,7 @@
 def order_pieces(group, pieces, before):
     def body(*refs):
         for r in range(group):
-            refs[-1][spot(group)[0] ^ hop(group, r)] = refs[r][...]
+            refs[-1][spot(group)[0] ^ r] = refs[r][...]
 
     outs = [jax.ShapeDtypeStruct((group,) + pieces[0].shape, jnp.bfloat16)]
     return call(body, outs, specs=[VMEM] * group + [ANY])(*pieces, before)[0]
@@ -132,7 +128,7 @@
 
     def body(*refs):
         for r in range(group):
-            there = lanes(spot(group)[0] ^ hop(group, r), rows)
+            there = lanes(spot(group)[0] ^ r, rows)
             total = refs[0][there, :]
             if len(terms) > 1:
                 total = total.astype(jnp.float32)
@@ -167,7 +163,7 @@
             for r in range(z.group):
                 for j in range(z.per_head):
                     lower = (head * z.per_head + j) * HEAD_SIZE
-                    refs[z.group][head, spot(z.group)[0] ^ hop(z.group, r), :, j * z.tokens : (j + 1) * z.tokens] = refs[r][
+                    refs[z.group][head, spot(z.group)[0] ^ r, :, j * z.tokens : (j + 1) * z.tokens] = refs[r][
                         :, lower : lower + HEAD_SIZE
                     ].T
 
@@ -241,7 +237,7 @@
             for r in range(z.group):
                 for j in range(z.per_head):
                     lower = (head * z.per_head + j) * HEAD_SIZE
-                    g_ref[head, place ^ hop(z.group, r), :, j * z.tokens : (j + 1) * z.tokens] = g_refs[r][
+                    g_ref[head, place ^ r, :, j * z.tokens : (j + 1) * z.tokens] = g_refs[r][
                         lower : lower + HEAD_SIZE, :
                     ]
             dv_all[...] = jnp.zeros_like(dv_all)
@@ -341,7 +337,7 @@
                     )
 
         for r in range(z.group):
-            member = spot(z.group)[0] ^ hop(z.group, r, near=True)
+            member = spot(z.group)[0] ^ r
             dv = term_refs[0][member]
             for term in term_refs[1:]:
                 dv = dv + term[member].astype(jnp.float32)
@@ -364,7 +360,7 @@
 
     def body(*refs):
         for r in range(group):
-            member = spot(group)[0] ^ hop(group, r)
+            member = spot(group)[0] ^ r
             number = 0
             for column, terms in enumerate(sums):
                 total = refs[number][member].astype(jnp.float32)
@@ -377,7 +373,7 @@
     return call(body, outs)(*flat)
 
 
-def unpack(group, pieces, widths, before=(), near=False):
+def unpack(group, pieces, widths, before=()):
     tokens = pieces[0].shape[0]
 
     def body(*refs):
@@ -385,7 +381,7 @@
         for r in range(group):
             lower = 0
             for number, width in enumerate(widths):
-                there = lanes(spot(group)[0] ^ hop(group, r, near), width)
+                there = lanes(spot(group)[0] ^ r, width)
                 out_refs[number][:, there] = refs[r][:, lower : lower + width]
                 lower += width
         out_refs[-1][...] = jnp.zeros_like(out_refs[-1])
@@ -411,8 +407,8 @@
     kv_width = heads * HEAD_SIZE
     back_groups = WINDOW_LENGTH // (group * tokens)
 
-    def trade(sent, near=False):
-        return [sent[0]] + [swapped(sent[r], "ctx", hop(group, r, near)) for r in range(1, group)]
+    def trade(sent):
+        return [sent[0]] + [swapped(sent[r], "ctx", r) for r in range(1, group)]
 
     def returned(earlier):
         return [
@@ -440,8 +436,8 @@
     dv_terms = [dv_own] + returned(dv_earlier)
     ds, dk_own, dk_earlier = key_terms(z, e, inverse, qt, g, kv_own, kv_earlier)
     dk_terms = [dk_own] + returned(dk_earlier)
-    pieces = trade(query_terms(z, ds, inverse, kv_own, kv_earlier, dv_terms), near=True)
-    query_grads, value_gradients, done = unpack(group, pieces, [z.width, kv_width], near=True)
+    pieces = trade(query_terms(z, ds, inverse, kv_own, kv_earlier, dv_terms))
+    query_grads, value_gradients, done = unpack(group, pieces, [z.width, kv_width])
     key_gradients, _ = unpack(group, trade(pack_terms(group, [dk_terms])), [kv_width], [done])
     return (query_grads, key_gradients, value_gradients)
 

time: 59.3 us -> 57.7 us (0.973)
  starting transfers between devices: 26.2 us -> 25.2 us
  waiting for transfers between devices: 11.3 us -> 10.6 us
    ppermute x3, starting transfers between devices: 7.36 us -> 6.02 us  [shifted(): lax.ppermute(value, axis, [(source, source + steps) for source in range(l...]
  transfers between devices with their start and end apart: 19 -> 19, of which waited for: 9 -> 5; matrix products, arithmetic and copies ran while one was open for 0% -> 0% of each run, Pallas kernels for 28% -> 29%
where the time goes in v12:
time: 57.7 us; the launch traced here: 57.3 us
  starting transfers between devices  25.2 us (44%)
  Pallas kernels  19.4 us (34%)
  waiting for transfers between devices  10.6 us (18%)
  local copies, waits for them, and re-layouts  1.28 us (2%)
  between operations  0.85 us (1%)
    pallas_call x15, Pallas kernels, run(): pl.pallas_call(body, out_shape=tuple(outs), in_specs=specs or [SMEM if a....  19.4 us
    ppermute x16, starting transfers between devices, swapped(): lax.ppermute(value, axis, [(source, source ^ bits) for source in range(co...  19.1 us
    ppermute x16, waiting for transfers between devices, swapped(): lax.ppermute(value, axis, [(source, source ^ bits) for source in range(co...  8.23 us
    ppermute x3, starting transfers between devices, shifted(): lax.ppermute(value, axis, [(source, source + steps) for source in range(l...  6.02 us
    ppermute x3, waiting for transfers between devices, shifted(): lax.ppermute(value, axis, [(source, source + steps) for source in range(l...  2.33 us
    unnamed x14, local copies, waits for them, and re-layouts  1.28 us
  transfers between devices with their start and end apart: 19, of which 5 were waited for; matrix products, arithmetic and copies ran while one was open for 0% of the time, Pallas kernels for 29%

profile of v12, /device:TPU:24, one launch (start us, length us, event | category | flops | bytes accessed | tf_op | source)
XLA Modules:
  0.0 57.3 jit_solution(11261447123185954176)
XLA Ops:
  0.7 0.9 %copy-done.3 = bf16[256,512]{1,0:T(8,128)(2,1)S(1)} copy-done((bf16[256,512]{1,0:T(8,128)(2,1)S(1)}, bf16[256,512]{1,0:T(8,128)(2,1)}, u32[]{:S(2)}) %copy-start.3) | copy-done | bytes 262168
  1.8 1.6 %collective-permute-start = (bf16[256,256]{1,0:T(8,128)(2,1)S(1)}, bf16[256,256]{1,0:T(8,128)(2,1)S(1)}, u32[]{:S(2)}, u32[]{:S(2)}) collective-permute-start(bf16[256,256]{1,0:T(8,128)(2,1)S(1)} %get-tuple-element.36), channel_id=1, source_target_pairs={{0,2},{2,0},{4,6},{6,4},{8,10},{10,8},{12,14},{14,12},{16,18},{18,... | collective-permute-start | bytes 393224 | tf_op jit(solution)/shard_map/ppermute | solution.py:32
  3.3 1.5 %collective-permute-start.1 = (bf16[256,256]{1,0:T(8,128)(2,1)S(1)}, bf16[256,256]{1,0:T(8,128)(2,1)S(1)}, u32[]{:S(2)}, u32[]{:S(2)}) collective-permute-start(bf16[256,256]{1,0:T(8,128)(2,1)S(1)} %get-tuple-element.37), channel_id=1, source_target_pairs={{0,4},{2,6},{4,0},{6,2},{8,12},{10,14},{12,8},{14,10},{16,20},{18,... | collective-permute-start | bytes 393224 | tf_op jit(solution)/shard_map/ppermute | solution.py:32
  4.8 0.5 collective-permute-start.2
  5.7 1.9 %shard_map.79.refs_4_.refs_1_ = bf16[1024,256]{1,0:T(8,128)(2,1)S(1)} custom-call(bf16[2048,2688]{1,0:T(8,128)(2,1)S(1)} %bitcast.1, bf16[256,2688]{1,0:T(8,128)(2,1)S(1)} %copy-done, bf16[256,256]{1,0:T(8,128)(2,1)S(1)} %get-tuple-element.39.refs_0_), custom_call_target="tpu_custom_call" | custom-call | flops 1409286144 | bytes 13041664 | tf_op jit(solution)/shard_map/pallas_call | solution.py:39
  7.7 3.4 %collective-permute-done.1.refs_2_ = bf16[256,256]{1,0:T(8,128)(2,1)S(1)} collective-permute-done((bf16[256,256]{1,0:T(8,128)(2,1)S(1)}, bf16[256,256]{1,0:T(8,128)(2,1)S(1)}, u32[]{:S(2)}, u32[]{:S(2)}) %collective-permute-start.1) | collective-permute-done | bytes 131104 | tf_op jit(solution)/shard_map/ppermute | solution.py:32
  11.2 1.3 %collective-permute-start.3 = (bf16[4,256,256]{2,1,0:T(8,128)(2,1)S(1)}, bf16[4,256,256]{2,1,0:T(8,128)(2,1)S(1)}, u32[]{:S(2)}, u32[]{:S(2)}) collective-permute-start(bf16[4,256,256]{2,1,0:T(8,128)(2,1)S(1)} %shard_map.80.refs_0_.refs_2_.own_ref), channel_id=1, source_target_pairs={{0,8},{2,10},{4,12},{6,14},{8,16},{10,18},{12,20},{14,22},{16,24},... | collective-permute-start | bytes 1572872 | tf_op jit(solution)/shard_map/ppermute | solution.py:27
  12.5 1.3 %collective-permute-start.4 = (bf16[256,256]{1,0:T(8,128)(2,1)S(1)}, bf16[256,256]{1,0:T(8,128)(2,1)S(1)}, u32[]{:S(2)}, u32[]{:S(2)}) collective-permute-start(bf16[256,256]{1,0:T(8,128)(2,1)S(1)} %get-tuple-element.40), channel_id=1, source_target_pairs={{0,2},{2,0},{4,6},{6,4},{8,10},{10,8},{12,14},{14,12},{16,18},{18,... | collective-permute-start | bytes 393224 | tf_op jit(solution)/shard_map/ppermute | solution.py:32
  13.7 0.8 %collective-permute-start.5 = (bf16[256,256]{1,0:T(8,128)(2,1)S(1)}, bf16[256,256]{1,0:T(8,128)(2,1)S(1)}, u32[]{:S(2)}, u32[]{:S(2)}) collective-permute-start(bf16[256,256]{1,0:T(8,128)(2,1)S(1)} %get-tuple-element.41), channel_id=1, source_target_pairs={{0,4},{2,6},{4,0},{6,2},{8,12},{10,14},{12,8},{14,10},{16,20},{18,... | collective-permute-start | bytes 393224 | tf_op jit(solution)/shard_map/ppermute | solution.py:32
  14.6 1.4 %collective-permute-start.6 = (bf16[256,256]{1,0:T(8,128)(2,1)S(1)}, bf16[256,256]{1,0:T(8,128)(2,1)S(1)}, u32[]{:S(2)}, u32[]{:S(2)}) collective-permute-start(bf16[256,256]{1,0:T(8,128)(2,1)S(1)} %get-tuple-element.42), channel_id=1, source_target_pairs={{0,6},{2,4},{4,2},{6,0},{8,14},{10,12},{12,10},{14,8},{16,22},{18,... | collective-permute-start | bytes 393224 | tf_op jit(solution)/shard_map/ppermute | solution.py:32
  16.0 1.9 %shard_map.83.refs_0_ = bf16[1024,256]{1,0:T(8,128)(2,1)S(1)} custom-call(bf16[2048,2688]{1,0:T(8,128)(2,1)S(1)} %bitcast.1, bf16[256,2688]{1,0:T(8,128)(2,1)S(1)} %copy-done, bf16[4,256,256]{2,1,0:T(8,128)(2,1)S(1)} %shard_map.80.refs_0_.refs_2_.own_ref, bf16[1024,256]{1,0:T(8,128)(2,1)S(1)} %shard_map.79.refs_4_.refs_1_), custom_call_target="tpu_custom_call" | custom-call | flops 1409286144 | bytes 13959168 | tf_op jit(solution)/shard_map/pallas_call | solution.py:39
  18.1 1.3 %collective-permute-start.8 = (bf16[256,256]{1,0:T(8,128)(2,1)S(1)}, bf16[256,256]{1,0:T(8,128)(2,1)S(1)}, u32[]{:S(2)}, u32[]{:S(2)}) collective-permute-start(bf16[256,256]{1,0:T(8,128)(2,1)S(1)} %get-tuple-element.46), channel_id=1, source_target_pairs={{0,2},{2,0},{4,6},{6,4},{8,10},{10,8},{12,14},{14,12},{16,18},{18,... | collective-permute-start | bytes 393224 | tf_op jit(solution)/shard_map/ppermute | solution.py:32
  19.3 0.8 %collective-permute-start.9 = (bf16[256,256]{1,0:T(8,128)(2,1)S(1)}, bf16[256,256]{1,0:T(8,128)(2,1)S(1)}, u32[]{:S(2)}, u32[]{:S(2)}) collective-permute-start(bf16[256,256]{1,0:T(8,128)(2,1)S(1)} %get-tuple-element.47), channel_id=1, source_target_pairs={{0,4},{2,6},{4,0},{6,2},{8,12},{10,14},{12,8},{14,10},{16,20},{18,... | collective-permute-start | bytes 393224 | tf_op jit(solution)/shard_map/ppermute | solution.py:32
  20.2 2.7 %collective-permute-start.10 = (bf16[256,256]{1,0:T(8,128)(2,1)S(1)}, bf16[256,256]{1,0:T(8,128)(2,1)S(1)}, u32[]{:S(2)}, u32[]{:S(2)}) collective-permute-start(bf16[256,256]{1,0:T(8,128)(2,1)S(1)} %get-tuple-element.48), channel_id=1, source_target_pairs={{0,6},{2,4},{4,2},{6,0},{8,14},{10,12},{12,10},{14,8},{16,22},{18,... | collective-permute-start | bytes 393224 | tf_op jit(solution)/shard_map/ppermute | solution.py:32
  23.1 2.3 %collective-permute-done.3.refs_1_.refs_0_ = bf16[4,256,256]{2,1,0:T(8,128)(2,1)S(1)} collective-permute-done((bf16[4,256,256]{2,1,0:T(8,128)(2,1)S(1)}, bf16[4,256,256]{2,1,0:T(8,128)(2,1)S(1)}, u32[]{:S(2)}, u32[]{:S(2)}) %collective-permute-start.3) | collective-permute-done | bytes 524320 | tf_op jit(solution)/shard_map/ppermute | solution.py:27
  25.4 3.8 %shard_map.82 = (bf16[1,4,5,256,512]{4,3,2,1,0:T(8,128)(2,1)S(1)}, f32[1,4,1,512]{3,2,1,0:T(1,128)S(1)}) custom-call(bf16[4,256,256]{2,1,0:T(8,128)(2,1)S(1)} %shard_map.80.refs_0_.refs_2_.own_ref, bf16[4,256,256]{2,1,0:T(8,128)(2,1)S(1)} %collective-permute-done.3.refs_1_.refs_0_, bf16[1,4,128,512]{3,2,1,0:T(8,128)(2,1)S(1)} %shard_map.81.refs_2_.qt_ref), custom_call_target="tpu_custom_call" | custom-call | flops 671088640 | bytes 6823936 | tf_op jit(solution)/shard_map/pallas_call | solution.py:39
  29.2 2.2 %shard_map.85 = (bf16[1,4,128,512]{3,2,1,0:T(8,128)(2,1)S(1)}, f32[4,256,128]{2,1,0:T(8,128)S(1)}, bf16[4,256,128]{2,1,0:T(8,128)(2,1)S(1)}) custom-call(bf16[1,4,5,256,512]{4,3,2,1,0:T(8,128)(2,1)S(1)} %get-tuple-element.43.e_ref, f32[1,4,1,512]{3,2,1,0:T(1,128)S(1)} %get-tuple-element.44.inverse_ref, bf16[256,256]{1,0:T(8,128)(2,1)S(1)} %get-tuple-element.45.refs_0_, ...), custom_call_target="tpu_custom_call" | custom-call | flops 671088640 | bytes 7086080 | tf_op jit(solution)/shard_map/pallas_call | solution.py:39
  31.5 2.4 %collective-permute-start.11 = (bf16[4,256,128]{2,1,0:T(8,128)(2,1)S(1)}, bf16[4,256,128]{2,1,0:T(8,128)(2,1)S(1)}, u32[]{:S(2)}, u32[]{:S(2)}) collective-permute-start(bf16[4,256,128]{2,1,0:T(8,128)(2,1)S(1)} %get-tuple-element.52), channel_id=1, source_target_pairs={{8,0},{10,2},{12,4},{14,6},{16,8},{18,10},{20,12},{22,14},{24,16},... | collective-permute-start | bytes 786440 | tf_op jit(solution)/shard_map/ppermute | solution.py:27
  33.8 5.4 %shard_map.86 = (bf16[1,4,5,256,512]{4,3,2,1,0:T(8,128)(2,1)S(1)}, f32[4,256,128]{2,1,0:T(8,128)S(1)}, bf16[4,256,128]{2,1,0:T(8,128)(2,1)S(1)}) custom-call(bf16[1,4,5,256,512]{4,3,2,1,0:T(8,128)(2,1)S(1)} %get-tuple-element.43.e_ref, f32[1,4,1,512]{3,2,1,0:T(1,128)S(1)} %get-tuple-element.44.inverse_ref, ...), custom_call_target="tpu_custom_call" | custom-call | flops 1342177280 | bytes 13377536 | tf_op jit(solution)/shard_map/pallas_call | solution.py:39
  39.2 2.4 %collective-permute-start.15 = (bf16[4,256,128]{2,1,0:T(8,128)(2,1)S(1)}, bf16[4,256,128]{2,1,0:T(8,128)(2,1)S(1)}, u32[]{:S(2)}, u32[]{:S(2)}) collective-permute-start(bf16[4,256,128]{2,1,0:T(8,128)(2,1)S(1)} %get-tuple-element.59), channel_id=1, source_target_pairs={{8,0},{10,2},{12,4},{14,6},{16,8},{18,10},{20,12},{22,14},{24,16},... | collective-permute-start | bytes 786440 | tf_op jit(solution)/shard_map/ppermute | solution.py:27
  41.6 2.0 %shard_map.87 = (bf16[256,384]{1,0:T(8,128)(2,1)S(1)}, bf16[256,384]{1,0:T(8,128)(2,1)S(1)}, bf16[256,384]{1,0:T(8,128)(2,1)S(1)}, bf16[256,384]{1,0:T(8,128)(2,1)S(1)}) custom-call(bf16[1,4,5,256,512]{4,3,2,1,0:T(8,128)(2,1)S(1)} %get-tuple-element.50.ds_ref, f32[1,4,1,512]{3,2,1,0:T(1,128)S(1)} %get-tuple-element.44.inverse_ref, ...), custom_call_target="tpu_custom_call" | custom-call | flops 671088640 | bytes 7872512 | tf_op jit(solution)/shard_map/pallas_call | solution.py:39
  43.5 1.7 %collective-permute-start.12 = (bf16[256,384]{1,0:T(8,128)(2,1)S(1)}, bf16[256,384]{1,0:T(8,128)(2,1)S(1)}, u32[]{:S(2)}, u32[]{:S(2)}) collective-permute-start(bf16[256,384]{1,0:T(8,128)(2,1)S(1)} %get-tuple-element.54), channel_id=1, source_target_pairs={{0,2},{2,0},{4,6},{6,4},{8,10},{10,8},{12,14},{14,12},{16,18},{18,... | collective-permute-start | bytes 589832 | tf_op jit(solution)/shard_map/ppermute | solution.py:32
  45.2 0.5 collective-permute-start.13
  45.7 1.3 %collective-permute-start.14 = (bf16[256,384]{1,0:T(8,128)(2,1)S(1)}, bf16[256,384]{1,0:T(8,128)(2,1)S(1)}, u32[]{:S(2)}, u32[]{:S(2)}) collective-permute-start(bf16[256,384]{1,0:T(8,128)(2,1)S(1)} %get-tuple-element.56), channel_id=1, source_target_pairs={{0,6},{2,4},{4,2},{6,0},{8,14},{10,12},{12,10},{14,8},{16,22},{18,... | collective-permute-start | bytes 589832 | tf_op jit(solution)/shard_map/ppermute | solution.py:32
  47.1 1.7 %collective-permute-start.16 = (bf16[256,128]{1,0:T(8,128)(2,1)S(1)}, bf16[256,128]{1,0:T(8,128)(2,1)S(1)}, u32[]{:S(2)}, u32[]{:S(2)}) collective-permute-start(bf16[256,128]{1,0:T(8,128)(2,1)S(1)} %get-tuple-element.61), channel_id=1, source_target_pairs={{0,2},{2,0},{4,6},{6,4},{8,10},{10,8},{12,14},{14,12},{16,18},{18,... | collective-permute-start | bytes 196616 | tf_op jit(solution)/shard_map/ppermute | solution.py:32
  48.9 0.5 collective-permute-start.17
  49.4 2.0 %collective-permute-done.12.refs_1_ = bf16[256,384]{1,0:T(8,128)(2,1)S(1)} collective-permute-done((bf16[256,384]{1,0:T(8,128)(2,1)S(1)}, bf16[256,384]{1,0:T(8,128)(2,1)S(1)}, u32[]{:S(2)}, u32[]{:S(2)}) %collective-permute-start.12) | collective-permute-done | bytes 196640 | tf_op jit(solution)/shard_map/ppermute | solution.py:32
  51.4 1.4 %collective-permute-start.18 = (bf16[256,128]{1,0:T(8,128)(2,1)S(1)}, bf16[256,128]{1,0:T(8,128)(2,1)S(1)}, u32[]{:S(2)}, u32[]{:S(2)}) collective-permute-start(bf16[256,128]{1,0:T(8,128)(2,1)S(1)} %get-tuple-element.63), channel_id=1, source_target_pairs={{0,6},{2,4},{4,2},{6,0},{8,14},{10,12},{12,10},{14,8},{16,22},{18,... | collective-permute-start | bytes 196616 | tf_op jit(solution)/shard_map/ppermute | solution.py:32
  52.7 2.2 %collective-permute-done.13.refs_2_ = bf16[256,384]{1,0:T(8,128)(2,1)S(1)} collective-permute-done((bf16[256,384]{1,0:T(8,128)(2,1)S(1)}, bf16[256,384]{1,0:T(8,128)(2,1)S(1)}, u32[]{:S(2)}, u32[]{:S(2)}) %collective-permute-start.13) | collective-permute-done | bytes 196640 | tf_op jit(solution)/shard_map/ppermute | solution.py:32
  54.9 1.0 %shard_map.88 = (bf16[256,1024]{1,0:T(8,128)(2,1)}, bf16[256,512]{1,0:T(8,128)(2,1)}, f32[8,128]{1,0:T(8,128)S(1)}) custom-call(bf16[256,384]{1,0:T(8,128)(2,1)S(1)} %get-tuple-element.53.refs_0_, bf16[256,384]{1,0:T(8,128)(2,1)S(1)} %collective-permute-done.12.refs_1_, bf16[256,384]{1,0:T(8,128)(2,1)S(1)} %collective-permute-done.13.refs_2_, ...), custom_call_target="tpu_custom_call" | custom-call | bytes 1576960 | tf_op jit(solution)/shard_map/pallas_call | solution.py:39
  55.9 0.6 %collective-permute-done.18.refs_3_ = bf16[256,128]{1,0:T(8,128)(2,1)S(1)} collective-permute-done((bf16[256,128]{1,0:T(8,128)(2,1)S(1)}, bf16[256,128]{1,0:T(8,128)(2,1)S(1)}, u32[]{:S(2)}, u32[]{:S(2)}) %collective-permute-start.18) | collective-permute-done | bytes 65568 | tf_op jit(solution)/shard_map/ppermute | solution.py:32
  56.5 0.8 %shard_map.90 = (bf16[256,512]{1,0:T(8,128)(2,1)}, f32[8,128]{1,0:T(8,128)}) custom-call(bf16[256,128]{1,0:T(8,128)(2,1)S(1)} %get-tuple-element.60.refs_0_, bf16[256,128]{1,0:T(8,128)(2,1)S(1)} %collective-permute-done.16.refs_1_, bf16[256,128]{1,0:T(8,128)(2,1)S(1)} %collective-permute-done.17.refs_2_, ...), custom_call_target="tpu_custom_call" | custom-call | bytes 532480 | tf_op jit(solution)/shard_map/pallas_call | solution.py:39
  (36 shorter events, 1.1 us)
Async XLA Ops:
  0.6 1.0 %copy-start.3 = (bf16[256,512]{1,0:T(8,128)(2,1)S(1)}, bf16[256,512]{1,0:T(8,128)(2,1)}, u32[]{:S(2)}) copy-start(bf16[256,512]{1,0:T(8,128)(2,1)} %v_ref.1) | copy-start | bytes 786436
  0.6 1.0 %copy-start.2 = (bf16[256,512]{1,0:T(8,128)(2,1)S(1)}, bf16[256,512]{1,0:T(8,128)(2,1)}, u32[]{:S(2)}) copy-start(bf16[256,512]{1,0:T(8,128)(2,1)} %k_ref.1) | copy-start | bytes 786436
  0.7 4.7 %slice-start = ((s8[11010048]{0:T(1024)(128)(4,1)}), s8[4194304]{0:T(1024)(128)(4,1)S(1)}, s32[]{:S(2)}) async-start(s8[11010048]{0:T(1024)(128)(4,1)} %bitcast), calls=%async_computation | async-start | bytes 8388608
  0.7 4.7 %slice-start.1 = ((s8[11010048]{0:T(1024)(128)(4,1)}), s8[4194304]{0:T(1024)(128)(4,1)S(1)}, s32[]{:S(2)}) async-start(s8[11010048]{0:T(1024)(128)(4,1)} %bitcast), calls=%async_computation.1 | async-start | bytes 8388608
  1.7 3.7 %copy-start.1 = (bf16[256,1024]{1,0:T(8,128)(2,1)S(1)}, bf16[256,1024]{1,0:T(8,128)(2,1)}, u32[]{:S(2)}) copy-start(bf16[256,1024]{1,0:T(8,128)(2,1)} %q_ref.1) | copy-start | bytes 1572868
  1.7 3.8 %slice-start.2 = ((s8[11010048]{0:T(1024)(128)(4,1)}), s8[2621440]{0:T(1024)(128)(4,1)S(1)}, s32[]{:S(2)}) async-start(s8[11010048]{0:T(1024)(128)(4,1)} %bitcast), calls=%async_computation.2 | async-start | bytes 5242880
  1.7 4.0 %copy-start = (bf16[256,2688]{1,0:T(8,128)(2,1)S(1)}, bf16[256,2688]{1,0:T(8,128)(2,1)}, u32[]{:S(2)}) copy-start(bf16[256,2688]{1,0:T(8,128)(2,1)} %c_ref.3) | copy-start | bytes 4128772
  1.8 5.9 %collective-permute-start = (bf16[256,256]{1,0:T(8,128)(2,1)S(1)}, bf16[256,256]{1,0:T(8,128)(2,1)S(1)}, u32[]{:S(2)}, u32[]{:S(2)}) collective-permute-start(bf16[256,256]{1,0:T(8,128)(2,1)S(1)} %get-tuple-element.36), channel_id=1, source_target_pairs={{0,2},{2,0},{4,6},{6,4},{8,10},{10,8},{12,14},{14,12},{16,18},{18,... | collective-permute-start | bytes 393224 | tf_op jit(solution)/shard_map/ppermute | solution.py:32
  3.3 7.8 %collective-permute-start.1 = (bf16[256,256]{1,0:T(8,128)(2,1)S(1)}, bf16[256,256]{1,0:T(8,128)(2,1)S(1)}, u32[]{:S(2)}, u32[]{:S(2)}) collective-permute-start(bf16[256,256]{1,0:T(8,128)(2,1)S(1)} %get-tuple-element.37), channel_id=1, source_target_pairs={{0,4},{2,6},{4,0},{6,2},{8,12},{10,14},{12,8},{14,10},{16,20},{18,... | collective-permute-start | bytes 393224 | tf_op jit(solution)/shard_map/ppermute | solution.py:32
  4.8 6.3 %collective-permute-start.2 = (bf16[256,256]{1,0:T(8,128)(2,1)S(1)}, bf16[256,256]{1,0:T(8,128)(2,1)S(1)}, u32[]{:S(2)}, u32[]{:S(2)}) collective-permute-start(bf16[256,256]{1,0:T(8,128)(2,1)S(1)} %get-tuple-element.38), channel_id=1, source_target_pairs={{0,6},{2,4},{4,2},{6,0},{8,14},{10,12},{12,10},{14,8},{16,22},{18,... | collective-permute-start | bytes 393224 | tf_op jit(solution)/shard_map/ppermute | solution.py:32
  7.6 10.3 %collective-permute-start.7 = (bf16[1024,256]{1,0:T(8,128)(2,1)S(1)}, bf16[1024,256]{1,0:T(8,128)(2,1)S(1)}, u32[]{:S(2)}, u32[]{:S(2)}) collective-permute-start(bf16[1024,256]{1,0:T(8,128)(2,1)S(1)} %shard_map.79.refs_4_.refs_1_), channel_id=1, source_target_pairs={{0,1},{1,0},{2,3},{3,2},{4,5},{5,4},{6,7},{7,6},{8,9},{9,8},{10,11... | collective-permute-start | bytes 1572872 | tf_op jit(solution)/shard_map/ppermute | solution.py:32
  11.2 14.3 %collective-permute-start.3 = (bf16[4,256,256]{2,1,0:T(8,128)(2,1)S(1)}, bf16[4,256,256]{2,1,0:T(8,128)(2,1)S(1)}, u32[]{:S(2)}, u32[]{:S(2)}) collective-permute-start(bf16[4,256,256]{2,1,0:T(8,128)(2,1)S(1)} %shard_map.80.refs_0_.refs_2_.own_ref), channel_id=1, source_target_pairs={{0,8},{2,10},{4,12},{6,14},{8,16},{10,18},{12,20},{14,22},{16,24},... | collective-permute-start | bytes 1572872 | tf_op jit(solution)/shard_map/ppermute | solution.py:27
  12.5 6.9 %collective-permute-start.4 = (bf16[256,256]{1,0:T(8,128)(2,1)S(1)}, bf16[256,256]{1,0:T(8,128)(2,1)S(1)}, u32[]{:S(2)}, u32[]{:S(2)}) collective-permute-start(bf16[256,256]{1,0:T(8,128)(2,1)S(1)} %get-tuple-element.40), channel_id=1, source_target_pairs={{0,2},{2,0},{4,6},{6,4},{8,10},{10,8},{12,14},{14,12},{16,18},{18,... | collective-permute-start | bytes 393224 | tf_op jit(solution)/shard_map/ppermute | solution.py:32
  13.7 6.4 %collective-permute-start.5 = (bf16[256,256]{1,0:T(8,128)(2,1)S(1)}, bf16[256,256]{1,0:T(8,128)(2,1)S(1)}, u32[]{:S(2)}, u32[]{:S(2)}) collective-permute-start(bf16[256,256]{1,0:T(8,128)(2,1)S(1)} %get-tuple-element.41), channel_id=1, source_target_pairs={{0,4},{2,6},{4,0},{6,2},{8,12},{10,14},{12,8},{14,10},{16,20},{18,... | collective-permute-start | bytes 393224 | tf_op jit(solution)/shard_map/ppermute | solution.py:32
  14.6 8.3 %collective-permute-start.6 = (bf16[256,256]{1,0:T(8,128)(2,1)S(1)}, bf16[256,256]{1,0:T(8,128)(2,1)S(1)}, u32[]{:S(2)}, u32[]{:S(2)}) collective-permute-start(bf16[256,256]{1,0:T(8,128)(2,1)S(1)} %get-tuple-element.42), channel_id=1, source_target_pairs={{0,6},{2,4},{4,2},{6,0},{8,14},{10,12},{12,10},{14,8},{16,22},{18,... | collective-permute-start | bytes 393224 | tf_op jit(solution)/shard_map/ppermute | solution.py:32
  18.1 11.2 %collective-permute-start.8 = (bf16[256,256]{1,0:T(8,128)(2,1)S(1)}, bf16[256,256]{1,0:T(8,128)(2,1)S(1)}, u32[]{:S(2)}, u32[]{:S(2)}) collective-permute-start(bf16[256,256]{1,0:T(8,128)(2,1)S(1)} %get-tuple-element.46), channel_id=1, source_target_pairs={{0,2},{2,0},{4,6},{6,4},{8,10},{10,8},{12,14},{14,12},{16,18},{18,... | collective-permute-start | bytes 393224 | tf_op jit(solution)/shard_map/ppermute | solution.py:32
  19.3 9.9 %collective-permute-start.9 = (bf16[256,256]{1,0:T(8,128)(2,1)S(1)}, bf16[256,256]{1,0:T(8,128)(2,1)S(1)}, u32[]{:S(2)}, u32[]{:S(2)}) collective-permute-start(bf16[256,256]{1,0:T(8,128)(2,1)S(1)} %get-tuple-element.47), channel_id=1, source_target_pairs={{0,4},{2,6},{4,0},{6,2},{8,12},{10,14},{12,8},{14,10},{16,20},{18,... | collective-permute-start | bytes 393224 | tf_op jit(solution)/shard_map/ppermute | solution.py:32
  20.2 9.1 %collective-permute-start.10 = (bf16[256,256]{1,0:T(8,128)(2,1)S(1)}, bf16[256,256]{1,0:T(8,128)(2,1)S(1)}, u32[]{:S(2)}, u32[]{:S(2)}) collective-permute-start(bf16[256,256]{1,0:T(8,128)(2,1)S(1)} %get-tuple-element.48), channel_id=1, source_target_pairs={{0,6},{2,4},{4,2},{6,0},{8,14},{10,12},{12,10},{14,8},{16,22},{18,... | collective-permute-start | bytes 393224 | tf_op jit(solution)/shard_map/ppermute | solution.py:32
  31.5 10.1 %collective-permute-start.11 = (bf16[4,256,128]{2,1,0:T(8,128)(2,1)S(1)}, bf16[4,256,128]{2,1,0:T(8,128)(2,1)S(1)}, u32[]{:S(2)}, u32[]{:S(2)}) collective-permute-start(bf16[4,256,128]{2,1,0:T(8,128)(2,1)S(1)} %get-tuple-element.52), channel_id=1, source_target_pairs={{8,0},{10,2},{12,4},{14,6},{16,8},{18,10},{20,12},{22,14},{24,16},... | collective-permute-start | bytes 786440 | tf_op jit(solution)/shard_map/ppermute | solution.py:27
  39.2 7.9 %collective-permute-start.15 = (bf16[4,256,128]{2,1,0:T(8,128)(2,1)S(1)}, bf16[4,256,128]{2,1,0:T(8,128)(2,1)S(1)}, u32[]{:S(2)}, u32[]{:S(2)}) collective-permute-start(bf16[4,256,128]{2,1,0:T(8,128)(2,1)S(1)} %get-tuple-element.59), channel_id=1, source_target_pairs={{8,0},{10,2},{12,4},{14,6},{16,8},{18,10},{20,12},{22,14},{24,16},... | collective-permute-start | bytes 786440 | tf_op jit(solution)/shard_map/ppermute | solution.py:27
  43.5 7.8 %collective-permute-start.12 = (bf16[256,384]{1,0:T(8,128)(2,1)S(1)}, bf16[256,384]{1,0:T(8,128)(2,1)S(1)}, u32[]{:S(2)}, u32[]{:S(2)}) collective-permute-start(bf16[256,384]{1,0:T(8,128)(2,1)S(1)} %get-tuple-element.54), channel_id=1, source_target_pairs={{0,2},{2,0},{4,6},{6,4},{8,10},{10,8},{12,14},{14,12},{16,18},{18,... | collective-permute-start | bytes 589832 | tf_op jit(solution)/shard_map/ppermute | solution.py:32
  45.2 9.6 %collective-permute-start.13 = (bf16[256,384]{1,0:T(8,128)(2,1)S(1)}, bf16[256,384]{1,0:T(8,128)(2,1)S(1)}, u32[]{:S(2)}, u32[]{:S(2)}) collective-permute-start(bf16[256,384]{1,0:T(8,128)(2,1)S(1)} %get-tuple-element.55), channel_id=1, source_target_pairs={{0,4},{2,6},{4,0},{6,2},{8,12},{10,14},{12,8},{14,10},{16,20},{18,... | collective-permute-start | bytes 589832 | tf_op jit(solution)/shard_map/ppermute | solution.py:32
  45.7 9.1 %collective-permute-start.14 = (bf16[256,384]{1,0:T(8,128)(2,1)S(1)}, bf16[256,384]{1,0:T(8,128)(2,1)S(1)}, u32[]{:S(2)}, u32[]{:S(2)}) collective-permute-start(bf16[256,384]{1,0:T(8,128)(2,1)S(1)} %get-tuple-element.56), channel_id=1, source_target_pairs={{0,6},{2,4},{4,2},{6,0},{8,14},{10,12},{12,10},{14,8},{16,22},{18,... | collective-permute-start | bytes 589832 | tf_op jit(solution)/shard_map/ppermute | solution.py:32
  47.1 8.7 %collective-permute-start.16 = (bf16[256,128]{1,0:T(8,128)(2,1)S(1)}, bf16[256,128]{1,0:T(8,128)(2,1)S(1)}, u32[]{:S(2)}, u32[]{:S(2)}) collective-permute-start(bf16[256,128]{1,0:T(8,128)(2,1)S(1)} %get-tuple-element.61), channel_id=1, source_target_pairs={{0,2},{2,0},{4,6},{6,4},{8,10},{10,8},{12,14},{14,12},{16,18},{18,... | collective-permute-start | bytes 196616 | tf_op jit(solution)/shard_map/ppermute | solution.py:32
  48.9 7.0 %collective-permute-start.17 = (bf16[256,128]{1,0:T(8,128)(2,1)S(1)}, bf16[256,128]{1,0:T(8,128)(2,1)S(1)}, u32[]{:S(2)}, u32[]{:S(2)}) collective-permute-start(bf16[256,128]{1,0:T(8,128)(2,1)S(1)} %get-tuple-element.62), channel_id=1, source_target_pairs={{0,4},{2,6},{4,0},{6,2},{8,12},{10,14},{12,8},{14,10},{16,20},{18,... | collective-permute-start | bytes 196616 | tf_op jit(solution)/shard_map/ppermute | solution.py:32
  51.4 5.2 %collective-permute-start.18 = (bf16[256,128]{1,0:T(8,128)(2,1)S(1)}, bf16[256,128]{1,0:T(8,128)(2,1)S(1)}, u32[]{:S(2)}, u32[]{:S(2)}) collective-permute-start(bf16[256,128]{1,0:T(8,128)(2,1)S(1)} %get-tuple-element.63), channel_id=1, source_target_pairs={{0,6},{2,4},{4,2},{6,0},{8,14},{10,12},{12,10},{14,8},{16,22},{18,... | collective-permute-start | bytes 196616 | tf_op jit(solution)/shard_map/ppermute | solution.py:32

commit v13 on v11

--- a/solution.py
+++ b/solution.py
@@ -55,8 +55,11 @@
     return place, index - place
 
 
-def hop(group, r, near=False):
-    return r if near or r == 0 else group - r
+def hop(group, r):
+    turned, bit = 0, 1
+    while bit < group:
+        turned, r, bit = 2 * turned + r % 2, r // 2, 2 * bit
+    return turned
 
 
 def lanes(index, width):
@@ -341,7 +344,7 @@
                     )
 
         for r in range(z.group):
-            member = spot(z.group)[0] ^ hop(z.group, r, near=True)
+            member = spot(z.group)[0] ^ hop(z.group, r)
             dv = term_refs[0][member]
             for term in term_refs[1:]:
                 dv = dv + term[member].astype(jnp.float32)
@@ -377,7 +380,7 @@
     return call(body, outs)(*flat)
 
 
-def unpack(group, pieces, widths, before=(), near=False):
+def unpack(group, pieces, widths, before=()):
     tokens = pieces[0].shape[0]
 
     def body(*refs):
@@ -385,7 +388,7 @@
         for r in range(group):
             lower = 0
             for number, width in enumerate(widths):
-                there = lanes(spot(group)[0] ^ hop(group, r, near), width)
+                there = lanes(spot(group)[0] ^ hop(group, r), width)
                 out_refs[number][:, there] = refs[r][:, lower : lower + width]
                 lower += width
         out_refs[-1][...] = jnp.zeros_like(out_refs[-1])
@@ -411,8 +414,8 @@
     kv_width = heads * HEAD_SIZE
     back_groups = WINDOW_LENGTH // (group * tokens)
 
-    def trade(sent, near=False):
-        return [sent[0]] + [swapped(sent[r], "ctx", hop(group, r, near)) for r in range(1, group)]
+    def trade(sent):
+        return [sent[0]] + [swapped(sent[r], "ctx", hop(group, r)) for r in range(1, group)]
 
     def returned(earlier):
         return [
@@ -440,8 +443,8 @@
     dv_terms = [dv_own] + returned(dv_earlier)
     ds, dk_own, dk_earlier = key_terms(z, e, inverse, qt, g, kv_own, kv_earlier)
     dk_terms = [dk_own] + returned(dk_earlier)
-    pieces = trade(query_terms(z, ds, inverse, kv_own, kv_earlier, dv_terms), near=True)
-    query_grads, value_gradients, done = unpack(group, pieces, [z.width, kv_width], near=True)
+    pieces = trade(query_terms(z, ds, inverse, kv_own, kv_earlier, dv_terms))
+    query_grads, value_gradients, done = unpack(group, pieces, [z.width, kv_width])
     key_gradients, _ = unpack(group, trade(pack_terms(group, [dk_terms])), [kv_width], [done])
     return (query_grads, key_gradients, value_gradients)
 

time: 59.3 us -> 58.6 us (0.988)
    ppermute x3, starting transfers between devices: 7.36 us -> 6.02 us  [shifted(): lax.ppermute(value, axis, [(source, source + steps) for source in range(l...]
    ppermute x16, starting transfers between devices: 18.8 us -> 19.7 us  [swapped(): lax.ppermute(value, axis, [(source, source ^ bits) for source in range(co...]
  transfers between devices with their start and end apart: 19 -> 19, of which waited for: 9 -> 6; matrix products, arithmetic and copies ran while one was open for 0% -> 0% of each run, Pallas kernels for 28% -> 28%
where the time goes in v13:
time: 58.6 us; the launch traced here: 58.1 us
  starting transfers between devices  25.7 us (44%)
  Pallas kernels  19.4 us (33%)
  waiting for transfers between devices  10.8 us (18%)
  local copies, waits for them, and re-layouts  1.28 us (2%)
  between operations  0.85 us (1%)
    ppermute x16, starting transfers between devices, swapped(): lax.ppermute(value, axis, [(source, source ^ bits) for source in range(co...  19.7 us
    pallas_call x15, Pallas kernels, run(): pl.pallas_call(body, out_shape=tuple(outs), in_specs=specs or [SMEM if a....  19.4 us
    ppermute x16, waiting for transfers between devices, swapped(): lax.ppermute(value, axis, [(source, source ^ bits) for source in range(co...  8.34 us
    ppermute x3, starting transfers between devices, shifted(): lax.ppermute(value, axis, [(source, source + steps) for source in range(l...  6.02 us
    ppermute x3, waiting for transfers between devices, shifted(): lax.ppermute(value, axis, [(source, source + steps) for source in range(l...  2.51 us
    unnamed x14, local copies, waits for them, and re-layouts  1.28 us
  transfers between devices with their start and end apart: 19, of which 6 were waited for; matrix products, arithmetic and copies ran while one was open for 0% of the time, Pallas kernels for 28%

profile of v13, /device:TPU:24, one launch (start us, length us, event | category | flops | bytes accessed | tf_op | source)
XLA Modules:
  0.0 58.1 jit_solution(5564778195580156931)
XLA Ops:
  0.7 0.9 %copy-done.3 = bf16[256,512]{1,0:T(8,128)(2,1)S(1)} copy-done((bf16[256,512]{1,0:T(8,128)(2,1)S(1)}, bf16[256,512]{1,0:T(8,128)(2,1)}, u32[]{:S(2)}) %copy-start.3) | copy-done | bytes 262168
  1.8 1.6 %collective-permute-start = (bf16[256,256]{1,0:T(8,128)(2,1)S(1)}, bf16[256,256]{1,0:T(8,128)(2,1)S(1)}, u32[]{:S(2)}, u32[]{:S(2)}) collective-permute-start(bf16[256,256]{1,0:T(8,128)(2,1)S(1)} %get-tuple-element.36), channel_id=1, source_target_pairs={{0,4},{2,6},{4,0},{6,2},{8,12},{10,14},{12,8},{14,10},{16,20},{18,... | collective-permute-start | bytes 393224 | tf_op jit(solution)/shard_map/ppermute | solution.py:32
  3.3 1.5 %collective-permute-start.1 = (bf16[256,256]{1,0:T(8,128)(2,1)S(1)}, bf16[256,256]{1,0:T(8,128)(2,1)S(1)}, u32[]{:S(2)}, u32[]{:S(2)}) collective-permute-start(bf16[256,256]{1,0:T(8,128)(2,1)S(1)} %get-tuple-element.37), channel_id=1, source_target_pairs={{0,2},{2,0},{4,6},{6,4},{8,10},{10,8},{12,14},{14,12},{16,18},{18,... | collective-permute-start | bytes 393224 | tf_op jit(solution)/shard_map/ppermute | solution.py:32
  5.7 1.9 %shard_map.79.refs_4_.refs_1_ = bf16[1024,256]{1,0:T(8,128)(2,1)S(1)} custom-call(bf16[2048,2688]{1,0:T(8,128)(2,1)S(1)} %bitcast.1, bf16[256,2688]{1,0:T(8,128)(2,1)S(1)} %copy-done, bf16[256,256]{1,0:T(8,128)(2,1)S(1)} %get-tuple-element.39.refs_0_), custom_call_target="tpu_custom_call" | custom-call | flops 1409286144 | bytes 13041664 | tf_op jit(solution)/shard_map/pallas_call | solution.py:39
  7.7 2.0 %collective-permute-done.1.refs_2_ = bf16[256,256]{1,0:T(8,128)(2,1)S(1)} collective-permute-done((bf16[256,256]{1,0:T(8,128)(2,1)S(1)}, bf16[256,256]{1,0:T(8,128)(2,1)S(1)}, u32[]{:S(2)}, u32[]{:S(2)}) %collective-permute-start.1) | collective-permute-done | bytes 131104 | tf_op jit(solution)/shard_map/ppermute | solution.py:32
  9.7 1.4 %collective-permute-done.2.refs_3_ = bf16[256,256]{1,0:T(8,128)(2,1)S(1)} collective-permute-done((bf16[256,256]{1,0:T(8,128)(2,1)S(1)}, bf16[256,256]{1,0:T(8,128)(2,1)S(1)}, u32[]{:S(2)}, u32[]{:S(2)}) %collective-permute-start.2) | collective-permute-done | bytes 131104 | tf_op jit(solution)/shard_map/ppermute | solution.py:32
  11.1 1.3 %collective-permute-start.3 = (bf16[4,256,256]{2,1,0:T(8,128)(2,1)S(1)}, bf16[4,256,256]{2,1,0:T(8,128)(2,1)S(1)}, u32[]{:S(2)}, u32[]{:S(2)}) collective-permute-start(bf16[4,256,256]{2,1,0:T(8,128)(2,1)S(1)} %shard_map.80.refs_0_.refs_2_.own_ref), channel_id=1, source_target_pairs={{0,8},{2,10},{4,12},{6,14},{8,16},{10,18},{12,20},{14,22},{16,24},... | collective-permute-start | bytes 1572872 | tf_op jit(solution)/shard_map/ppermute | solution.py:27
  12.4 1.6 %collective-permute-start.4 = (bf16[256,256]{1,0:T(8,128)(2,1)S(1)}, bf16[256,256]{1,0:T(8,128)(2,1)S(1)}, u32[]{:S(2)}, u32[]{:S(2)}) collective-permute-start(bf16[256,256]{1,0:T(8,128)(2,1)S(1)} %get-tuple-element.40), channel_id=1, source_target_pairs={{0,4},{2,6},{4,0},{6,2},{8,12},{10,14},{12,8},{14,10},{16,20},{18,... | collective-permute-start | bytes 393224 | tf_op jit(solution)/shard_map/ppermute | solution.py:32
  14.0 1.5 %collective-permute-start.5 = (bf16[256,256]{1,0:T(8,128)(2,1)S(1)}, bf16[256,256]{1,0:T(8,128)(2,1)S(1)}, u32[]{:S(2)}, u32[]{:S(2)}) collective-permute-start(bf16[256,256]{1,0:T(8,128)(2,1)S(1)} %get-tuple-element.41), channel_id=1, source_target_pairs={{0,2},{2,0},{4,6},{6,4},{8,10},{10,8},{12,14},{14,12},{16,18},{18,... | collective-permute-start | bytes 393224 | tf_op jit(solution)/shard_map/ppermute | solution.py:32
  15.5 0.5 collective-permute-start.6
  16.0 1.9 %shard_map.83.refs_0_ = bf16[1024,256]{1,0:T(8,128)(2,1)S(1)} custom-call(bf16[2048,2688]{1,0:T(8,128)(2,1)S(1)} %bitcast.1, bf16[256,2688]{1,0:T(8,128)(2,1)S(1)} %copy-done, bf16[4,256,256]{2,1,0:T(8,128)(2,1)S(1)} %shard_map.80.refs_0_.refs_2_.own_ref, bf16[1024,256]{1,0:T(8,128)(2,1)S(1)} %shard_map.79.refs_4_.refs_1_), custom_call_target="tpu_custom_call" | custom-call | flops 1409286144 | bytes 13959168 | tf_op jit(solution)/shard_map/pallas_call | solution.py:39
  18.0 1.6 %collective-permute-start.8 = (bf16[256,256]{1,0:T(8,128)(2,1)S(1)}, bf16[256,256]{1,0:T(8,128)(2,1)S(1)}, u32[]{:S(2)}, u32[]{:S(2)}) collective-permute-start(bf16[256,256]{1,0:T(8,128)(2,1)S(1)} %get-tuple-element.46), channel_id=1, source_target_pairs={{0,4},{2,6},{4,0},{6,2},{8,12},{10,14},{12,8},{14,10},{16,20},{18,... | collective-permute-start | bytes 393224 | tf_op jit(solution)/shard_map/ppermute | solution.py:32
  19.6 1.9 %collective-permute-start.9 = (bf16[256,256]{1,0:T(8,128)(2,1)S(1)}, bf16[256,256]{1,0:T(8,128)(2,1)S(1)}, u32[]{:S(2)}, u32[]{:S(2)}) collective-permute-start(bf16[256,256]{1,0:T(8,128)(2,1)S(1)} %get-tuple-element.47), channel_id=1, source_target_pairs={{0,2},{2,0},{4,6},{6,4},{8,10},{10,8},{12,14},{14,12},{16,18},{18,... | collective-permute-start | bytes 393224 | tf_op jit(solution)/shard_map/ppermute | solution.py:32
  21.5 1.6 %collective-permute-start.10 = (bf16[256,256]{1,0:T(8,128)(2,1)S(1)}, bf16[256,256]{1,0:T(8,128)(2,1)S(1)}, u32[]{:S(2)}, u32[]{:S(2)}) collective-permute-start(bf16[256,256]{1,0:T(8,128)(2,1)S(1)} %get-tuple-element.48), channel_id=1, source_target_pairs={{0,6},{2,4},{4,2},{6,0},{8,14},{10,12},{12,10},{14,8},{16,22},{18,... | collective-permute-start | bytes 393224 | tf_op jit(solution)/shard_map/ppermute | solution.py:32
  23.3 2.5 %collective-permute-done.3.refs_1_.refs_0_ = bf16[4,256,256]{2,1,0:T(8,128)(2,1)S(1)} collective-permute-done((bf16[4,256,256]{2,1,0:T(8,128)(2,1)S(1)}, bf16[4,256,256]{2,1,0:T(8,128)(2,1)S(1)}, u32[]{:S(2)}, u32[]{:S(2)}) %collective-permute-start.3) | collective-permute-done | bytes 524320 | tf_op jit(solution)/shard_map/ppermute | solution.py:27
  25.8 3.8 %shard_map.82 = (bf16[1,4,5,256,512]{4,3,2,1,0:T(8,128)(2,1)S(1)}, f32[1,4,1,512]{3,2,1,0:T(1,128)S(1)}) custom-call(bf16[4,256,256]{2,1,0:T(8,128)(2,1)S(1)} %shard_map.80.refs_0_.refs_2_.own_ref, bf16[4,256,256]{2,1,0:T(8,128)(2,1)S(1)} %collective-permute-done.3.refs_1_.refs_0_, bf16[1,4,128,512]{3,2,1,0:T(8,128)(2,1)S(1)} %shard_map.81.refs_2_.qt_ref), custom_call_target="tpu_custom_call" | custom-call | flops 671088640 | bytes 6823936 | tf_op jit(solution)/shard_map/pallas_call | solution.py:39
  29.7 2.2 %shard_map.85 = (bf16[1,4,128,512]{3,2,1,0:T(8,128)(2,1)S(1)}, f32[4,256,128]{2,1,0:T(8,128)S(1)}, bf16[4,256,128]{2,1,0:T(8,128)(2,1)S(1)}) custom-call(bf16[1,4,5,256,512]{4,3,2,1,0:T(8,128)(2,1)S(1)} %get-tuple-element.43.e_ref, f32[1,4,1,512]{3,2,1,0:T(1,128)S(1)} %get-tuple-element.44.inverse_ref, bf16[256,256]{1,0:T(8,128)(2,1)S(1)} %get-tuple-element.45.refs_0_, ...), custom_call_target="tpu_custom_call" | custom-call | flops 671088640 | bytes 7086080 | tf_op jit(solution)/shard_map/pallas_call | solution.py:39
  31.9 2.4 %collective-permute-start.11 = (bf16[4,256,128]{2,1,0:T(8,128)(2,1)S(1)}, bf16[4,256,128]{2,1,0:T(8,128)(2,1)S(1)}, u32[]{:S(2)}, u32[]{:S(2)}) collective-permute-start(bf16[4,256,128]{2,1,0:T(8,128)(2,1)S(1)} %get-tuple-element.52), channel_id=1, source_target_pairs={{8,0},{10,2},{12,4},{14,6},{16,8},{18,10},{20,12},{22,14},{24,16},... | collective-permute-start | bytes 786440 | tf_op jit(solution)/shard_map/ppermute | solution.py:27
  34.3 5.4 %shard_map.86 = (bf16[1,4,5,256,512]{4,3,2,1,0:T(8,128)(2,1)S(1)}, f32[4,256,128]{2,1,0:T(8,128)S(1)}, bf16[4,256,128]{2,1,0:T(8,128)(2,1)S(1)}) custom-call(bf16[1,4,5,256,512]{4,3,2,1,0:T(8,128)(2,1)S(1)} %get-tuple-element.43.e_ref, f32[1,4,1,512]{3,2,1,0:T(1,128)S(1)} %get-tuple-element.44.inverse_ref, ...), custom_call_target="tpu_custom_call" | custom-call | flops 1342177280 | bytes 13377536 | tf_op jit(solution)/shard_map/pallas_call | solution.py:39
  39.6 2.4 %collective-permute-start.15 = (bf16[4,256,128]{2,1,0:T(8,128)(2,1)S(1)}, bf16[4,256,128]{2,1,0:T(8,128)(2,1)S(1)}, u32[]{:S(2)}, u32[]{:S(2)}) collective-permute-start(bf16[4,256,128]{2,1,0:T(8,128)(2,1)S(1)} %get-tuple-element.59), channel_id=1, source_target_pairs={{8,0},{10,2},{12,4},{14,6},{16,8},{18,10},{20,12},{22,14},{24,16},... | collective-permute-start | bytes 786440 | tf_op jit(solution)/shard_map/ppermute | solution.py:27
  42.0 2.0 %shard_map.87 = (bf16[256,384]{1,0:T(8,128)(2,1)S(1)}, bf16[256,384]{1,0:T(8,128)(2,1)S(1)}, bf16[256,384]{1,0:T(8,128)(2,1)S(1)}, bf16[256,384]{1,0:T(8,128)(2,1)S(1)}) custom-call(bf16[1,4,5,256,512]{4,3,2,1,0:T(8,128)(2,1)S(1)} %get-tuple-element.50.ds_ref, f32[1,4,1,512]{3,2,1,0:T(1,128)S(1)} %get-tuple-element.44.inverse_ref, ...), custom_call_target="tpu_custom_call" | custom-call | flops 671088640 | bytes 7872512 | tf_op jit(solution)/shard_map/pallas_call | solution.py:39
  44.0 1.0 %collective-permute-start.12 = (bf16[256,384]{1,0:T(8,128)(2,1)S(1)}, bf16[256,384]{1,0:T(8,128)(2,1)S(1)}, u32[]{:S(2)}, u32[]{:S(2)}) collective-permute-start(bf16[256,384]{1,0:T(8,128)(2,1)S(1)} %get-tuple-element.54), channel_id=1, source_target_pairs={{0,4},{2,6},{4,0},{6,2},{8,12},{10,14},{12,8},{14,10},{16,20},{18,... | collective-permute-start | bytes 589832 | tf_op jit(solution)/shard_map/ppermute | solution.py:32
  45.0 1.4 %collective-permute-start.13 = (bf16[256,384]{1,0:T(8,128)(2,1)S(1)}, bf16[256,384]{1,0:T(8,128)(2,1)S(1)}, u32[]{:S(2)}, u32[]{:S(2)}) collective-permute-start(bf16[256,384]{1,0:T(8,128)(2,1)S(1)} %get-tuple-element.55), channel_id=1, source_target_pairs={{0,2},{2,0},{4,6},{6,4},{8,10},{10,8},{12,14},{14,12},{16,18},{18,... | collective-permute-start | bytes 589832 | tf_op jit(solution)/shard_map/ppermute | solution.py:32
  46.4 1.1 %collective-permute-start.14 = (bf16[256,384]{1,0:T(8,128)(2,1)S(1)}, bf16[256,384]{1,0:T(8,128)(2,1)S(1)}, u32[]{:S(2)}, u32[]{:S(2)}) collective-permute-start(bf16[256,384]{1,0:T(8,128)(2,1)S(1)} %get-tuple-element.56), channel_id=1, source_target_pairs={{0,6},{2,4},{4,2},{6,0},{8,14},{10,12},{12,10},{14,8},{16,22},{18,... | collective-permute-start | bytes 589832 | tf_op jit(solution)/shard_map/ppermute | solution.py:32
  47.6 1.0 %collective-permute-start.16 = (bf16[256,128]{1,0:T(8,128)(2,1)S(1)}, bf16[256,128]{1,0:T(8,128)(2,1)S(1)}, u32[]{:S(2)}, u32[]{:S(2)}) collective-permute-start(bf16[256,128]{1,0:T(8,128)(2,1)S(1)} %get-tuple-element.61), channel_id=1, source_target_pairs={{0,4},{2,6},{4,0},{6,2},{8,12},{10,14},{12,8},{14,10},{16,20},{18,... | collective-permute-start | bytes 196616 | tf_op jit(solution)/shard_map/ppermute | solution.py:32
  48.6 1.4 %collective-permute-start.17 = (bf16[256,128]{1,0:T(8,128)(2,1)S(1)}, bf16[256,128]{1,0:T(8,128)(2,1)S(1)}, u32[]{:S(2)}, u32[]{:S(2)}) collective-permute-start(bf16[256,128]{1,0:T(8,128)(2,1)S(1)} %get-tuple-element.62), channel_id=1, source_target_pairs={{0,2},{2,0},{4,6},{6,4},{8,10},{10,8},{12,14},{14,12},{16,18},{18,... | collective-permute-start | bytes 196616 | tf_op jit(solution)/shard_map/ppermute | solution.py:32
  50.0 2.2 %collective-permute-done.12.refs_1_ = bf16[256,384]{1,0:T(8,128)(2,1)S(1)} collective-permute-done((bf16[256,384]{1,0:T(8,128)(2,1)S(1)}, bf16[256,384]{1,0:T(8,128)(2,1)S(1)}, u32[]{:S(2)}, u32[]{:S(2)}) %collective-permute-start.12) | collective-permute-done | bytes 196640 | tf_op jit(solution)/shard_map/ppermute | solution.py:32
  52.2 1.5 %collective-permute-start.18 = (bf16[256,128]{1,0:T(8,128)(2,1)S(1)}, bf16[256,128]{1,0:T(8,128)(2,1)S(1)}, u32[]{:S(2)}, u32[]{:S(2)}) collective-permute-start(bf16[256,128]{1,0:T(8,128)(2,1)S(1)} %get-tuple-element.63), channel_id=1, source_target_pairs={{0,6},{2,4},{4,2},{6,0},{8,14},{10,12},{12,10},{14,8},{16,22},{18,... | collective-permute-start | bytes 196616 | tf_op jit(solution)/shard_map/ppermute | solution.py:32
  53.7 1.6 %collective-permute-done.14.refs_3_ = bf16[256,384]{1,0:T(8,128)(2,1)S(1)} collective-permute-done((bf16[256,384]{1,0:T(8,128)(2,1)S(1)}, bf16[256,384]{1,0:T(8,128)(2,1)S(1)}, u32[]{:S(2)}, u32[]{:S(2)}) %collective-permute-start.14) | collective-permute-done | bytes 196640 | tf_op jit(solution)/shard_map/ppermute | solution.py:32
  55.3 1.0 %shard_map.88 = (bf16[256,1024]{1,0:T(8,128)(2,1)}, bf16[256,512]{1,0:T(8,128)(2,1)}, f32[8,128]{1,0:T(8,128)S(1)}) custom-call(bf16[256,384]{1,0:T(8,128)(2,1)S(1)} %get-tuple-element.53.refs_0_, bf16[256,384]{1,0:T(8,128)(2,1)S(1)} %collective-permute-done.12.refs_1_, bf16[256,384]{1,0:T(8,128)(2,1)S(1)} %collective-permute-done.13.refs_2_, ...), custom_call_target="tpu_custom_call" | custom-call | bytes 1576960 | tf_op jit(solution)/shard_map/pallas_call | solution.py:39
  56.3 1.1 %collective-permute-done.18.refs_3_ = bf16[256,128]{1,0:T(8,128)(2,1)S(1)} collective-permute-done((bf16[256,128]{1,0:T(8,128)(2,1)S(1)}, bf16[256,128]{1,0:T(8,128)(2,1)S(1)}, u32[]{:S(2)}, u32[]{:S(2)}) %collective-permute-start.18) | collective-permute-done | bytes 65568 | tf_op jit(solution)/shard_map/ppermute | solution.py:32
  57.4 0.8 %shard_map.90 = (bf16[256,512]{1,0:T(8,128)(2,1)}, f32[8,128]{1,0:T(8,128)}) custom-call(bf16[256,128]{1,0:T(8,128)(2,1)S(1)} %get-tuple-element.60.refs_0_, bf16[256,128]{1,0:T(8,128)(2,1)S(1)} %collective-permute-done.16.refs_1_, bf16[256,128]{1,0:T(8,128)(2,1)S(1)} %collective-permute-done.17.refs_2_, ...), custom_call_target="tpu_custom_call" | custom-call | bytes 532480 | tf_op jit(solution)/shard_map/pallas_call | solution.py:39
  (36 shorter events, 1.6 us)
Async XLA Ops:
  0.6 1.0 %copy-start.3 = (bf16[256,512]{1,0:T(8,128)(2,1)S(1)}, bf16[256,512]{1,0:T(8,128)(2,1)}, u32[]{:S(2)}) copy-start(bf16[256,512]{1,0:T(8,128)(2,1)} %v_ref.1) | copy-start | bytes 786436
  0.6 1.0 %copy-start.2 = (bf16[256,512]{1,0:T(8,128)(2,1)S(1)}, bf16[256,512]{1,0:T(8,128)(2,1)}, u32[]{:S(2)}) copy-start(bf16[256,512]{1,0:T(8,128)(2,1)} %k_ref.1) | copy-start | bytes 786436
  0.7 4.7 %slice-start = ((s8[11010048]{0:T(1024)(128)(4,1)}), s8[4194304]{0:T(1024)(128)(4,1)S(1)}, s32[]{:S(2)}) async-start(s8[11010048]{0:T(1024)(128)(4,1)} %bitcast), calls=%async_computation | async-start | bytes 8388608
  0.7 4.7 %slice-start.1 = ((s8[11010048]{0:T(1024)(128)(4,1)}), s8[4194304]{0:T(1024)(128)(4,1)S(1)}, s32[]{:S(2)}) async-start(s8[11010048]{0:T(1024)(128)(4,1)} %bitcast), calls=%async_computation.1 | async-start | bytes 8388608
  1.7 3.7 %copy-start.1 = (bf16[256,1024]{1,0:T(8,128)(2,1)S(1)}, bf16[256,1024]{1,0:T(8,128)(2,1)}, u32[]{:S(2)}) copy-start(bf16[256,1024]{1,0:T(8,128)(2,1)} %q_ref.1) | copy-start | bytes 1572868
  1.7 3.8 %slice-start.2 = ((s8[11010048]{0:T(1024)(128)(4,1)}), s8[2621440]{0:T(1024)(128)(4,1)S(1)}, s32[]{:S(2)}) async-start(s8[11010048]{0:T(1024)(128)(4,1)} %bitcast), calls=%async_computation.2 | async-start | bytes 5242880
  1.7 4.0 %copy-start = (bf16[256,2688]{1,0:T(8,128)(2,1)S(1)}, bf16[256,2688]{1,0:T(8,128)(2,1)}, u32[]{:S(2)}) copy-start(bf16[256,2688]{1,0:T(8,128)(2,1)} %c_ref.3) | copy-start | bytes 4128772
  1.8 5.9 %collective-permute-start = (bf16[256,256]{1,0:T(8,128)(2,1)S(1)}, bf16[256,256]{1,0:T(8,128)(2,1)S(1)}, u32[]{:S(2)}, u32[]{:S(2)}) collective-permute-start(bf16[256,256]{1,0:T(8,128)(2,1)S(1)} %get-tuple-element.36), channel_id=1, source_target_pairs={{0,4},{2,6},{4,0},{6,2},{8,12},{10,14},{12,8},{14,10},{16,20},{18,... | collective-permute-start | bytes 393224 | tf_op jit(solution)/shard_map/ppermute | solution.py:32
  3.3 6.4 %collective-permute-start.1 = (bf16[256,256]{1,0:T(8,128)(2,1)S(1)}, bf16[256,256]{1,0:T(8,128)(2,1)S(1)}, u32[]{:S(2)}, u32[]{:S(2)}) collective-permute-start(bf16[256,256]{1,0:T(8,128)(2,1)S(1)} %get-tuple-element.37), channel_id=1, source_target_pairs={{0,2},{2,0},{4,6},{6,4},{8,10},{10,8},{12,14},{14,12},{16,18},{18,... | collective-permute-start | bytes 393224 | tf_op jit(solution)/shard_map/ppermute | solution.py:32
  4.8 6.2 %collective-permute-start.2 = (bf16[256,256]{1,0:T(8,128)(2,1)S(1)}, bf16[256,256]{1,0:T(8,128)(2,1)S(1)}, u32[]{:S(2)}, u32[]{:S(2)}) collective-permute-start(bf16[256,256]{1,0:T(8,128)(2,1)S(1)} %get-tuple-element.38), channel_id=1, source_target_pairs={{0,6},{2,4},{4,2},{6,0},{8,14},{10,12},{12,10},{14,8},{16,22},{18,... | collective-permute-start | bytes 393224 | tf_op jit(solution)/shard_map/ppermute | solution.py:32
  7.6 10.3 %collective-permute-start.7 = (bf16[1024,256]{1,0:T(8,128)(2,1)S(1)}, bf16[1024,256]{1,0:T(8,128)(2,1)S(1)}, u32[]{:S(2)}, u32[]{:S(2)}) collective-permute-start(bf16[1024,256]{1,0:T(8,128)(2,1)S(1)} %shard_map.79.refs_4_.refs_1_), channel_id=1, source_target_pairs={{0,1},{1,0},{2,3},{3,2},{4,5},{5,4},{6,7},{7,6},{8,9},{9,8},{10,11... | collective-permute-start | bytes 1572872 | tf_op jit(solution)/shard_map/ppermute | solution.py:32
  11.1 14.7 %collective-permute-start.3 = (bf16[4,256,256]{2,1,0:T(8,128)(2,1)S(1)}, bf16[4,256,256]{2,1,0:T(8,128)(2,1)S(1)}, u32[]{:S(2)}, u32[]{:S(2)}) collective-permute-start(bf16[4,256,256]{2,1,0:T(8,128)(2,1)S(1)} %shard_map.80.refs_0_.refs_2_.own_ref), channel_id=1, source_target_pairs={{0,8},{2,10},{4,12},{6,14},{8,16},{10,18},{12,20},{14,22},{16,24},... | collective-permute-start | bytes 1572872 | tf_op jit(solution)/shard_map/ppermute | solution.py:27
  12.4 7.2 %collective-permute-start.4 = (bf16[256,256]{1,0:T(8,128)(2,1)S(1)}, bf16[256,256]{1,0:T(8,128)(2,1)S(1)}, u32[]{:S(2)}, u32[]{:S(2)}) collective-permute-start(bf16[256,256]{1,0:T(8,128)(2,1)S(1)} %get-tuple-element.40), channel_id=1, source_target_pairs={{0,4},{2,6},{4,0},{6,2},{8,12},{10,14},{12,8},{14,10},{16,20},{18,... | collective-permute-start | bytes 393224 | tf_op jit(solution)/shard_map/ppermute | solution.py:32
  14.0 7.5 %collective-permute-start.5 = (bf16[256,256]{1,0:T(8,128)(2,1)S(1)}, bf16[256,256]{1,0:T(8,128)(2,1)S(1)}, u32[]{:S(2)}, u32[]{:S(2)}) collective-permute-start(bf16[256,256]{1,0:T(8,128)(2,1)S(1)} %get-tuple-element.41), channel_id=1, source_target_pairs={{0,2},{2,0},{4,6},{6,4},{8,10},{10,8},{12,14},{14,12},{16,18},{18,... | collective-permute-start | bytes 393224 | tf_op jit(solution)/shard_map/ppermute | solution.py:32
  15.5 7.7 %collective-permute-start.6 = (bf16[256,256]{1,0:T(8,128)(2,1)S(1)}, bf16[256,256]{1,0:T(8,128)(2,1)S(1)}, u32[]{:S(2)}, u32[]{:S(2)}) collective-permute-start(bf16[256,256]{1,0:T(8,128)(2,1)S(1)} %get-tuple-element.42), channel_id=1, source_target_pairs={{0,6},{2,4},{4,2},{6,0},{8,14},{10,12},{12,10},{14,8},{16,22},{18,... | collective-permute-start | bytes 393224 | tf_op jit(solution)/shard_map/ppermute | solution.py:32
  18.0 11.6 %collective-permute-start.8 = (bf16[256,256]{1,0:T(8,128)(2,1)S(1)}, bf16[256,256]{1,0:T(8,128)(2,1)S(1)}, u32[]{:S(2)}, u32[]{:S(2)}) collective-permute-start(bf16[256,256]{1,0:T(8,128)(2,1)S(1)} %get-tuple-element.46), channel_id=1, source_target_pairs={{0,4},{2,6},{4,0},{6,2},{8,12},{10,14},{12,8},{14,10},{16,20},{18,... | collective-permute-start | bytes 393224 | tf_op jit(solution)/shard_map/ppermute | solution.py:32
  19.6 10.0 %collective-permute-start.9 = (bf16[256,256]{1,0:T(8,128)(2,1)S(1)}, bf16[256,256]{1,0:T(8,128)(2,1)S(1)}, u32[]{:S(2)}, u32[]{:S(2)}) collective-permute-start(bf16[256,256]{1,0:T(8,128)(2,1)S(1)} %get-tuple-element.47), channel_id=1, source_target_pairs={{0,2},{2,0},{4,6},{6,4},{8,10},{10,8},{12,14},{14,12},{16,18},{18,... | collective-permute-start | bytes 393224 | tf_op jit(solution)/shard_map/ppermute | solution.py:32
  21.5 8.1 %collective-permute-start.10 = (bf16[256,256]{1,0:T(8,128)(2,1)S(1)}, bf16[256,256]{1,0:T(8,128)(2,1)S(1)}, u32[]{:S(2)}, u32[]{:S(2)}) collective-permute-start(bf16[256,256]{1,0:T(8,128)(2,1)S(1)} %get-tuple-element.48), channel_id=1, source_target_pairs={{0,6},{2,4},{4,2},{6,0},{8,14},{10,12},{12,10},{14,8},{16,22},{18,... | collective-permute-start | bytes 393224 | tf_op jit(solution)/shard_map/ppermute | solution.py:32
  31.9 10.1 %collective-permute-start.11 = (bf16[4,256,128]{2,1,0:T(8,128)(2,1)S(1)}, bf16[4,256,128]{2,1,0:T(8,128)(2,1)S(1)}, u32[]{:S(2)}, u32[]{:S(2)}) collective-permute-start(bf16[4,256,128]{2,1,0:T(8,128)(2,1)S(1)} %get-tuple-element.52), channel_id=1, source_target_pairs={{8,0},{10,2},{12,4},{14,6},{16,8},{18,10},{20,12},{22,14},{24,16},... | collective-permute-start | bytes 786440 | tf_op jit(solution)/shard_map/ppermute | solution.py:27
  39.6 7.9 %collective-permute-start.15 = (bf16[4,256,128]{2,1,0:T(8,128)(2,1)S(1)}, bf16[4,256,128]{2,1,0:T(8,128)(2,1)S(1)}, u32[]{:S(2)}, u32[]{:S(2)}) collective-permute-start(bf16[4,256,128]{2,1,0:T(8,128)(2,1)S(1)} %get-tuple-element.59), channel_id=1, source_target_pairs={{8,0},{10,2},{12,4},{14,6},{16,8},{18,10},{20,12},{22,14},{24,16},... | collective-permute-start | bytes 786440 | tf_op jit(solution)/shard_map/ppermute | solution.py:27
  44.0 8.3 %collective-permute-start.12 = (bf16[256,384]{1,0:T(8,128)(2,1)S(1)}, bf16[256,384]{1,0:T(8,128)(2,1)S(1)}, u32[]{:S(2)}, u32[]{:S(2)}) collective-permute-start(bf16[256,384]{1,0:T(8,128)(2,1)S(1)} %get-tuple-element.54), channel_id=1, source_target_pairs={{0,4},{2,6},{4,0},{6,2},{8,12},{10,14},{12,8},{14,10},{16,20},{18,... | collective-permute-start | bytes 589832 | tf_op jit(solution)/shard_map/ppermute | solution.py:32
  45.0 8.7 %collective-permute-start.13 = (bf16[256,384]{1,0:T(8,128)(2,1)S(1)}, bf16[256,384]{1,0:T(8,128)(2,1)S(1)}, u32[]{:S(2)}, u32[]{:S(2)}) collective-permute-start(bf16[256,384]{1,0:T(8,128)(2,1)S(1)} %get-tuple-element.55), channel_id=1, source_target_pairs={{0,2},{2,0},{4,6},{6,4},{8,10},{10,8},{12,14},{14,12},{16,18},{18,... | collective-permute-start | bytes 589832 | tf_op jit(solution)/shard_map/ppermute | solution.py:32
  46.4 8.9 %collective-permute-start.14 = (bf16[256,384]{1,0:T(8,128)(2,1)S(1)}, bf16[256,384]{1,0:T(8,128)(2,1)S(1)}, u32[]{:S(2)}, u32[]{:S(2)}) collective-permute-start(bf16[256,384]{1,0:T(8,128)(2,1)S(1)} %get-tuple-element.56), channel_id=1, source_target_pairs={{0,6},{2,4},{4,2},{6,0},{8,14},{10,12},{12,10},{14,8},{16,22},{18,... | collective-permute-start | bytes 589832 | tf_op jit(solution)/shard_map/ppermute | solution.py:32
  47.6 8.7 %collective-permute-start.16 = (bf16[256,128]{1,0:T(8,128)(2,1)S(1)}, bf16[256,128]{1,0:T(8,128)(2,1)S(1)}, u32[]{:S(2)}, u32[]{:S(2)}) collective-permute-start(bf16[256,128]{1,0:T(8,128)(2,1)S(1)} %get-tuple-element.61), channel_id=1, source_target_pairs={{0,4},{2,6},{4,0},{6,2},{8,12},{10,14},{12,8},{14,10},{16,20},{18,... | collective-permute-start | bytes 196616 | tf_op jit(solution)/shard_map/ppermute | solution.py:32
  48.6 7.7 %collective-permute-start.17 = (bf16[256,128]{1,0:T(8,128)(2,1)S(1)}, bf16[256,128]{1,0:T(8,128)(2,1)S(1)}, u32[]{:S(2)}, u32[]{:S(2)}) collective-permute-start(bf16[256,128]{1,0:T(8,128)(2,1)S(1)} %get-tuple-element.62), channel_id=1, source_target_pairs={{0,2},{2,0},{4,6},{6,4},{8,10},{10,8},{12,14},{14,12},{16,18},{18,... | collective-permute-start | bytes 196616 | tf_op jit(solution)/shard_map/ppermute | solution.py:32
  52.2 5.2 %collective-permute-start.18 = (bf16[256,128]{1,0:T(8,128)(2,1)S(1)}, bf16[256,128]{1,0:T(8,128)(2,1)S(1)}, u32[]{:S(2)}, u32[]{:S(2)}) collective-permute-start(bf16[256,128]{1,0:T(8,128)(2,1)S(1)} %get-tuple-element.63), channel_id=1, source_target_pairs={{0,6},{2,4},{4,2},{6,0},{8,14},{10,12},{12,10},{14,8},{16,22},{18,... | collective-permute-start | bytes 196616 | tf_op jit(solution)/shard_map/ppermute | solution.py:32

commit v14 on v12

--- a/solution.py
+++ b/solution.py
@@ -66,37 +66,30 @@
     return call(body, [jax.ShapeDtypeStruct((8, 128), jnp.float32)], flops=AHEAD)()[0]
 
 
-def pack_kv(group, keys, values, before):
-    tokens, width = keys.shape[0], keys.shape[1] // group
-
-    def body(k_ref, v_ref, before_ref, *refs):
+def pack_heads(group, arrays, before, flops):
+    tokens = arrays[0].shape[0]
+    widths = [array.shape[1] // group for array in arrays]
+
+    def body(*refs):
         for r in range(group):
-            member = spot(group)[0] ^ r
-            refs[r][:, :width] = k_ref[:, lanes(member, width)]
-            refs[r][:, width:] = v_ref[:, lanes(member, width)]
-
-    outs = [jax.ShapeDtypeStruct((tokens, 2 * width), jnp.bfloat16)] * group
-    return call(body, outs, flops=AHEAD, specs=[VMEM, VMEM, ANY])(keys, values, before)
-
-
-def pack_queries(group, queries, before):
-    tokens, width = queries.shape[0], queries.shape[1] // group
-
-    def body(q_ref, before_ref, *out_refs):
+            lower = 0
+            for ref, width in zip(refs, widths):
+                refs[len(arrays) + 1 + r][:, lower : lower + width] = ref[:, lanes(spot(group)[0] ^ r, width)]
+                lower += width
+
+    outs = [jax.ShapeDtypeStruct((tokens, sum(widths)), jnp.bfloat16)] * group
+    return call(body, outs, flops=flops, specs=[VMEM] * len(arrays) + [ANY])(*arrays, before)
+
+
+def order_pieces(group, pieces, width, before, flops):
+    tokens = pieces[0].shape[0]
+
+    def body(*refs):
         for r in range(group):
-            out_refs[r][...] = q_ref[:, lanes(spot(group)[0] ^ r, width)]
-
-    outs = [jax.ShapeDtypeStruct((tokens, width), jnp.bfloat16)] * group
-    return call(body, outs, specs=[VMEM, ANY])(queries, before)
-
-
-def order_pieces(group, pieces, before):
-    def body(*refs):
-        for r in range(group):
-            refs[-1][spot(group)[0] ^ r] = refs[r][...]
-
-    outs = [jax.ShapeDtypeStruct((group,) + pieces[0].shape, jnp.bfloat16)]
-    return call(body, outs, specs=[VMEM] * group + [ANY])(*pieces, before)[0]
+            refs[-1][spot(group)[0] ^ r] = refs[r][:, :width]
+
+    outs = [jax.ShapeDtypeStruct((group, tokens, width), jnp.bfloat16)]
+    return call(body, outs, flops=flops, specs=[VMEM] * group + [ANY])(*pieces, before)[0]
 
 
 def head_product(parts, part, out_weight, layer_cotangent, before):
@@ -162,7 +155,7 @@
         for head in range(z.heads):
             for r in range(z.group):
                 for j in range(z.per_head):
-                    lower = (head * z.per_head + j) * HEAD_SIZE
+                    lower = z.kv_width + (head * z.per_head + j) * HEAD_SIZE
                     refs[z.group][head, spot(z.group)[0] ^ r, :, j * z.tokens : (j + 1) * z.tokens] = refs[r][
                         :, lower : lower + HEAD_SIZE
                     ].T
@@ -171,19 +164,19 @@
     return call(body, outs)(*pieces)[0]
 
 
-def softmax(z, kv_own, kv_earlier, qt):
+def softmax(z, k_own, k_earlier, qt):
     factor = score_scale * LOG2_E
 
-    def body(*refs):
-        own_ref, earlier_refs = refs[0], refs[1 : 1 + z.steps]
-        qt_ref, e_ref, inverse_ref, k_all, s_all = refs[1 + z.steps :]
+    def body(own_ref, *refs):
+        earlier_refs = refs[: z.steps]
+        qt_ref, e_ref, inverse_ref, k_all, s_all = refs[z.steps :]
         first = spot(z.group)[1]
         key_id = lax.broadcasted_iota(jnp.int32, (z.tokens, z.wide), 0)
         query_id = lax.broadcasted_iota(jnp.int32, (z.tokens, z.wide), 1) & (z.tokens - 1)
         for head in range(z.heads):
-            at_k = slice(head * HEAD_SIZE, (head + 1) * HEAD_SIZE)
+            at = slice(head * HEAD_SIZE, (head + 1) * HEAD_SIZE)
             for number in range(z.total):
-                k_all[number] = z.block(own_ref, earlier_refs, number)[:, at_k]
+                k_all[number] = z.block(own_ref, earlier_refs, number)[:, at]
 
             @pl.loop(0, z.group)
             def _(b):
@@ -219,7 +212,7 @@
         pltpu.VMEM((z.span, z.tokens, z.wide), jnp.float32),
     ]
     return call(body, outs, scratch, flops=2 * z.entries * HEAD_SIZE, exps=z.entries)(
-        kv_own, *kv_earlier, qt
+        k_own, *k_earlier, qt
     )
 
 
@@ -251,8 +244,9 @@
                     )
 
             for number in range(z.total):
-                part = dv_all[number]
-                z.block(own_ref, earlier_refs, number)[:, at] = part.astype(own_ref.dtype if number >= z.back else jnp.bfloat16)
+                z.block(own_ref, earlier_refs, number)[:, at] = dv_all[number].astype(
+                    own_ref.dtype if number >= z.back else jnp.bfloat16
+                )
 
     outs = [
         jax.ShapeDtypeStruct((z.heads, z.group, HEAD_SIZE, z.wide), jnp.bfloat16),
@@ -264,16 +258,15 @@
     return results[0], results[1], results[2:]
 
 
-def key_terms(z, e, inverse, qt, g, kv_own, kv_earlier):
+def key_terms(z, e, inverse, qt, g, v_own, v_earlier):
     def body(e_ref, inverse_ref, qt_ref, g_ref, own_ref, *refs):
         earlier_refs, ds_ref = refs[: z.steps], refs[z.steps]
         dk_own, dk_earlier = refs[z.steps + 1], refs[z.steps + 2 : 2 * z.steps + 2]
         v_all, dk_all, dp_all = refs[2 * z.steps + 2 :]
         for head in range(z.heads):
             at = slice(head * HEAD_SIZE, (head + 1) * HEAD_SIZE)
-            at_v = slice(z.kv_width + head * HEAD_SIZE, z.kv_width + (head + 1) * HEAD_SIZE)
             for number in range(z.total):
-                v_all[number] = z.block(own_ref, earlier_refs, number)[:, at_v]
+                v_all[number] = z.block(own_ref, earlier_refs, number)[:, at]
             dk_all[...] = jnp.zeros_like(dk_all)
 
             @pl.loop(0, z.group)
@@ -307,12 +300,12 @@
         pltpu.VMEM((z.span, z.tokens, z.wide), jnp.float32),
     ]
     results = call(body, outs, scratch, flops=4 * z.entries * HEAD_SIZE)(
-        e, inverse, qt, g, kv_own, *kv_earlier
+        e, inverse, qt, g, v_own, *v_earlier
     )
     return results[0], results[1], results[2:]
 
 
-def query_terms(z, ds, inverse, kv_own, kv_earlier, dv_terms):
+def query_terms(z, ds, inverse, k_own, k_earlier, dv_terms):
     def body(ds_ref, inverse_ref, own_ref, *refs):
         earlier_refs, term_refs = refs[: z.steps], refs[z.steps : 2 * z.steps + 1]
         out_refs = refs[2 * z.steps + 1 : 2 * z.steps + 1 + z.group]
@@ -350,7 +343,7 @@
         pltpu.VMEM((z.group, z.tokens, z.width), jnp.bfloat16),
     ]
     return call(body, outs, scratch, flops=2 * z.entries * HEAD_SIZE)(
-        ds, inverse, kv_own, *kv_earlier, *dv_terms
+        ds, inverse, k_own, *k_earlier, *dv_terms
     )
 
 
@@ -406,7 +399,6 @@
     heads = kv_heads // group
     kv_width = heads * HEAD_SIZE
     back_groups = WINDOW_LENGTH // (group * tokens)
-
     def trade(sent):
         return [sent[0]] + [swapped(sent[r], "ctx", r) for r in range(1, group)]
 
@@ -415,28 +407,31 @@
             shifted(earlier[number], "ctx", -group * (back_groups - number)) for number in range(back_groups)
         ]
 
-    sent = pack_kv(group, keys, values, begin())
-    kv_pieces = trade(sent)
     z = Shape(group, back_groups, heads, per_head, tokens)
-    query_sent = pack_queries(group, queries, sent[0])
+    key_sent = pack_heads(group, [keys], begin(), AHEAD)
+    sent = pack_heads(group, [values, queries], key_sent[0], 0)
     if tp_count == 2:
-        other = head_product(2, 1, out_weight, layer_cotangent, [query_sent[0]])
+        other = head_product(2, 1, out_weight, layer_cotangent, [sent[0]])
     else:
-        other = head_product(1, 0, out_weight, layer_cotangent, [query_sent[0]])
-    kv_own = order_pieces(group, kv_pieces, other)
-    kv_earlier = [shifted(kv_own, "ctx", group * step) for step in range(back_groups, 0, -1)]
+        other = head_product(1, 0, out_weight, layer_cotangent, [sent[0]])
+    k_own = order_pieces(group, trade(key_sent), kv_width, other, AHEAD)
     if tp_count == 2:
-        terms = [head_product(2, 0, out_weight, layer_cotangent, [kv_own, other]), swapped(other, "tp", 1)]
+        terms = [head_product(2, 0, out_weight, layer_cotangent, [other, k_own]), swapped(other, "tp", 1)]
     else:
         terms = [lax.psum_scatter(other, "tp", scatter_dimension=0, tiled=True)]
-    qt = turn_queries(z, trade(query_sent))
-    grads = trade(pack_grads(group, terms, kv_own))
-    e, inverse = softmax(z, kv_own, kv_earlier, qt)
+    pieces = trade(sent)
+    v_own = order_pieces(group, pieces, kv_width, terms[0], 0)
+    k_earlier, v_earlier = (
+        [shifted(own, "ctx", group * step) for step in range(back_groups, 0, -1)] for own in (k_own, v_own)
+    )
+    qt = turn_queries(z, pieces)
+    grads = trade(pack_grads(group, terms, k_own))
+    e, inverse = softmax(z, k_own, k_earlier, qt)
     g, dv_own, dv_earlier = value_terms(z, e, inverse, grads)
     dv_terms = [dv_own] + returned(dv_earlier)
-    ds, dk_own, dk_earlier = key_terms(z, e, inverse, qt, g, kv_own, kv_earlier)
+    ds, dk_own, dk_earlier = key_terms(z, e, inverse, qt, g, v_own, v_earlier)
     dk_terms = [dk_own] + returned(dk_earlier)
-    pieces = trade(query_terms(z, ds, inverse, kv_own, kv_earlier, dv_terms))
+    pieces = trade(query_terms(z, ds, inverse, k_own, k_earlier, dv_terms))
     query_grads, value_gradients, done = unpack(group, pieces, [z.width, kv_width])
     key_gradients, _ = unpack(group, trade(pack_terms(group, [dk_terms])), [kv_width], [done])
     return (query_grads, key_gradients, value_gradients)

time: 57.7 us -> 58.5 us (1.014)
  starting transfers between devices: 25.2 us -> 27.4 us
  waiting for transfers between devices: 10.6 us -> 9.75 us
    ppermute x3 -> x4, starting transfers between devices: 6.02 us -> 11.8 us  [shifted(): lax.ppermute(value, axis, [(source, source + steps) for source in range(l...]
    ppermute x16, starting transfers between devices: 19.1 us -> 15.6 us  [swapped(): lax.ppermute(value, axis, [(source, source ^ bits) for source in range(co...]
    ppermute x3 -> x4, waiting for transfers between devices: 2.33 us -> 0.01 us  [shifted(): lax.ppermute(value, axis, [(source, source + steps) for source in range(l...]
    ppermute x16, waiting for transfers between devices: 8.23 us -> 9.74 us  [swapped(): lax.ppermute(value, axis, [(source, source ^ bits) for source in range(co...]
    pallas_call x15 -> x16, Pallas kernels: 19.4 us -> 19.3 us  [run(): pl.pallas_call(body, out_shape=tuple(outs), in_specs=specs or [SMEM if a....]
  transfers between devices with their start and end apart: 19 -> 20, of which waited for: 5 -> 5; matrix products, arithmetic and copies ran while one was open for 0% -> 0% of each run, Pallas kernels for 29% -> 32%
where the time goes in v14:
time: 58.5 us; the launch traced here: 58.3 us
  starting transfers between devices  27.4 us (47%)
  Pallas kernels  19.3 us (33%)
  waiting for transfers between devices  9.75 us (17%)
  local copies, waits for them, and re-layouts  0.94 us (2%)
  between operations  0.88 us (2%)
    pallas_call x16, Pallas kernels, run(): pl.pallas_call(body, out_shape=tuple(outs), in_specs=specs or [SMEM if a....  19.3 us
    ppermute x16, starting transfers between devices, swapped(): lax.ppermute(value, axis, [(source, source ^ bits) for source in range(co...  15.6 us
    ppermute x4, starting transfers between devices, shifted(): lax.ppermute(value, axis, [(source, source + steps) for source in range(l...  11.8 us
    ppermute x16, waiting for transfers between devices, swapped(): lax.ppermute(value, axis, [(source, source ^ bits) for source in range(co...  9.74 us
  transfers between devices with their start and end apart: 20, of which 5 were waited for; matrix products, arithmetic and copies ran while one was open for 0% of the time, Pallas kernels for 32%

profile of v14, /device:TPU:24, one launch (start us, length us, event | category | flops | bytes accessed | tf_op | source)
XLA Modules:
  0.0 58.3 jit_solution(16733328503924669956)
XLA Ops:
  0.7 0.9 %copy-done.3 = bf16[256,512]{1,0:T(8,128)(2,1)S(1)} copy-done((bf16[256,512]{1,0:T(8,128)(2,1)S(1)}, bf16[256,512]{1,0:T(8,128)(2,1)}, u32[]{:S(2)}) %copy-start.3) | copy-done | bytes 262168
  1.7 1.6 %collective-permute-start = (bf16[256,128]{1,0:T(8,128)(2,1)S(1)}, bf16[256,128]{1,0:T(8,128)(2,1)S(1)}, u32[]{:S(2)}, u32[]{:S(2)}) collective-permute-start(bf16[256,128]{1,0:T(8,128)(2,1)S(1)} %get-tuple-element.36), channel_id=1, source_target_pairs={{0,2},{2,0},{4,6},{6,4},{8,10},{10,8},{12,14},{14,12},{16,18},{18,... | collective-permute-start | bytes 196616 | tf_op jit(solution)/shard_map/ppermute | solution.py:32
  3.2 1.5 %collective-permute-start.1 = (bf16[256,128]{1,0:T(8,128)(2,1)S(1)}, bf16[256,128]{1,0:T(8,128)(2,1)S(1)}, u32[]{:S(2)}, u32[]{:S(2)}) collective-permute-start(bf16[256,128]{1,0:T(8,128)(2,1)S(1)} %get-tuple-element.37), channel_id=1, source_target_pairs={{0,4},{2,6},{4,0},{6,2},{8,12},{10,14},{12,8},{14,10},{16,20},{18,... | collective-permute-start | bytes 196616 | tf_op jit(solution)/shard_map/ppermute | solution.py:32
  4.7 0.5 collective-permute-start.2
  5.3 1.6 %collective-permute-start.4 = (bf16[256,384]{1,0:T(8,128)(2,1)S(1)}, bf16[256,384]{1,0:T(8,128)(2,1)S(1)}, u32[]{:S(2)}, u32[]{:S(2)}) collective-permute-start(bf16[256,384]{1,0:T(8,128)(2,1)S(1)} %get-tuple-element.40), channel_id=1, source_target_pairs={{0,2},{2,0},{4,6},{6,4},{8,10},{10,8},{12,14},{14,12},{16,18},{18,... | collective-permute-start | bytes 589832 | tf_op jit(solution)/shard_map/ppermute | solution.py:32
  6.9 1.5 %collective-permute-start.5 = (bf16[256,384]{1,0:T(8,128)(2,1)S(1)}, bf16[256,384]{1,0:T(8,128)(2,1)S(1)}, u32[]{:S(2)}, u32[]{:S(2)}) collective-permute-start(bf16[256,384]{1,0:T(8,128)(2,1)S(1)} %get-tuple-element.41), channel_id=1, source_target_pairs={{0,4},{2,6},{4,0},{6,2},{8,12},{10,14},{12,8},{14,10},{16,20},{18,... | collective-permute-start | bytes 589832 | tf_op jit(solution)/shard_map/ppermute | solution.py:32
  8.4 1.9 %shard_map.79.refs_4_.refs_0_ = bf16[1024,256]{1,0:T(8,128)(2,1)S(1)} custom-call(bf16[2048,2688]{1,0:T(8,128)(2,1)S(1)} %bitcast.1, bf16[256,2688]{1,0:T(8,128)(2,1)S(1)} %copy-done, bf16[256,384]{1,0:T(8,128)(2,1)S(1)} %get-tuple-element.39.refs_0_), custom_call_target="tpu_custom_call" | custom-call | flops 1409286144 | bytes 13107200 | tf_op jit(solution)/shard_map/pallas_call | solution.py:39
  10.7 1.3 %collective-permute-start.3 = (bf16[4,256,128]{2,1,0:T(8,128)(2,1)S(1)}, bf16[4,256,128]{2,1,0:T(8,128)(2,1)S(1)}, u32[]{:S(2)}, u32[]{:S(2)}) collective-permute-start(bf16[4,256,128]{2,1,0:T(8,128)(2,1)S(1)} %shard_map.80.own_ref.refs_1_.refs_2_), channel_id=1, source_target_pairs={{0,8},{2,10},{4,12},{6,14},{8,16},{10,18},{12,20},{14,22},{16,24},... | collective-permute-start | bytes 786440 | tf_op jit(solution)/shard_map/ppermute | solution.py:27
  12.0 0.5 collective-permute-start.6
  12.5 1.9 %shard_map.83.refs_0_.refs_4_ = bf16[1024,256]{1,0:T(8,128)(2,1)S(1)} custom-call(bf16[2048,2688]{1,0:T(8,128)(2,1)S(1)} %bitcast.1, bf16[256,2688]{1,0:T(8,128)(2,1)S(1)} %copy-done, bf16[1024,256]{1,0:T(8,128)(2,1)S(1)} %shard_map.79.refs_4_.refs_0_, bf16[4,256,128]{2,1,0:T(8,128)(2,1)S(1)} %shard_map.80.own_ref.refs_1_.refs_2_), custom_call_target="tpu_custom_call" | custom-call | flops 1409286144 | bytes 13697024 | tf_op jit(solution)/shard_map/pallas_call | solution.py:39
  14.5 1.6 %collective-permute-start.8 = (bf16[256,256]{1,0:T(8,128)(2,1)S(1)}, bf16[256,256]{1,0:T(8,128)(2,1)S(1)}, u32[]{:S(2)}, u32[]{:S(2)}) collective-permute-start(bf16[256,256]{1,0:T(8,128)(2,1)S(1)} %get-tuple-element.46), channel_id=1, source_target_pairs={{0,2},{2,0},{4,6},{6,4},{8,10},{10,8},{12,14},{14,12},{16,18},{18,... | collective-permute-start | bytes 393224 | tf_op jit(solution)/shard_map/ppermute | solution.py:32
  16.2 1.5 %collective-permute-start.9 = (bf16[256,256]{1,0:T(8,128)(2,1)S(1)}, bf16[256,256]{1,0:T(8,128)(2,1)S(1)}, u32[]{:S(2)}, u32[]{:S(2)}) collective-permute-start(bf16[256,256]{1,0:T(8,128)(2,1)S(1)} %get-tuple-element.47), channel_id=1, source_target_pairs={{0,4},{2,6},{4,0},{6,2},{8,12},{10,14},{12,8},{14,10},{16,20},{18,... | collective-permute-start | bytes 393224 | tf_op jit(solution)/shard_map/ppermute | solution.py:32
  17.7 0.4 collective-permute-start.10
  18.1 2.6 %collective-permute-done.6.refs_3_ = bf16[256,384]{1,0:T(8,128)(2,1)S(1)} collective-permute-done((bf16[256,384]{1,0:T(8,128)(2,1)S(1)}, bf16[256,384]{1,0:T(8,128)(2,1)S(1)}, u32[]{:S(2)}, u32[]{:S(2)}) %collective-permute-start.6) | collective-permute-done | bytes 196640 | tf_op jit(solution)/shard_map/ppermute | solution.py:32
  20.8 1.3 %collective-permute-start.11 = (bf16[4,256,128]{2,1,0:T(8,128)(2,1)S(1)}, bf16[4,256,128]{2,1,0:T(8,128)(2,1)S(1)}, u32[]{:S(2)}, u32[]{:S(2)}) collective-permute-start(bf16[4,256,128]{2,1,0:T(8,128)(2,1)S(1)} %shard_map.86.own_ref), channel_id=1, source_target_pairs={{0,8},{2,10},{4,12},{6,14},{8,16},{10,18},{12,20},{14,22},{16,24},... | collective-permute-start | bytes 786440 | tf_op jit(solution)/shard_map/ppermute | solution.py:27
  22.3 3.7 %shard_map.82 = (bf16[1,4,5,256,512]{4,3,2,1,0:T(8,128)(2,1)S(1)}, f32[1,4,1,512]{3,2,1,0:T(1,128)S(1)}) custom-call(bf16[4,256,128]{2,1,0:T(8,128)(2,1)S(1)} %shard_map.80.own_ref.refs_1_.refs_2_, bf16[4,256,128]{2,1,0:T(8,128)(2,1)S(1)} %collective-permute-done.3.refs_0_, bf16[1,4,128,512]{3,2,1,0:T(8,128)(2,1)S(1)} %shard_map.81.refs_1_.qt_ref), custom_call_target="tpu_custom_call" | custom-call | flops 671088640 | bytes 6299648 | tf_op jit(solution)/shard_map/pallas_call | solution.py:39
  26.0 2.2 %shard_map.85 = (bf16[1,4,128,512]{3,2,1,0:T(8,128)(2,1)S(1)}, f32[4,256,128]{2,1,0:T(8,128)S(1)}, bf16[4,256,128]{2,1,0:T(8,128)(2,1)S(1)}) custom-call(bf16[1,4,5,256,512]{4,3,2,1,0:T(8,128)(2,1)S(1)} %get-tuple-element.43.e_ref, f32[1,4,1,512]{3,2,1,0:T(1,128)S(1)} %get-tuple-element.44.inverse_ref, bf16[256,256]{1,0:T(8,128)(2,1)S(1)} %get-tuple-element.45.refs_0_, ...), custom_call_target="tpu_custom_call" | custom-call | flops 671088640 | bytes 7086080 | tf_op jit(solution)/shard_map/pallas_call | solution.py:39
  28.2 5.2 %collective-permute-start.12 = (bf16[4,256,128]{2,1,0:T(8,128)(2,1)S(1)}, bf16[4,256,128]{2,1,0:T(8,128)(2,1)S(1)}, u32[]{:S(2)}, u32[]{:S(2)}) collective-permute-start(bf16[4,256,128]{2,1,0:T(8,128)(2,1)S(1)} %get-tuple-element.52), channel_id=1, source_target_pairs={{8,0},{10,2},{12,4},{14,6},{16,8},{18,10},{20,12},{22,14},{24,16},... | collective-permute-start | bytes 786440 | tf_op jit(solution)/shard_map/ppermute | solution.py:27
  33.5 5.3 %shard_map.87 = (bf16[1,4,5,256,512]{4,3,2,1,0:T(8,128)(2,1)S(1)}, f32[4,256,128]{2,1,0:T(8,128)S(1)}, bf16[4,256,128]{2,1,0:T(8,128)(2,1)S(1)}) custom-call(bf16[1,4,5,256,512]{4,3,2,1,0:T(8,128)(2,1)S(1)} %get-tuple-element.43.e_ref, f32[1,4,1,512]{3,2,1,0:T(1,128)S(1)} %get-tuple-element.44.inverse_ref, ...), custom_call_target="tpu_custom_call" | custom-call | flops 1342177280 | bytes 12853248 | tf_op jit(solution)/shard_map/pallas_call | solution.py:39
  38.8 3.9 %collective-permute-start.16 = (bf16[4,256,128]{2,1,0:T(8,128)(2,1)S(1)}, bf16[4,256,128]{2,1,0:T(8,128)(2,1)S(1)}, u32[]{:S(2)}, u32[]{:S(2)}) collective-permute-start(bf16[4,256,128]{2,1,0:T(8,128)(2,1)S(1)} %get-tuple-element.59), channel_id=1, source_target_pairs={{8,0},{10,2},{12,4},{14,6},{16,8},{18,10},{20,12},{22,14},{24,16},... | collective-permute-start | bytes 786440 | tf_op jit(solution)/shard_map/ppermute | solution.py:27
  42.8 1.9 %shard_map.88 = (bf16[256,384]{1,0:T(8,128)(2,1)S(1)}, bf16[256,384]{1,0:T(8,128)(2,1)S(1)}, bf16[256,384]{1,0:T(8,128)(2,1)S(1)}, bf16[256,384]{1,0:T(8,128)(2,1)S(1)}) custom-call(bf16[1,4,5,256,512]{4,3,2,1,0:T(8,128)(2,1)S(1)} %get-tuple-element.50.ds_ref, f32[1,4,1,512]{3,2,1,0:T(1,128)S(1)} %get-tuple-element.44.inverse_ref, ...), custom_call_target="tpu_custom_call" | custom-call | flops 671088640 | bytes 7348224 | tf_op jit(solution)/shard_map/pallas_call | solution.py:39
  44.7 0.4 collective-permute-start.13
  45.1 0.5 collective-permute-start.14
  45.6 2.6 %collective-permute-start.15 = (bf16[256,384]{1,0:T(8,128)(2,1)S(1)}, bf16[256,384]{1,0:T(8,128)(2,1)S(1)}, u32[]{:S(2)}, u32[]{:S(2)}) collective-permute-start(bf16[256,384]{1,0:T(8,128)(2,1)S(1)} %get-tuple-element.56), channel_id=1, source_target_pairs={{0,6},{2,4},{4,2},{6,0},{8,14},{10,12},{12,10},{14,8},{16,22},{18,... | collective-permute-start | bytes 589832 | tf_op jit(solution)/shard_map/ppermute | solution.py:32
  48.3 0.4 collective-permute-start.17
  48.7 0.5 collective-permute-start.18
  49.2 3.1 %collective-permute-done.13.refs_1_ = bf16[256,384]{1,0:T(8,128)(2,1)S(1)} collective-permute-done((bf16[256,384]{1,0:T(8,128)(2,1)S(1)}, bf16[256,384]{1,0:T(8,128)(2,1)S(1)}, u32[]{:S(2)}, u32[]{:S(2)}) %collective-permute-start.13) | collective-permute-done | bytes 196640 | tf_op jit(solution)/shard_map/ppermute | solution.py:32
  52.4 0.5 collective-permute-start.19
  52.8 2.0 %collective-permute-done.14.refs_2_ = bf16[256,384]{1,0:T(8,128)(2,1)S(1)} collective-permute-done((bf16[256,384]{1,0:T(8,128)(2,1)S(1)}, bf16[256,384]{1,0:T(8,128)(2,1)S(1)}, u32[]{:S(2)}, u32[]{:S(2)}) %collective-permute-start.14) | collective-permute-done | bytes 196640 | tf_op jit(solution)/shard_map/ppermute | solution.py:32
  54.8 1.0 %shard_map.89 = (bf16[256,1024]{1,0:T(8,128)(2,1)}, bf16[256,512]{1,0:T(8,128)(2,1)}, f32[8,128]{1,0:T(8,128)S(1)}) custom-call(bf16[256,384]{1,0:T(8,128)(2,1)S(1)} %get-tuple-element.53.refs_0_, bf16[256,384]{1,0:T(8,128)(2,1)S(1)} %collective-permute-done.13.refs_1_, bf16[256,384]{1,0:T(8,128)(2,1)S(1)} %collective-permute-done.14.refs_2_, ...), custom_call_target="tpu_custom_call" | custom-call | bytes 1576960 | tf_op jit(solution)/shard_map/pallas_call | solution.py:39
  55.8 1.7 %collective-permute-done.19.refs_3_ = bf16[256,128]{1,0:T(8,128)(2,1)S(1)} collective-permute-done((bf16[256,128]{1,0:T(8,128)(2,1)S(1)}, bf16[256,128]{1,0:T(8,128)(2,1)S(1)}, u32[]{:S(2)}, u32[]{:S(2)}) %collective-permute-start.19) | collective-permute-done | bytes 65568 | tf_op jit(solution)/shard_map/ppermute | solution.py:32
  57.5 0.8 %shard_map.91 = (bf16[256,512]{1,0:T(8,128)(2,1)}, f32[8,128]{1,0:T(8,128)}) custom-call(bf16[256,128]{1,0:T(8,128)(2,1)S(1)} %get-tuple-element.60.refs_0_, bf16[256,128]{1,0:T(8,128)(2,1)S(1)} %collective-permute-done.17.refs_1_, bf16[256,128]{1,0:T(8,128)(2,1)S(1)} %collective-permute-done.18.refs_2_, ...), custom_call_target="tpu_custom_call" | custom-call | bytes 532480 | tf_op jit(solution)/shard_map/pallas_call | solution.py:39
  (39 shorter events, 1.0 us)
Async XLA Ops:
  0.6 1.0 %copy-start.3 = (bf16[256,512]{1,0:T(8,128)(2,1)S(1)}, bf16[256,512]{1,0:T(8,128)(2,1)}, u32[]{:S(2)}) copy-start(bf16[256,512]{1,0:T(8,128)(2,1)} %refs_0_.2) | copy-start | bytes 786436
  0.6 7.8 %slice-start = ((s8[11010048]{0:T(1024)(128)(4,1)}), s8[4194304]{0:T(1024)(128)(4,1)S(1)}, s32[]{:S(2)}) async-start(s8[11010048]{0:T(1024)(128)(4,1)} %bitcast), calls=%async_computation | async-start | bytes 8388608
  0.7 7.8 %slice-start.1 = ((s8[11010048]{0:T(1024)(128)(4,1)}), s8[4194304]{0:T(1024)(128)(4,1)S(1)}, s32[]{:S(2)}) async-start(s8[11010048]{0:T(1024)(128)(4,1)} %bitcast), calls=%async_computation.1 | async-start | bytes 8388608
  1.6 3.6 %copy-start.1 = (bf16[256,1024]{1,0:T(8,128)(2,1)S(1)}, bf16[256,1024]{1,0:T(8,128)(2,1)}, u32[]{:S(2)}) copy-start(bf16[256,1024]{1,0:T(8,128)(2,1)} %refs_1_.1) | copy-start | bytes 1572868
  1.6 3.6 %copy-start.2 = (bf16[256,512]{1,0:T(8,128)(2,1)S(1)}, bf16[256,512]{1,0:T(8,128)(2,1)}, u32[]{:S(2)}) copy-start(bf16[256,512]{1,0:T(8,128)(2,1)} %refs_0_.3) | copy-start | bytes 786436
  1.6 6.8 %slice-start.2 = ((s8[11010048]{0:T(1024)(128)(4,1)}), s8[2621440]{0:T(1024)(128)(4,1)S(1)}, s32[]{:S(2)}) async-start(s8[11010048]{0:T(1024)(128)(4,1)} %bitcast), calls=%async_computation.2 | async-start | bytes 5242880
  1.6 6.8 %copy-start = (bf16[256,2688]{1,0:T(8,128)(2,1)S(1)}, bf16[256,2688]{1,0:T(8,128)(2,1)}, u32[]{:S(2)}) copy-start(bf16[256,2688]{1,0:T(8,128)(2,1)} %c_ref.3) | copy-start | bytes 4128772
  1.7 8.7 %collective-permute-start = (bf16[256,128]{1,0:T(8,128)(2,1)S(1)}, bf16[256,128]{1,0:T(8,128)(2,1)S(1)}, u32[]{:S(2)}, u32[]{:S(2)}) collective-permute-start(bf16[256,128]{1,0:T(8,128)(2,1)S(1)} %get-tuple-element.36), channel_id=1, source_target_pairs={{0,2},{2,0},{4,6},{6,4},{8,10},{10,8},{12,14},{14,12},{16,18},{18,... | collective-permute-start | bytes 196616 | tf_op jit(solution)/shard_map/ppermute | solution.py:32
  3.2 7.2 %collective-permute-start.1 = (bf16[256,128]{1,0:T(8,128)(2,1)S(1)}, bf16[256,128]{1,0:T(8,128)(2,1)S(1)}, u32[]{:S(2)}, u32[]{:S(2)}) collective-permute-start(bf16[256,128]{1,0:T(8,128)(2,1)S(1)} %get-tuple-element.37), channel_id=1, source_target_pairs={{0,4},{2,6},{4,0},{6,2},{8,12},{10,14},{12,8},{14,10},{16,20},{18,... | collective-permute-start | bytes 196616 | tf_op jit(solution)/shard_map/ppermute | solution.py:32
  4.7 5.9 %collective-permute-start.2 = (bf16[256,128]{1,0:T(8,128)(2,1)S(1)}, bf16[256,128]{1,0:T(8,128)(2,1)S(1)}, u32[]{:S(2)}, u32[]{:S(2)}) collective-permute-start(bf16[256,128]{1,0:T(8,128)(2,1)S(1)} %get-tuple-element.38), channel_id=1, source_target_pairs={{0,6},{2,4},{4,2},{6,0},{8,14},{10,12},{12,10},{14,8},{16,22},{18,... | collective-permute-start | bytes 196616 | tf_op jit(solution)/shard_map/ppermute | solution.py:32
  5.3 10.8 %collective-permute-start.4 = (bf16[256,384]{1,0:T(8,128)(2,1)S(1)}, bf16[256,384]{1,0:T(8,128)(2,1)S(1)}, u32[]{:S(2)}, u32[]{:S(2)}) collective-permute-start(bf16[256,384]{1,0:T(8,128)(2,1)S(1)} %get-tuple-element.40), channel_id=1, source_target_pairs={{0,2},{2,0},{4,6},{6,4},{8,10},{10,8},{12,14},{14,12},{16,18},{18,... | collective-permute-start | bytes 589832 | tf_op jit(solution)/shard_map/ppermute | solution.py:32
  6.9 10.8 %collective-permute-start.5 = (bf16[256,384]{1,0:T(8,128)(2,1)S(1)}, bf16[256,384]{1,0:T(8,128)(2,1)S(1)}, u32[]{:S(2)}, u32[]{:S(2)}) collective-permute-start(bf16[256,384]{1,0:T(8,128)(2,1)S(1)} %get-tuple-element.41), channel_id=1, source_target_pairs={{0,4},{2,6},{4,0},{6,2},{8,12},{10,14},{12,8},{14,10},{16,20},{18,... | collective-permute-start | bytes 589832 | tf_op jit(solution)/shard_map/ppermute | solution.py:32
  10.3 4.0 %collective-permute-start.7 = (bf16[1024,256]{1,0:T(8,128)(2,1)S(1)}, bf16[1024,256]{1,0:T(8,128)(2,1)S(1)}, u32[]{:S(2)}, u32[]{:S(2)}) collective-permute-start(bf16[1024,256]{1,0:T(8,128)(2,1)S(1)} %shard_map.79.refs_4_.refs_0_), channel_id=1, source_target_pairs={{0,1},{1,0},{2,3},{3,2},{4,5},{5,4},{6,7},{7,6},{8,9},{9,8},{10,11... | collective-permute-start | bytes 1572872 | tf_op jit(solution)/shard_map/ppermute | solution.py:32
  10.7 11.5 %collective-permute-start.3 = (bf16[4,256,128]{2,1,0:T(8,128)(2,1)S(1)}, bf16[4,256,128]{2,1,0:T(8,128)(2,1)S(1)}, u32[]{:S(2)}, u32[]{:S(2)}) collective-permute-start(bf16[4,256,128]{2,1,0:T(8,128)(2,1)S(1)} %shard_map.80.own_ref.refs_1_.refs_2_), channel_id=1, source_target_pairs={{0,8},{2,10},{4,12},{6,14},{8,16},{10,18},{12,20},{14,22},{16,24},... | collective-permute-start | bytes 786440 | tf_op jit(solution)/shard_map/ppermute | solution.py:27
  12.0 8.7 %collective-permute-start.6 = (bf16[256,384]{1,0:T(8,128)(2,1)S(1)}, bf16[256,384]{1,0:T(8,128)(2,1)S(1)}, u32[]{:S(2)}, u32[]{:S(2)}) collective-permute-start(bf16[256,384]{1,0:T(8,128)(2,1)S(1)} %get-tuple-element.42), channel_id=1, source_target_pairs={{0,6},{2,4},{4,2},{6,0},{8,14},{10,12},{12,10},{14,8},{16,22},{18,... | collective-permute-start | bytes 589832 | tf_op jit(solution)/shard_map/ppermute | solution.py:32
  14.5 11.5 %collective-permute-start.8 = (bf16[256,256]{1,0:T(8,128)(2,1)S(1)}, bf16[256,256]{1,0:T(8,128)(2,1)S(1)}, u32[]{:S(2)}, u32[]{:S(2)}) collective-permute-start(bf16[256,256]{1,0:T(8,128)(2,1)S(1)} %get-tuple-element.46), channel_id=1, source_target_pairs={{0,2},{2,0},{4,6},{6,4},{8,10},{10,8},{12,14},{14,12},{16,18},{18,... | collective-permute-start | bytes 393224 | tf_op jit(solution)/shard_map/ppermute | solution.py:32
  16.2 9.8 %collective-permute-start.9 = (bf16[256,256]{1,0:T(8,128)(2,1)S(1)}, bf16[256,256]{1,0:T(8,128)(2,1)S(1)}, u32[]{:S(2)}, u32[]{:S(2)}) collective-permute-start(bf16[256,256]{1,0:T(8,128)(2,1)S(1)} %get-tuple-element.47), channel_id=1, source_target_pairs={{0,4},{2,6},{4,0},{6,2},{8,12},{10,14},{12,8},{14,10},{16,20},{18,... | collective-permute-start | bytes 393224 | tf_op jit(solution)/shard_map/ppermute | solution.py:32
  17.7 8.3 %collective-permute-start.10 = (bf16[256,256]{1,0:T(8,128)(2,1)S(1)}, bf16[256,256]{1,0:T(8,128)(2,1)S(1)}, u32[]{:S(2)}, u32[]{:S(2)}) collective-permute-start(bf16[256,256]{1,0:T(8,128)(2,1)S(1)} %get-tuple-element.48), channel_id=1, source_target_pairs={{0,6},{2,4},{4,2},{6,0},{8,14},{10,12},{12,10},{14,8},{16,22},{18,... | collective-permute-start | bytes 393224 | tf_op jit(solution)/shard_map/ppermute | solution.py:32
  20.8 12.7 %collective-permute-start.11 = (bf16[4,256,128]{2,1,0:T(8,128)(2,1)S(1)}, bf16[4,256,128]{2,1,0:T(8,128)(2,1)S(1)}, u32[]{:S(2)}, u32[]{:S(2)}) collective-permute-start(bf16[4,256,128]{2,1,0:T(8,128)(2,1)S(1)} %shard_map.86.own_ref), channel_id=1, source_target_pairs={{0,8},{2,10},{4,12},{6,14},{8,16},{10,18},{12,20},{14,22},{16,24},... | collective-permute-start | bytes 786440 | tf_op jit(solution)/shard_map/ppermute | solution.py:27
  28.2 14.5 %collective-permute-start.12 = (bf16[4,256,128]{2,1,0:T(8,128)(2,1)S(1)}, bf16[4,256,128]{2,1,0:T(8,128)(2,1)S(1)}, u32[]{:S(2)}, u32[]{:S(2)}) collective-permute-start(bf16[4,256,128]{2,1,0:T(8,128)(2,1)S(1)} %get-tuple-element.52), channel_id=1, source_target_pairs={{8,0},{10,2},{12,4},{14,6},{16,8},{18,10},{20,12},{22,14},{24,16},... | collective-permute-start | bytes 786440 | tf_op jit(solution)/shard_map/ppermute | solution.py:27
  38.8 9.5 %collective-permute-start.16 = (bf16[4,256,128]{2,1,0:T(8,128)(2,1)S(1)}, bf16[4,256,128]{2,1,0:T(8,128)(2,1)S(1)}, u32[]{:S(2)}, u32[]{:S(2)}) collective-permute-start(bf16[4,256,128]{2,1,0:T(8,128)(2,1)S(1)} %get-tuple-element.59), channel_id=1, source_target_pairs={{8,0},{10,2},{12,4},{14,6},{16,8},{18,10},{20,12},{22,14},{24,16},... | collective-permute-start | bytes 786440 | tf_op jit(solution)/shard_map/ppermute | solution.py:27
  44.7 7.7 %collective-permute-start.13 = (bf16[256,384]{1,0:T(8,128)(2,1)S(1)}, bf16[256,384]{1,0:T(8,128)(2,1)S(1)}, u32[]{:S(2)}, u32[]{:S(2)}) collective-permute-start(bf16[256,384]{1,0:T(8,128)(2,1)S(1)} %get-tuple-element.54), channel_id=1, source_target_pairs={{0,2},{2,0},{4,6},{6,4},{8,10},{10,8},{12,14},{14,12},{16,18},{18,... | collective-permute-start | bytes 589832 | tf_op jit(solution)/shard_map/ppermute | solution.py:32
  45.1 9.7 %collective-permute-start.14 = (bf16[256,384]{1,0:T(8,128)(2,1)S(1)}, bf16[256,384]{1,0:T(8,128)(2,1)S(1)}, u32[]{:S(2)}, u32[]{:S(2)}) collective-permute-start(bf16[256,384]{1,0:T(8,128)(2,1)S(1)} %get-tuple-element.55), channel_id=1, source_target_pairs={{0,4},{2,6},{4,0},{6,2},{8,12},{10,14},{12,8},{14,10},{16,20},{18,... | collective-permute-start | bytes 589832 | tf_op jit(solution)/shard_map/ppermute | solution.py:32
  45.6 9.2 %collective-permute-start.15 = (bf16[256,384]{1,0:T(8,128)(2,1)S(1)}, bf16[256,384]{1,0:T(8,128)(2,1)S(1)}, u32[]{:S(2)}, u32[]{:S(2)}) collective-permute-start(bf16[256,384]{1,0:T(8,128)(2,1)S(1)} %get-tuple-element.56), channel_id=1, source_target_pairs={{0,6},{2,4},{4,2},{6,0},{8,14},{10,12},{12,10},{14,8},{16,22},{18,... | collective-permute-start | bytes 589832 | tf_op jit(solution)/shard_map/ppermute | solution.py:32
  48.3 7.5 %collective-permute-start.17 = (bf16[256,128]{1,0:T(8,128)(2,1)S(1)}, bf16[256,128]{1,0:T(8,128)(2,1)S(1)}, u32[]{:S(2)}, u32[]{:S(2)}) collective-permute-start(bf16[256,128]{1,0:T(8,128)(2,1)S(1)} %get-tuple-element.61), channel_id=1, source_target_pairs={{0,2},{2,0},{4,6},{6,4},{8,10},{10,8},{12,14},{14,12},{16,18},{18,... | collective-permute-start | bytes 196616 | tf_op jit(solution)/shard_map/ppermute | solution.py:32
  48.7 7.1 %collective-permute-start.18 = (bf16[256,128]{1,0:T(8,128)(2,1)S(1)}, bf16[256,128]{1,0:T(8,128)(2,1)S(1)}, u32[]{:S(2)}, u32[]{:S(2)}) collective-permute-start(bf16[256,128]{1,0:T(8,128)(2,1)S(1)} %get-tuple-element.62), channel_id=1, source_target_pairs={{0,4},{2,6},{4,0},{6,2},{8,12},{10,14},{12,8},{14,10},{16,20},{18,... | collective-permute-start | bytes 196616 | tf_op jit(solution)/shard_map/ppermute | solution.py:32
  52.4 5.2 %collective-permute-start.19 = (bf16[256,128]{1,0:T(8,128)(2,1)S(1)}, bf16[256,128]{1,0:T(8,128)(2,1)S(1)}, u32[]{:S(2)}, u32[]{:S(2)}) collective-permute-start(bf16[256,128]{1,0:T(8,128)(2,1)S(1)} %get-tuple-element.63), channel_id=1, source_target_pairs={{0,6},{2,4},{4,2},{6,0},{8,14},{10,12},{12,10},{14,8},{16,22},{18,... | collective-permute-start | bytes 196616 | tf_op jit(solution)/shard_map/ppermute | solution.py:32

commit v15 on v12

--- a/solution.py
+++ b/solution.py
@@ -188,26 +188,30 @@
             @pl.loop(0, z.group)
             def _(b):
                 qt = qt_ref[head, b]
+                last = lax.dot_general(k_all[b + z.back], qt, NN, preferred_element_type=jnp.float32)
                 top = None
-                for c in range(z.span):
+                for c in range(z.back):
                     s = lax.dot_general(k_all[b + c], qt, NN, preferred_element_type=jnp.float32)
+                    there = first + b + c >= z.back
                     if c == 0:
-                        s = jnp.where(key_id > query_id, s, -jnp.inf)
-                    if c == z.back:
-                        s = jnp.where(key_id <= query_id, s, -jnp.inf)
+                        s = jnp.where(key_id > query_id, s + jnp.where(there, 0.0, -jnp.inf), last)
                     s_all[c] = s
                     here = jnp.max(s, axis=0, keepdims=True)
-                    if c < z.back:
-                        here = jnp.where(first + b + c >= z.back, here, -jnp.inf)
+                    if c > 0:
+                        here = jnp.where(there, here, -jnp.inf)
                     top = here if top is None else jnp.maximum(top, here)
                 norm = jnp.zeros((1, z.wide), jnp.float32)
-                for c in range(z.span):
+                for c in range(z.back):
                     base = top
-                    if c < z.back:
+                    if c > 0:
                         base = jnp.where(first + b + c >= z.back, top, jnp.inf)
                     e = jnp.exp2((s_all[c] - base) * factor)
                     norm = norm + jnp.sum(e, axis=0, keepdims=True)
-                    e_ref[head, b, c] = e.astype(jnp.bfloat16)
+                    if c == 0:
+                        e_ref[head, b, 0] = jnp.where(key_id > query_id, e, 0.0).astype(jnp.bfloat16)
+                        e_ref[head, b, z.back] = jnp.where(key_id > query_id, 0.0, e).astype(jnp.bfloat16)
+                    else:
+                        e_ref[head, b, c] = e.astype(jnp.bfloat16)
                 inverse_ref[head, b] = 1.0 / norm
 
     outs = [

time: 57.7 us -> 57.7 us (level)
  no operation moved by 1% of the time
where the time goes in v15:
time: 57.7 us; the launch traced here: 57.2 us
  starting transfers between devices  25.2 us (44%)
  Pallas kernels  19.4 us (34%)
  waiting for transfers between devices  10.6 us (18%)
  local copies, waits for them, and re-layouts  1.28 us (2%)
  between operations  0.86 us (1%)
    pallas_call x15, Pallas kernels, run(): pl.pallas_call(body, out_shape=tuple(outs), in_specs=specs or [SMEM if a....  19.4 us
    ppermute x16, starting transfers between devices, swapped(): lax.ppermute(value, axis, [(source, source ^ bits) for source in range(co...  19.1 us
    ppermute x16, waiting for transfers between devices, swapped(): lax.ppermute(value, axis, [(source, source ^ bits) for source in range(co...  8.25 us
    ppermute x3, starting transfers between devices, shifted(): lax.ppermute(value, axis, [(source, source + steps) for source in range(l...  6.02 us
    ppermute x3, waiting for transfers between devices, shifted(): lax.ppermute(value, axis, [(source, source + steps) for source in range(l...  2.33 us
    unnamed x14, local copies, waits for them, and re-layouts  1.28 us
  transfers between devices with their start and end apart: 19, of which 5 were waited for; matrix products, arithmetic and copies ran while one was open for 0% of the time, Pallas kernels for 29%

profile of v15, /device:TPU:24, one launch (start us, length us, event | category | flops | bytes accessed | tf_op | source)
XLA Modules:
  0.0 57.2 jit_solution(12784208919494472460)
XLA Ops:
  0.7 0.9 %copy-done.3 = bf16[256,512]{1,0:T(8,128)(2,1)S(1)} copy-done((bf16[256,512]{1,0:T(8,128)(2,1)S(1)}, bf16[256,512]{1,0:T(8,128)(2,1)}, u32[]{:S(2)}) %copy-start.3) | copy-done | bytes 262168
  1.8 1.6 %collective-permute-start = (bf16[256,256]{1,0:T(8,128)(2,1)S(1)}, bf16[256,256]{1,0:T(8,128)(2,1)S(1)}, u32[]{:S(2)}, u32[]{:S(2)}) collective-permute-start(bf16[256,256]{1,0:T(8,128)(2,1)S(1)} %get-tuple-element.36), channel_id=1, source_target_pairs={{0,2},{2,0},{4,6},{6,4},{8,10},{10,8},{12,14},{14,12},{16,18},{18,... | collective-permute-start | bytes 393224 | tf_op jit(solution)/shard_map/ppermute | solution.py:32
  3.3 1.5 %collective-permute-start.1 = (bf16[256,256]{1,0:T(8,128)(2,1)S(1)}, bf16[256,256]{1,0:T(8,128)(2,1)S(1)}, u32[]{:S(2)}, u32[]{:S(2)}) collective-permute-start(bf16[256,256]{1,0:T(8,128)(2,1)S(1)} %get-tuple-element.37), channel_id=1, source_target_pairs={{0,4},{2,6},{4,0},{6,2},{8,12},{10,14},{12,8},{14,10},{16,20},{18,... | collective-permute-start | bytes 393224 | tf_op jit(solution)/shard_map/ppermute | solution.py:32
  4.8 0.5 collective-permute-start.2
  5.7 1.9 %shard_map.79.refs_4_.refs_1_ = bf16[1024,256]{1,0:T(8,128)(2,1)S(1)} custom-call(bf16[2048,2688]{1,0:T(8,128)(2,1)S(1)} %bitcast.1, bf16[256,2688]{1,0:T(8,128)(2,1)S(1)} %copy-done, bf16[256,256]{1,0:T(8,128)(2,1)S(1)} %get-tuple-element.39.refs_0_), custom_call_target="tpu_custom_call" | custom-call | flops 1409286144 | bytes 13041664 | tf_op jit(solution)/shard_map/pallas_call | solution.py:39
  7.7 3.4 %collective-permute-done.1.refs_2_ = bf16[256,256]{1,0:T(8,128)(2,1)S(1)} collective-permute-done((bf16[256,256]{1,0:T(8,128)(2,1)S(1)}, bf16[256,256]{1,0:T(8,128)(2,1)S(1)}, u32[]{:S(2)}, u32[]{:S(2)}) %collective-permute-start.1) | collective-permute-done | bytes 131104 | tf_op jit(solution)/shard_map/ppermute | solution.py:32
  11.2 1.3 %collective-permute-start.3 = (bf16[4,256,256]{2,1,0:T(8,128)(2,1)S(1)}, bf16[4,256,256]{2,1,0:T(8,128)(2,1)S(1)}, u32[]{:S(2)}, u32[]{:S(2)}) collective-permute-start(bf16[4,256,256]{2,1,0:T(8,128)(2,1)S(1)} %shard_map.80.refs_0_.refs_2_.own_ref), channel_id=1, source_target_pairs={{0,8},{2,10},{4,12},{6,14},{8,16},{10,18},{12,20},{14,22},{16,24},... | collective-permute-start | bytes 1572872 | tf_op jit(solution)/shard_map/ppermute | solution.py:27
  12.5 1.3 %collective-permute-start.4 = (bf16[256,256]{1,0:T(8,128)(2,1)S(1)}, bf16[256,256]{1,0:T(8,128)(2,1)S(1)}, u32[]{:S(2)}, u32[]{:S(2)}) collective-permute-start(bf16[256,256]{1,0:T(8,128)(2,1)S(1)} %get-tuple-element.40), channel_id=1, source_target_pairs={{0,2},{2,0},{4,6},{6,4},{8,10},{10,8},{12,14},{14,12},{16,18},{18,... | collective-permute-start | bytes 393224 | tf_op jit(solution)/shard_map/ppermute | solution.py:32
  13.7 0.8 %collective-permute-start.5 = (bf16[256,256]{1,0:T(8,128)(2,1)S(1)}, bf16[256,256]{1,0:T(8,128)(2,1)S(1)}, u32[]{:S(2)}, u32[]{:S(2)}) collective-permute-start(bf16[256,256]{1,0:T(8,128)(2,1)S(1)} %get-tuple-element.41), channel_id=1, source_target_pairs={{0,4},{2,6},{4,0},{6,2},{8,12},{10,14},{12,8},{14,10},{16,20},{18,... | collective-permute-start | bytes 393224 | tf_op jit(solution)/shard_map/ppermute | solution.py:32
  14.6 1.4 %collective-permute-start.6 = (bf16[256,256]{1,0:T(8,128)(2,1)S(1)}, bf16[256,256]{1,0:T(8,128)(2,1)S(1)}, u32[]{:S(2)}, u32[]{:S(2)}) collective-permute-start(bf16[256,256]{1,0:T(8,128)(2,1)S(1)} %get-tuple-element.42), channel_id=1, source_target_pairs={{0,6},{2,4},{4,2},{6,0},{8,14},{10,12},{12,10},{14,8},{16,22},{18,... | collective-permute-start | bytes 393224 | tf_op jit(solution)/shard_map/ppermute | solution.py:32
  16.0 1.9 %shard_map.83.refs_0_ = bf16[1024,256]{1,0:T(8,128)(2,1)S(1)} custom-call(bf16[2048,2688]{1,0:T(8,128)(2,1)S(1)} %bitcast.1, bf16[256,2688]{1,0:T(8,128)(2,1)S(1)} %copy-done, bf16[4,256,256]{2,1,0:T(8,128)(2,1)S(1)} %shard_map.80.refs_0_.refs_2_.own_ref, bf16[1024,256]{1,0:T(8,128)(2,1)S(1)} %shard_map.79.refs_4_.refs_1_), custom_call_target="tpu_custom_call" | custom-call | flops 1409286144 | bytes 13959168 | tf_op jit(solution)/shard_map/pallas_call | solution.py:39
  18.1 1.3 %collective-permute-start.8 = (bf16[256,256]{1,0:T(8,128)(2,1)S(1)}, bf16[256,256]{1,0:T(8,128)(2,1)S(1)}, u32[]{:S(2)}, u32[]{:S(2)}) collective-permute-start(bf16[256,256]{1,0:T(8,128)(2,1)S(1)} %get-tuple-element.46), channel_id=1, source_target_pairs={{0,2},{2,0},{4,6},{6,4},{8,10},{10,8},{12,14},{14,12},{16,18},{18,... | collective-permute-start | bytes 393224 | tf_op jit(solution)/shard_map/ppermute | solution.py:32
  19.3 0.8 %collective-permute-start.9 = (bf16[256,256]{1,0:T(8,128)(2,1)S(1)}, bf16[256,256]{1,0:T(8,128)(2,1)S(1)}, u32[]{:S(2)}, u32[]{:S(2)}) collective-permute-start(bf16[256,256]{1,0:T(8,128)(2,1)S(1)} %get-tuple-element.47), channel_id=1, source_target_pairs={{0,4},{2,6},{4,0},{6,2},{8,12},{10,14},{12,8},{14,10},{16,20},{18,... | collective-permute-start | bytes 393224 | tf_op jit(solution)/shard_map/ppermute | solution.py:32
  20.2 2.7 %collective-permute-start.10 = (bf16[256,256]{1,0:T(8,128)(2,1)S(1)}, bf16[256,256]{1,0:T(8,128)(2,1)S(1)}, u32[]{:S(2)}, u32[]{:S(2)}) collective-permute-start(bf16[256,256]{1,0:T(8,128)(2,1)S(1)} %get-tuple-element.48), channel_id=1, source_target_pairs={{0,6},{2,4},{4,2},{6,0},{8,14},{10,12},{12,10},{14,8},{16,22},{18,... | collective-permute-start | bytes 393224 | tf_op jit(solution)/shard_map/ppermute | solution.py:32
  23.1 2.3 %collective-permute-done.3.refs_1_.refs_0_ = bf16[4,256,256]{2,1,0:T(8,128)(2,1)S(1)} collective-permute-done((bf16[4,256,256]{2,1,0:T(8,128)(2,1)S(1)}, bf16[4,256,256]{2,1,0:T(8,128)(2,1)S(1)}, u32[]{:S(2)}, u32[]{:S(2)}) %collective-permute-start.3) | collective-permute-done | bytes 524320 | tf_op jit(solution)/shard_map/ppermute | solution.py:27
  25.4 3.8 %shard_map.82 = (bf16[1,4,5,256,512]{4,3,2,1,0:T(8,128)(2,1)S(1)}, f32[1,4,1,512]{3,2,1,0:T(1,128)S(1)}) custom-call(bf16[4,256,256]{2,1,0:T(8,128)(2,1)S(1)} %shard_map.80.refs_0_.refs_2_.own_ref, bf16[4,256,256]{2,1,0:T(8,128)(2,1)S(1)} %collective-permute-done.3.refs_1_.refs_0_, bf16[1,4,128,512]{3,2,1,0:T(8,128)(2,1)S(1)} %shard_map.81.refs_2_.qt_ref), custom_call_target="tpu_custom_call" | custom-call | flops 671088640 | bytes 6823936 | tf_op jit(solution)/shard_map/pallas_call | solution.py:39
  29.2 2.2 %shard_map.85 = (bf16[1,4,128,512]{3,2,1,0:T(8,128)(2,1)S(1)}, f32[4,256,128]{2,1,0:T(8,128)S(1)}, bf16[4,256,128]{2,1,0:T(8,128)(2,1)S(1)}) custom-call(bf16[1,4,5,256,512]{4,3,2,1,0:T(8,128)(2,1)S(1)} %get-tuple-element.43.e_ref, f32[1,4,1,512]{3,2,1,0:T(1,128)S(1)} %get-tuple-element.44.inverse_ref, bf16[256,256]{1,0:T(8,128)(2,1)S(1)} %get-tuple-element.45.refs_0_, ...), custom_call_target="tpu_custom_call" | custom-call | flops 671088640 | bytes 7086080 | tf_op jit(solution)/shard_map/pallas_call | solution.py:39
  31.4 2.4 %collective-permute-start.11 = (bf16[4,256,128]{2,1,0:T(8,128)(2,1)S(1)}, bf16[4,256,128]{2,1,0:T(8,128)(2,1)S(1)}, u32[]{:S(2)}, u32[]{:S(2)}) collective-permute-start(bf16[4,256,128]{2,1,0:T(8,128)(2,1)S(1)} %get-tuple-element.52), channel_id=1, source_target_pairs={{8,0},{10,2},{12,4},{14,6},{16,8},{18,10},{20,12},{22,14},{24,16},... | collective-permute-start | bytes 786440 | tf_op jit(solution)/shard_map/ppermute | solution.py:27
  33.8 5.4 %shard_map.86 = (bf16[1,4,5,256,512]{4,3,2,1,0:T(8,128)(2,1)S(1)}, f32[4,256,128]{2,1,0:T(8,128)S(1)}, bf16[4,256,128]{2,1,0:T(8,128)(2,1)S(1)}) custom-call(bf16[1,4,5,256,512]{4,3,2,1,0:T(8,128)(2,1)S(1)} %get-tuple-element.43.e_ref, f32[1,4,1,512]{3,2,1,0:T(1,128)S(1)} %get-tuple-element.44.inverse_ref, ...), custom_call_target="tpu_custom_call" | custom-call | flops 1342177280 | bytes 13377536 | tf_op jit(solution)/shard_map/pallas_call | solution.py:39
  39.2 2.4 %collective-permute-start.15 = (bf16[4,256,128]{2,1,0:T(8,128)(2,1)S(1)}, bf16[4,256,128]{2,1,0:T(8,128)(2,1)S(1)}, u32[]{:S(2)}, u32[]{:S(2)}) collective-permute-start(bf16[4,256,128]{2,1,0:T(8,128)(2,1)S(1)} %get-tuple-element.59), channel_id=1, source_target_pairs={{8,0},{10,2},{12,4},{14,6},{16,8},{18,10},{20,12},{22,14},{24,16},... | collective-permute-start | bytes 786440 | tf_op jit(solution)/shard_map/ppermute | solution.py:27
  41.5 2.0 %shard_map.87 = (bf16[256,384]{1,0:T(8,128)(2,1)S(1)}, bf16[256,384]{1,0:T(8,128)(2,1)S(1)}, bf16[256,384]{1,0:T(8,128)(2,1)S(1)}, bf16[256,384]{1,0:T(8,128)(2,1)S(1)}) custom-call(bf16[1,4,5,256,512]{4,3,2,1,0:T(8,128)(2,1)S(1)} %get-tuple-element.50.ds_ref, f32[1,4,1,512]{3,2,1,0:T(1,128)S(1)} %get-tuple-element.44.inverse_ref, ...), custom_call_target="tpu_custom_call" | custom-call | flops 671088640 | bytes 7872512 | tf_op jit(solution)/shard_map/pallas_call | solution.py:39
  43.5 1.7 %collective-permute-start.12 = (bf16[256,384]{1,0:T(8,128)(2,1)S(1)}, bf16[256,384]{1,0:T(8,128)(2,1)S(1)}, u32[]{:S(2)}, u32[]{:S(2)}) collective-permute-start(bf16[256,384]{1,0:T(8,128)(2,1)S(1)} %get-tuple-element.54), channel_id=1, source_target_pairs={{0,2},{2,0},{4,6},{6,4},{8,10},{10,8},{12,14},{14,12},{16,18},{18,... | collective-permute-start | bytes 589832 | tf_op jit(solution)/shard_map/ppermute | solution.py:32
  45.2 0.5 collective-permute-start.13
  45.7 1.3 %collective-permute-start.14 = (bf16[256,384]{1,0:T(8,128)(2,1)S(1)}, bf16[256,384]{1,0:T(8,128)(2,1)S(1)}, u32[]{:S(2)}, u32[]{:S(2)}) collective-permute-start(bf16[256,384]{1,0:T(8,128)(2,1)S(1)} %get-tuple-element.56), channel_id=1, source_target_pairs={{0,6},{2,4},{4,2},{6,0},{8,14},{10,12},{12,10},{14,8},{16,22},{18,... | collective-permute-start | bytes 589832 | tf_op jit(solution)/shard_map/ppermute | solution.py:32
  47.1 1.7 %collective-permute-start.16 = (bf16[256,128]{1,0:T(8,128)(2,1)S(1)}, bf16[256,128]{1,0:T(8,128)(2,1)S(1)}, u32[]{:S(2)}, u32[]{:S(2)}) collective-permute-start(bf16[256,128]{1,0:T(8,128)(2,1)S(1)} %get-tuple-element.61), channel_id=1, source_target_pairs={{0,2},{2,0},{4,6},{6,4},{8,10},{10,8},{12,14},{14,12},{16,18},{18,... | collective-permute-start | bytes 196616 | tf_op jit(solution)/shard_map/ppermute | solution.py:32
  48.8 0.5 collective-permute-start.17
  49.3 2.0 %collective-permute-done.12.refs_1_ = bf16[256,384]{1,0:T(8,128)(2,1)S(1)} collective-permute-done((bf16[256,384]{1,0:T(8,128)(2,1)S(1)}, bf16[256,384]{1,0:T(8,128)(2,1)S(1)}, u32[]{:S(2)}, u32[]{:S(2)}) %collective-permute-start.12) | collective-permute-done | bytes 196640 | tf_op jit(solution)/shard_map/ppermute | solution.py:32
  51.3 1.4 %collective-permute-start.18 = (bf16[256,128]{1,0:T(8,128)(2,1)S(1)}, bf16[256,128]{1,0:T(8,128)(2,1)S(1)}, u32[]{:S(2)}, u32[]{:S(2)}) collective-permute-start(bf16[256,128]{1,0:T(8,128)(2,1)S(1)} %get-tuple-element.63), channel_id=1, source_target_pairs={{0,6},{2,4},{4,2},{6,0},{8,14},{10,12},{12,10},{14,8},{16,22},{18,... | collective-permute-start | bytes 196616 | tf_op jit(solution)/shard_map/ppermute | solution.py:32
  52.7 2.2 %collective-permute-done.13.refs_2_ = bf16[256,384]{1,0:T(8,128)(2,1)S(1)} collective-permute-done((bf16[256,384]{1,0:T(8,128)(2,1)S(1)}, bf16[256,384]{1,0:T(8,128)(2,1)S(1)}, u32[]{:S(2)}, u32[]{:S(2)}) %collective-permute-start.13) | collective-permute-done | bytes 196640 | tf_op jit(solution)/shard_map/ppermute | solution.py:32
  54.8 1.0 %shard_map.88 = (bf16[256,1024]{1,0:T(8,128)(2,1)}, bf16[256,512]{1,0:T(8,128)(2,1)}, f32[8,128]{1,0:T(8,128)S(1)}) custom-call(bf16[256,384]{1,0:T(8,128)(2,1)S(1)} %get-tuple-element.53.refs_0_, bf16[256,384]{1,0:T(8,128)(2,1)S(1)} %collective-permute-done.12.refs_1_, bf16[256,384]{1,0:T(8,128)(2,1)S(1)} %collective-permute-done.13.refs_2_, ...), custom_call_target="tpu_custom_call" | custom-call | bytes 1576960 | tf_op jit(solution)/shard_map/pallas_call | solution.py:39
  55.8 0.7 %collective-permute-done.18.refs_3_ = bf16[256,128]{1,0:T(8,128)(2,1)S(1)} collective-permute-done((bf16[256,128]{1,0:T(8,128)(2,1)S(1)}, bf16[256,128]{1,0:T(8,128)(2,1)S(1)}, u32[]{:S(2)}, u32[]{:S(2)}) %collective-permute-start.18) | collective-permute-done | bytes 65568 | tf_op jit(solution)/shard_map/ppermute | solution.py:32
  56.5 0.8 %shard_map.90 = (bf16[256,512]{1,0:T(8,128)(2,1)}, f32[8,128]{1,0:T(8,128)}) custom-call(bf16[256,128]{1,0:T(8,128)(2,1)S(1)} %get-tuple-element.60.refs_0_, bf16[256,128]{1,0:T(8,128)(2,1)S(1)} %collective-permute-done.16.refs_1_, bf16[256,128]{1,0:T(8,128)(2,1)S(1)} %collective-permute-done.17.refs_2_, ...), custom_call_target="tpu_custom_call" | custom-call | bytes 532480 | tf_op jit(solution)/shard_map/pallas_call | solution.py:39
  (36 shorter events, 1.1 us)
Async XLA Ops:
  0.6 1.0 %copy-start.3 = (bf16[256,512]{1,0:T(8,128)(2,1)S(1)}, bf16[256,512]{1,0:T(8,128)(2,1)}, u32[]{:S(2)}) copy-start(bf16[256,512]{1,0:T(8,128)(2,1)} %v_ref.1) | copy-start | bytes 786436
  0.6 1.0 %copy-start.2 = (bf16[256,512]{1,0:T(8,128)(2,1)S(1)}, bf16[256,512]{1,0:T(8,128)(2,1)}, u32[]{:S(2)}) copy-start(bf16[256,512]{1,0:T(8,128)(2,1)} %k_ref.1) | copy-start | bytes 786436
  0.7 4.7 %slice-start = ((s8[11010048]{0:T(1024)(128)(4,1)}), s8[4194304]{0:T(1024)(128)(4,1)S(1)}, s32[]{:S(2)}) async-start(s8[11010048]{0:T(1024)(128)(4,1)} %bitcast), calls=%async_computation | async-start | bytes 8388608
  0.7 4.7 %slice-start.1 = ((s8[11010048]{0:T(1024)(128)(4,1)}), s8[4194304]{0:T(1024)(128)(4,1)S(1)}, s32[]{:S(2)}) async-start(s8[11010048]{0:T(1024)(128)(4,1)} %bitcast), calls=%async_computation.1 | async-start | bytes 8388608
  1.7 3.7 %copy-start.1 = (bf16[256,1024]{1,0:T(8,128)(2,1)S(1)}, bf16[256,1024]{1,0:T(8,128)(2,1)}, u32[]{:S(2)}) copy-start(bf16[256,1024]{1,0:T(8,128)(2,1)} %q_ref.1) | copy-start | bytes 1572868
  1.7 3.8 %slice-start.2 = ((s8[11010048]{0:T(1024)(128)(4,1)}), s8[2621440]{0:T(1024)(128)(4,1)S(1)}, s32[]{:S(2)}) async-start(s8[11010048]{0:T(1024)(128)(4,1)} %bitcast), calls=%async_computation.2 | async-start | bytes 5242880
  1.7 4.0 %copy-start = (bf16[256,2688]{1,0:T(8,128)(2,1)S(1)}, bf16[256,2688]{1,0:T(8,128)(2,1)}, u32[]{:S(2)}) copy-start(bf16[256,2688]{1,0:T(8,128)(2,1)} %c_ref.3) | copy-start | bytes 4128772
  1.8 5.9 %collective-permute-start = (bf16[256,256]{1,0:T(8,128)(2,1)S(1)}, bf16[256,256]{1,0:T(8,128)(2,1)S(1)}, u32[]{:S(2)}, u32[]{:S(2)}) collective-permute-start(bf16[256,256]{1,0:T(8,128)(2,1)S(1)} %get-tuple-element.36), channel_id=1, source_target_pairs={{0,2},{2,0},{4,6},{6,4},{8,10},{10,8},{12,14},{14,12},{16,18},{18,... | collective-permute-start | bytes 393224 | tf_op jit(solution)/shard_map/ppermute | solution.py:32
  3.3 7.8 %collective-permute-start.1 = (bf16[256,256]{1,0:T(8,128)(2,1)S(1)}, bf16[256,256]{1,0:T(8,128)(2,1)S(1)}, u32[]{:S(2)}, u32[]{:S(2)}) collective-permute-start(bf16[256,256]{1,0:T(8,128)(2,1)S(1)} %get-tuple-element.37), channel_id=1, source_target_pairs={{0,4},{2,6},{4,0},{6,2},{8,12},{10,14},{12,8},{14,10},{16,20},{18,... | collective-permute-start | bytes 393224 | tf_op jit(solution)/shard_map/ppermute | solution.py:32
  4.8 6.3 %collective-permute-start.2 = (bf16[256,256]{1,0:T(8,128)(2,1)S(1)}, bf16[256,256]{1,0:T(8,128)(2,1)S(1)}, u32[]{:S(2)}, u32[]{:S(2)}) collective-permute-start(bf16[256,256]{1,0:T(8,128)(2,1)S(1)} %get-tuple-element.38), channel_id=1, source_target_pairs={{0,6},{2,4},{4,2},{6,0},{8,14},{10,12},{12,10},{14,8},{16,22},{18,... | collective-permute-start | bytes 393224 | tf_op jit(solution)/shard_map/ppermute | solution.py:32
  7.6 10.3 %collective-permute-start.7 = (bf16[1024,256]{1,0:T(8,128)(2,1)S(1)}, bf16[1024,256]{1,0:T(8,128)(2,1)S(1)}, u32[]{:S(2)}, u32[]{:S(2)}) collective-permute-start(bf16[1024,256]{1,0:T(8,128)(2,1)S(1)} %shard_map.79.refs_4_.refs_1_), channel_id=1, source_target_pairs={{0,1},{1,0},{2,3},{3,2},{4,5},{5,4},{6,7},{7,6},{8,9},{9,8},{10,11... | collective-permute-start | bytes 1572872 | tf_op jit(solution)/shard_map/ppermute | solution.py:32
  11.2 14.3 %collective-permute-start.3 = (bf16[4,256,256]{2,1,0:T(8,128)(2,1)S(1)}, bf16[4,256,256]{2,1,0:T(8,128)(2,1)S(1)}, u32[]{:S(2)}, u32[]{:S(2)}) collective-permute-start(bf16[4,256,256]{2,1,0:T(8,128)(2,1)S(1)} %shard_map.80.refs_0_.refs_2_.own_ref), channel_id=1, source_target_pairs={{0,8},{2,10},{4,12},{6,14},{8,16},{10,18},{12,20},{14,22},{16,24},... | collective-permute-start | bytes 1572872 | tf_op jit(solution)/shard_map/ppermute | solution.py:27
  12.5 6.9 %collective-permute-start.4 = (bf16[256,256]{1,0:T(8,128)(2,1)S(1)}, bf16[256,256]{1,0:T(8,128)(2,1)S(1)}, u32[]{:S(2)}, u32[]{:S(2)}) collective-permute-start(bf16[256,256]{1,0:T(8,128)(2,1)S(1)} %get-tuple-element.40), channel_id=1, source_target_pairs={{0,2},{2,0},{4,6},{6,4},{8,10},{10,8},{12,14},{14,12},{16,18},{18,... | collective-permute-start | bytes 393224 | tf_op jit(solution)/shard_map/ppermute | solution.py:32
  13.7 6.4 %collective-permute-start.5 = (bf16[256,256]{1,0:T(8,128)(2,1)S(1)}, bf16[256,256]{1,0:T(8,128)(2,1)S(1)}, u32[]{:S(2)}, u32[]{:S(2)}) collective-permute-start(bf16[256,256]{1,0:T(8,128)(2,1)S(1)} %get-tuple-element.41), channel_id=1, source_target_pairs={{0,4},{2,6},{4,0},{6,2},{8,12},{10,14},{12,8},{14,10},{16,20},{18,... | collective-permute-start | bytes 393224 | tf_op jit(solution)/shard_map/ppermute | solution.py:32
  14.6 8.3 %collective-permute-start.6 = (bf16[256,256]{1,0:T(8,128)(2,1)S(1)}, bf16[256,256]{1,0:T(8,128)(2,1)S(1)}, u32[]{:S(2)}, u32[]{:S(2)}) collective-permute-start(bf16[256,256]{1,0:T(8,128)(2,1)S(1)} %get-tuple-element.42), channel_id=1, source_target_pairs={{0,6},{2,4},{4,2},{6,0},{8,14},{10,12},{12,10},{14,8},{16,22},{18,... | collective-permute-start | bytes 393224 | tf_op jit(solution)/shard_map/ppermute | solution.py:32
  18.1 11.1 %collective-permute-start.8 = (bf16[256,256]{1,0:T(8,128)(2,1)S(1)}, bf16[256,256]{1,0:T(8,128)(2,1)S(1)}, u32[]{:S(2)}, u32[]{:S(2)}) collective-permute-start(bf16[256,256]{1,0:T(8,128)(2,1)S(1)} %get-tuple-element.46), channel_id=1, source_target_pairs={{0,2},{2,0},{4,6},{6,4},{8,10},{10,8},{12,14},{14,12},{16,18},{18,... | collective-permute-start | bytes 393224 | tf_op jit(solution)/shard_map/ppermute | solution.py:32
  19.3 9.9 %collective-permute-start.9 = (bf16[256,256]{1,0:T(8,128)(2,1)S(1)}, bf16[256,256]{1,0:T(8,128)(2,1)S(1)}, u32[]{:S(2)}, u32[]{:S(2)}) collective-permute-start(bf16[256,256]{1,0:T(8,128)(2,1)S(1)} %get-tuple-element.47), channel_id=1, source_target_pairs={{0,4},{2,6},{4,0},{6,2},{8,12},{10,14},{12,8},{14,10},{16,20},{18,... | collective-permute-start | bytes 393224 | tf_op jit(solution)/shard_map/ppermute | solution.py:32
  20.2 9.0 %collective-permute-start.10 = (bf16[256,256]{1,0:T(8,128)(2,1)S(1)}, bf16[256,256]{1,0:T(8,128)(2,1)S(1)}, u32[]{:S(2)}, u32[]{:S(2)}) collective-permute-start(bf16[256,256]{1,0:T(8,128)(2,1)S(1)} %get-tuple-element.48), channel_id=1, source_target_pairs={{0,6},{2,4},{4,2},{6,0},{8,14},{10,12},{12,10},{14,8},{16,22},{18,... | collective-permute-start | bytes 393224 | tf_op jit(solution)/shard_map/ppermute | solution.py:32
  31.4 10.1 %collective-permute-start.11 = (bf16[4,256,128]{2,1,0:T(8,128)(2,1)S(1)}, bf16[4,256,128]{2,1,0:T(8,128)(2,1)S(1)}, u32[]{:S(2)}, u32[]{:S(2)}) collective-permute-start(bf16[4,256,128]{2,1,0:T(8,128)(2,1)S(1)} %get-tuple-element.52), channel_id=1, source_target_pairs={{8,0},{10,2},{12,4},{14,6},{16,8},{18,10},{20,12},{22,14},{24,16},... | collective-permute-start | bytes 786440 | tf_op jit(solution)/shard_map/ppermute | solution.py:27
  39.2 7.9 %collective-permute-start.15 = (bf16[4,256,128]{2,1,0:T(8,128)(2,1)S(1)}, bf16[4,256,128]{2,1,0:T(8,128)(2,1)S(1)}, u32[]{:S(2)}, u32[]{:S(2)}) collective-permute-start(bf16[4,256,128]{2,1,0:T(8,128)(2,1)S(1)} %get-tuple-element.59), channel_id=1, source_target_pairs={{8,0},{10,2},{12,4},{14,6},{16,8},{18,10},{20,12},{22,14},{24,16},... | collective-permute-start | bytes 786440 | tf_op jit(solution)/shard_map/ppermute | solution.py:27
  43.5 7.8 %collective-permute-start.12 = (bf16[256,384]{1,0:T(8,128)(2,1)S(1)}, bf16[256,384]{1,0:T(8,128)(2,1)S(1)}, u32[]{:S(2)}, u32[]{:S(2)}) collective-permute-start(bf16[256,384]{1,0:T(8,128)(2,1)S(1)} %get-tuple-element.54), channel_id=1, source_target_pairs={{0,2},{2,0},{4,6},{6,4},{8,10},{10,8},{12,14},{14,12},{16,18},{18,... | collective-permute-start | bytes 589832 | tf_op jit(solution)/shard_map/ppermute | solution.py:32
  45.2 9.6 %collective-permute-start.13 = (bf16[256,384]{1,0:T(8,128)(2,1)S(1)}, bf16[256,384]{1,0:T(8,128)(2,1)S(1)}, u32[]{:S(2)}, u32[]{:S(2)}) collective-permute-start(bf16[256,384]{1,0:T(8,128)(2,1)S(1)} %get-tuple-element.55), channel_id=1, source_target_pairs={{0,4},{2,6},{4,0},{6,2},{8,12},{10,14},{12,8},{14,10},{16,20},{18,... | collective-permute-start | bytes 589832 | tf_op jit(solution)/shard_map/ppermute | solution.py:32
  45.7 9.1 %collective-permute-start.14 = (bf16[256,384]{1,0:T(8,128)(2,1)S(1)}, bf16[256,384]{1,0:T(8,128)(2,1)S(1)}, u32[]{:S(2)}, u32[]{:S(2)}) collective-permute-start(bf16[256,384]{1,0:T(8,128)(2,1)S(1)} %get-tuple-element.56), channel_id=1, source_target_pairs={{0,6},{2,4},{4,2},{6,0},{8,14},{10,12},{12,10},{14,8},{16,22},{18,... | collective-permute-start | bytes 589832 | tf_op jit(solution)/shard_map/ppermute | solution.py:32
  47.1 8.7 %collective-permute-start.16 = (bf16[256,128]{1,0:T(8,128)(2,1)S(1)}, bf16[256,128]{1,0:T(8,128)(2,1)S(1)}, u32[]{:S(2)}, u32[]{:S(2)}) collective-permute-start(bf16[256,128]{1,0:T(8,128)(2,1)S(1)} %get-tuple-element.61), channel_id=1, source_target_pairs={{0,2},{2,0},{4,6},{6,4},{8,10},{10,8},{12,14},{14,12},{16,18},{18,... | collective-permute-start | bytes 196616 | tf_op jit(solution)/shard_map/ppermute | solution.py:32
  48.8 7.0 %collective-permute-start.17 = (bf16[256,128]{1,0:T(8,128)(2,1)S(1)}, bf16[256,128]{1,0:T(8,128)(2,1)S(1)}, u32[]{:S(2)}, u32[]{:S(2)}) collective-permute-start(bf16[256,128]{1,0:T(8,128)(2,1)S(1)} %get-tuple-element.62), channel_id=1, source_target_pairs={{0,4},{2,6},{4,0},{6,2},{8,12},{10,14},{12,8},{14,10},{16,20},{18,... | collective-permute-start | bytes 196616 | tf_op jit(solution)/shard_map/ppermute | solution.py:32
  51.3 5.2 %collective-permute-start.18 = (bf16[256,128]{1,0:T(8,128)(2,1)S(1)}, bf16[256,128]{1,0:T(8,128)(2,1)S(1)}, u32[]{:S(2)}, u32[]{:S(2)}) collective-permute-start(bf16[256,128]{1,0:T(8,128)(2,1)S(1)} %get-tuple-element.63), channel_id=1, source_target_pairs={{0,6},{2,4},{4,2},{6,0},{8,14},{10,12},{12,10},{14,8},{16,22},{18,... | collective-permute-start | bytes 196616 | tf_op jit(solution)/shard_map/ppermute | solution.py:32

commit v16 on v12

--- a/solution.py
+++ b/solution.py
@@ -102,7 +102,7 @@
 def head_product(parts, part, out_weight, layer_cotangent, before):
     tokens, depth = layer_cotangent.shape
     rows = out_weight.shape[0] // parts
-    tile = min(rows, 512)
+    tile = min(rows, 1024)
 
     def body(w_ref, c_ref, *refs):
         first = (lax.axis_index("tp") ^ part) * rows if parts > 1 else 0

time: 57.7 us -> 57.7 us (level)
  transfers between devices with their start and end apart: 19 -> 19, of which waited for: 5 -> 5; matrix products, arithmetic and copies ran while one was open for 0% -> 0% of each run, Pallas kernels for 29% -> 28%
where the time goes in v16:
time: 57.7 us; the launch traced here: 57.3 us
  starting transfers between devices  25.6 us (44%)
  Pallas kernels  19 us (33%)
  waiting for transfers between devices  10.5 us (18%)
  local copies, waits for them, and re-layouts  1.28 us (2%)
  between operations  0.85 us (1%)
    ppermute x16, starting transfers between devices, swapped(): lax.ppermute(value, axis, [(source, source ^ bits) for source in range(co...  19.6 us
    pallas_call x15, Pallas kernels, run(): pl.pallas_call(body, out_shape=tuple(outs), in_specs=specs or [SMEM if a....  19 us
    ppermute x16, waiting for transfers between devices, swapped(): lax.ppermute(value, axis, [(source, source ^ bits) for source in range(co...  8.43 us
    ppermute x3, starting transfers between devices, shifted(): lax.ppermute(value, axis, [(source, source + steps) for source in range(l...  6.02 us
    ppermute x3, waiting for transfers between devices, shifted(): lax.ppermute(value, axis, [(source, source + steps) for source in range(l...  2.09 us
    unnamed x14, local copies, waits for them, and re-layouts  1.28 us
  transfers between devices with their start and end apart: 19, of which 5 were waited for; matrix products, arithmetic and copies ran while one was open for 0% of the time, Pallas kernels for 28%

profile of v16, /device:TPU:24, one launch (start us, length us, event | category | flops | bytes accessed | tf_op | source)
XLA Modules:
  0.0 57.3 jit_solution(6043277274256342973)
XLA Ops:
  0.7 0.9 %copy-done.3 = bf16[256,512]{1,0:T(8,128)(2,1)S(1)} copy-done((bf16[256,512]{1,0:T(8,128)(2,1)S(1)}, bf16[256,512]{1,0:T(8,128)(2,1)}, u32[]{:S(2)}) %copy-start.3) | copy-done | bytes 262168
  1.8 1.6 %collective-permute-start = (bf16[256,256]{1,0:T(8,128)(2,1)S(1)}, bf16[256,256]{1,0:T(8,128)(2,1)S(1)}, u32[]{:S(2)}, u32[]{:S(2)}) collective-permute-start(bf16[256,256]{1,0:T(8,128)(2,1)S(1)} %get-tuple-element.36), channel_id=1, source_target_pairs={{0,2},{2,0},{4,6},{6,4},{8,10},{10,8},{12,14},{14,12},{16,18},{18,... | collective-permute-start | bytes 393224 | tf_op jit(solution)/shard_map/ppermute | solution.py:32
  3.3 1.5 %collective-permute-start.1 = (bf16[256,256]{1,0:T(8,128)(2,1)S(1)}, bf16[256,256]{1,0:T(8,128)(2,1)S(1)}, u32[]{:S(2)}, u32[]{:S(2)}) collective-permute-start(bf16[256,256]{1,0:T(8,128)(2,1)S(1)} %get-tuple-element.37), channel_id=1, source_target_pairs={{0,4},{2,6},{4,0},{6,2},{8,12},{10,14},{12,8},{14,10},{16,20},{18,... | collective-permute-start | bytes 393224 | tf_op jit(solution)/shard_map/ppermute | solution.py:32
  4.8 0.5 collective-permute-start.2
  5.7 1.7 %shard_map.79.refs_4_.refs_1_ = bf16[1024,256]{1,0:T(8,128)(2,1)S(1)} custom-call(bf16[2048,2688]{1,0:T(8,128)(2,1)S(1)} %bitcast.1, bf16[256,2688]{1,0:T(8,128)(2,1)S(1)} %copy-done, bf16[256,256]{1,0:T(8,128)(2,1)S(1)} %get-tuple-element.39.refs_0_), custom_call_target="tpu_custom_call" | custom-call | flops 1409286144 | bytes 13041664 | tf_op jit(solution)/shard_map/pallas_call | solution.py:39
  7.5 3.6 %collective-permute-done.1.refs_2_ = bf16[256,256]{1,0:T(8,128)(2,1)S(1)} collective-permute-done((bf16[256,256]{1,0:T(8,128)(2,1)S(1)}, bf16[256,256]{1,0:T(8,128)(2,1)S(1)}, u32[]{:S(2)}, u32[]{:S(2)}) %collective-permute-start.1) | collective-permute-done | bytes 131104 | tf_op jit(solution)/shard_map/ppermute | solution.py:32
  11.2 1.3 %collective-permute-start.3 = (bf16[4,256,256]{2,1,0:T(8,128)(2,1)S(1)}, bf16[4,256,256]{2,1,0:T(8,128)(2,1)S(1)}, u32[]{:S(2)}, u32[]{:S(2)}) collective-permute-start(bf16[4,256,256]{2,1,0:T(8,128)(2,1)S(1)} %shard_map.80.refs_0_.refs_2_.own_ref), channel_id=1, source_target_pairs={{0,8},{2,10},{4,12},{6,14},{8,16},{10,18},{12,20},{14,22},{16,24},... | collective-permute-start | bytes 1572872 | tf_op jit(solution)/shard_map/ppermute | solution.py:27
  12.5 1.3 %collective-permute-start.4 = (bf16[256,256]{1,0:T(8,128)(2,1)S(1)}, bf16[256,256]{1,0:T(8,128)(2,1)S(1)}, u32[]{:S(2)}, u32[]{:S(2)}) collective-permute-start(bf16[256,256]{1,0:T(8,128)(2,1)S(1)} %get-tuple-element.40), channel_id=1, source_target_pairs={{0,2},{2,0},{4,6},{6,4},{8,10},{10,8},{12,14},{14,12},{16,18},{18,... | collective-permute-start | bytes 393224 | tf_op jit(solution)/shard_map/ppermute | solution.py:32
  13.7 0.8 %collective-permute-start.5 = (bf16[256,256]{1,0:T(8,128)(2,1)S(1)}, bf16[256,256]{1,0:T(8,128)(2,1)S(1)}, u32[]{:S(2)}, u32[]{:S(2)}) collective-permute-start(bf16[256,256]{1,0:T(8,128)(2,1)S(1)} %get-tuple-element.41), channel_id=1, source_target_pairs={{0,4},{2,6},{4,0},{6,2},{8,12},{10,14},{12,8},{14,10},{16,20},{18,... | collective-permute-start | bytes 393224 | tf_op jit(solution)/shard_map/ppermute | solution.py:32
  14.6 1.4 %collective-permute-start.6 = (bf16[256,256]{1,0:T(8,128)(2,1)S(1)}, bf16[256,256]{1,0:T(8,128)(2,1)S(1)}, u32[]{:S(2)}, u32[]{:S(2)}) collective-permute-start(bf16[256,256]{1,0:T(8,128)(2,1)S(1)} %get-tuple-element.42), channel_id=1, source_target_pairs={{0,6},{2,4},{4,2},{6,0},{8,14},{10,12},{12,10},{14,8},{16,22},{18,... | collective-permute-start | bytes 393224 | tf_op jit(solution)/shard_map/ppermute | solution.py:32
  16.0 1.7 %shard_map.83.refs_0_ = bf16[1024,256]{1,0:T(8,128)(2,1)S(1)} custom-call(bf16[2048,2688]{1,0:T(8,128)(2,1)S(1)} %bitcast.1, bf16[256,2688]{1,0:T(8,128)(2,1)S(1)} %copy-done, bf16[4,256,256]{2,1,0:T(8,128)(2,1)S(1)} %shard_map.80.refs_0_.refs_2_.own_ref, bf16[1024,256]{1,0:T(8,128)(2,1)S(1)} %shard_map.79.refs_4_.refs_1_), custom_call_target="tpu_custom_call" | custom-call | flops 1409286144 | bytes 13959168 | tf_op jit(solution)/shard_map/pallas_call | solution.py:39
  17.9 1.3 %collective-permute-start.8 = (bf16[256,256]{1,0:T(8,128)(2,1)S(1)}, bf16[256,256]{1,0:T(8,128)(2,1)S(1)}, u32[]{:S(2)}, u32[]{:S(2)}) collective-permute-start(bf16[256,256]{1,0:T(8,128)(2,1)S(1)} %get-tuple-element.46), channel_id=1, source_target_pairs={{0,2},{2,0},{4,6},{6,4},{8,10},{10,8},{12,14},{14,12},{16,18},{18,... | collective-permute-start | bytes 393224 | tf_op jit(solution)/shard_map/ppermute | solution.py:32
  19.1 1.2 %collective-permute-start.9 = (bf16[256,256]{1,0:T(8,128)(2,1)S(1)}, bf16[256,256]{1,0:T(8,128)(2,1)S(1)}, u32[]{:S(2)}, u32[]{:S(2)}) collective-permute-start(bf16[256,256]{1,0:T(8,128)(2,1)S(1)} %get-tuple-element.47), channel_id=1, source_target_pairs={{0,4},{2,6},{4,0},{6,2},{8,12},{10,14},{12,8},{14,10},{16,20},{18,... | collective-permute-start | bytes 393224 | tf_op jit(solution)/shard_map/ppermute | solution.py:32
  20.3 2.8 %collective-permute-start.10 = (bf16[256,256]{1,0:T(8,128)(2,1)S(1)}, bf16[256,256]{1,0:T(8,128)(2,1)S(1)}, u32[]{:S(2)}, u32[]{:S(2)}) collective-permute-start(bf16[256,256]{1,0:T(8,128)(2,1)S(1)} %get-tuple-element.48), channel_id=1, source_target_pairs={{0,6},{2,4},{4,2},{6,0},{8,14},{10,12},{12,10},{14,8},{16,22},{18,... | collective-permute-start | bytes 393224 | tf_op jit(solution)/shard_map/ppermute | solution.py:32
  23.3 2.1 %collective-permute-done.3.refs_1_.refs_0_ = bf16[4,256,256]{2,1,0:T(8,128)(2,1)S(1)} collective-permute-done((bf16[4,256,256]{2,1,0:T(8,128)(2,1)S(1)}, bf16[4,256,256]{2,1,0:T(8,128)(2,1)S(1)}, u32[]{:S(2)}, u32[]{:S(2)}) %collective-permute-start.3) | collective-permute-done | bytes 524320 | tf_op jit(solution)/shard_map/ppermute | solution.py:27
  25.4 3.8 %shard_map.82 = (bf16[1,4,5,256,512]{4,3,2,1,0:T(8,128)(2,1)S(1)}, f32[1,4,1,512]{3,2,1,0:T(1,128)S(1)}) custom-call(bf16[4,256,256]{2,1,0:T(8,128)(2,1)S(1)} %shard_map.80.refs_0_.refs_2_.own_ref, bf16[4,256,256]{2,1,0:T(8,128)(2,1)S(1)} %collective-permute-done.3.refs_1_.refs_0_, bf16[1,4,128,512]{3,2,1,0:T(8,128)(2,1)S(1)} %shard_map.81.refs_2_.qt_ref), custom_call_target="tpu_custom_call" | custom-call | flops 671088640 | bytes 6823936 | tf_op jit(solution)/shard_map/pallas_call | solution.py:39
  29.2 2.2 %shard_map.85 = (bf16[1,4,128,512]{3,2,1,0:T(8,128)(2,1)S(1)}, f32[4,256,128]{2,1,0:T(8,128)S(1)}, bf16[4,256,128]{2,1,0:T(8,128)(2,1)S(1)}) custom-call(bf16[1,4,5,256,512]{4,3,2,1,0:T(8,128)(2,1)S(1)} %get-tuple-element.43.e_ref, f32[1,4,1,512]{3,2,1,0:T(1,128)S(1)} %get-tuple-element.44.inverse_ref, bf16[256,256]{1,0:T(8,128)(2,1)S(1)} %get-tuple-element.45.refs_0_, ...), custom_call_target="tpu_custom_call" | custom-call | flops 671088640 | bytes 7086080 | tf_op jit(solution)/shard_map/pallas_call | solution.py:39
  31.5 2.4 %collective-permute-start.11 = (bf16[4,256,128]{2,1,0:T(8,128)(2,1)S(1)}, bf16[4,256,128]{2,1,0:T(8,128)(2,1)S(1)}, u32[]{:S(2)}, u32[]{:S(2)}) collective-permute-start(bf16[4,256,128]{2,1,0:T(8,128)(2,1)S(1)} %get-tuple-element.52), channel_id=1, source_target_pairs={{8,0},{10,2},{12,4},{14,6},{16,8},{18,10},{20,12},{22,14},{24,16},... | collective-permute-start | bytes 786440 | tf_op jit(solution)/shard_map/ppermute | solution.py:27
  33.8 5.4 %shard_map.86 = (bf16[1,4,5,256,512]{4,3,2,1,0:T(8,128)(2,1)S(1)}, f32[4,256,128]{2,1,0:T(8,128)S(1)}, bf16[4,256,128]{2,1,0:T(8,128)(2,1)S(1)}) custom-call(bf16[1,4,5,256,512]{4,3,2,1,0:T(8,128)(2,1)S(1)} %get-tuple-element.43.e_ref, f32[1,4,1,512]{3,2,1,0:T(1,128)S(1)} %get-tuple-element.44.inverse_ref, ...), custom_call_target="tpu_custom_call" | custom-call | flops 1342177280 | bytes 13377536 | tf_op jit(solution)/shard_map/pallas_call | solution.py:39
  39.2 2.4 %collective-permute-start.15 = (bf16[4,256,128]{2,1,0:T(8,128)(2,1)S(1)}, bf16[4,256,128]{2,1,0:T(8,128)(2,1)S(1)}, u32[]{:S(2)}, u32[]{:S(2)}) collective-permute-start(bf16[4,256,128]{2,1,0:T(8,128)(2,1)S(1)} %get-tuple-element.59), channel_id=1, source_target_pairs={{8,0},{10,2},{12,4},{14,6},{16,8},{18,10},{20,12},{22,14},{24,16},... | collective-permute-start | bytes 786440 | tf_op jit(solution)/shard_map/ppermute | solution.py:27
  41.6 2.0 %shard_map.87 = (bf16[256,384]{1,0:T(8,128)(2,1)S(1)}, bf16[256,384]{1,0:T(8,128)(2,1)S(1)}, bf16[256,384]{1,0:T(8,128)(2,1)S(1)}, bf16[256,384]{1,0:T(8,128)(2,1)S(1)}) custom-call(bf16[1,4,5,256,512]{4,3,2,1,0:T(8,128)(2,1)S(1)} %get-tuple-element.50.ds_ref, f32[1,4,1,512]{3,2,1,0:T(1,128)S(1)} %get-tuple-element.44.inverse_ref, ...), custom_call_target="tpu_custom_call" | custom-call | flops 671088640 | bytes 7872512 | tf_op jit(solution)/shard_map/pallas_call | solution.py:39
  43.5 1.7 %collective-permute-start.12 = (bf16[256,384]{1,0:T(8,128)(2,1)S(1)}, bf16[256,384]{1,0:T(8,128)(2,1)S(1)}, u32[]{:S(2)}, u32[]{:S(2)}) collective-permute-start(bf16[256,384]{1,0:T(8,128)(2,1)S(1)} %get-tuple-element.54), channel_id=1, source_target_pairs={{0,2},{2,0},{4,6},{6,4},{8,10},{10,8},{12,14},{14,12},{16,18},{18,... | collective-permute-start | bytes 589832 | tf_op jit(solution)/shard_map/ppermute | solution.py:32
  45.2 0.5 collective-permute-start.13
  45.7 1.3 %collective-permute-start.14 = (bf16[256,384]{1,0:T(8,128)(2,1)S(1)}, bf16[256,384]{1,0:T(8,128)(2,1)S(1)}, u32[]{:S(2)}, u32[]{:S(2)}) collective-permute-start(bf16[256,384]{1,0:T(8,128)(2,1)S(1)} %get-tuple-element.56), channel_id=1, source_target_pairs={{0,6},{2,4},{4,2},{6,0},{8,14},{10,12},{12,10},{14,8},{16,22},{18,... | collective-permute-start | bytes 589832 | tf_op jit(solution)/shard_map/ppermute | solution.py:32
  47.1 1.7 %collective-permute-start.16 = (bf16[256,128]{1,0:T(8,128)(2,1)S(1)}, bf16[256,128]{1,0:T(8,128)(2,1)S(1)}, u32[]{:S(2)}, u32[]{:S(2)}) collective-permute-start(bf16[256,128]{1,0:T(8,128)(2,1)S(1)} %get-tuple-element.61), channel_id=1, source_target_pairs={{0,2},{2,0},{4,6},{6,4},{8,10},{10,8},{12,14},{14,12},{16,18},{18,... | collective-permute-start | bytes 196616 | tf_op jit(solution)/shard_map/ppermute | solution.py:32
  48.9 0.5 collective-permute-start.17
  49.4 2.0 %collective-permute-done.12.refs_1_ = bf16[256,384]{1,0:T(8,128)(2,1)S(1)} collective-permute-done((bf16[256,384]{1,0:T(8,128)(2,1)S(1)}, bf16[256,384]{1,0:T(8,128)(2,1)S(1)}, u32[]{:S(2)}, u32[]{:S(2)}) %collective-permute-start.12) | collective-permute-done | bytes 196640 | tf_op jit(solution)/shard_map/ppermute | solution.py:32
  51.4 1.4 %collective-permute-start.18 = (bf16[256,128]{1,0:T(8,128)(2,1)S(1)}, bf16[256,128]{1,0:T(8,128)(2,1)S(1)}, u32[]{:S(2)}, u32[]{:S(2)}) collective-permute-start(bf16[256,128]{1,0:T(8,128)(2,1)S(1)} %get-tuple-element.63), channel_id=1, source_target_pairs={{0,6},{2,4},{4,2},{6,0},{8,14},{10,12},{12,10},{14,8},{16,22},{18,... | collective-permute-start | bytes 196616 | tf_op jit(solution)/shard_map/ppermute | solution.py:32
  52.7 2.2 %collective-permute-done.13.refs_2_ = bf16[256,384]{1,0:T(8,128)(2,1)S(1)} collective-permute-done((bf16[256,384]{1,0:T(8,128)(2,1)S(1)}, bf16[256,384]{1,0:T(8,128)(2,1)S(1)}, u32[]{:S(2)}, u32[]{:S(2)}) %collective-permute-start.13) | collective-permute-done | bytes 196640 | tf_op jit(solution)/shard_map/ppermute | solution.py:32
  54.9 1.0 %shard_map.88 = (bf16[256,1024]{1,0:T(8,128)(2,1)}, bf16[256,512]{1,0:T(8,128)(2,1)}, f32[8,128]{1,0:T(8,128)S(1)}) custom-call(bf16[256,384]{1,0:T(8,128)(2,1)S(1)} %get-tuple-element.53.refs_0_, bf16[256,384]{1,0:T(8,128)(2,1)S(1)} %collective-permute-done.12.refs_1_, bf16[256,384]{1,0:T(8,128)(2,1)S(1)} %collective-permute-done.13.refs_2_, ...), custom_call_target="tpu_custom_call" | custom-call | bytes 1576960 | tf_op jit(solution)/shard_map/pallas_call | solution.py:39
  55.9 0.6 %collective-permute-done.18.refs_3_ = bf16[256,128]{1,0:T(8,128)(2,1)S(1)} collective-permute-done((bf16[256,128]{1,0:T(8,128)(2,1)S(1)}, bf16[256,128]{1,0:T(8,128)(2,1)S(1)}, u32[]{:S(2)}, u32[]{:S(2)}) %collective-permute-start.18) | collective-permute-done | bytes 65568 | tf_op jit(solution)/shard_map/ppermute | solution.py:32
  56.5 0.8 %shard_map.90 = (bf16[256,512]{1,0:T(8,128)(2,1)}, f32[8,128]{1,0:T(8,128)}) custom-call(bf16[256,128]{1,0:T(8,128)(2,1)S(1)} %get-tuple-element.60.refs_0_, bf16[256,128]{1,0:T(8,128)(2,1)S(1)} %collective-permute-done.16.refs_1_, bf16[256,128]{1,0:T(8,128)(2,1)S(1)} %collective-permute-done.17.refs_2_, ...), custom_call_target="tpu_custom_call" | custom-call | bytes 532480 | tf_op jit(solution)/shard_map/pallas_call | solution.py:39
  (36 shorter events, 1.1 us)
Async XLA Ops:
  0.6 1.0 %copy-start.3 = (bf16[256,512]{1,0:T(8,128)(2,1)S(1)}, bf16[256,512]{1,0:T(8,128)(2,1)}, u32[]{:S(2)}) copy-start(bf16[256,512]{1,0:T(8,128)(2,1)} %v_ref.1) | copy-start | bytes 786436
  0.6 1.0 %copy-start.2 = (bf16[256,512]{1,0:T(8,128)(2,1)S(1)}, bf16[256,512]{1,0:T(8,128)(2,1)}, u32[]{:S(2)}) copy-start(bf16[256,512]{1,0:T(8,128)(2,1)} %k_ref.1) | copy-start | bytes 786436
  0.7 4.7 %slice-start = ((s8[11010048]{0:T(1024)(128)(4,1)}), s8[4194304]{0:T(1024)(128)(4,1)S(1)}, s32[]{:S(2)}) async-start(s8[11010048]{0:T(1024)(128)(4,1)} %bitcast), calls=%async_computation | async-start | bytes 8388608
  0.7 4.7 %slice-start.1 = ((s8[11010048]{0:T(1024)(128)(4,1)}), s8[4194304]{0:T(1024)(128)(4,1)S(1)}, s32[]{:S(2)}) async-start(s8[11010048]{0:T(1024)(128)(4,1)} %bitcast), calls=%async_computation.1 | async-start | bytes 8388608
  1.7 3.7 %copy-start.1 = (bf16[256,1024]{1,0:T(8,128)(2,1)S(1)}, bf16[256,1024]{1,0:T(8,128)(2,1)}, u32[]{:S(2)}) copy-start(bf16[256,1024]{1,0:T(8,128)(2,1)} %q_ref.1) | copy-start | bytes 1572868
  1.7 3.8 %slice-start.2 = ((s8[11010048]{0:T(1024)(128)(4,1)}), s8[2621440]{0:T(1024)(128)(4,1)S(1)}, s32[]{:S(2)}) async-start(s8[11010048]{0:T(1024)(128)(4,1)} %bitcast), calls=%async_computation.2 | async-start | bytes 5242880
  1.7 4.0 %copy-start = (bf16[256,2688]{1,0:T(8,128)(2,1)S(1)}, bf16[256,2688]{1,0:T(8,128)(2,1)}, u32[]{:S(2)}) copy-start(bf16[256,2688]{1,0:T(8,128)(2,1)} %c_ref.3) | copy-start | bytes 4128772
  1.8 5.7 %collective-permute-start = (bf16[256,256]{1,0:T(8,128)(2,1)S(1)}, bf16[256,256]{1,0:T(8,128)(2,1)S(1)}, u32[]{:S(2)}, u32[]{:S(2)}) collective-permute-start(bf16[256,256]{1,0:T(8,128)(2,1)S(1)} %get-tuple-element.36), channel_id=1, source_target_pairs={{0,2},{2,0},{4,6},{6,4},{8,10},{10,8},{12,14},{14,12},{16,18},{18,... | collective-permute-start | bytes 393224 | tf_op jit(solution)/shard_map/ppermute | solution.py:32
  3.3 7.8 %collective-permute-start.1 = (bf16[256,256]{1,0:T(8,128)(2,1)S(1)}, bf16[256,256]{1,0:T(8,128)(2,1)S(1)}, u32[]{:S(2)}, u32[]{:S(2)}) collective-permute-start(bf16[256,256]{1,0:T(8,128)(2,1)S(1)} %get-tuple-element.37), channel_id=1, source_target_pairs={{0,4},{2,6},{4,0},{6,2},{8,12},{10,14},{12,8},{14,10},{16,20},{18,... | collective-permute-start | bytes 393224 | tf_op jit(solution)/shard_map/ppermute | solution.py:32
  4.8 6.3 %collective-permute-start.2 = (bf16[256,256]{1,0:T(8,128)(2,1)S(1)}, bf16[256,256]{1,0:T(8,128)(2,1)S(1)}, u32[]{:S(2)}, u32[]{:S(2)}) collective-permute-start(bf16[256,256]{1,0:T(8,128)(2,1)S(1)} %get-tuple-element.38), channel_id=1, source_target_pairs={{0,6},{2,4},{4,2},{6,0},{8,14},{10,12},{12,10},{14,8},{16,22},{18,... | collective-permute-start | bytes 393224 | tf_op jit(solution)/shard_map/ppermute | solution.py:32
  7.4 10.3 %collective-permute-start.7 = (bf16[1024,256]{1,0:T(8,128)(2,1)S(1)}, bf16[1024,256]{1,0:T(8,128)(2,1)S(1)}, u32[]{:S(2)}, u32[]{:S(2)}) collective-permute-start(bf16[1024,256]{1,0:T(8,128)(2,1)S(1)} %shard_map.79.refs_4_.refs_1_), channel_id=1, source_target_pairs={{0,1},{1,0},{2,3},{3,2},{4,5},{5,4},{6,7},{7,6},{8,9},{9,8},{10,11... | collective-permute-start | bytes 1572872 | tf_op jit(solution)/shard_map/ppermute | solution.py:32
  11.2 14.3 %collective-permute-start.3 = (bf16[4,256,256]{2,1,0:T(8,128)(2,1)S(1)}, bf16[4,256,256]{2,1,0:T(8,128)(2,1)S(1)}, u32[]{:S(2)}, u32[]{:S(2)}) collective-permute-start(bf16[4,256,256]{2,1,0:T(8,128)(2,1)S(1)} %shard_map.80.refs_0_.refs_2_.own_ref), channel_id=1, source_target_pairs={{0,8},{2,10},{4,12},{6,14},{8,16},{10,18},{12,20},{14,22},{16,24},... | collective-permute-start | bytes 1572872 | tf_op jit(solution)/shard_map/ppermute | solution.py:27
  12.5 6.7 %collective-permute-start.4 = (bf16[256,256]{1,0:T(8,128)(2,1)S(1)}, bf16[256,256]{1,0:T(8,128)(2,1)S(1)}, u32[]{:S(2)}, u32[]{:S(2)}) collective-permute-start(bf16[256,256]{1,0:T(8,128)(2,1)S(1)} %get-tuple-element.40), channel_id=1, source_target_pairs={{0,2},{2,0},{4,6},{6,4},{8,10},{10,8},{12,14},{14,12},{16,18},{18,... | collective-permute-start | bytes 393224 | tf_op jit(solution)/shard_map/ppermute | solution.py:32
  13.7 6.6 %collective-permute-start.5 = (bf16[256,256]{1,0:T(8,128)(2,1)S(1)}, bf16[256,256]{1,0:T(8,128)(2,1)S(1)}, u32[]{:S(2)}, u32[]{:S(2)}) collective-permute-start(bf16[256,256]{1,0:T(8,128)(2,1)S(1)} %get-tuple-element.41), channel_id=1, source_target_pairs={{0,4},{2,6},{4,0},{6,2},{8,12},{10,14},{12,8},{14,10},{16,20},{18,... | collective-permute-start | bytes 393224 | tf_op jit(solution)/shard_map/ppermute | solution.py:32
  14.6 8.6 %collective-permute-start.6 = (bf16[256,256]{1,0:T(8,128)(2,1)S(1)}, bf16[256,256]{1,0:T(8,128)(2,1)S(1)}, u32[]{:S(2)}, u32[]{:S(2)}) collective-permute-start(bf16[256,256]{1,0:T(8,128)(2,1)S(1)} %get-tuple-element.42), channel_id=1, source_target_pairs={{0,6},{2,4},{4,2},{6,0},{8,14},{10,12},{12,10},{14,8},{16,22},{18,... | collective-permute-start | bytes 393224 | tf_op jit(solution)/shard_map/ppermute | solution.py:32
  17.9 11.4 %collective-permute-start.8 = (bf16[256,256]{1,0:T(8,128)(2,1)S(1)}, bf16[256,256]{1,0:T(8,128)(2,1)S(1)}, u32[]{:S(2)}, u32[]{:S(2)}) collective-permute-start(bf16[256,256]{1,0:T(8,128)(2,1)S(1)} %get-tuple-element.46), channel_id=1, source_target_pairs={{0,2},{2,0},{4,6},{6,4},{8,10},{10,8},{12,14},{14,12},{16,18},{18,... | collective-permute-start | bytes 393224 | tf_op jit(solution)/shard_map/ppermute | solution.py:32
  19.1 10.1 %collective-permute-start.9 = (bf16[256,256]{1,0:T(8,128)(2,1)S(1)}, bf16[256,256]{1,0:T(8,128)(2,1)S(1)}, u32[]{:S(2)}, u32[]{:S(2)}) collective-permute-start(bf16[256,256]{1,0:T(8,128)(2,1)S(1)} %get-tuple-element.47), channel_id=1, source_target_pairs={{0,4},{2,6},{4,0},{6,2},{8,12},{10,14},{12,8},{14,10},{16,20},{18,... | collective-permute-start | bytes 393224 | tf_op jit(solution)/shard_map/ppermute | solution.py:32
  20.3 8.9 %collective-permute-start.10 = (bf16[256,256]{1,0:T(8,128)(2,1)S(1)}, bf16[256,256]{1,0:T(8,128)(2,1)S(1)}, u32[]{:S(2)}, u32[]{:S(2)}) collective-permute-start(bf16[256,256]{1,0:T(8,128)(2,1)S(1)} %get-tuple-element.48), channel_id=1, source_target_pairs={{0,6},{2,4},{4,2},{6,0},{8,14},{10,12},{12,10},{14,8},{16,22},{18,... | collective-permute-start | bytes 393224 | tf_op jit(solution)/shard_map/ppermute | solution.py:32
  31.5 10.1 %collective-permute-start.11 = (bf16[4,256,128]{2,1,0:T(8,128)(2,1)S(1)}, bf16[4,256,128]{2,1,0:T(8,128)(2,1)S(1)}, u32[]{:S(2)}, u32[]{:S(2)}) collective-permute-start(bf16[4,256,128]{2,1,0:T(8,128)(2,1)S(1)} %get-tuple-element.52), channel_id=1, source_target_pairs={{8,0},{10,2},{12,4},{14,6},{16,8},{18,10},{20,12},{22,14},{24,16},... | collective-permute-start | bytes 786440 | tf_op jit(solution)/shard_map/ppermute | solution.py:27
  39.2 7.9 %collective-permute-start.15 = (bf16[4,256,128]{2,1,0:T(8,128)(2,1)S(1)}, bf16[4,256,128]{2,1,0:T(8,128)(2,1)S(1)}, u32[]{:S(2)}, u32[]{:S(2)}) collective-permute-start(bf16[4,256,128]{2,1,0:T(8,128)(2,1)S(1)} %get-tuple-element.59), channel_id=1, source_target_pairs={{8,0},{10,2},{12,4},{14,6},{16,8},{18,10},{20,12},{22,14},{24,16},... | collective-permute-start | bytes 786440 | tf_op jit(solution)/shard_map/ppermute | solution.py:27
  43.5 7.8 %collective-permute-start.12 = (bf16[256,384]{1,0:T(8,128)(2,1)S(1)}, bf16[256,384]{1,0:T(8,128)(2,1)S(1)}, u32[]{:S(2)}, u32[]{:S(2)}) collective-permute-start(bf16[256,384]{1,0:T(8,128)(2,1)S(1)} %get-tuple-element.54), channel_id=1, source_target_pairs={{0,2},{2,0},{4,6},{6,4},{8,10},{10,8},{12,14},{14,12},{16,18},{18,... | collective-permute-start | bytes 589832 | tf_op jit(solution)/shard_map/ppermute | solution.py:32
  45.2 9.6 %collective-permute-start.13 = (bf16[256,384]{1,0:T(8,128)(2,1)S(1)}, bf16[256,384]{1,0:T(8,128)(2,1)S(1)}, u32[]{:S(2)}, u32[]{:S(2)}) collective-permute-start(bf16[256,384]{1,0:T(8,128)(2,1)S(1)} %get-tuple-element.55), channel_id=1, source_target_pairs={{0,4},{2,6},{4,0},{6,2},{8,12},{10,14},{12,8},{14,10},{16,20},{18,... | collective-permute-start | bytes 589832 | tf_op jit(solution)/shard_map/ppermute | solution.py:32
  45.7 9.1 %collective-permute-start.14 = (bf16[256,384]{1,0:T(8,128)(2,1)S(1)}, bf16[256,384]{1,0:T(8,128)(2,1)S(1)}, u32[]{:S(2)}, u32[]{:S(2)}) collective-permute-start(bf16[256,384]{1,0:T(8,128)(2,1)S(1)} %get-tuple-element.56), channel_id=1, source_target_pairs={{0,6},{2,4},{4,2},{6,0},{8,14},{10,12},{12,10},{14,8},{16,22},{18,... | collective-permute-start | bytes 589832 | tf_op jit(solution)/shard_map/ppermute | solution.py:32
  47.1 8.7 %collective-permute-start.16 = (bf16[256,128]{1,0:T(8,128)(2,1)S(1)}, bf16[256,128]{1,0:T(8,128)(2,1)S(1)}, u32[]{:S(2)}, u32[]{:S(2)}) collective-permute-start(bf16[256,128]{1,0:T(8,128)(2,1)S(1)} %get-tuple-element.61), channel_id=1, source_target_pairs={{0,2},{2,0},{4,6},{6,4},{8,10},{10,8},{12,14},{14,12},{16,18},{18,... | collective-permute-start | bytes 196616 | tf_op jit(solution)/shard_map/ppermute | solution.py:32
  48.9 7.0 %collective-permute-start.17 = (bf16[256,128]{1,0:T(8,128)(2,1)S(1)}, bf16[256,128]{1,0:T(8,128)(2,1)S(1)}, u32[]{:S(2)}, u32[]{:S(2)}) collective-permute-start(bf16[256,128]{1,0:T(8,128)(2,1)S(1)} %get-tuple-element.62), channel_id=1, source_target_pairs={{0,4},{2,6},{4,0},{6,2},{8,12},{10,14},{12,8},{14,10},{16,20},{18,... | collective-permute-start | bytes 196616 | tf_op jit(solution)/shard_map/ppermute | solution.py:32
  51.4 5.2 %collective-permute-start.18 = (bf16[256,128]{1,0:T(8,128)(2,1)S(1)}, bf16[256,128]{1,0:T(8,128)(2,1)S(1)}, u32[]{:S(2)}, u32[]{:S(2)}) collective-permute-start(bf16[256,128]{1,0:T(8,128)(2,1)S(1)} %get-tuple-element.63), channel_id=1, source_target_pairs={{0,6},{2,4},{4,2},{6,0},{8,14},{10,12},{12,10},{14,8},{16,22},{18,... | collective-permute-start | bytes 196616 | tf_op jit(solution)/shard_map/ppermute | solution.py:32
